TPU v7x, 32 devices: a whole 2x2x4 slice. The times are simulated.
32 devices in a mesh: groups: 2 (over y), seq: 8 (over z, x), branch: 2 (over core).
Axes of the slice: x: 2, y: 2, z: 4, core: 2. Of those that a mesh axis runs over, the one named last changes fastest.
Arguments:
- queries: bfloat16 [2, 256, 1536], P('branch', ('groups', 'seq')), parts along dimension 1, may hold values from -8 to 8
- key_rows: bfloat16 [2, 256, 1536], P('branch', ('groups', 'seq')), parts along dimension 1, may hold values from -8 to 8
- value_rows: bfloat16 [2, 256, 1536], P('branch', ('groups', 'seq')), parts along dimension 1, may hold values from -40 to 40
- counts: int32 [16], P('groups'), parts along dimension 0, may hold values from 1 to 16, 112 in all
- head_of: int32 [8, 2], replicated, may hold values from 0 to 11, as said below
- out_weight: bfloat16 [1536, 1536], P(None, 'branch'), may hold values from -0.15625 to 0.15625
Outputs:
- projected: bfloat16 [256, 1536], P(('groups', 'seq'), 'branch'), parts along dimension 0
- saved_logsumexp: float32 [2, 16, 2, 16, 8], P('branch', ('groups', 'seq')), parts along dimension 1
There are 2 independent parts, one for each index of `groups`. A program takes and returns all parts, laid end to end along the dimension named above; an argument that names none is the same for every part. Nothing has to cross between parts.
Inputs may be any that keep to these rules, and one draw needn't show every extreme that they name: `head_of`: each of the 12 heads is named by at least 1 entries, and one head by exactly 1.
All inputs are finite; a program needn't handle non-finite values. Where the computation divides by a largest or mean magnitude, that divisor is 1e-20 or more.
Results may differ from a plain program's by a relative error of at most 0.0063.
Values may be sent and summed in bfloat16 or wider, within the bound.
No kernel may reach another device: no remote copies, remote signals or barrier semaphores. Data moves between devices by JAX's collectives and lax.ppermute only.
A program may use at most 64 MiB of HBM per device.

v0:
```python
import functools
import math

import jax
import jax.numpy as jnp
from jax import lax
from jax.experimental import pallas as pl
from jax.experimental.pallas import tpu as pltpu
from jax.sharding import PartitionSpec as P

HEADS = 12
HDIM = 128


GUIDE_SCALE = 3.0
EPSILON = 1e-06


def partner_2(array, axis, stride):
    return lax.ppermute(array, axis, [(i, i ^ 1 << stride) for i in range(lax.axis_size(axis))])


def slot_layout(head_of):
    flat_heads = head_of.reshape(-1)
    slot_order = jnp.arange(flat_heads.shape[0], dtype=jnp.int32)
    same_head = flat_heads[:, None] == flat_heads[None, :]
    group_size = jnp.sum(same_head.astype(jnp.int32), axis=1)
    earlier = same_head & (slot_order[None, :] < slot_order[:, None])
    group_rank = jnp.sum(earlier.astype(jnp.int32), axis=1)
    return (flat_heads, group_size, group_rank)


def key_grouping(seq_count, tok_dev):
    shard_limit = max(1, 2048 // tok_dev)
    grouping = 1
    for attempt in range(16):
        if grouping * 2 <= shard_limit and seq_count % (grouping * 2) == 0:
            grouping = grouping * 2
    return grouping


def attend_rows(query_block, key_slot, value_slot, key_valid, key_block):
    row_count = query_block.shape[0]
    head_size = query_block.shape[1]
    block_count = key_slot.shape[0] // key_block
    scale_factor = 1.0 / math.sqrt(head_size)

    def fold_block(block_id, state_in):
        top_score, weight_sum, summed = state_in
        scores = (
            jnp.einsum("qd,kd->qk", query_block, key_slot, preferred_element_type=jnp.float32)
            * scale_factor
        )
        scores = jnp.where(key_valid[None, :], scores, -jnp.inf)
        new_top = jnp.maximum(top_score, jnp.max(scores, axis=1))
        fading = jnp.exp(top_score - new_top)
        weights = jnp.exp(scores - new_top[:, None])
        weight_sum = weight_sum * fading + jnp.sum(weights, axis=1)
        summed = summed * fading[:, None] + jnp.dot(
            weights.astype(jnp.bfloat16), value_slot, preferred_element_type=jnp.float32
        )
        return (new_top, weight_sum, summed)

    start_state = (
        jnp.full((row_count,), -jnp.inf, jnp.float32),
        jnp.zeros((row_count,), jnp.float32),
        jnp.zeros((row_count, head_size), jnp.float32),
    )
    top_score, weight_sum, summed = lax.fori_loop(0, block_count, fold_block, start_state)
    return (summed / weight_sum[:, None], top_score + jnp.log(weight_sum))


def serve_slots(query_items, mask_items, key_recv, value_recv, key_valid, key_block):
    source_count, slot_count, item_count, head_size = query_items.shape
    all_tokens = key_recv.shape[0] * key_recv.shape[2]
    per_block = max(1, 512 // source_count)
    slot_outputs = []
    slot_logsum = []
    for slot_id in range(slot_count):
        key_slot = key_recv[:, slot_id].reshape(all_tokens, head_size)
        value_slot = value_recv[:, slot_id].reshape(all_tokens, head_size)
        taken_items = min(per_block, item_count)
        query_block = query_items[:, slot_id, 0:taken_items].reshape(
            source_count * taken_items, head_size
        )
        attended, logsum = attend_rows(query_block, key_slot, value_slot, key_valid, key_block)
        pieces_out = attended.reshape(source_count, taken_items, head_size)
        pieces_sum = logsum.reshape(source_count, taken_items)
        slot_outputs.append(pieces_out)
        slot_logsum.append(pieces_sum)
    attended = jnp.stack(slot_outputs, axis=1)
    logsum = jnp.stack(slot_logsum, axis=1)
    keep_rows = mask_items > 0
    attended = jnp.where(keep_rows[:, :, :, None], attended, 0.0).astype(jnp.bfloat16)
    logsum = jnp.where(keep_rows, logsum, 0.0)
    return (attended, logsum)


def per_device_exchange(queries, key_rows, value_rows, counts, head_of, out_weight):
    seq_count = lax.axis_size("seq")
    tok_dev = queries.shape[1]
    slot_count = head_of.shape[1]
    fewest = max(1, seq_count * slot_count // (2 * HEADS))
    row_cap = (tok_dev + fewest - 1) // fewest
    my_index = lax.axis_index("seq")
    flat_heads, group_size, group_rank = slot_layout(head_of)
    row_steps = jnp.arange(row_cap, dtype=jnp.int32)
    served_rows = group_rank[:, None] + group_size[:, None] * row_steps[None, :]
    my_count = counts[my_index]
    clipped = jnp.minimum(served_rows, tok_dev - 1)
    query_grid = queries[0].reshape(tok_dev, HEADS, HDIM)
    row_live = served_rows < my_count
    query_send = query_grid[clipped, flat_heads[:, None]]
    query_send = jnp.where(row_live[:, :, None], query_send, jnp.zeros((), jnp.bfloat16)).reshape(
        seq_count, slot_count, row_cap, HDIM
    )
    mask_send = row_live.astype(jnp.bfloat16).reshape(seq_count, slot_count, row_cap)
    token_ids = jnp.arange(tok_dev, dtype=jnp.int32)
    key_grid = key_rows[0].reshape(tok_dev, HEADS, HDIM)
    value_grid = value_rows[0].reshape(tok_dev, HEADS, HDIM)
    key_send = key_grid[token_ids[None, :], flat_heads[:, None]].reshape(
        seq_count, slot_count, tok_dev, HDIM
    )
    value_send = value_grid[token_ids[None, :], flat_heads[:, None]].reshape(
        seq_count, slot_count, tok_dev, HDIM
    )
    key_valid = (token_ids[None, :] < counts[:, None]).reshape(-1)
    key_block = tok_dev * key_grouping(seq_count, tok_dev)
    query_recv, mask_recv, key_recv, value_recv = (
        lax.all_to_all(query_send, "seq", split_axis=0, concat_axis=0, tiled=True),
        lax.all_to_all(mask_send, "seq", split_axis=0, concat_axis=0, tiled=True),
        lax.all_to_all(key_send, "seq", split_axis=0, concat_axis=0, tiled=True),
        lax.all_to_all(value_send, "seq", split_axis=0, concat_axis=0, tiled=True),
    )
    attended, logsum = serve_slots(
        query_recv, mask_recv, key_recv, value_recv, key_valid, key_block
    )
    returned = lax.all_to_all(attended, "seq", split_axis=0, concat_axis=0, tiled=True)
    head_ids = jnp.arange(HEADS, dtype=jnp.int32)
    head_group = jnp.sum((flat_heads[None, :] == head_ids[:, None]).astype(jnp.int32), axis=1)
    row_rank = token_ids[:, None] % head_group[None, :]
    row_step = token_ids[:, None] // head_group[None, :]
    slot_ids = jnp.arange(flat_heads.shape[0], dtype=jnp.int32)
    matched = (flat_heads[None, None, :] == head_ids[None, :, None]) & (
        group_rank[None, None, :] == row_rank[:, :, None]
    )
    owner_slot = jnp.sum(jnp.where(matched, slot_ids[None, None, :], 0), axis=2)
    flat_index = owner_slot * row_cap + row_step
    returned_rows = returned.reshape(-1, HDIM)
    attended_home = returned_rows[flat_index].reshape(tok_dev, HEADS * HDIM)
    partner = partner_2(attended_home, "branch", 0)
    on_positive = lax.axis_index("branch") == 0
    own_value = attended_home.astype(jnp.float32)
    partner_value = partner.astype(jnp.float32)
    positive = jnp.where(on_positive, own_value, partner_value)
    negative = jnp.where(on_positive, partner_value, own_value)
    guided = GUIDE_SCALE * positive - (GUIDE_SCALE - 1.0) * negative
    magnitude = jnp.mean(jnp.abs(guided), axis=1, keepdims=True)
    normed = (guided / (magnitude + EPSILON)).astype(jnp.bfloat16)
    projected = jnp.dot(normed, out_weight, preferred_element_type=jnp.float32).astype(jnp.bfloat16)
    saved_rows = jnp.transpose(logsum, (1, 2, 0)).reshape(1, 1, slot_count, row_cap, seq_count)
    return (projected, saved_rows)


KERNEL_PARAMS = pltpu.CompilerParams(vmem_limit_bytes=16 * 1024 * 1024)


SPLIT = 2


def swap_shards(array, offset):
    pairs = [(i, i ^ offset) for i in range(lax.axis_size("seq"))]
    return lax.ppermute(array, "seq", pairs)


def set_order(shard_count):
    line = list(range(0, shard_count, SPLIT))
    return line + [offset + 1 for offset in line]


def pack_kernel(
    query_hbm,
    key_hbm,
    value_hbm,
    counts_hbm,
    head_hbm,
    own_ref,
    other_ref,
    limits_ref,
    pick_ref,
    slot_head_ref,
    counts_ref,
    head_ref,
    copy_sems,
):
    tok_dev = own_ref.shape[0] // 3
    half_width = own_ref.shape[1]
    slot_count, shard_count = head_ref.shape
    shard = lax.axis_index("seq")
    half = (shard // SPLIT) % 2
    copies = [
        pltpu.make_async_copy(counts_hbm, counts_ref, copy_sems.at[0]),
        pltpu.make_async_copy(head_hbm, head_ref, copy_sems.at[1]),
    ]
    for target, place in ((other_ref, 1 - half), (own_ref, half)):
        columns = pl.ds(pl.multiple_of(place * half_width, half_width), half_width)
        for part, source in enumerate((key_hbm, value_hbm, query_hbm)):
            rows = pl.ds(part * tok_dev, tok_dev)
            copies.append(
                pltpu.make_async_copy(
                    source.at[0, :, columns], target.at[rows, :], copy_sems.at[len(copies)]
                )
            )
    for copy in copies:
        copy.start()
    copies[0].wait()
    copies[1].wait()

    lane = lax.broadcasted_iota(jnp.int32, (1, limits_ref.shape[1]), 1)
    lane_limit = jnp.zeros(lane.shape, jnp.int32)
    for place, offset in enumerate(set_order(shard_count)):
        lane_limit = jnp.where(lane // tok_dev == place, counts_ref[shard ^ offset], lane_limit)
    limits_ref[0:1, :] = (lane % tok_dev < lane_limit).astype(jnp.int32)
    limits_ref[1:2, :] = jnp.full(lane.shape, counts_ref[shard], jnp.int32)
    limits_ref[2:3, :] = jnp.full(lane.shape, counts_ref[shard ^ SPLIT], jnp.int32)

    step = lax.broadcasted_iota(jnp.int32, (1, pick_ref.shape[2]), 1)
    for slot in range(slot_count):
        head = head_ref[slot, shard]
        group_size = jnp.int32(0)
        group_rank = jnp.int32(0)
        for other_shard in range(shard_count):
            for other_slot in range(slot_count):
                same = (head_ref[other_slot, other_shard] == head).astype(jnp.int32)
                before = other_shard * slot_count + other_slot < shard * slot_count + slot
                group_size = group_size + same
                group_rank = group_rank + same * before.astype(jnp.int32)
        served = group_rank + group_size * step
        for source in range(shard_count):
            pick_ref[slot, source : source + 1, :] = jnp.where(
                served < counts_ref[source], served + source * tok_dev, -1
            )
        slot_head_ref[slot] = jnp.full(slot_head_ref.shape[1:], head, jnp.int32)
    for copy in copies[2:]:
        copy.wait()


def gathered(set_refs, part, columns):
    tok_dev = set_refs[0].shape[0] // 3
    rows = pl.ds(part * tok_dev, tok_dev)
    return jnp.concatenate([ref[rows, columns] for ref in set_refs], axis=0)


def head_scores(query_rows, key_all):
    return lax.dot_general(
        query_rows, key_all, (((1,), (1,)), ((), ())), preferred_element_type=jnp.float32
    )


def attend_kernel(set_count, limits_ref, *refs):
    set_refs = refs[:set_count]
    weight_hbm, keep_ref, send_ref, weight_ref, weight_sem = refs[set_count:]
    weight_copy = pltpu.make_async_copy(weight_hbm, weight_ref, weight_sem)
    weight_copy.start()
    tok_dev, half_width = keep_ref.shape
    heads = [pl.ds(start, HDIM) for start in range(0, half_width, HDIM)]
    scores = jnp.concatenate(
        [
            head_scores(gathered(set_refs[:2], 2, columns), gathered(set_refs, 0, columns))
            for columns in heads
        ],
        axis=0,
    ) * (1.0 / math.sqrt(HDIM))
    scores = jnp.where(limits_ref[0:1, :] > 0, scores, -jnp.inf)
    weights = jnp.exp(scores - jnp.max(scores, axis=1, keepdims=True))
    weight_sum = jnp.sum(weights, axis=1, keepdims=True)
    rounded = weights.astype(jnp.bfloat16)
    row = lax.broadcasted_iota(jnp.int32, (tok_dev, HDIM), 0)
    for number, columns in enumerate(heads):
        first = 2 * tok_dev * number
        mixed = jnp.dot(
            rounded[first : first + 2 * tok_dev],
            gathered(set_refs, 1, columns),
            preferred_element_type=jnp.float32,
        )
        attended = mixed / weight_sum[first : first + 2 * tok_dev]
        for target, rows, limit in (
            (keep_ref, attended[:tok_dev], limits_ref[1:2, :HDIM]),
            (send_ref, attended[tok_dev:], limits_ref[2:3, :HDIM]),
        ):
            target[:, columns] = jnp.where(row < limit, rows, 0.0).astype(jnp.bfloat16)
    weight_copy.wait()


def logsum_kernel(set_count, limits_ref, *refs):
    set_refs = refs[:set_count]
    table_ref, lines_ref = refs[set_count:]
    tok_dev = set_refs[0].shape[0] // 3
    half_heads = set_refs[0].shape[1] // HDIM
    shard = lax.axis_index("seq")
    first_head = (shard // SPLIT) % 2 * half_heads
    key_valid = limits_ref[0:1, :] > 0
    lane = lax.broadcasted_iota(jnp.int32, lines_ref.shape, 1)
    lines = jnp.zeros(lines_ref.shape, jnp.float32)
    for head in range(half_heads):
        columns = pl.ds(head * HDIM, HDIM)
        scores = head_scores(gathered(set_refs, 2, columns), gathered(set_refs, 0, columns))
        scores = jnp.where(key_valid, scores * (1.0 / math.sqrt(HDIM)), -jnp.inf)
        top_score = jnp.max(scores, axis=1, keepdims=True)
        weight_sum = jnp.sum(jnp.exp(scores - top_score), axis=1, keepdims=True)
        lines = jnp.where(lane == first_head + head, top_score + jnp.log(weight_sum), lines)
    for place, offset in enumerate(set_order(set_count)):
        rows = pl.ds(pl.multiple_of((shard ^ offset) * tok_dev, tok_dev), tok_dev)
        lines_ref[rows, :] = lines[place * tok_dev : (place + 1) * tok_dev]
    table_ref[...] = jnp.transpose(lines_ref[...])[: table_ref.shape[0]]


def project_kernel(
    keep_ref, back_ref, partner_keep_ref, partner_back_ref, weight_ref, projected_ref
):
    half_width = keep_ref.shape[1]
    half = (lax.axis_index("seq") // SPLIT) % 2
    on_positive = lax.axis_index("branch") == 0
    own_scale = jnp.where(on_positive, GUIDE_SCALE, 1.0 - GUIDE_SCALE)
    partner_scale = jnp.where(on_positive, 1.0 - GUIDE_SCALE, GUIDE_SCALE)
    parts = [
        own_scale * own_ref[...].astype(jnp.float32)
        + partner_scale * partner_ref[...].astype(jnp.float32)
        for own_ref, partner_ref in ((keep_ref, partner_keep_ref), (back_ref, partner_back_ref))
    ]
    magnitude = jnp.sum(
        jnp.abs(parts[0]) + jnp.abs(parts[1]), axis=1, keepdims=True
    ) / (2 * half_width)
    total = jnp.zeros(projected_ref.shape, jnp.float32)
    for part, place in zip(parts, (half, 1 - half)):
        normed = (part / (magnitude + EPSILON)).astype(jnp.bfloat16)
        rows = pl.ds(pl.multiple_of(place * half_width, half_width), half_width)
        total = total + jnp.dot(normed, weight_ref[rows, :], preferred_element_type=jnp.float32)
    projected_ref[...] = total.astype(jnp.bfloat16)


def serve_kernel(table_ref, other_table_ref, pick_ref, slot_head_ref, saved_ref):
    table = table_ref[...] + other_table_ref[...]
    head = lax.broadcasted_iota(jnp.int32, table.shape, 0)
    for slot in range(saved_ref.shape[0]):
        line = jnp.sum(
            jnp.where(head == slot_head_ref[slot, 0:1, :], table, 0.0), axis=0, keepdims=True
        )
        pick = pick_ref[slot]
        spread = jnp.broadcast_to(line, pick.shape)
        taken = jnp.take_along_axis(spread, jnp.maximum(pick, 0), axis=1)
        saved_ref[slot] = jnp.where(pick >= 0, taken, 0.0)[:, : saved_ref.shape[2]]


def per_device_halves(queries, key_rows, value_rows, counts, head_of, out_weight):
    seq_count = lax.axis_size("seq")
    tok_dev, width = queries.shape[1:]
    half_width = width // 2
    tokens = seq_count * tok_dev
    slot_count = head_of.shape[1]
    fewest = max(1, seq_count * slot_count // (2 * HEADS))
    row_cap = (tok_dev + fewest - 1) // fewest
    table_rows = (HEADS + 7) // 8 * 8
    any_spec = pl.BlockSpec(memory_space=pl.ANY)
    vmem = pl.BlockSpec(memory_space=pltpu.VMEM)

    def held(*arrays):
        return [pltpu.with_memory_space_constraint(array, pltpu.VMEM) for array in arrays]

    def far(*arrays):
        return [pltpu.with_memory_space_constraint(array, pltpu.HBM) for array in arrays]

    own, other, limits, pick, slot_head = pl.pallas_call(
        pack_kernel,
        out_shape=[
            pltpu.VMEM((3 * tok_dev, half_width), jnp.bfloat16),
            pltpu.VMEM((3 * tok_dev, half_width), jnp.bfloat16),
            pltpu.VMEM((8, tokens), jnp.int32),
            pltpu.VMEM((slot_count, seq_count, tokens), jnp.int32),
            pltpu.VMEM((slot_count, 8, tokens), jnp.int32),
        ],
        in_specs=[any_spec] * 5,
        out_specs=[vmem] * 5,
        scratch_shapes=[
            pltpu.SMEM((seq_count,), jnp.int32),
            pltpu.SMEM((slot_count, seq_count), jnp.int32),
            pltpu.SemaphoreType.DMA((8,)),
        ],
        compiler_params=KERNEL_PARAMS,
        name="pack",
    )(*far(queries, key_rows, value_rows, counts, jnp.transpose(head_of)))

    sets = {0: own}
    for offset in reversed(range(SPLIT, seq_count, SPLIT)):
        sets[offset] = swap_shards(other if offset & SPLIT else own, offset)
    for offset in range(0, seq_count, SPLIT):
        sets[offset + 1] = swap_shards(sets[offset], 1)
    set_list = held(*[sets[offset] for offset in set_order(seq_count)])
    limits = held(limits)[0]
    keep, send, weight_held = pl.pallas_call(
        functools.partial(attend_kernel, seq_count),
        out_shape=[
            pltpu.VMEM((tok_dev, half_width), jnp.bfloat16),
            pltpu.VMEM((tok_dev, half_width), jnp.bfloat16),
            pltpu.VMEM(out_weight.shape, jnp.bfloat16),
        ],
        in_specs=[vmem] * (1 + seq_count) + [any_spec],
        out_specs=[vmem] * 3,
        scratch_shapes=[pltpu.SemaphoreType.DMA],
        compiler_params=KERNEL_PARAMS,
        name="attend",
    )(limits, *set_list, *far(out_weight))
    across = [(2 * i + b, 2 * (i ^ SPLIT) + 1 - b) for i in range(seq_count) for b in range(2)]
    partner_back = lax.ppermute(send, ("seq", "branch"), across)
    back = swap_shards(send, SPLIT)
    table = pl.pallas_call(
        functools.partial(logsum_kernel, seq_count),
        out_shape=pltpu.VMEM((table_rows, tokens), jnp.float32),
        in_specs=[vmem] * (1 + seq_count),
        out_specs=vmem,
        scratch_shapes=[pltpu.VMEM((tokens, HDIM), jnp.float32)],
        compiler_params=KERNEL_PARAMS,
        name="logsum",
    )(limits, *set_list)
    other_table = swap_shards(table, SPLIT)
    partner_keep = partner_2(keep, "branch", 0)
    projected = pl.pallas_call(
        project_kernel,
        out_shape=jax.ShapeDtypeStruct((tok_dev, out_weight.shape[1]), jnp.bfloat16),
        in_specs=[vmem] * 5,
        out_specs=vmem,
        compiler_params=KERNEL_PARAMS,
        name="project",
    )(*held(keep, back, partner_keep, partner_back, weight_held))
    saved = pl.pallas_call(
        serve_kernel,
        out_shape=jax.ShapeDtypeStruct((slot_count, seq_count, row_cap), jnp.float32),
        in_specs=[vmem] * 4,
        out_specs=vmem,
        compiler_params=KERNEL_PARAMS,
        name="serve",
    )(*held(table, other_table, pick, slot_head))
    saved = jnp.transpose(saved, (0, 2, 1))
    return (projected, saved.reshape(1, 1, slot_count, row_cap, seq_count))


def solution(mesh):
    seq_count = mesh.shape["seq"]
    hypercube = seq_count > SPLIT and seq_count & (seq_count - 1) == 0
    small = hypercube and seq_count <= HEADS
    return jax.shard_map(
        per_device_halves if small else per_device_exchange,
        mesh=mesh,
        in_specs=(
            P("branch", ("groups", "seq"), None),
            P("branch", ("groups", "seq"), None),
            P("branch", ("groups", "seq"), None),
            P("groups"),
            P(),
            P(None, "branch"),
        ),
        out_specs=(
            P(("groups", "seq"), "branch"),
            P("branch", ("groups", "seq"), None, None, None),
        ),
        check_vma=False,
    )
```

profile of v0, /device:TPU:0, one launch (start us, length us, event | category | flops | bytes accessed | tf_op | source)
XLA Modules:
  0.0 27.6 jit_solution(3874218919912743522)
XLA Ops:
  0.6 0.9 %pack.1 = (bf16[48,768]{1,0:T(8,128)(2,1)S(1)}, bf16[48,768]{1,0:T(8,128)(2,1)S(1)}, s32[8,128]{1,0:T(8,128)S(1)}, s32[2,8,128]{2,1,0:T(8,128)S(1)}, s32[2,8,128]{2,1,0:T(8,128)S(1)}) custom-call(bf16[1,16,1536]{2,1,0:T(8,128)(2,1)} %query_hbm.1, bf16[1,16,1536]{2,1,0:T(8,128)(2,1)} %key_hbm.1, bf16[1,16,1536]{2,1,0:T(8,128)(2,1)} %value_hbm.1, ...), custom_call_target="tpu_custom_call" | custom-call | tf_op jit(solution)/shard_map/pack/pallas_call | solution.py:373
  1.6 5.1 %collective-permute-start.2 = (bf16[48,768]{1,0:T(8,128)(2,1)S(1)}, bf16[48,768]{1,0:T(8,128)(2,1)S(1)}, u32[]{:S(2)}, u32[]{:S(2)}) collective-permute-start(bf16[48,768]{1,0:T(8,128)(2,1)S(1)} %get-tuple-element.12), channel_id=1, source_target_pairs={{0,12},{2,14},{4,8},{6,10},{8,4},{10,6},{12,0},{14,2},{1,13},{3,15... | collective-permute-start | bytes 221192 | tf_op jit(solution)/shard_map/ppermute | solution.py:173
  6.7 0.0 collective-permute-start
  6.7 0.6 %collective-permute-start.1 = (bf16[48,768]{1,0:T(8,128)(2,1)S(1)}, bf16[48,768]{1,0:T(8,128)(2,1)S(1)}, u32[]{:S(2)}, u32[]{:S(2)}) collective-permute-start(bf16[48,768]{1,0:T(8,128)(2,1)S(1)} %get-tuple-element.11.refs_0_), channel_id=1, source_target_pairs={{0,8},{2,10},{4,12},{6,14},{8,0},{10,2},{12,4},{14,6},{1,9},{3,11}... | collective-permute-start | bytes 221192 | tf_op jit(solution)/shard_map/ppermute | solution.py:173
  7.3 1.6 %collective-permute-start.3 = (bf16[48,768]{1,0:T(8,128)(2,1)S(1)}, bf16[48,768]{1,0:T(8,128)(2,1)S(1)}, u32[]{:S(2)}, u32[]{:S(2)}) collective-permute-start(bf16[48,768]{1,0:T(8,128)(2,1)S(1)} %get-tuple-element.11.refs_0_), channel_id=1, source_target_pairs={{0,2},{2,0},{4,6},{6,4},{8,10},{10,8},{12,14},{14,12},{1,3},{3,1},... | collective-permute-start | bytes 221192 | tf_op jit(solution)/shard_map/ppermute | solution.py:173
  9.0 0.9 %collective-permute-done.2.refs_3_ = bf16[48,768]{1,0:T(8,128)(2,1)S(1)} collective-permute-done((bf16[48,768]{1,0:T(8,128)(2,1)S(1)}, bf16[48,768]{1,0:T(8,128)(2,1)S(1)}, u32[]{:S(2)}, u32[]{:S(2)}) %collective-permute-start.2) | collective-permute-done | bytes 73760 | tf_op jit(solution)/shard_map/ppermute | solution.py:173
  9.8 1.5 %collective-permute-start.6 = (bf16[48,768]{1,0:T(8,128)(2,1)S(1)}, bf16[48,768]{1,0:T(8,128)(2,1)S(1)}, u32[]{:S(2)}, u32[]{:S(2)}) collective-permute-start(bf16[48,768]{1,0:T(8,128)(2,1)S(1)} %collective-permute-done.2.refs_3_), channel_id=1, source_target_pairs={{0,2},{2,0},{4,6},{6,4},{8,10},{10,8},{12,14},{14,12},{1,3},{3,1},... | collective-permute-start | bytes 221192 | tf_op jit(solution)/shard_map/ppermute | solution.py:173
  11.3 0.4 %collective-permute-done.refs_1_ = bf16[48,768]{1,0:T(8,128)(2,1)S(1)} collective-permute-done((bf16[48,768]{1,0:T(8,128)(2,1)S(1)}, bf16[48,768]{1,0:T(8,128)(2,1)S(1)}, u32[]{:S(2)}, u32[]{:S(2)}) %collective-permute-start) | collective-permute-done | bytes 73760 | tf_op jit(solution)/shard_map/ppermute | solution.py:173
  11.7 1.6 %collective-permute-start.4 = (bf16[48,768]{1,0:T(8,128)(2,1)S(1)}, bf16[48,768]{1,0:T(8,128)(2,1)S(1)}, u32[]{:S(2)}, u32[]{:S(2)}) collective-permute-start(bf16[48,768]{1,0:T(8,128)(2,1)S(1)} %collective-permute-done.refs_1_), channel_id=1, source_target_pairs={{0,2},{2,0},{4,6},{6,4},{8,10},{10,8},{12,14},{14,12},{1,3},{3,1},... | collective-permute-start | bytes 221192 | tf_op jit(solution)/shard_map/ppermute | solution.py:173
  13.4 0.0 collective-permute-done.1.refs_2_
  13.4 0.7 %collective-permute-start.5 = (bf16[48,768]{1,0:T(8,128)(2,1)S(1)}, bf16[48,768]{1,0:T(8,128)(2,1)S(1)}, u32[]{:S(2)}, u32[]{:S(2)}) collective-permute-start(bf16[48,768]{1,0:T(8,128)(2,1)S(1)} %collective-permute-done.1.refs_2_), channel_id=1, source_target_pairs={{0,2},{2,0},{4,6},{6,4},{8,10},{10,8},{12,14},{14,12},{1,3},{3,1},... | collective-permute-start | bytes 221192 | tf_op jit(solution)/shard_map/ppermute | solution.py:173
  14.1 0.0 collective-permute-done.3.refs_4_
  14.1 0.6 %collective-permute-done.6.refs_7_ = bf16[48,768]{1,0:T(8,128)(2,1)S(1)} collective-permute-done((bf16[48,768]{1,0:T(8,128)(2,1)S(1)}, bf16[48,768]{1,0:T(8,128)(2,1)S(1)}, u32[]{:S(2)}, u32[]{:S(2)}) %collective-permute-start.6) | collective-permute-done | bytes 73760 | tf_op jit(solution)/shard_map/ppermute | solution.py:173
  14.7 2.2 %collective-permute-done.4.refs_5_ = bf16[48,768]{1,0:T(8,128)(2,1)S(1)} collective-permute-done((bf16[48,768]{1,0:T(8,128)(2,1)S(1)}, bf16[48,768]{1,0:T(8,128)(2,1)S(1)}, u32[]{:S(2)}, u32[]{:S(2)}) %collective-permute-start.4) | collective-permute-done | bytes 73760 | tf_op jit(solution)/shard_map/ppermute | solution.py:173
  16.8 0.9 %collective-permute-done.5.refs_6_ = bf16[48,768]{1,0:T(8,128)(2,1)S(1)} collective-permute-done((bf16[48,768]{1,0:T(8,128)(2,1)S(1)}, bf16[48,768]{1,0:T(8,128)(2,1)S(1)}, u32[]{:S(2)}, u32[]{:S(2)}) %collective-permute-start.5) | collective-permute-done | bytes 73760 | tf_op jit(solution)/shard_map/ppermute | solution.py:173
  17.7 1.7 %attend.1 = (bf16[16,768]{1,0:T(8,128)(2,1)S(1)}, bf16[16,768]{1,0:T(8,128)(2,1)S(1)}, bf16[1536,768]{1,0:T(8,128)(2,1)S(1)}) custom-call(s32[8,128]{1,0:T(8,128)S(1)} %get-tuple-element.10.limits_ref, bf16[48,768]{1,0:T(8,128)(2,1)S(1)} %get-tuple-element.11.refs_0_, bf16[48,768]{1,0:T(8,128)(2,1)S(1)} %collective-permute-done.refs_1_, ...), custom_call_target="tpu_custom_call" | custom-call | tf_op jit(solution)/shard_map/attend/pallas_call | solution.py:400
  19.4 0.1 collective-permute-start.8
  19.5 1.3 %collective-permute-start.9 = (bf16[16,768]{1,0:T(8,128)(2,1)S(1)}, bf16[16,768]{1,0:T(8,128)(2,1)S(1)}, u32[]{:S(2)}, u32[]{:S(2)}) collective-permute-start(bf16[16,768]{1,0:T(8,128)(2,1)S(1)} %get-tuple-element.14), channel_id=1, source_target_pairs={{0,5},{1,4},{2,7},{3,6},{4,1},{5,0},{6,3},{7,2},{8,13},{9,12},{10,... | collective-permute-start | bytes 73736 | tf_op jit(solution)/shard_map/ppermute | solution.py:414
  20.8 0.8 %collective-permute-start.7 = (bf16[16,768]{1,0:T(8,128)(2,1)S(1)}, bf16[16,768]{1,0:T(8,128)(2,1)S(1)}, u32[]{:S(2)}, u32[]{:S(2)}) collective-permute-start(bf16[16,768]{1,0:T(8,128)(2,1)S(1)} %get-tuple-element.14), channel_id=1, source_target_pairs={{0,4},{2,6},{4,0},{6,2},{8,12},{10,14},{12,8},{14,10},{1,5},{3,7},... | collective-permute-start | bytes 73736 | tf_op jit(solution)/shard_map/ppermute | solution.py:173
  21.6 0.5 %logsum.1.table_ref = f32[16,128]{1,0:T(8,128)S(1)} custom-call(s32[8,128]{1,0:T(8,128)S(1)} %get-tuple-element.10.limits_ref, bf16[48,768]{1,0:T(8,128)(2,1)S(1)} %get-tuple-element.11.refs_0_, bf16[48,768]{1,0:T(8,128)(2,1)S(1)} %collective-permute-done.refs_1_, bf16[48,768]{1,0:T(8,128)(2,1)S(1)} %collective-permute-done.1.refs_2_, ...), custom_call_target="tpu_custom_call" | custom-call | tf_op jit(solution)/shard_map/logsum/pallas_call | solution.py:416
  22.1 1.2 %collective-permute-start.10 = (f32[16,128]{1,0:T(8,128)S(1)}, f32[16,128]{1,0:T(8,128)S(1)}, u32[]{:S(2)}, u32[]{:S(2)}) collective-permute-start(f32[16,128]{1,0:T(8,128)S(1)} %logsum.1.table_ref), channel_id=1, source_target_pairs={{0,4},{2,6},{4,0},{6,2},{8,12},{10,14},{12,8},{14,10},{1,5},{3,7},... | collective-permute-start | bytes 24584 | tf_op jit(solution)/shard_map/ppermute | solution.py:173
  23.4 2.5 %collective-permute-done.10.other_table_ref = f32[16,128]{1,0:T(8,128)S(1)} collective-permute-done((f32[16,128]{1,0:T(8,128)S(1)}, f32[16,128]{1,0:T(8,128)S(1)}, u32[]{:S(2)}, u32[]{:S(2)}) %collective-permute-start.10) | collective-permute-done | bytes 8224 | tf_op jit(solution)/shard_map/ppermute | solution.py:173
  25.8 0.7 %serve.1 = f32[2,8,16]{2,1,0:T(8,128)} custom-call(f32[16,128]{1,0:T(8,128)S(1)} %logsum.1.table_ref, f32[16,128]{1,0:T(8,128)S(1)} %collective-permute-done.10.other_table_ref, s32[2,8,128]{2,1,0:T(8,128)S(1)} %get-tuple-element.16.pick_ref, s32[2,8,128]{2,1,0:T(8,128)S(1)} %get-tuple-element.17.slot_head_ref), custom_call_target="tpu_custom_call" | custom-call | tf_op jit(solution)/shard_map/serve/pallas_call | solution.py:435
  26.5 0.0 collective-permute-done.8.partner_keep_ref
  26.5 0.0 collective-permute-done.9.partner_back_ref
  26.5 0.0 collective-permute-done.7.back_ref
  26.5 1.1 %project.1 = bf16[16,768]{1,0:T(8,128)(2,1)} custom-call(bf16[16,768]{1,0:T(8,128)(2,1)S(1)} %get-tuple-element.13.keep_ref, bf16[16,768]{1,0:T(8,128)(2,1)S(1)} %collective-permute-done.7.back_ref, bf16[16,768]{1,0:T(8,128)(2,1)S(1)} %collective-permute-done.8.partner_keep_ref, bf16[16,768]{1,0:T(8,128)(2,1)S(1)} %collective-permute-done.9.partner_back_ref, ...), custom_call_target="tpu_custom_call" | custom-call | tf_op jit(solution)/shard_map/project/pallas_call | solution.py:427
Async XLA Ops:
  1.6 8.3 %collective-permute-start.2 = (bf16[48,768]{1,0:T(8,128)(2,1)S(1)}, bf16[48,768]{1,0:T(8,128)(2,1)S(1)}, u32[]{:S(2)}, u32[]{:S(2)}) collective-permute-start(bf16[48,768]{1,0:T(8,128)(2,1)S(1)} %get-tuple-element.12), channel_id=1, source_target_pairs={{0,12},{2,14},{4,8},{6,10},{8,4},{10,6},{12,0},{14,2},{1,13},{3,15... | collective-permute-start | bytes 221192 | tf_op jit(solution)/shard_map/ppermute | solution.py:173
  6.7 5.0 %collective-permute-start = (bf16[48,768]{1,0:T(8,128)(2,1)S(1)}, bf16[48,768]{1,0:T(8,128)(2,1)S(1)}, u32[]{:S(2)}, u32[]{:S(2)}) collective-permute-start(bf16[48,768]{1,0:T(8,128)(2,1)S(1)} %get-tuple-element.12), channel_id=1, source_target_pairs={{0,4},{2,6},{4,0},{6,2},{8,12},{10,14},{12,8},{14,10},{1,5},{3,7},... | collective-permute-start | bytes 221192 | tf_op jit(solution)/shard_map/ppermute | solution.py:173
  6.7 6.7 %collective-permute-start.1 = (bf16[48,768]{1,0:T(8,128)(2,1)S(1)}, bf16[48,768]{1,0:T(8,128)(2,1)S(1)}, u32[]{:S(2)}, u32[]{:S(2)}) collective-permute-start(bf16[48,768]{1,0:T(8,128)(2,1)S(1)} %get-tuple-element.11.refs_0_), channel_id=1, source_target_pairs={{0,8},{2,10},{4,12},{6,14},{8,0},{10,2},{12,4},{14,6},{1,9},{3,11}... | collective-permute-start | bytes 221192 | tf_op jit(solution)/shard_map/ppermute | solution.py:173
  7.3 6.8 %collective-permute-start.3 = (bf16[48,768]{1,0:T(8,128)(2,1)S(1)}, bf16[48,768]{1,0:T(8,128)(2,1)S(1)}, u32[]{:S(2)}, u32[]{:S(2)}) collective-permute-start(bf16[48,768]{1,0:T(8,128)(2,1)S(1)} %get-tuple-element.11.refs_0_), channel_id=1, source_target_pairs={{0,2},{2,0},{4,6},{6,4},{8,10},{10,8},{12,14},{14,12},{1,3},{3,1},... | collective-permute-start | bytes 221192 | tf_op jit(solution)/shard_map/ppermute | solution.py:173
  9.8 4.8 %collective-permute-start.6 = (bf16[48,768]{1,0:T(8,128)(2,1)S(1)}, bf16[48,768]{1,0:T(8,128)(2,1)S(1)}, u32[]{:S(2)}, u32[]{:S(2)}) collective-permute-start(bf16[48,768]{1,0:T(8,128)(2,1)S(1)} %collective-permute-done.2.refs_3_), channel_id=1, source_target_pairs={{0,2},{2,0},{4,6},{6,4},{8,10},{10,8},{12,14},{14,12},{1,3},{3,1},... | collective-permute-start | bytes 221192 | tf_op jit(solution)/shard_map/ppermute | solution.py:173
  11.7 5.1 %collective-permute-start.4 = (bf16[48,768]{1,0:T(8,128)(2,1)S(1)}, bf16[48,768]{1,0:T(8,128)(2,1)S(1)}, u32[]{:S(2)}, u32[]{:S(2)}) collective-permute-start(bf16[48,768]{1,0:T(8,128)(2,1)S(1)} %collective-permute-done.refs_1_), channel_id=1, source_target_pairs={{0,2},{2,0},{4,6},{6,4},{8,10},{10,8},{12,14},{14,12},{1,3},{3,1},... | collective-permute-start | bytes 221192 | tf_op jit(solution)/shard_map/ppermute | solution.py:173
  13.4 4.4 %collective-permute-start.5 = (bf16[48,768]{1,0:T(8,128)(2,1)S(1)}, bf16[48,768]{1,0:T(8,128)(2,1)S(1)}, u32[]{:S(2)}, u32[]{:S(2)}) collective-permute-start(bf16[48,768]{1,0:T(8,128)(2,1)S(1)} %collective-permute-done.1.refs_2_), channel_id=1, source_target_pairs={{0,2},{2,0},{4,6},{6,4},{8,10},{10,8},{12,14},{14,12},{1,3},{3,1},... | collective-permute-start | bytes 221192 | tf_op jit(solution)/shard_map/ppermute | solution.py:173
  19.4 7.1 %collective-permute-start.8 = (bf16[16,768]{1,0:T(8,128)(2,1)S(1)}, bf16[16,768]{1,0:T(8,128)(2,1)S(1)}, u32[]{:S(2)}, u32[]{:S(2)}) collective-permute-start(bf16[16,768]{1,0:T(8,128)(2,1)S(1)} %get-tuple-element.13.keep_ref), channel_id=1, source_target_pairs={{0,1},{1,0},{2,3},{3,2},{4,5},{5,4},{6,7},{7,6},{8,9},{9,8},{10,11... | collective-permute-start | bytes 73736 | tf_op jit(solution)/shard_map/ppermute | solution.py:20
  19.5 7.0 %collective-permute-start.9 = (bf16[16,768]{1,0:T(8,128)(2,1)S(1)}, bf16[16,768]{1,0:T(8,128)(2,1)S(1)}, u32[]{:S(2)}, u32[]{:S(2)}) collective-permute-start(bf16[16,768]{1,0:T(8,128)(2,1)S(1)} %get-tuple-element.14), channel_id=1, source_target_pairs={{0,5},{1,4},{2,7},{3,6},{4,1},{5,0},{6,3},{7,2},{8,13},{9,12},{10,... | collective-permute-start | bytes 73736 | tf_op jit(solution)/shard_map/ppermute | solution.py:414
  20.8 5.7 %collective-permute-start.7 = (bf16[16,768]{1,0:T(8,128)(2,1)S(1)}, bf16[16,768]{1,0:T(8,128)(2,1)S(1)}, u32[]{:S(2)}, u32[]{:S(2)}) collective-permute-start(bf16[16,768]{1,0:T(8,128)(2,1)S(1)} %get-tuple-element.14), channel_id=1, source_target_pairs={{0,4},{2,6},{4,0},{6,2},{8,12},{10,14},{12,8},{14,10},{1,5},{3,7},... | collective-permute-start | bytes 73736 | tf_op jit(solution)/shard_map/ppermute | solution.py:173
  22.1 3.7 %collective-permute-start.10 = (f32[16,128]{1,0:T(8,128)S(1)}, f32[16,128]{1,0:T(8,128)S(1)}, u32[]{:S(2)}, u32[]{:S(2)}) collective-permute-start(f32[16,128]{1,0:T(8,128)S(1)} %logsum.1.table_ref), channel_id=1, source_target_pairs={{0,4},{2,6},{4,0},{6,2},{8,12},{10,14},{12,8},{14,10},{1,5},{3,7},... | collective-permute-start | bytes 24584 | tf_op jit(solution)/shard_map/ppermute | solution.py:173
where the time goes:
time: 27.8 us; the launch traced here: 27.6 us
  starting transfers between devices  14.7 us (53%)
  waiting for transfers between devices  7.38 us (27%)
  Pallas kernels  4.91 us (18%)
  between operations  0.67 us (2%)
    ppermute x9, starting transfers between devices, swap_shards(): return lax.ppermute(array, 'seq', pairs)  13.3 us
    ppermute x9, waiting for transfers between devices, swap_shards(): return lax.ppermute(array, 'seq', pairs)  7.38 us
    pallas_call x1, Pallas kernels, per_device_halves(): pl.pallas_call(functools.partial(attend_kernel, seq_count), out_shape=[pl...  1.68 us
    ppermute x1, starting transfers between devices, per_device_halves(): partner_back = lax.ppermute(send, ('seq', 'branch'), across)  1.31 us
    pallas_call x1, Pallas kernels, per_device_halves(): pl.pallas_call(project_kernel, out_shape=jax.ShapeDtypeStruct((tok_dev, o...  1.11 us
    pallas_call x1, Pallas kernels, per_device_halves(): pl.pallas_call(pack_kernel, out_shape=[pltpu.VMEM((3 * tok_dev, half_widt...  0.92 us
    pallas_call x1, Pallas kernels, per_device_halves(): pl.pallas_call(serve_kernel, out_shape=jax.ShapeDtypeStruct((slot_count,...  0.68 us
  transfers between devices with their start and end apart: 11, of which 6 were waited for; matrix products, arithmetic and copies ran while one was open for 0% of the time, Pallas kernels for 4%

commit v1 on v0

--- a/solution.py
+++ b/solution.py
@@ -166,6 +166,8 @@
 
 
 SPLIT = 2
+TABLE_PIECES = 3
+SPLITTER = 65537.0
 
 
 def swap_shards(array, offset):
@@ -186,6 +188,7 @@
     head_hbm,
     own_ref,
     other_ref,
+    line_copy_ref,
     limits_ref,
     pick_ref,
     slot_head_ref,
@@ -202,7 +205,7 @@
         pltpu.make_async_copy(counts_hbm, counts_ref, copy_sems.at[0]),
         pltpu.make_async_copy(head_hbm, head_ref, copy_sems.at[1]),
     ]
-    for target, place in ((other_ref, 1 - half), (own_ref, half)):
+    for target, place in ((line_copy_ref, half), (other_ref, 1 - half), (own_ref, half)):
         columns = pl.ds(pl.multiple_of(place * half_width, half_width), half_width)
         for part, source in enumerate((key_hbm, value_hbm, query_hbm)):
             rows = pl.ds(part * tok_dev, tok_dev)
@@ -245,6 +248,12 @@
         copy.wait()
 
 
+def hold_kernel(weight_hbm, after_ref, weight_ref, weight_sem):
+    copy = pltpu.make_async_copy(weight_hbm, weight_ref, weight_sem)
+    copy.start()
+    copy.wait()
+
+
 def gathered(set_refs, part, columns):
     tok_dev = set_refs[0].shape[0] // 3
     rows = pl.ds(part * tok_dev, tok_dev)
@@ -259,9 +268,7 @@
 
 def attend_kernel(set_count, limits_ref, *refs):
     set_refs = refs[:set_count]
-    weight_hbm, keep_ref, send_ref, weight_ref, weight_sem = refs[set_count:]
-    weight_copy = pltpu.make_async_copy(weight_hbm, weight_ref, weight_sem)
-    weight_copy.start()
+    keep_ref, send_ref = refs[set_count:]
     tok_dev, half_width = keep_ref.shape
     heads = [pl.ds(start, HDIM) for start in range(0, half_width, HDIM)]
     scores = jnp.concatenate(
@@ -289,44 +296,68 @@
             (send_ref, attended[tok_dev:], limits_ref[2:3, :HDIM]),
         ):
             target[:, columns] = jnp.where(row < limit, rows, 0.0).astype(jnp.bfloat16)
-    weight_copy.wait()
-
-
-def logsum_kernel(set_count, limits_ref, *refs):
+
+
+def logsum_kernel(set_count, limits_ref, send_ref, *refs):
     set_refs = refs[:set_count]
-    table_ref, lines_ref = refs[set_count:]
-    tok_dev = set_refs[0].shape[0] // 3
-    half_heads = set_refs[0].shape[1] // HDIM
+    message_ref, table_ref, lines_ref = refs[set_count:]
+    tok_dev, half_width = send_ref.shape
+    half_heads = half_width // HDIM
     shard = lax.axis_index("seq")
-    first_head = (shard // SPLIT) % 2 * half_heads
+    message_ref[pl.ds(0, tok_dev), :] = send_ref[...]
     key_valid = limits_ref[0:1, :] > 0
-    lane = lax.broadcasted_iota(jnp.int32, lines_ref.shape, 1)
-    lines = jnp.zeros(lines_ref.shape, jnp.float32)
+    lane = lax.broadcasted_iota(jnp.int32, (set_count * tok_dev, HDIM), 1)
+    lines = jnp.zeros(lane.shape, jnp.float32)
     for head in range(half_heads):
         columns = pl.ds(head * HDIM, HDIM)
         scores = head_scores(gathered(set_refs, 2, columns), gathered(set_refs, 0, columns))
         scores = jnp.where(key_valid, scores * (1.0 / math.sqrt(HDIM)), -jnp.inf)
         top_score = jnp.max(scores, axis=1, keepdims=True)
         weight_sum = jnp.sum(jnp.exp(scores - top_score), axis=1, keepdims=True)
-        lines = jnp.where(lane == first_head + head, top_score + jnp.log(weight_sum), lines)
+        lines = jnp.where(lane == head, top_score + jnp.log(weight_sum), lines)
     for place, offset in enumerate(set_order(set_count)):
         rows = pl.ds(pl.multiple_of((shard ^ offset) * tok_dev, tok_dev), tok_dev)
         lines_ref[rows, :] = lines[place * tok_dev : (place + 1) * tok_dev]
-    table_ref[...] = jnp.transpose(lines_ref[...])[: table_ref.shape[0]]
+    table = jnp.transpose(lines_ref[...])[: table_ref.shape[0]]
+    table_ref[...] = table
+    row = lax.broadcasted_iota(jnp.int32, (tok_dev, lines.shape[0]), 0)
+    for head in range(half_heads):
+        rest = jnp.broadcast_to(table[head : head + 1], row.shape)
+        block = jnp.zeros(row.shape, jnp.float32)
+        for piece in range(TABLE_PIECES):
+            scaled = rest * SPLITTER
+            part = scaled - (scaled - rest)
+            block = jnp.where(row == piece, part, block)
+            rest = rest - part
+        columns = pl.ds(head * lines.shape[0], lines.shape[0])
+        message_ref[pl.ds(tok_dev, tok_dev), columns] = block.astype(jnp.bfloat16)
 
 
 def project_kernel(
-    keep_ref, back_ref, partner_keep_ref, partner_back_ref, weight_ref, projected_ref
+    keep_ref,
+    message_ref,
+    partner_keep_ref,
+    partner_back_ref,
+    weight_ref,
+    table_ref,
+    pick_ref,
+    slot_head_ref,
+    projected_ref,
+    saved_ref,
 ):
-    half_width = keep_ref.shape[1]
+    tok_dev, half_width = keep_ref.shape
+    half_heads = half_width // HDIM
+    tokens = table_ref.shape[1]
     half = (lax.axis_index("seq") // SPLIT) % 2
     on_positive = lax.axis_index("branch") == 0
     own_scale = jnp.where(on_positive, GUIDE_SCALE, 1.0 - GUIDE_SCALE)
     partner_scale = jnp.where(on_positive, 1.0 - GUIDE_SCALE, GUIDE_SCALE)
     parts = [
-        own_scale * own_ref[...].astype(jnp.float32)
-        + partner_scale * partner_ref[...].astype(jnp.float32)
-        for own_ref, partner_ref in ((keep_ref, partner_keep_ref), (back_ref, partner_back_ref))
+        own_scale * own.astype(jnp.float32) + partner_scale * partner.astype(jnp.float32)
+        for own, partner in (
+            (keep_ref[...], partner_keep_ref[...]),
+            (message_ref[pl.ds(0, tok_dev), :], partner_back_ref[...]),
+        )
     ]
     magnitude = jnp.sum(
         jnp.abs(parts[0]) + jnp.abs(parts[1]), axis=1, keepdims=True
@@ -338,14 +369,17 @@
         total = total + jnp.dot(normed, weight_ref[rows, :], preferred_element_type=jnp.float32)
     projected_ref[...] = total.astype(jnp.bfloat16)
 
-
-def serve_kernel(table_ref, other_table_ref, pick_ref, slot_head_ref, saved_ref):
-    table = table_ref[...] + other_table_ref[...]
-    head = lax.broadcasted_iota(jnp.int32, table.shape, 0)
     for slot in range(saved_ref.shape[0]):
-        line = jnp.sum(
-            jnp.where(head == slot_head_ref[slot, 0:1, :], table, 0.0), axis=0, keepdims=True
-        )
+        slot_head = slot_head_ref[slot, 0:1, :]
+        line = jnp.zeros((1, tokens), jnp.float32)
+        for head in range(half_heads):
+            pieces = message_ref[pl.ds(tok_dev, tok_dev), pl.ds(head * tokens, tokens)]
+            pieces = pieces.astype(jnp.float32)
+            other = pieces[0:1]
+            for piece in range(1, TABLE_PIECES):
+                other = other + pieces[piece : piece + 1]
+            line = jnp.where(slot_head == half * half_heads + head, table_ref[head : head + 1], line)
+            line = jnp.where(slot_head == (1 - half) * half_heads + head, other, line)
         pick = pick_ref[slot]
         spread = jnp.broadcast_to(line, pick.shape)
         taken = jnp.take_along_axis(spread, jnp.maximum(pick, 0), axis=1)
@@ -360,7 +394,6 @@
     slot_count = head_of.shape[1]
     fewest = max(1, seq_count * slot_count // (2 * HEADS))
     row_cap = (tok_dev + fewest - 1) // fewest
-    table_rows = (HEADS + 7) // 8 * 8
     any_spec = pl.BlockSpec(memory_space=pl.ANY)
     vmem = pl.BlockSpec(memory_space=pltpu.VMEM)
 
@@ -370,9 +403,10 @@
     def far(*arrays):
         return [pltpu.with_memory_space_constraint(array, pltpu.HBM) for array in arrays]
 
-    own, other, limits, pick, slot_head = pl.pallas_call(
+    own, other, line_copy, limits, pick, slot_head = pl.pallas_call(
         pack_kernel,
         out_shape=[
+            pltpu.VMEM((3 * tok_dev, half_width), jnp.bfloat16),
             pltpu.VMEM((3 * tok_dev, half_width), jnp.bfloat16),
             pltpu.VMEM((3 * tok_dev, half_width), jnp.bfloat16),
             pltpu.VMEM((8, tokens), jnp.int32),
@@ -380,66 +414,70 @@
             pltpu.VMEM((slot_count, 8, tokens), jnp.int32),
         ],
         in_specs=[any_spec] * 5,
-        out_specs=[vmem] * 5,
+        out_specs=[vmem] * 6,
         scratch_shapes=[
             pltpu.SMEM((seq_count,), jnp.int32),
             pltpu.SMEM((slot_count, seq_count), jnp.int32),
-            pltpu.SemaphoreType.DMA((8,)),
+            pltpu.SemaphoreType.DMA((11,)),
         ],
         compiler_params=KERNEL_PARAMS,
         name="pack",
     )(*far(queries, key_rows, value_rows, counts, jnp.transpose(head_of)))
 
     sets = {0: own}
-    for offset in reversed(range(SPLIT, seq_count, SPLIT)):
-        sets[offset] = swap_shards(other if offset & SPLIT else own, offset)
+    for offset in range(SPLIT, seq_count, SPLIT):
+        sets[offset] = swap_shards(other if offset & SPLIT else line_copy, offset)
     for offset in range(0, seq_count, SPLIT):
         sets[offset + 1] = swap_shards(sets[offset], 1)
     set_list = held(*[sets[offset] for offset in set_order(seq_count)])
     limits = held(limits)[0]
-    keep, send, weight_held = pl.pallas_call(
+    keep, send = pl.pallas_call(
         functools.partial(attend_kernel, seq_count),
-        out_shape=[
-            pltpu.VMEM((tok_dev, half_width), jnp.bfloat16),
-            pltpu.VMEM((tok_dev, half_width), jnp.bfloat16),
-            pltpu.VMEM(out_weight.shape, jnp.bfloat16),
-        ],
-        in_specs=[vmem] * (1 + seq_count) + [any_spec],
-        out_specs=[vmem] * 3,
-        scratch_shapes=[pltpu.SemaphoreType.DMA],
+        out_shape=[pltpu.VMEM((tok_dev, half_width), jnp.bfloat16)] * 2,
+        in_specs=[vmem] * (1 + seq_count),
+        out_specs=[vmem] * 2,
         compiler_params=KERNEL_PARAMS,
         name="attend",
-    )(limits, *set_list, *far(out_weight))
+    )(limits, *set_list)
     across = [(2 * i + b, 2 * (i ^ SPLIT) + 1 - b) for i in range(seq_count) for b in range(2)]
     partner_back = lax.ppermute(send, ("seq", "branch"), across)
-    back = swap_shards(send, SPLIT)
-    table = pl.pallas_call(
+    partner_keep = partner_2(keep, "branch", 0)
+    message, table = pl.pallas_call(
         functools.partial(logsum_kernel, seq_count),
-        out_shape=pltpu.VMEM((table_rows, tokens), jnp.float32),
-        in_specs=[vmem] * (1 + seq_count),
-        out_specs=vmem,
+        out_shape=[
+            pltpu.VMEM((2 * tok_dev, half_width), jnp.bfloat16),
+            pltpu.VMEM((half_width // HDIM + 7 & -8, tokens), jnp.float32),
+        ],
+        in_specs=[vmem] * (2 + seq_count),
+        out_specs=[vmem] * 2,
         scratch_shapes=[pltpu.VMEM((tokens, HDIM), jnp.float32)],
         compiler_params=KERNEL_PARAMS,
         name="logsum",
-    )(limits, *set_list)
-    other_table = swap_shards(table, SPLIT)
-    partner_keep = partner_2(keep, "branch", 0)
-    projected = pl.pallas_call(
+    )(limits, *held(send), *set_list)
+    weight_held = pl.pallas_call(
+        hold_kernel,
+        out_shape=pltpu.VMEM(out_weight.shape, jnp.bfloat16),
+        in_specs=[any_spec, vmem],
+        out_specs=vmem,
+        scratch_shapes=[pltpu.SemaphoreType.DMA],
+        compiler_params=KERNEL_PARAMS,
+        cost_estimate=pl.CostEstimate(
+            flops=0, bytes_accessed=4 * out_weight.size, transcendentals=0
+        ),
+        name="hold",
+    )(*far(out_weight), *held(table))
+    back = swap_shards(message, SPLIT)
+    projected, saved = pl.pallas_call(
         project_kernel,
-        out_shape=jax.ShapeDtypeStruct((tok_dev, out_weight.shape[1]), jnp.bfloat16),
-        in_specs=[vmem] * 5,
-        out_specs=vmem,
+        out_shape=[
+            jax.ShapeDtypeStruct((tok_dev, out_weight.shape[1]), jnp.bfloat16),
+            jax.ShapeDtypeStruct((slot_count, seq_count, row_cap), jnp.float32),
+        ],
+        in_specs=[vmem] * 8,
+        out_specs=[vmem] * 2,
         compiler_params=KERNEL_PARAMS,
         name="project",
-    )(*held(keep, back, partner_keep, partner_back, weight_held))
-    saved = pl.pallas_call(
-        serve_kernel,
-        out_shape=jax.ShapeDtypeStruct((slot_count, seq_count, row_cap), jnp.float32),
-        in_specs=[vmem] * 4,
-        out_specs=vmem,
-        compiler_params=KERNEL_PARAMS,
-        name="serve",
-    )(*held(table, other_table, pick, slot_head))
+    )(*held(keep, back, partner_keep, partner_back, weight_held, table, pick, slot_head))
     saved = jnp.transpose(saved, (0, 2, 1))
     return (projected, saved.reshape(1, 1, slot_count, row_cap, seq_count))
 

time: 27.8 us -> 25.4 us (0.914)
  starting transfers between devices: 14.7 us -> 13.4 us
  waiting for transfers between devices: 7.38 us -> 6.35 us
    ppermute x9 -> x8, waiting for transfers between devices: 7.38 us -> 5.25 us  [swap_shards(): return lax.ppermute(array, 'seq', pairs)]
    pallas_call x1, Pallas kernels: 1.68 us -> 0.42 us  [per_device_halves(): pl.pallas_call(functools.partial(attend_kernel, seq_count), out_shape=[pl...]
    ppermute x1, waiting for transfers between devices: 0.01 us -> 1.1 us  [per_device_halves(): partner_back = lax.ppermute(send, ('seq', 'branch'), across)]
    pallas_call x3, Pallas kernels: 2.31 us -> 3.34 us  [the longest x1 1.67 us: per_device_halves(): pl.pallas_call(hold_kernel, out_shape=pltpu.VMEM(out_weight.shape, jnp.bf...]
    ppermute x1, starting transfers between devices: 1.31 us -> 0.46 us  [per_device_halves(): partner_back = lax.ppermute(send, ('seq', 'branch'), across)]
    ppermute x9 -> x8, starting transfers between devices: 13.3 us -> 12.9 us  [swap_shards(): return lax.ppermute(array, 'seq', pairs)]
  transfers between devices with their start and end apart: 11 -> 10, of which waited for: 6 -> 5; matrix products, arithmetic and copies ran while one was open for 0% -> 0% of each run, Pallas kernels for 4% -> 7%
where the time goes in v1:
time: 25.4 us; the launch traced here: 25.2 us
  starting transfers between devices  13.4 us (53%)
  waiting for transfers between devices  6.35 us (25%)
  Pallas kernels  4.77 us (19%)
  between operations  0.67 us (3%)
    ppermute x8, starting transfers between devices, swap_shards(): return lax.ppermute(array, 'seq', pairs)  12.9 us
    ppermute x8, waiting for transfers between devices, swap_shards(): return lax.ppermute(array, 'seq', pairs)  5.25 us
    pallas_call x1, Pallas kernels, per_device_halves(): pl.pallas_call(hold_kernel, out_shape=pltpu.VMEM(out_weight.shape, jnp.bf...  1.67 us
    pallas_call x1, Pallas kernels, per_device_halves(): pl.pallas_call(project_kernel, out_shape=[jax.ShapeDtypeStruct((tok_dev,...  1.11 us
    ppermute x1, waiting for transfers between devices, per_device_halves(): partner_back = lax.ppermute(send, ('seq', 'branch'), across)  1.1 us
    pallas_call x1, Pallas kernels, per_device_halves(): pl.pallas_call(pack_kernel, out_shape=[pltpu.VMEM((3 * tok_dev, half_widt...  1 us
    pallas_call x1, Pallas kernels, per_device_halves(): pl.pallas_call(functools.partial(logsum_kernel, seq_count), out_shape=[pl...  0.56 us
  transfers between devices with their start and end apart: 10, of which 5 were waited for; matrix products, arithmetic and copies ran while one was open for 0% of the time, Pallas kernels for 7%

profile of v1, /device:TPU:0, one launch (start us, length us, event | category | flops | bytes accessed | tf_op | source)
XLA Modules:
  0.0 25.2 jit_solution(17263196389099392623)
XLA Ops:
  0.6 1.0 %pack.1 = (bf16[48,768]{1,0:T(8,128)(2,1)S(1)}, bf16[48,768]{1,0:T(8,128)(2,1)S(1)}, bf16[48,768]{1,0:T(8,128)(2,1)S(1)}, s32[8,128]{1,0:T(8,128)S(1)}, s32[2,8,...) custom-call(bf16[1,16,1536]{2,1,0:T(8,128)(2,1)} %query_hbm.1, bf16[1,16,1536]{2,1,0:T(8,128)(2,1)} %key_hbm.1, ...), custom_call_target="tpu_custom_call" | custom-call | tf_op jit(solution)/shard_map/pack/pallas_call | solution.py:406
  1.6 4.1 %collective-permute-start.1 = (bf16[48,768]{1,0:T(8,128)(2,1)S(1)}, bf16[48,768]{1,0:T(8,128)(2,1)S(1)}, u32[]{:S(2)}, u32[]{:S(2)}) collective-permute-start(bf16[48,768]{1,0:T(8,128)(2,1)S(1)} %get-tuple-element.17), channel_id=1, source_target_pairs={{0,8},{2,10},{4,12},{6,14},{8,0},{10,2},{12,4},{14,6},{1,9},{3,11}... | collective-permute-start | bytes 221192 | tf_op jit(solution)/shard_map/ppermute | solution.py:175
  5.7 1.3 %collective-permute-start.2 = (bf16[48,768]{1,0:T(8,128)(2,1)S(1)}, bf16[48,768]{1,0:T(8,128)(2,1)S(1)}, u32[]{:S(2)}, u32[]{:S(2)}) collective-permute-start(bf16[48,768]{1,0:T(8,128)(2,1)S(1)} %get-tuple-element.16), channel_id=1, source_target_pairs={{0,12},{2,14},{4,8},{6,10},{8,4},{10,6},{12,0},{14,2},{1,13},{3,15... | collective-permute-start | bytes 221192 | tf_op jit(solution)/shard_map/ppermute | solution.py:175
  7.1 0.2 collective-permute-start
  7.3 1.5 %collective-permute-start.3 = (bf16[48,768]{1,0:T(8,128)(2,1)S(1)}, bf16[48,768]{1,0:T(8,128)(2,1)S(1)}, u32[]{:S(2)}, u32[]{:S(2)}) collective-permute-start(bf16[48,768]{1,0:T(8,128)(2,1)S(1)} %get-tuple-element.15.refs_0_), channel_id=1, source_target_pairs={{0,2},{2,0},{4,6},{6,4},{8,10},{10,8},{12,14},{14,12},{1,3},{3,1},... | collective-permute-start | bytes 221192 | tf_op jit(solution)/shard_map/ppermute | solution.py:175
  8.8 1.8 %collective-permute-done.1.refs_2_ = bf16[48,768]{1,0:T(8,128)(2,1)S(1)} collective-permute-done((bf16[48,768]{1,0:T(8,128)(2,1)S(1)}, bf16[48,768]{1,0:T(8,128)(2,1)S(1)}, u32[]{:S(2)}, u32[]{:S(2)}) %collective-permute-start.1) | collective-permute-done | bytes 73760 | tf_op jit(solution)/shard_map/ppermute | solution.py:175
  10.6 2.0 %collective-permute-start.5 = (bf16[48,768]{1,0:T(8,128)(2,1)S(1)}, bf16[48,768]{1,0:T(8,128)(2,1)S(1)}, u32[]{:S(2)}, u32[]{:S(2)}) collective-permute-start(bf16[48,768]{1,0:T(8,128)(2,1)S(1)} %collective-permute-done.1.refs_2_), channel_id=1, source_target_pairs={{0,2},{2,0},{4,6},{6,4},{8,10},{10,8},{12,14},{14,12},{1,3},{3,1},... | collective-permute-start | bytes 221192 | tf_op jit(solution)/shard_map/ppermute | solution.py:175
  12.6 0.0 collective-permute-done.2.refs_3_
  12.6 1.1 %collective-permute-start.6 = (bf16[48,768]{1,0:T(8,128)(2,1)S(1)}, bf16[48,768]{1,0:T(8,128)(2,1)S(1)}, u32[]{:S(2)}, u32[]{:S(2)}) collective-permute-start(bf16[48,768]{1,0:T(8,128)(2,1)S(1)} %collective-permute-done.2.refs_3_), channel_id=1, source_target_pairs={{0,2},{2,0},{4,6},{6,4},{8,10},{10,8},{12,14},{14,12},{1,3},{3,1},... | collective-permute-start | bytes 221192 | tf_op jit(solution)/shard_map/ppermute | solution.py:175
  13.7 0.0 collective-permute-done.refs_1_
  13.7 0.9 %collective-permute-start.4 = (bf16[48,768]{1,0:T(8,128)(2,1)S(1)}, bf16[48,768]{1,0:T(8,128)(2,1)S(1)}, u32[]{:S(2)}, u32[]{:S(2)}) collective-permute-start(bf16[48,768]{1,0:T(8,128)(2,1)S(1)} %collective-permute-done.refs_1_), channel_id=1, source_target_pairs={{0,2},{2,0},{4,6},{6,4},{8,10},{10,8},{12,14},{14,12},{1,3},{3,1},... | collective-permute-start | bytes 221192 | tf_op jit(solution)/shard_map/ppermute | solution.py:175
  14.6 0.0 collective-permute-done.3.refs_4_
  14.6 1.1 %collective-permute-done.5.refs_6_ = bf16[48,768]{1,0:T(8,128)(2,1)S(1)} collective-permute-done((bf16[48,768]{1,0:T(8,128)(2,1)S(1)}, bf16[48,768]{1,0:T(8,128)(2,1)S(1)}, u32[]{:S(2)}, u32[]{:S(2)}) %collective-permute-start.5) | collective-permute-done | bytes 73760 | tf_op jit(solution)/shard_map/ppermute | solution.py:175
  15.7 1.2 %collective-permute-done.6.refs_7_ = bf16[48,768]{1,0:T(8,128)(2,1)S(1)} collective-permute-done((bf16[48,768]{1,0:T(8,128)(2,1)S(1)}, bf16[48,768]{1,0:T(8,128)(2,1)S(1)}, u32[]{:S(2)}, u32[]{:S(2)}) %collective-permute-start.6) | collective-permute-done | bytes 73760 | tf_op jit(solution)/shard_map/ppermute | solution.py:175
  16.9 1.1 %collective-permute-done.4.refs_5_ = bf16[48,768]{1,0:T(8,128)(2,1)S(1)} collective-permute-done((bf16[48,768]{1,0:T(8,128)(2,1)S(1)}, bf16[48,768]{1,0:T(8,128)(2,1)S(1)}, u32[]{:S(2)}, u32[]{:S(2)}) %collective-permute-start.4) | collective-permute-done | bytes 73760 | tf_op jit(solution)/shard_map/ppermute | solution.py:175
  18.1 0.4 %attend.1 = (bf16[16,768]{1,0:T(8,128)(2,1)S(1)}, bf16[16,768]{1,0:T(8,128)(2,1)S(1)}) custom-call(s32[8,128]{1,0:T(8,128)S(1)} %get-tuple-element.14.limits_ref, bf16[48,768]{1,0:T(8,128)(2,1)S(1)} %get-tuple-element.15.refs_0_, bf16[48,768]{1,0:T(8,128)(2,1)S(1)} %collective-permute-done.refs_1_, bf16[48,768]{1,0:T(8,128)(2,1)S(1)} %collective-permute-done.1.refs_2_, ...), custom_call_target="tpu_custom_call" | custom-call | tf_op jit(solution)/shard_map/attend/pallas_call | solution.py:434
  18.5 0.6 %logsum.1 = (bf16[32,768]{1,0:T(8,128)(2,1)S(1)}, f32[8,128]{1,0:T(8,128)S(1)}) custom-call(s32[8,128]{1,0:T(8,128)S(1)} %get-tuple-element.14.limits_ref, bf16[16,768]{1,0:T(8,128)(2,1)S(1)} %get-tuple-element.19.send_ref, bf16[48,768]{1,0:T(8,128)(2,1)S(1)} %get-tuple-element.15.refs_0_, bf16[48,768]{1,0:T(8,128)(2,1)S(1)} %collective-permute-done.refs_1_, ...), custom_call_target="tpu_custom_call" | custom-call | tf_op jit(solution)/shard_map/logsum/pallas_call | solution.py:445
  19.1 1.7 %collective-permute-start.7 = (bf16[32,768]{1,0:T(8,128)(2,1)S(1)}, bf16[32,768]{1,0:T(8,128)(2,1)S(1)}, u32[]{:S(2)}, u32[]{:S(2)}) collective-permute-start(bf16[32,768]{1,0:T(8,128)(2,1)S(1)} %get-tuple-element.20), channel_id=1, source_target_pairs={{0,4},{2,6},{4,0},{6,2},{8,12},{10,14},{12,8},{14,10},{1,5},{3,7},... | collective-permute-start | bytes 147464 | tf_op jit(solution)/shard_map/ppermute | solution.py:175
  20.8 0.0 collective-permute-start.8
  20.8 0.5 %collective-permute-start.9 = (bf16[16,768]{1,0:T(8,128)(2,1)S(1)}, bf16[16,768]{1,0:T(8,128)(2,1)S(1)}, u32[]{:S(2)}, u32[]{:S(2)}) collective-permute-start(bf16[16,768]{1,0:T(8,128)(2,1)S(1)} %get-tuple-element.19.send_ref), channel_id=1, source_target_pairs={{0,5},{1,4},{2,7},{3,6},{4,1},{5,0},{6,3},{7,2},{8,13},{9,12},{10,... | collective-permute-start | bytes 73736 | tf_op jit(solution)/shard_map/ppermute | solution.py:443
  21.3 1.7 %hold.1.weight_ref = bf16[1536,768]{1,0:T(8,128)(2,1)S(1)} custom-call(bf16[1536,768]{1,0:T(8,128)(2,1)} %weight_hbm.1, f32[8,128]{1,0:T(8,128)S(1)} %get-tuple-element.21.after_ref.table_ref), custom_call_target="tpu_custom_call" | custom-call | bytes 4718592 | tf_op jit(solution)/shard_map/hold/pallas_call | solution.py:457
  22.9 0.0 collective-permute-done.8.partner_keep_ref
  23.0 1.1 %collective-permute-done.9.partner_back_ref = bf16[16,768]{1,0:T(8,128)(2,1)S(1)} collective-permute-done((bf16[16,768]{1,0:T(8,128)(2,1)S(1)}, bf16[16,768]{1,0:T(8,128)(2,1)S(1)}, u32[]{:S(2)}, u32[]{:S(2)}) %collective-permute-start.9) | collective-permute-done | bytes 24608 | tf_op jit(solution)/shard_map/ppermute | solution.py:443
  24.1 0.0 collective-permute-done.7.message_ref
  24.1 1.1 %project.1 = (bf16[16,768]{1,0:T(8,128)(2,1)}, f32[2,8,16]{2,1,0:T(8,128)}) custom-call(bf16[16,768]{1,0:T(8,128)(2,1)S(1)} %get-tuple-element.18.keep_ref, bf16[32,768]{1,0:T(8,128)(2,1)S(1)} %collective-permute-done.7.message_ref, bf16[16,768]{1,0:T(8,128)(2,1)S(1)} %collective-permute-done.8.partner_keep_ref, ...), custom_call_target="tpu_custom_call" | custom-call | tf_op jit(solution)/shard_map/project/pallas_call | solution.py:470
Async XLA Ops:
  1.6 9.0 %collective-permute-start.1 = (bf16[48,768]{1,0:T(8,128)(2,1)S(1)}, bf16[48,768]{1,0:T(8,128)(2,1)S(1)}, u32[]{:S(2)}, u32[]{:S(2)}) collective-permute-start(bf16[48,768]{1,0:T(8,128)(2,1)S(1)} %get-tuple-element.17), channel_id=1, source_target_pairs={{0,8},{2,10},{4,12},{6,14},{8,0},{10,2},{12,4},{14,6},{1,9},{3,11}... | collective-permute-start | bytes 221192 | tf_op jit(solution)/shard_map/ppermute | solution.py:175
  5.7 6.9 %collective-permute-start.2 = (bf16[48,768]{1,0:T(8,128)(2,1)S(1)}, bf16[48,768]{1,0:T(8,128)(2,1)S(1)}, u32[]{:S(2)}, u32[]{:S(2)}) collective-permute-start(bf16[48,768]{1,0:T(8,128)(2,1)S(1)} %get-tuple-element.16), channel_id=1, source_target_pairs={{0,12},{2,14},{4,8},{6,10},{8,4},{10,6},{12,0},{14,2},{1,13},{3,15... | collective-permute-start | bytes 221192 | tf_op jit(solution)/shard_map/ppermute | solution.py:175
  7.1 6.6 %collective-permute-start = (bf16[48,768]{1,0:T(8,128)(2,1)S(1)}, bf16[48,768]{1,0:T(8,128)(2,1)S(1)}, u32[]{:S(2)}, u32[]{:S(2)}) collective-permute-start(bf16[48,768]{1,0:T(8,128)(2,1)S(1)} %get-tuple-element.16), channel_id=1, source_target_pairs={{0,4},{2,6},{4,0},{6,2},{8,12},{10,14},{12,8},{14,10},{1,5},{3,7},... | collective-permute-start | bytes 221192 | tf_op jit(solution)/shard_map/ppermute | solution.py:175
  7.3 7.3 %collective-permute-start.3 = (bf16[48,768]{1,0:T(8,128)(2,1)S(1)}, bf16[48,768]{1,0:T(8,128)(2,1)S(1)}, u32[]{:S(2)}, u32[]{:S(2)}) collective-permute-start(bf16[48,768]{1,0:T(8,128)(2,1)S(1)} %get-tuple-element.15.refs_0_), channel_id=1, source_target_pairs={{0,2},{2,0},{4,6},{6,4},{8,10},{10,8},{12,14},{14,12},{1,3},{3,1},... | collective-permute-start | bytes 221192 | tf_op jit(solution)/shard_map/ppermute | solution.py:175
  10.6 5.1 %collective-permute-start.5 = (bf16[48,768]{1,0:T(8,128)(2,1)S(1)}, bf16[48,768]{1,0:T(8,128)(2,1)S(1)}, u32[]{:S(2)}, u32[]{:S(2)}) collective-permute-start(bf16[48,768]{1,0:T(8,128)(2,1)S(1)} %collective-permute-done.1.refs_2_), channel_id=1, source_target_pairs={{0,2},{2,0},{4,6},{6,4},{8,10},{10,8},{12,14},{14,12},{1,3},{3,1},... | collective-permute-start | bytes 221192 | tf_op jit(solution)/shard_map/ppermute | solution.py:175
  12.6 4.4 %collective-permute-start.6 = (bf16[48,768]{1,0:T(8,128)(2,1)S(1)}, bf16[48,768]{1,0:T(8,128)(2,1)S(1)}, u32[]{:S(2)}, u32[]{:S(2)}) collective-permute-start(bf16[48,768]{1,0:T(8,128)(2,1)S(1)} %collective-permute-done.2.refs_3_), channel_id=1, source_target_pairs={{0,2},{2,0},{4,6},{6,4},{8,10},{10,8},{12,14},{14,12},{1,3},{3,1},... | collective-permute-start | bytes 221192 | tf_op jit(solution)/shard_map/ppermute | solution.py:175
  13.7 4.4 %collective-permute-start.4 = (bf16[48,768]{1,0:T(8,128)(2,1)S(1)}, bf16[48,768]{1,0:T(8,128)(2,1)S(1)}, u32[]{:S(2)}, u32[]{:S(2)}) collective-permute-start(bf16[48,768]{1,0:T(8,128)(2,1)S(1)} %collective-permute-done.refs_1_), channel_id=1, source_target_pairs={{0,2},{2,0},{4,6},{6,4},{8,10},{10,8},{12,14},{14,12},{1,3},{3,1},... | collective-permute-start | bytes 221192 | tf_op jit(solution)/shard_map/ppermute | solution.py:175
  19.1 5.0 %collective-permute-start.7 = (bf16[32,768]{1,0:T(8,128)(2,1)S(1)}, bf16[32,768]{1,0:T(8,128)(2,1)S(1)}, u32[]{:S(2)}, u32[]{:S(2)}) collective-permute-start(bf16[32,768]{1,0:T(8,128)(2,1)S(1)} %get-tuple-element.20), channel_id=1, source_target_pairs={{0,4},{2,6},{4,0},{6,2},{8,12},{10,14},{12,8},{14,10},{1,5},{3,7},... | collective-permute-start | bytes 147464 | tf_op jit(solution)/shard_map/ppermute | solution.py:175
  20.8 2.1 %collective-permute-start.8 = (bf16[16,768]{1,0:T(8,128)(2,1)S(1)}, bf16[16,768]{1,0:T(8,128)(2,1)S(1)}, u32[]{:S(2)}, u32[]{:S(2)}) collective-permute-start(bf16[16,768]{1,0:T(8,128)(2,1)S(1)} %get-tuple-element.18.keep_ref), channel_id=1, source_target_pairs={{0,1},{1,0},{2,3},{3,2},{4,5},{5,4},{6,7},{7,6},{8,9},{9,8},{10,11... | collective-permute-start | bytes 73736 | tf_op jit(solution)/shard_map/ppermute | solution.py:20
  20.8 3.3 %collective-permute-start.9 = (bf16[16,768]{1,0:T(8,128)(2,1)S(1)}, bf16[16,768]{1,0:T(8,128)(2,1)S(1)}, u32[]{:S(2)}, u32[]{:S(2)}) collective-permute-start(bf16[16,768]{1,0:T(8,128)(2,1)S(1)} %get-tuple-element.19.send_ref), channel_id=1, source_target_pairs={{0,5},{1,4},{2,7},{3,6},{4,1},{5,0},{6,3},{7,2},{8,13},{9,12},{10,... | collective-permute-start | bytes 73736 | tf_op jit(solution)/shard_map/ppermute | solution.py:443

commit v2 on v1

--- a/solution.py
+++ b/solution.py
@@ -166,6 +166,7 @@
 
 
 SPLIT = 2
+HOLD_COPIES = 4
 TABLE_PIECES = 3
 SPLITTER = 65537.0
 
@@ -188,7 +189,6 @@
     head_hbm,
     own_ref,
     other_ref,
-    line_copy_ref,
     limits_ref,
     pick_ref,
     slot_head_ref,
@@ -205,7 +205,7 @@
         pltpu.make_async_copy(counts_hbm, counts_ref, copy_sems.at[0]),
         pltpu.make_async_copy(head_hbm, head_ref, copy_sems.at[1]),
     ]
-    for target, place in ((line_copy_ref, half), (other_ref, 1 - half), (own_ref, half)):
+    for target, place in ((other_ref, 1 - half), (own_ref, half)):
         columns = pl.ds(pl.multiple_of(place * half_width, half_width), half_width)
         for part, source in enumerate((key_hbm, value_hbm, query_hbm)):
             rows = pl.ds(part * tok_dev, tok_dev)
@@ -248,10 +248,20 @@
         copy.wait()
 
 
-def hold_kernel(weight_hbm, after_ref, weight_ref, weight_sem):
-    copy = pltpu.make_async_copy(weight_hbm, weight_ref, weight_sem)
-    copy.start()
-    copy.wait()
+def hold_kernel(weight_hbm, after_ref, weight_ref, copy_sems):
+    share = weight_ref.shape[0] // HOLD_COPIES
+    copies = []
+    for number in range(HOLD_COPIES):
+        rows = pl.ds(number * share, share)
+        copies.append(
+            pltpu.make_async_copy(
+                weight_hbm.at[rows, :], weight_ref.at[rows, :], copy_sems.at[number]
+            )
+        )
+    for copy in copies:
+        copy.start()
+    for copy in copies:
+        copy.wait()
 
 
 def gathered(set_refs, part, columns):
@@ -333,10 +343,33 @@
         message_ref[pl.ds(tok_dev, tok_dev), columns] = block.astype(jnp.bfloat16)
 
 
+def guidance(own, partner):
+    on_positive = lax.axis_index("branch") == 0
+    own_scale = jnp.where(on_positive, GUIDE_SCALE, 1.0 - GUIDE_SCALE)
+    partner_scale = jnp.where(on_positive, 1.0 - GUIDE_SCALE, GUIDE_SCALE)
+    return own_scale * own.astype(jnp.float32) + partner_scale * partner.astype(jnp.float32)
+
+
+def half_product(guided, weight_ref, place):
+    half_width = guided.shape[1]
+    rows = pl.ds(pl.multiple_of(place * half_width, half_width), half_width)
+    return jnp.dot(
+        guided.astype(jnp.bfloat16), weight_ref[rows, :], preferred_element_type=jnp.float32
+    )
+
+
+def keep_kernel(keep_ref, partner_keep_ref, weight_ref, total_ref, size_ref):
+    half = (lax.axis_index("seq") // SPLIT) % 2
+    guided = guidance(keep_ref[...], partner_keep_ref[...])
+    size = jnp.sum(jnp.abs(guided), axis=1, keepdims=True)
+    size_ref[...] = jnp.broadcast_to(size, size_ref.shape)
+    total_ref[...] = half_product(guided, weight_ref, half)
+
+
 def project_kernel(
-    keep_ref,
+    total_ref,
+    size_ref,
     message_ref,
-    partner_keep_ref,
     partner_back_ref,
     weight_ref,
     table_ref,
@@ -345,29 +378,15 @@
     projected_ref,
     saved_ref,
 ):
-    tok_dev, half_width = keep_ref.shape
+    tok_dev, half_width = partner_back_ref.shape
     half_heads = half_width // HDIM
     tokens = table_ref.shape[1]
     half = (lax.axis_index("seq") // SPLIT) % 2
-    on_positive = lax.axis_index("branch") == 0
-    own_scale = jnp.where(on_positive, GUIDE_SCALE, 1.0 - GUIDE_SCALE)
-    partner_scale = jnp.where(on_positive, 1.0 - GUIDE_SCALE, GUIDE_SCALE)
-    parts = [
-        own_scale * own.astype(jnp.float32) + partner_scale * partner.astype(jnp.float32)
-        for own, partner in (
-            (keep_ref[...], partner_keep_ref[...]),
-            (message_ref[pl.ds(0, tok_dev), :], partner_back_ref[...]),
-        )
-    ]
-    magnitude = jnp.sum(
-        jnp.abs(parts[0]) + jnp.abs(parts[1]), axis=1, keepdims=True
-    ) / (2 * half_width)
-    total = jnp.zeros(projected_ref.shape, jnp.float32)
-    for part, place in zip(parts, (half, 1 - half)):
-        normed = (part / (magnitude + EPSILON)).astype(jnp.bfloat16)
-        rows = pl.ds(pl.multiple_of(place * half_width, half_width), half_width)
-        total = total + jnp.dot(normed, weight_ref[rows, :], preferred_element_type=jnp.float32)
-    projected_ref[...] = total.astype(jnp.bfloat16)
+    guided = guidance(message_ref[pl.ds(0, tok_dev), :], partner_back_ref[...])
+    size = size_ref[:, 0:1] + jnp.sum(jnp.abs(guided), axis=1, keepdims=True)
+    magnitude = size / (2 * half_width)
+    total = total_ref[...] + half_product(guided, weight_ref, 1 - half)
+    projected_ref[...] = (total / (magnitude + EPSILON)).astype(jnp.bfloat16)
 
     for slot in range(saved_ref.shape[0]):
         slot_head = slot_head_ref[slot, 0:1, :]
@@ -403,10 +422,9 @@
     def far(*arrays):
         return [pltpu.with_memory_space_constraint(array, pltpu.HBM) for array in arrays]
 
-    own, other, line_copy, limits, pick, slot_head = pl.pallas_call(
+    own, other, limits, pick, slot_head = pl.pallas_call(
         pack_kernel,
         out_shape=[
-            pltpu.VMEM((3 * tok_dev, half_width), jnp.bfloat16),
             pltpu.VMEM((3 * tok_dev, half_width), jnp.bfloat16),
             pltpu.VMEM((3 * tok_dev, half_width), jnp.bfloat16),
             pltpu.VMEM((8, tokens), jnp.int32),
@@ -414,22 +432,35 @@
             pltpu.VMEM((slot_count, 8, tokens), jnp.int32),
         ],
         in_specs=[any_spec] * 5,
-        out_specs=[vmem] * 6,
+        out_specs=[vmem] * 5,
         scratch_shapes=[
             pltpu.SMEM((seq_count,), jnp.int32),
             pltpu.SMEM((slot_count, seq_count), jnp.int32),
-            pltpu.SemaphoreType.DMA((11,)),
+            pltpu.SemaphoreType.DMA((8,)),
         ],
         compiler_params=KERNEL_PARAMS,
         name="pack",
     )(*far(queries, key_rows, value_rows, counts, jnp.transpose(head_of)))
 
+    weight_held = pl.pallas_call(
+        hold_kernel,
+        out_shape=pltpu.VMEM(out_weight.shape, jnp.bfloat16),
+        in_specs=[any_spec, vmem],
+        out_specs=vmem,
+        scratch_shapes=[pltpu.SemaphoreType.DMA((HOLD_COPIES,))],
+        compiler_params=KERNEL_PARAMS,
+        cost_estimate=pl.CostEstimate(
+            flops=0, bytes_accessed=4 * out_weight.size, transcendentals=0
+        ),
+        name="hold",
+    )(*far(out_weight), *held(limits))
     sets = {0: own}
     for offset in range(SPLIT, seq_count, SPLIT):
-        sets[offset] = swap_shards(other if offset & SPLIT else line_copy, offset)
+        sets[offset] = swap_shards(other if offset & SPLIT else own, offset)
     for offset in range(0, seq_count, SPLIT):
         sets[offset + 1] = swap_shards(sets[offset], 1)
     set_list = held(*[sets[offset] for offset in set_order(seq_count)])
+    limits, weight_held = lax.optimization_barrier((limits, weight_held))
     limits = held(limits)[0]
     keep, send = pl.pallas_call(
         functools.partial(attend_kernel, seq_count),
@@ -454,19 +485,18 @@
         compiler_params=KERNEL_PARAMS,
         name="logsum",
     )(limits, *held(send), *set_list)
-    weight_held = pl.pallas_call(
-        hold_kernel,
-        out_shape=pltpu.VMEM(out_weight.shape, jnp.bfloat16),
-        in_specs=[any_spec, vmem],
-        out_specs=vmem,
-        scratch_shapes=[pltpu.SemaphoreType.DMA],
+    back = swap_shards(message, SPLIT)
+    total, size = pl.pallas_call(
+        keep_kernel,
+        out_shape=[
+            pltpu.VMEM((tok_dev, out_weight.shape[1]), jnp.float32),
+            pltpu.VMEM((tok_dev, HDIM), jnp.float32),
+        ],
+        in_specs=[vmem] * 3,
+        out_specs=[vmem] * 2,
         compiler_params=KERNEL_PARAMS,
-        cost_estimate=pl.CostEstimate(
-            flops=0, bytes_accessed=4 * out_weight.size, transcendentals=0
-        ),
-        name="hold",
-    )(*far(out_weight), *held(table))
-    back = swap_shards(message, SPLIT)
+        name="keep",
+    )(*held(keep, partner_keep, weight_held))
     projected, saved = pl.pallas_call(
         project_kernel,
         out_shape=[
@@ -477,7 +507,7 @@
         out_specs=[vmem] * 2,
         compiler_params=KERNEL_PARAMS,
         name="project",
-    )(*held(keep, back, partner_keep, partner_back, weight_held, table, pick, slot_head))
+    )(*held(total, size, back, partner_back, weight_held, table, pick, slot_head))
     saved = jnp.transpose(saved, (0, 2, 1))
     return (projected, saved.reshape(1, 1, slot_count, row_cap, seq_count))
 

time: 25.4 us -> 24.4 us (0.961)
  waiting for transfers between devices: 6.35 us -> 5.29 us
    ppermute x8, waiting for transfers between devices: 5.25 us -> 3.27 us  [swap_shards(): return lax.ppermute(array, 'seq', pairs)]
    ppermute x1, waiting for transfers between devices: 1.1 us -> 1.78 us  [per_device_halves(): partner_back = lax.ppermute(send, ('seq', 'branch'), across)]
    ppermute x1, starting transfers between devices: 0.46 us -> 0.95 us  [per_device_halves(): partner_back = lax.ppermute(send, ('seq', 'branch'), across)]
    ppermute x8, starting transfers between devices: 12.9 us -> 12.5 us  [swap_shards(): return lax.ppermute(array, 'seq', pairs)]
    pallas_call x0 -> x1, Pallas kernels: none -> 0.28 us  [per_device_halves(): pl.pallas_call(keep_kernel, out_shape=[pltpu.VMEM((tok_dev, out_weight.sh...]
  transfers between devices with their start and end apart: 10 -> 10, of which waited for: 5 -> 6; matrix products, arithmetic and copies ran while one was open for 0% -> 0% of each run, Pallas kernels for 7% -> 8%
where the time goes in v2:
time: 24.4 us; the launch traced here: 24.1 us
  starting transfers between devices  13.4 us (55%)
  waiting for transfers between devices  5.29 us (22%)
  Pallas kernels  4.73 us (19%)
  between operations  0.68 us (3%)
    ppermute x8, starting transfers between devices, swap_shards(): return lax.ppermute(array, 'seq', pairs)  12.5 us
    ppermute x8, waiting for transfers between devices, swap_shards(): return lax.ppermute(array, 'seq', pairs)  3.27 us
    ppermute x1, waiting for transfers between devices, per_device_halves(): partner_back = lax.ppermute(send, ('seq', 'branch'), across)  1.78 us
    pallas_call x1, Pallas kernels, per_device_halves(): pl.pallas_call(hold_kernel, out_shape=pltpu.VMEM(out_weight.shape, jnp.bf...  1.63 us
    ppermute x1, starting transfers between devices, per_device_halves(): partner_back = lax.ppermute(send, ('seq', 'branch'), across)  0.95 us
    pallas_call x1, Pallas kernels, per_device_halves(): pl.pallas_call(pack_kernel, out_shape=[pltpu.VMEM((3 * tok_dev, half_widt...  0.92 us
    pallas_call x1, Pallas kernels, per_device_halves(): pl.pallas_call(project_kernel, out_shape=[jax.ShapeDtypeStruct((tok_dev,...  0.92 us
    pallas_call x1, Pallas kernels, per_device_halves(): pl.pallas_call(functools.partial(logsum_kernel, seq_count), out_shape=[pl...  0.55 us
  transfers between devices with their start and end apart: 10, of which 6 were waited for; matrix products, arithmetic and copies ran while one was open for 0% of the time, Pallas kernels for 8%

profile of v2, /device:TPU:0, one launch (start us, length us, event | category | flops | bytes accessed | tf_op | source)
XLA Modules:
  0.0 24.1 jit_solution(10998259837688519275)
XLA Ops:
  0.6 0.9 %pack.1 = (bf16[48,768]{1,0:T(8,128)(2,1)S(1)}, bf16[48,768]{1,0:T(8,128)(2,1)S(1)}, s32[8,128]{1,0:T(8,128)S(1)}, s32[2,8,128]{2,1,0:T(8,128)S(1)}, s32[2,8,128]{2,1,0:T(8,128)S(1)}) custom-call(bf16[1,16,1536]{2,1,0:T(8,128)(2,1)} %query_hbm.1, bf16[1,16,1536]{2,1,0:T(8,128)(2,1)} %key_hbm.1, bf16[1,16,1536]{2,1,0:T(8,128)(2,1)} %value_hbm.1, ...), custom_call_target="tpu_custom_call" | custom-call | tf_op jit(solution)/shard_map/pack/pallas_call | solution.py:425
  1.6 5.1 %collective-permute-start.2 = (bf16[48,768]{1,0:T(8,128)(2,1)S(1)}, bf16[48,768]{1,0:T(8,128)(2,1)S(1)}, u32[]{:S(2)}, u32[]{:S(2)}) collective-permute-start(bf16[48,768]{1,0:T(8,128)(2,1)S(1)} %get-tuple-element.20), channel_id=1, source_target_pairs={{0,12},{2,14},{4,8},{6,10},{8,4},{10,6},{12,0},{14,2},{1,13},{3,15... | collective-permute-start | bytes 221192 | tf_op jit(solution)/shard_map/ppermute | solution.py:176
  6.7 0.0 collective-permute-start
  6.7 0.6 %collective-permute-start.1 = (bf16[48,768]{1,0:T(8,128)(2,1)S(1)}, bf16[48,768]{1,0:T(8,128)(2,1)S(1)}, u32[]{:S(2)}, u32[]{:S(2)}) collective-permute-start(bf16[48,768]{1,0:T(8,128)(2,1)S(1)} %get-tuple-element.19.refs_0_), channel_id=1, source_target_pairs={{0,8},{2,10},{4,12},{6,14},{8,0},{10,2},{12,4},{14,6},{1,9},{3,11}... | collective-permute-start | bytes 221192 | tf_op jit(solution)/shard_map/ppermute | solution.py:176
  7.3 1.6 %collective-permute-start.3 = (bf16[48,768]{1,0:T(8,128)(2,1)S(1)}, bf16[48,768]{1,0:T(8,128)(2,1)S(1)}, u32[]{:S(2)}, u32[]{:S(2)}) collective-permute-start(bf16[48,768]{1,0:T(8,128)(2,1)S(1)} %get-tuple-element.19.refs_0_), channel_id=1, source_target_pairs={{0,2},{2,0},{4,6},{6,4},{8,10},{10,8},{12,14},{14,12},{1,3},{3,1},... | collective-permute-start | bytes 221192 | tf_op jit(solution)/shard_map/ppermute | solution.py:176
  9.0 0.9 %collective-permute-done.2.refs_3_ = bf16[48,768]{1,0:T(8,128)(2,1)S(1)} collective-permute-done((bf16[48,768]{1,0:T(8,128)(2,1)S(1)}, bf16[48,768]{1,0:T(8,128)(2,1)S(1)}, u32[]{:S(2)}, u32[]{:S(2)}) %collective-permute-start.2) | collective-permute-done | bytes 73760 | tf_op jit(solution)/shard_map/ppermute | solution.py:176
  9.8 1.5 %collective-permute-start.6 = (bf16[48,768]{1,0:T(8,128)(2,1)S(1)}, bf16[48,768]{1,0:T(8,128)(2,1)S(1)}, u32[]{:S(2)}, u32[]{:S(2)}) collective-permute-start(bf16[48,768]{1,0:T(8,128)(2,1)S(1)} %collective-permute-done.2.refs_3_), channel_id=1, source_target_pairs={{0,2},{2,0},{4,6},{6,4},{8,10},{10,8},{12,14},{14,12},{1,3},{3,1},... | collective-permute-start | bytes 221192 | tf_op jit(solution)/shard_map/ppermute | solution.py:176
  11.3 0.4 %collective-permute-done.refs_1_ = bf16[48,768]{1,0:T(8,128)(2,1)S(1)} collective-permute-done((bf16[48,768]{1,0:T(8,128)(2,1)S(1)}, bf16[48,768]{1,0:T(8,128)(2,1)S(1)}, u32[]{:S(2)}, u32[]{:S(2)}) %collective-permute-start) | collective-permute-done | bytes 73760 | tf_op jit(solution)/shard_map/ppermute | solution.py:176
  11.7 1.6 %collective-permute-start.4 = (bf16[48,768]{1,0:T(8,128)(2,1)S(1)}, bf16[48,768]{1,0:T(8,128)(2,1)S(1)}, u32[]{:S(2)}, u32[]{:S(2)}) collective-permute-start(bf16[48,768]{1,0:T(8,128)(2,1)S(1)} %collective-permute-done.refs_1_), channel_id=1, source_target_pairs={{0,2},{2,0},{4,6},{6,4},{8,10},{10,8},{12,14},{14,12},{1,3},{3,1},... | collective-permute-start | bytes 221192 | tf_op jit(solution)/shard_map/ppermute | solution.py:176
  13.4 0.0 collective-permute-done.1.refs_2_
  13.4 0.7 %collective-permute-start.5 = (bf16[48,768]{1,0:T(8,128)(2,1)S(1)}, bf16[48,768]{1,0:T(8,128)(2,1)S(1)}, u32[]{:S(2)}, u32[]{:S(2)}) collective-permute-start(bf16[48,768]{1,0:T(8,128)(2,1)S(1)} %collective-permute-done.1.refs_2_), channel_id=1, source_target_pairs={{0,2},{2,0},{4,6},{6,4},{8,10},{10,8},{12,14},{14,12},{1,3},{3,1},... | collective-permute-start | bytes 221192 | tf_op jit(solution)/shard_map/ppermute | solution.py:176
  14.1 1.6 %hold.1.weight_ref = bf16[1536,768]{1,0:T(8,128)(2,1)S(1)} custom-call(bf16[1536,768]{1,0:T(8,128)(2,1)} %weight_hbm.1, s32[8,128]{1,0:T(8,128)S(1)} %get-tuple-element.18.after_ref.limits_ref), custom_call_target="tpu_custom_call" | custom-call | bytes 4718592 | tf_op jit(solution)/shard_map/hold/pallas_call | solution.py:445
  15.7 0.0 collective-permute-done.3.refs_4_
  15.7 0.0 collective-permute-done.6.refs_7_
  15.7 1.1 %collective-permute-done.4.refs_5_ = bf16[48,768]{1,0:T(8,128)(2,1)S(1)} collective-permute-done((bf16[48,768]{1,0:T(8,128)(2,1)S(1)}, bf16[48,768]{1,0:T(8,128)(2,1)S(1)}, u32[]{:S(2)}, u32[]{:S(2)}) %collective-permute-start.4) | collective-permute-done | bytes 73760 | tf_op jit(solution)/shard_map/ppermute | solution.py:176
  16.8 0.9 %collective-permute-done.5.refs_6_ = bf16[48,768]{1,0:T(8,128)(2,1)S(1)} collective-permute-done((bf16[48,768]{1,0:T(8,128)(2,1)S(1)}, bf16[48,768]{1,0:T(8,128)(2,1)S(1)}, u32[]{:S(2)}, u32[]{:S(2)}) %collective-permute-start.5) | collective-permute-done | bytes 73760 | tf_op jit(solution)/shard_map/ppermute | solution.py:176
  17.7 0.4 %attend.1 = (bf16[16,768]{1,0:T(8,128)(2,1)S(1)}, bf16[16,768]{1,0:T(8,128)(2,1)S(1)}) custom-call(s32[8,128]{1,0:T(8,128)S(1)} %get-tuple-element.18.after_ref.limits_ref, bf16[48,768]{1,0:T(8,128)(2,1)S(1)} %get-tuple-element.19.refs_0_, bf16[48,768]{1,0:T(8,128)(2,1)S(1)} %collective-permute-done.refs_1_, ...), custom_call_target="tpu_custom_call" | custom-call | tf_op jit(solution)/shard_map/attend/pallas_call | solution.py:465
  18.1 0.6 %logsum.1 = (bf16[32,768]{1,0:T(8,128)(2,1)S(1)}, f32[8,128]{1,0:T(8,128)S(1)}) custom-call(s32[8,128]{1,0:T(8,128)S(1)} %get-tuple-element.18.after_ref.limits_ref, bf16[16,768]{1,0:T(8,128)(2,1)S(1)} %get-tuple-element.25.send_ref, bf16[48,768]{1,0:T(8,128)(2,1)S(1)} %get-tuple-element.19.refs_0_, bf16[48,768]{1,0:T(8,128)(2,1)S(1)} %collective-permute-done.refs_1_, ...), custom_call_target="tpu_custom_call" | custom-call | tf_op jit(solution)/shard_map/logsum/pallas_call | solution.py:476
  18.7 1.3 %collective-permute-start.8 = (bf16[32,768]{1,0:T(8,128)(2,1)S(1)}, bf16[32,768]{1,0:T(8,128)(2,1)S(1)}, u32[]{:S(2)}, u32[]{:S(2)}) collective-permute-start(bf16[32,768]{1,0:T(8,128)(2,1)S(1)} %get-tuple-element.26), channel_id=1, source_target_pairs={{0,4},{2,6},{4,0},{6,2},{8,12},{10,14},{12,8},{14,10},{1,5},{3,7},... | collective-permute-start | bytes 147464 | tf_op jit(solution)/shard_map/ppermute | solution.py:176
  19.9 0.0 collective-permute-start.7
  20.0 0.9 %collective-permute-start.9 = (bf16[16,768]{1,0:T(8,128)(2,1)S(1)}, bf16[16,768]{1,0:T(8,128)(2,1)S(1)}, u32[]{:S(2)}, u32[]{:S(2)}) collective-permute-start(bf16[16,768]{1,0:T(8,128)(2,1)S(1)} %get-tuple-element.25.send_ref), channel_id=1, source_target_pairs={{0,5},{1,4},{2,7},{3,6},{4,1},{5,0},{6,3},{7,2},{8,13},{9,12},{10,... | collective-permute-start | bytes 73736 | tf_op jit(solution)/shard_map/ppermute | solution.py:474
  20.9 0.2 %collective-permute-done.7.partner_keep_ref = bf16[16,768]{1,0:T(8,128)(2,1)S(1)} collective-permute-done((bf16[16,768]{1,0:T(8,128)(2,1)S(1)}, bf16[16,768]{1,0:T(8,128)(2,1)S(1)}, u32[]{:S(2)}, u32[]{:S(2)}) %collective-permute-start.7) | collective-permute-done | bytes 24608 | tf_op jit(solution)/shard_map/ppermute | solution.py:20
  21.1 0.3 %keep.1 = (f32[16,768]{1,0:T(8,128)S(1)}, f32[16,128]{1,0:T(8,128)S(1)}) custom-call(bf16[16,768]{1,0:T(8,128)(2,1)S(1)} %get-tuple-element.21.keep_ref, bf16[16,768]{1,0:T(8,128)(2,1)S(1)} %collective-permute-done.7.partner_keep_ref, bf16[1536,768]{1,0:T(8,128)(2,1)S(1)} %hold.1.weight_ref), custom_call_target="tpu_custom_call" | custom-call | tf_op jit(solution)/shard_map/keep/pallas_call | solution.py:489
  21.4 1.8 %collective-permute-done.9.partner_back_ref = bf16[16,768]{1,0:T(8,128)(2,1)S(1)} collective-permute-done((bf16[16,768]{1,0:T(8,128)(2,1)S(1)}, bf16[16,768]{1,0:T(8,128)(2,1)S(1)}, u32[]{:S(2)}, u32[]{:S(2)}) %collective-permute-start.9) | collective-permute-done | bytes 24608 | tf_op jit(solution)/shard_map/ppermute | solution.py:474
  23.2 0.0 collective-permute-done.8.message_ref
  23.2 0.9 %project.1 = (bf16[16,768]{1,0:T(8,128)(2,1)}, f32[2,8,16]{2,1,0:T(8,128)}) custom-call(f32[16,768]{1,0:T(8,128)S(1)} %get-tuple-element.23.total_ref, f32[16,128]{1,0:T(8,128)S(1)} %get-tuple-element.24.size_ref, bf16[32,768]{1,0:T(8,128)(2,1)S(1)} %collective-permute-done.8.message_ref, bf16[16,768]{1,0:T(8,128)(2,1)S(1)} %collective-permute-done.9.partner_back_ref, ...), custom_call_target="tpu_custom_call" | custom-call | tf_op jit(solution)/shard_map/project/pallas_call | solution.py:500
Async XLA Ops:
  1.6 8.3 %collective-permute-start.2 = (bf16[48,768]{1,0:T(8,128)(2,1)S(1)}, bf16[48,768]{1,0:T(8,128)(2,1)S(1)}, u32[]{:S(2)}, u32[]{:S(2)}) collective-permute-start(bf16[48,768]{1,0:T(8,128)(2,1)S(1)} %get-tuple-element.20), channel_id=1, source_target_pairs={{0,12},{2,14},{4,8},{6,10},{8,4},{10,6},{12,0},{14,2},{1,13},{3,15... | collective-permute-start | bytes 221192 | tf_op jit(solution)/shard_map/ppermute | solution.py:176
  6.7 5.0 %collective-permute-start = (bf16[48,768]{1,0:T(8,128)(2,1)S(1)}, bf16[48,768]{1,0:T(8,128)(2,1)S(1)}, u32[]{:S(2)}, u32[]{:S(2)}) collective-permute-start(bf16[48,768]{1,0:T(8,128)(2,1)S(1)} %get-tuple-element.20), channel_id=1, source_target_pairs={{0,4},{2,6},{4,0},{6,2},{8,12},{10,14},{12,8},{14,10},{1,5},{3,7},... | collective-permute-start | bytes 221192 | tf_op jit(solution)/shard_map/ppermute | solution.py:176
  6.7 6.7 %collective-permute-start.1 = (bf16[48,768]{1,0:T(8,128)(2,1)S(1)}, bf16[48,768]{1,0:T(8,128)(2,1)S(1)}, u32[]{:S(2)}, u32[]{:S(2)}) collective-permute-start(bf16[48,768]{1,0:T(8,128)(2,1)S(1)} %get-tuple-element.19.refs_0_), channel_id=1, source_target_pairs={{0,8},{2,10},{4,12},{6,14},{8,0},{10,2},{12,4},{14,6},{1,9},{3,11}... | collective-permute-start | bytes 221192 | tf_op jit(solution)/shard_map/ppermute | solution.py:176
  7.3 8.4 %collective-permute-start.3 = (bf16[48,768]{1,0:T(8,128)(2,1)S(1)}, bf16[48,768]{1,0:T(8,128)(2,1)S(1)}, u32[]{:S(2)}, u32[]{:S(2)}) collective-permute-start(bf16[48,768]{1,0:T(8,128)(2,1)S(1)} %get-tuple-element.19.refs_0_), channel_id=1, source_target_pairs={{0,2},{2,0},{4,6},{6,4},{8,10},{10,8},{12,14},{14,12},{1,3},{3,1},... | collective-permute-start | bytes 221192 | tf_op jit(solution)/shard_map/ppermute | solution.py:176
  9.8 5.9 %collective-permute-start.6 = (bf16[48,768]{1,0:T(8,128)(2,1)S(1)}, bf16[48,768]{1,0:T(8,128)(2,1)S(1)}, u32[]{:S(2)}, u32[]{:S(2)}) collective-permute-start(bf16[48,768]{1,0:T(8,128)(2,1)S(1)} %collective-permute-done.2.refs_3_), channel_id=1, source_target_pairs={{0,2},{2,0},{4,6},{6,4},{8,10},{10,8},{12,14},{14,12},{1,3},{3,1},... | collective-permute-start | bytes 221192 | tf_op jit(solution)/shard_map/ppermute | solution.py:176
  11.7 5.1 %collective-permute-start.4 = (bf16[48,768]{1,0:T(8,128)(2,1)S(1)}, bf16[48,768]{1,0:T(8,128)(2,1)S(1)}, u32[]{:S(2)}, u32[]{:S(2)}) collective-permute-start(bf16[48,768]{1,0:T(8,128)(2,1)S(1)} %collective-permute-done.refs_1_), channel_id=1, source_target_pairs={{0,2},{2,0},{4,6},{6,4},{8,10},{10,8},{12,14},{14,12},{1,3},{3,1},... | collective-permute-start | bytes 221192 | tf_op jit(solution)/shard_map/ppermute | solution.py:176
  13.4 4.4 %collective-permute-start.5 = (bf16[48,768]{1,0:T(8,128)(2,1)S(1)}, bf16[48,768]{1,0:T(8,128)(2,1)S(1)}, u32[]{:S(2)}, u32[]{:S(2)}) collective-permute-start(bf16[48,768]{1,0:T(8,128)(2,1)S(1)} %collective-permute-done.1.refs_2_), channel_id=1, source_target_pairs={{0,2},{2,0},{4,6},{6,4},{8,10},{10,8},{12,14},{14,12},{1,3},{3,1},... | collective-permute-start | bytes 221192 | tf_op jit(solution)/shard_map/ppermute | solution.py:176
  18.7 4.5 %collective-permute-start.8 = (bf16[32,768]{1,0:T(8,128)(2,1)S(1)}, bf16[32,768]{1,0:T(8,128)(2,1)S(1)}, u32[]{:S(2)}, u32[]{:S(2)}) collective-permute-start(bf16[32,768]{1,0:T(8,128)(2,1)S(1)} %get-tuple-element.26), channel_id=1, source_target_pairs={{0,4},{2,6},{4,0},{6,2},{8,12},{10,14},{12,8},{14,10},{1,5},{3,7},... | collective-permute-start | bytes 147464 | tf_op jit(solution)/shard_map/ppermute | solution.py:176
  19.9 1.2 %collective-permute-start.7 = (bf16[16,768]{1,0:T(8,128)(2,1)S(1)}, bf16[16,768]{1,0:T(8,128)(2,1)S(1)}, u32[]{:S(2)}, u32[]{:S(2)}) collective-permute-start(bf16[16,768]{1,0:T(8,128)(2,1)S(1)} %get-tuple-element.21.keep_ref), channel_id=1, source_target_pairs={{0,1},{1,0},{2,3},{3,2},{4,5},{5,4},{6,7},{7,6},{8,9},{9,8},{10,11... | collective-permute-start | bytes 73736 | tf_op jit(solution)/shard_map/ppermute | solution.py:20
  20.0 3.3 %collective-permute-start.9 = (bf16[16,768]{1,0:T(8,128)(2,1)S(1)}, bf16[16,768]{1,0:T(8,128)(2,1)S(1)}, u32[]{:S(2)}, u32[]{:S(2)}) collective-permute-start(bf16[16,768]{1,0:T(8,128)(2,1)S(1)} %get-tuple-element.25.send_ref), channel_id=1, source_target_pairs={{0,5},{1,4},{2,7},{3,6},{4,1},{5,0},{6,3},{7,2},{8,13},{9,12},{10,... | collective-permute-start | bytes 73736 | tf_op jit(solution)/shard_map/ppermute | solution.py:474

commit v3 on v2

--- a/solution.py
+++ b/solution.py
@@ -166,6 +166,7 @@
 
 
 SPLIT = 2
+FAR = 4
 HOLD_COPIES = 4
 TABLE_PIECES = 3
 SPLITTER = 65537.0
@@ -176,9 +177,26 @@
     return lax.ppermute(array, "seq", pairs)
 
 
-def set_order(shard_count):
-    line = list(range(0, shard_count, SPLIT))
-    return line + [offset + 1 for offset in line]
+def swap_by_core(array, offsets):
+    pairs = [
+        (2 * i + core, 2 * (i ^ offsets[core]) + core)
+        for i in range(lax.axis_size("seq"))
+        for core in range(2)
+    ]
+    return lax.ppermute(array, ("seq", "branch"), pairs)
+
+
+FIRST = (SPLIT, SPLIT + FAR)
+SECOND = (SPLIT + FAR, SPLIT)
+THIRD = (1, FAR)
+FOURTH = (FAR, 1)
+
+
+def place_offsets():
+    received = [(0, 0), FIRST, SECOND, THIRD, FOURTH]
+    passed_on = [(a + 1, b + 1) for a, b in (FIRST, SECOND, (FAR, FAR))]
+    core = lax.axis_index("branch")
+    return [jnp.where(core == 0, a, b) for a, b in received + passed_on]
 
 
 def pack_kernel(
@@ -221,7 +239,7 @@
 
     lane = lax.broadcasted_iota(jnp.int32, (1, limits_ref.shape[1]), 1)
     lane_limit = jnp.zeros(lane.shape, jnp.int32)
-    for place, offset in enumerate(set_order(shard_count)):
+    for place, offset in enumerate(place_offsets()):
         lane_limit = jnp.where(lane // tok_dev == place, counts_ref[shard ^ offset], lane_limit)
     limits_ref[0:1, :] = (lane % tok_dev < lane_limit).astype(jnp.int32)
     limits_ref[1:2, :] = jnp.full(lane.shape, counts_ref[shard], jnp.int32)
@@ -278,54 +296,47 @@
 
 def attend_kernel(set_count, limits_ref, *refs):
     set_refs = refs[:set_count]
-    keep_ref, send_ref = refs[set_count:]
+    keep_ref, send_ref, message_ref, table_ref, lines_ref = refs[set_count:]
     tok_dev, half_width = keep_ref.shape
-    heads = [pl.ds(start, HDIM) for start in range(0, half_width, HDIM)]
-    scores = jnp.concatenate(
-        [
-            head_scores(gathered(set_refs[:2], 2, columns), gathered(set_refs, 0, columns))
-            for columns in heads
-        ],
-        axis=0,
-    ) * (1.0 / math.sqrt(HDIM))
-    scores = jnp.where(limits_ref[0:1, :] > 0, scores, -jnp.inf)
-    weights = jnp.exp(scores - jnp.max(scores, axis=1, keepdims=True))
-    weight_sum = jnp.sum(weights, axis=1, keepdims=True)
-    rounded = weights.astype(jnp.bfloat16)
-    row = lax.broadcasted_iota(jnp.int32, (tok_dev, HDIM), 0)
-    for number, columns in enumerate(heads):
-        first = 2 * tok_dev * number
-        mixed = jnp.dot(
-            rounded[first : first + 2 * tok_dev],
-            gathered(set_refs, 1, columns),
-            preferred_element_type=jnp.float32,
+    half_heads = half_width // HDIM
+    on_first_core = lax.axis_index("branch") == 0
+    shard = lax.axis_index("seq")
+    head_columns = [pl.ds(head * HDIM, HDIM) for head in range(half_heads)]
+    key_valid = limits_ref[0:1, :] > 0
+
+    def served_rows(array):
+        near = jnp.where(
+            on_first_core, array[tok_dev : 2 * tok_dev], array[2 * tok_dev : 3 * tok_dev]
         )
-        attended = mixed / weight_sum[first : first + 2 * tok_dev]
-        for target, rows, limit in (
-            (keep_ref, attended[:tok_dev], limits_ref[1:2, :HDIM]),
-            (send_ref, attended[tok_dev:], limits_ref[2:3, :HDIM]),
-        ):
-            target[:, columns] = jnp.where(row < limit, rows, 0.0).astype(jnp.bfloat16)
-
-
-def logsum_kernel(set_count, limits_ref, send_ref, *refs):
-    set_refs = refs[:set_count]
-    message_ref, table_ref, lines_ref = refs[set_count:]
-    tok_dev, half_width = send_ref.shape
-    half_heads = half_width // HDIM
-    shard = lax.axis_index("seq")
-    message_ref[pl.ds(0, tok_dev), :] = send_ref[...]
-    key_valid = limits_ref[0:1, :] > 0
-    lane = lax.broadcasted_iota(jnp.int32, (set_count * tok_dev, HDIM), 1)
+        return jnp.concatenate([array[:tok_dev], near], axis=0)
+
+    all_scores = [
+        head_scores(gathered(set_refs, 2, columns), gathered(set_refs, 0, columns))
+        for columns in head_columns
+    ]
+    lane = lax.broadcasted_iota(jnp.int32, all_scores[0].shape, 1)
     lines = jnp.zeros(lane.shape, jnp.float32)
-    for head in range(half_heads):
-        columns = pl.ds(head * HDIM, HDIM)
-        scores = head_scores(gathered(set_refs, 2, columns), gathered(set_refs, 0, columns))
+    served = []
+    for head, scores in enumerate(all_scores):
         scores = jnp.where(key_valid, scores * (1.0 / math.sqrt(HDIM)), -jnp.inf)
         top_score = jnp.max(scores, axis=1, keepdims=True)
-        weight_sum = jnp.sum(jnp.exp(scores - top_score), axis=1, keepdims=True)
+        weights = jnp.exp(scores - top_score)
+        weight_sum = jnp.sum(weights, axis=1, keepdims=True)
         lines = jnp.where(lane == head, top_score + jnp.log(weight_sum), lines)
-    for place, offset in enumerate(set_order(set_count)):
+        served.append((served_rows(weights).astype(jnp.bfloat16), served_rows(weight_sum)))
+    row = lax.broadcasted_iota(jnp.int32, (tok_dev, HDIM), 0)
+    for columns, (rounded, weight_sum) in zip(head_columns, served):
+        mixed = jnp.dot(
+            rounded, gathered(set_refs, 1, columns), preferred_element_type=jnp.float32
+        )
+        attended = mixed / weight_sum
+        kept = jnp.where(row < limits_ref[1:2, :HDIM], attended[:tok_dev], 0.0)
+        sent = jnp.where(row < limits_ref[2:3, :HDIM], attended[tok_dev:], 0.0)
+        keep_ref[:, columns] = kept.astype(jnp.bfloat16)
+        send_ref[:, columns] = sent.astype(jnp.bfloat16)
+        message_ref[pl.ds(0, tok_dev), columns] = sent.astype(jnp.bfloat16)
+
+    for place, offset in enumerate(place_offsets()):
         rows = pl.ds(pl.multiple_of((shard ^ offset) * tok_dev, tok_dev), tok_dev)
         lines_ref[rows, :] = lines[place * tok_dev : (place + 1) * tok_dev]
     table = jnp.transpose(lines_ref[...])[: table_ref.shape[0]]
@@ -419,7 +430,7 @@
     def held(*arrays):
         return [pltpu.with_memory_space_constraint(array, pltpu.VMEM) for array in arrays]
 
-    def far(*arrays):
+    def distant(*arrays):
         return [pltpu.with_memory_space_constraint(array, pltpu.HBM) for array in arrays]
 
     own, other, limits, pick, slot_head = pl.pallas_call(
@@ -440,7 +451,7 @@
         ],
         compiler_params=KERNEL_PARAMS,
         name="pack",
-    )(*far(queries, key_rows, value_rows, counts, jnp.transpose(head_of)))
+    )(*distant(queries, key_rows, value_rows, counts, jnp.transpose(head_of)))
 
     weight_held = pl.pallas_call(
         hold_kernel,
@@ -453,38 +464,31 @@
             flops=0, bytes_accessed=4 * out_weight.size, transcendentals=0
         ),
         name="hold",
-    )(*far(out_weight), *held(limits))
-    sets = {0: own}
-    for offset in range(SPLIT, seq_count, SPLIT):
-        sets[offset] = swap_shards(other if offset & SPLIT else own, offset)
-    for offset in range(0, seq_count, SPLIT):
-        sets[offset + 1] = swap_shards(sets[offset], 1)
-    set_list = held(*[sets[offset] for offset in set_order(seq_count)])
+    )(*distant(out_weight), *held(limits))
+    first = swap_by_core(other, FIRST)
+    second = swap_by_core(other, SECOND)
+    third = swap_by_core(own, THIRD)
+    fourth = swap_by_core(own, FOURTH)
+    far = jnp.where(lax.axis_index("branch") == 0, fourth, third)
+    passed_on = [swap_shards(array, 1) for array in (first, second, far)]
+    sets = [own, first, second, third, fourth] + passed_on
     limits, weight_held = lax.optimization_barrier((limits, weight_held))
-    limits = held(limits)[0]
-    keep, send = pl.pallas_call(
-        functools.partial(attend_kernel, seq_count),
-        out_shape=[pltpu.VMEM((tok_dev, half_width), jnp.bfloat16)] * 2,
-        in_specs=[vmem] * (1 + seq_count),
-        out_specs=[vmem] * 2,
+    keep, send, message, table = pl.pallas_call(
+        functools.partial(attend_kernel, len(sets)),
+        out_shape=[pltpu.VMEM((tok_dev, half_width), jnp.bfloat16)] * 2
+        + [
+            pltpu.VMEM((2 * tok_dev, half_width), jnp.bfloat16),
+            pltpu.VMEM((half_width // HDIM + 7 & -8, tokens), jnp.float32),
+        ],
+        in_specs=[vmem] * (1 + len(sets)),
+        out_specs=[vmem] * 4,
+        scratch_shapes=[pltpu.VMEM((tokens, HDIM), jnp.float32)],
         compiler_params=KERNEL_PARAMS,
         name="attend",
-    )(limits, *set_list)
+    )(*held(limits, *sets))
     across = [(2 * i + b, 2 * (i ^ SPLIT) + 1 - b) for i in range(seq_count) for b in range(2)]
     partner_back = lax.ppermute(send, ("seq", "branch"), across)
     partner_keep = partner_2(keep, "branch", 0)
-    message, table = pl.pallas_call(
-        functools.partial(logsum_kernel, seq_count),
-        out_shape=[
-            pltpu.VMEM((2 * tok_dev, half_width), jnp.bfloat16),
-            pltpu.VMEM((half_width // HDIM + 7 & -8, tokens), jnp.float32),
-        ],
-        in_specs=[vmem] * (2 + seq_count),
-        out_specs=[vmem] * 2,
-        scratch_shapes=[pltpu.VMEM((tokens, HDIM), jnp.float32)],
-        compiler_params=KERNEL_PARAMS,
-        name="logsum",
-    )(limits, *held(send), *set_list)
     back = swap_shards(message, SPLIT)
     total, size = pl.pallas_call(
         keep_kernel,
@@ -514,8 +518,7 @@
 
 def solution(mesh):
     seq_count = mesh.shape["seq"]
-    hypercube = seq_count > SPLIT and seq_count & (seq_count - 1) == 0
-    small = hypercube and seq_count <= HEADS
+    small = seq_count == 2 * FAR
     return jax.shard_map(
         per_device_halves if small else per_device_exchange,
         mesh=mesh,

time: 24.4 us -> 24.7 us (1.012)
  waiting for transfers between devices: 5.29 us -> 5.72 us
  Pallas kernels: 4.73 us -> 4.35 us
  starting transfers between devices: 13.4 us -> 13.7 us
    ppermute x8 -> x4, starting transfers between devices: 12.5 us -> 4.3 us  [swap_shards(): return lax.ppermute(array, 'seq', pairs)]
    ppermute x0 -> x4, starting transfers between devices: none -> 7.39 us  [swap_by_core(): return lax.ppermute(array, ('seq', 'branch'), pairs)]
    ppermute x0 -> x4, waiting for transfers between devices: none -> 2.46 us  [swap_by_core(): return lax.ppermute(array, ('seq', 'branch'), pairs)]
    ppermute x8 -> x4, waiting for transfers between devices: 3.27 us -> 1.95 us  [swap_shards(): return lax.ppermute(array, 'seq', pairs)]
    ppermute x1, starting transfers between devices: 0.95 us -> 2.01 us  [per_device_halves(): partner_back = lax.ppermute(send, ('seq', 'branch'), across)]
    ppermute x1, waiting for transfers between devices: 1.78 us -> 1.3 us  [per_device_halves(): partner_back = lax.ppermute(send, ('seq', 'branch'), across)]
    pallas_call x2 -> x1, Pallas kernels: 0.97 us -> 0.6 us  [per_device_halves(): pl.pallas_call(functools.partial(attend_kernel, len(sets)), out_shape=[pl...]
  transfers between devices with their start and end apart: 10 -> 10, of which waited for: 6 -> 5; matrix products, arithmetic and copies ran while one was open for 0% -> 0% of each run, Pallas kernels for 8% -> 8%
where the time goes in v3:
time: 24.7 us; the launch traced here: 24.5 us
  starting transfers between devices  13.7 us (55%)
  waiting for transfers between devices  5.72 us (23%)
  Pallas kernels  4.35 us (18%)
  between operations  0.69 us (3%)
    ppermute x4, starting transfers between devices, swap_by_core(): return lax.ppermute(array, ('seq', 'branch'), pairs)  7.39 us
    ppermute x4, starting transfers between devices, swap_shards(): return lax.ppermute(array, 'seq', pairs)  4.3 us
    ppermute x4, waiting for transfers between devices, swap_by_core(): return lax.ppermute(array, ('seq', 'branch'), pairs)  2.46 us
    ppermute x1, starting transfers between devices, per_device_halves(): partner_back = lax.ppermute(send, ('seq', 'branch'), across)  2.01 us
    ppermute x4, waiting for transfers between devices, swap_shards(): return lax.ppermute(array, 'seq', pairs)  1.95 us
    pallas_call x1, Pallas kernels, per_device_halves(): pl.pallas_call(hold_kernel, out_shape=pltpu.VMEM(out_weight.shape, jnp.bf...  1.63 us
    ppermute x1, waiting for transfers between devices, per_device_halves(): partner_back = lax.ppermute(send, ('seq', 'branch'), across)  1.3 us
    pallas_call x1, Pallas kernels, per_device_halves(): pl.pallas_call(pack_kernel, out_shape=[pltpu.VMEM((3 * tok_dev, half_widt...  0.92 us
  transfers between devices with their start and end apart: 10, of which 5 were waited for; matrix products, arithmetic and copies ran while one was open for 0% of the time, Pallas kernels for 8%

profile of v3, /device:TPU:0, one launch (start us, length us, event | category | flops | bytes accessed | tf_op | source)
XLA Modules:
  0.0 24.5 jit_solution(5391938485140577496)
XLA Ops:
  0.6 0.9 %pack.1 = (bf16[48,768]{1,0:T(8,128)(2,1)S(1)}, bf16[48,768]{1,0:T(8,128)(2,1)S(1)}, s32[8,128]{1,0:T(8,128)S(1)}, s32[2,8,128]{2,1,0:T(8,128)S(1)}, s32[2,8,128]{2,1,0:T(8,128)S(1)}) custom-call(bf16[1,16,1536]{2,1,0:T(8,128)(2,1)} %query_hbm.1, bf16[1,16,1536]{2,1,0:T(8,128)(2,1)} %key_hbm.1, bf16[1,16,1536]{2,1,0:T(8,128)(2,1)} %value_hbm.1, ...), custom_call_target="tpu_custom_call" | custom-call | tf_op jit(solution)/shard_map/pack/pallas_call | solution.py:436
  1.6 5.1 %collective-permute-start.1 = (bf16[48,768]{1,0:T(8,128)(2,1)S(1)}, bf16[48,768]{1,0:T(8,128)(2,1)S(1)}, u32[]{:S(2)}, u32[]{:S(2)}) collective-permute-start(bf16[48,768]{1,0:T(8,128)(2,1)S(1)} %get-tuple-element.20), channel_id=1, source_target_pairs={{0,12},{1,5},{2,14},{3,7},{4,8},{5,1},{6,10},{7,3},{8,4},{9,13},{1... | collective-permute-start | bytes 221192 | tf_op jit(solution)/shard_map/ppermute | solution.py:186
  6.7 0.0 collective-permute-start
  6.7 0.6 %collective-permute-start.3 = (bf16[48,768]{1,0:T(8,128)(2,1)S(1)}, bf16[48,768]{1,0:T(8,128)(2,1)S(1)}, u32[]{:S(2)}, u32[]{:S(2)}) collective-permute-start(bf16[48,768]{1,0:T(8,128)(2,1)S(1)} %get-tuple-element.19.refs_0_), channel_id=1, source_target_pairs={{0,8},{1,3},{2,10},{3,1},{4,12},{5,7},{6,14},{7,5},{8,0},{9,11},{1... | collective-permute-start | bytes 221192 | tf_op jit(solution)/shard_map/ppermute | solution.py:186
  7.3 1.6 %collective-permute-start.2 = (bf16[48,768]{1,0:T(8,128)(2,1)S(1)}, bf16[48,768]{1,0:T(8,128)(2,1)S(1)}, u32[]{:S(2)}, u32[]{:S(2)}) collective-permute-start(bf16[48,768]{1,0:T(8,128)(2,1)S(1)} %get-tuple-element.19.refs_0_), channel_id=1, source_target_pairs={{0,2},{1,9},{2,0},{3,11},{4,6},{5,13},{6,4},{7,15},{8,10},{9,1},{1... | collective-permute-start | bytes 221192 | tf_op jit(solution)/shard_map/ppermute | solution.py:186
  9.0 0.7 %collective-permute-done.1.refs_2_ = bf16[48,768]{1,0:T(8,128)(2,1)S(1)} collective-permute-done((bf16[48,768]{1,0:T(8,128)(2,1)S(1)}, bf16[48,768]{1,0:T(8,128)(2,1)S(1)}, u32[]{:S(2)}, u32[]{:S(2)}) %collective-permute-start.1) | collective-permute-done | bytes 73760 | tf_op jit(solution)/shard_map/ppermute | solution.py:186
  9.7 1.8 %collective-permute-start.5 = (bf16[48,768]{1,0:T(8,128)(2,1)S(1)}, bf16[48,768]{1,0:T(8,128)(2,1)S(1)}, u32[]{:S(2)}, u32[]{:S(2)}) collective-permute-start(bf16[48,768]{1,0:T(8,128)(2,1)S(1)} %collective-permute-done.1.refs_2_), channel_id=1, source_target_pairs={{0,2},{2,0},{4,6},{6,4},{8,10},{10,8},{12,14},{14,12},{1,3},{3,1},... | collective-permute-start | bytes 221192 | tf_op jit(solution)/shard_map/ppermute | solution.py:177
  11.4 0.0 collective-permute-done.refs_1_
  11.4 1.1 %collective-permute-start.4 = (bf16[48,768]{1,0:T(8,128)(2,1)S(1)}, bf16[48,768]{1,0:T(8,128)(2,1)S(1)}, u32[]{:S(2)}, u32[]{:S(2)}) collective-permute-start(bf16[48,768]{1,0:T(8,128)(2,1)S(1)} %collective-permute-done.refs_1_), channel_id=1, source_target_pairs={{0,2},{2,0},{4,6},{6,4},{8,10},{10,8},{12,14},{14,12},{1,3},{3,1},... | collective-permute-start | bytes 221192 | tf_op jit(solution)/shard_map/ppermute | solution.py:177
  12.5 1.7 %collective-permute-done.3.refs_4_ = bf16[48,768]{1,0:T(8,128)(2,1)S(1)} collective-permute-done((bf16[48,768]{1,0:T(8,128)(2,1)S(1)}, bf16[48,768]{1,0:T(8,128)(2,1)S(1)}, u32[]{:S(2)}, u32[]{:S(2)}) %collective-permute-start.3) | collective-permute-done | bytes 73760 | tf_op jit(solution)/shard_map/ppermute | solution.py:186
  14.3 0.0 collective-permute-done.2.refs_3_
  14.3 1.3 %collective-permute-start.6 = (bf16[48,768]{1,0:T(8,128)(2,1)S(1)}, bf16[48,768]{1,0:T(8,128)(2,1)S(1)}, u32[]{:S(2)}, u32[]{:S(2)}) collective-permute-start(bf16[48,768]{1,0:T(8,128)(2,1)S(1)} %broadcast_select_fusion), channel_id=1, source_target_pairs={{0,2},{2,0},{4,6},{6,4},{8,10},{10,8},{12,14},{14,12},{1,3},{3,1},... | collective-permute-start | bytes 221192 | tf_op jit(solution)/shard_map/ppermute | solution.py:177
  15.5 1.6 %hold.1.weight_ref = bf16[1536,768]{1,0:T(8,128)(2,1)S(1)} custom-call(bf16[1536,768]{1,0:T(8,128)(2,1)} %weight_hbm.1, s32[8,128]{1,0:T(8,128)S(1)} %get-tuple-element.18.after_ref.limits_ref), custom_call_target="tpu_custom_call" | custom-call | bytes 4718592 | tf_op jit(solution)/shard_map/hold/pallas_call | solution.py:456
  17.2 0.0 collective-permute-done.5.refs_6_
  17.2 0.0 collective-permute-done.4.refs_5_
  17.2 1.5 %collective-permute-done.6.refs_7_ = bf16[48,768]{1,0:T(8,128)(2,1)S(1)} collective-permute-done((bf16[48,768]{1,0:T(8,128)(2,1)S(1)}, bf16[48,768]{1,0:T(8,128)(2,1)S(1)}, u32[]{:S(2)}, u32[]{:S(2)}) %collective-permute-start.6) | collective-permute-done | bytes 73760 | tf_op jit(solution)/shard_map/ppermute | solution.py:177
  18.7 0.6 %attend.1 = (bf16[16,768]{1,0:T(8,128)(2,1)S(1)}, bf16[16,768]{1,0:T(8,128)(2,1)S(1)}, bf16[32,768]{1,0:T(8,128)(2,1)S(1)}, f32[8,128]{1,0:T(8,128)S(1)}) custom-call(s32[8,128]{1,0:T(8,128)S(1)} %get-tuple-element.18.after_ref.limits_ref, bf16[48,768]{1,0:T(8,128)(2,1)S(1)} %get-tuple-element.19.refs_0_, bf16[48,768]{1,0:T(8,128)(2,1)S(1)} %collective-permute-done.refs_1_, ...), custom_call_target="tpu_custom_call" | custom-call | tf_op jit(solution)/shard_map/attend/pallas_call | solution.py:476
  19.3 0.2 collective-permute-start.8
  19.5 0.0 collective-permute-start.7
  19.5 2.0 %collective-permute-start.9 = (bf16[16,768]{1,0:T(8,128)(2,1)S(1)}, bf16[16,768]{1,0:T(8,128)(2,1)S(1)}, u32[]{:S(2)}, u32[]{:S(2)}) collective-permute-start(bf16[16,768]{1,0:T(8,128)(2,1)S(1)} %get-tuple-element.26), channel_id=1, source_target_pairs={{0,5},{1,4},{2,7},{3,6},{4,1},{5,0},{6,3},{7,2},{8,13},{9,12},{10,... | collective-permute-start | bytes 73736 | tf_op jit(solution)/shard_map/ppermute | solution.py:490
  21.5 0.0 collective-permute-done.7.partner_keep_ref
  21.5 0.3 %keep.1 = (f32[16,768]{1,0:T(8,128)S(1)}, f32[16,128]{1,0:T(8,128)S(1)}) custom-call(bf16[16,768]{1,0:T(8,128)(2,1)S(1)} %get-tuple-element.21.keep_ref, bf16[16,768]{1,0:T(8,128)(2,1)S(1)} %collective-permute-done.7.partner_keep_ref, bf16[1536,768]{1,0:T(8,128)(2,1)S(1)} %hold.1.weight_ref), custom_call_target="tpu_custom_call" | custom-call | tf_op jit(solution)/shard_map/keep/pallas_call | solution.py:493
  21.8 1.3 %collective-permute-done.9.partner_back_ref = bf16[16,768]{1,0:T(8,128)(2,1)S(1)} collective-permute-done((bf16[16,768]{1,0:T(8,128)(2,1)S(1)}, bf16[16,768]{1,0:T(8,128)(2,1)S(1)}, u32[]{:S(2)}, u32[]{:S(2)}) %collective-permute-start.9) | collective-permute-done | bytes 24608 | tf_op jit(solution)/shard_map/ppermute | solution.py:490
  23.1 0.4 %collective-permute-done.8.message_ref = bf16[32,768]{1,0:T(8,128)(2,1)S(1)} collective-permute-done((bf16[32,768]{1,0:T(8,128)(2,1)S(1)}, bf16[32,768]{1,0:T(8,128)(2,1)S(1)}, u32[]{:S(2)}, u32[]{:S(2)}) %collective-permute-start.8) | collective-permute-done | bytes 49184 | tf_op jit(solution)/shard_map/ppermute | solution.py:177
  23.6 0.9 %project.1 = (bf16[16,768]{1,0:T(8,128)(2,1)}, f32[2,8,16]{2,1,0:T(8,128)}) custom-call(f32[16,768]{1,0:T(8,128)S(1)} %get-tuple-element.23.total_ref, f32[16,128]{1,0:T(8,128)S(1)} %get-tuple-element.24.size_ref, bf16[32,768]{1,0:T(8,128)(2,1)S(1)} %collective-permute-done.8.message_ref, bf16[16,768]{1,0:T(8,128)(2,1)S(1)} %collective-permute-done.9.partner_back_ref, ...), custom_call_target="tpu_custom_call" | custom-call | tf_op jit(solution)/shard_map/project/pallas_call | solution.py:504
  (1 shorter events, 0.0 us)
Async XLA Ops:
  1.6 8.1 %collective-permute-start.1 = (bf16[48,768]{1,0:T(8,128)(2,1)S(1)}, bf16[48,768]{1,0:T(8,128)(2,1)S(1)}, u32[]{:S(2)}, u32[]{:S(2)}) collective-permute-start(bf16[48,768]{1,0:T(8,128)(2,1)S(1)} %get-tuple-element.20), channel_id=1, source_target_pairs={{0,12},{1,5},{2,14},{3,7},{4,8},{5,1},{6,10},{7,3},{8,4},{9,13},{1... | collective-permute-start | bytes 221192 | tf_op jit(solution)/shard_map/ppermute | solution.py:186
  6.7 4.8 %collective-permute-start = (bf16[48,768]{1,0:T(8,128)(2,1)S(1)}, bf16[48,768]{1,0:T(8,128)(2,1)S(1)}, u32[]{:S(2)}, u32[]{:S(2)}) collective-permute-start(bf16[48,768]{1,0:T(8,128)(2,1)S(1)} %get-tuple-element.20), channel_id=1, source_target_pairs={{0,4},{1,13},{2,6},{3,15},{4,0},{5,9},{6,2},{7,11},{8,12},{9,5},{1... | collective-permute-start | bytes 221192 | tf_op jit(solution)/shard_map/ppermute | solution.py:186
  6.7 7.6 %collective-permute-start.3 = (bf16[48,768]{1,0:T(8,128)(2,1)S(1)}, bf16[48,768]{1,0:T(8,128)(2,1)S(1)}, u32[]{:S(2)}, u32[]{:S(2)}) collective-permute-start(bf16[48,768]{1,0:T(8,128)(2,1)S(1)} %get-tuple-element.19.refs_0_), channel_id=1, source_target_pairs={{0,8},{1,3},{2,10},{3,1},{4,12},{5,7},{6,14},{7,5},{8,0},{9,11},{1... | collective-permute-start | bytes 221192 | tf_op jit(solution)/shard_map/ppermute | solution.py:186
  7.3 6.9 %collective-permute-start.2 = (bf16[48,768]{1,0:T(8,128)(2,1)S(1)}, bf16[48,768]{1,0:T(8,128)(2,1)S(1)}, u32[]{:S(2)}, u32[]{:S(2)}) collective-permute-start(bf16[48,768]{1,0:T(8,128)(2,1)S(1)} %get-tuple-element.19.refs_0_), channel_id=1, source_target_pairs={{0,2},{1,9},{2,0},{3,11},{4,6},{5,13},{6,4},{7,15},{8,10},{9,1},{1... | collective-permute-start | bytes 221192 | tf_op jit(solution)/shard_map/ppermute | solution.py:186
  9.7 7.5 %collective-permute-start.5 = (bf16[48,768]{1,0:T(8,128)(2,1)S(1)}, bf16[48,768]{1,0:T(8,128)(2,1)S(1)}, u32[]{:S(2)}, u32[]{:S(2)}) collective-permute-start(bf16[48,768]{1,0:T(8,128)(2,1)S(1)} %collective-permute-done.1.refs_2_), channel_id=1, source_target_pairs={{0,2},{2,0},{4,6},{6,4},{8,10},{10,8},{12,14},{14,12},{1,3},{3,1},... | collective-permute-start | bytes 221192 | tf_op jit(solution)/shard_map/ppermute | solution.py:177
  11.4 5.7 %collective-permute-start.4 = (bf16[48,768]{1,0:T(8,128)(2,1)S(1)}, bf16[48,768]{1,0:T(8,128)(2,1)S(1)}, u32[]{:S(2)}, u32[]{:S(2)}) collective-permute-start(bf16[48,768]{1,0:T(8,128)(2,1)S(1)} %collective-permute-done.refs_1_), channel_id=1, source_target_pairs={{0,2},{2,0},{4,6},{6,4},{8,10},{10,8},{12,14},{14,12},{1,3},{3,1},... | collective-permute-start | bytes 221192 | tf_op jit(solution)/shard_map/ppermute | solution.py:177
  14.3 4.4 %collective-permute-start.6 = (bf16[48,768]{1,0:T(8,128)(2,1)S(1)}, bf16[48,768]{1,0:T(8,128)(2,1)S(1)}, u32[]{:S(2)}, u32[]{:S(2)}) collective-permute-start(bf16[48,768]{1,0:T(8,128)(2,1)S(1)} %broadcast_select_fusion), channel_id=1, source_target_pairs={{0,2},{2,0},{4,6},{6,4},{8,10},{10,8},{12,14},{14,12},{1,3},{3,1},... | collective-permute-start | bytes 221192 | tf_op jit(solution)/shard_map/ppermute | solution.py:177
  19.3 4.2 %collective-permute-start.8 = (bf16[32,768]{1,0:T(8,128)(2,1)S(1)}, bf16[32,768]{1,0:T(8,128)(2,1)S(1)}, u32[]{:S(2)}, u32[]{:S(2)}) collective-permute-start(bf16[32,768]{1,0:T(8,128)(2,1)S(1)} %get-tuple-element.25), channel_id=1, source_target_pairs={{0,4},{2,6},{4,0},{6,2},{8,12},{10,14},{12,8},{14,10},{1,5},{3,7},... | collective-permute-start | bytes 147464 | tf_op jit(solution)/shard_map/ppermute | solution.py:177
  19.5 2.0 %collective-permute-start.7 = (bf16[16,768]{1,0:T(8,128)(2,1)S(1)}, bf16[16,768]{1,0:T(8,128)(2,1)S(1)}, u32[]{:S(2)}, u32[]{:S(2)}) collective-permute-start(bf16[16,768]{1,0:T(8,128)(2,1)S(1)} %get-tuple-element.21.keep_ref), channel_id=1, source_target_pairs={{0,1},{1,0},{2,3},{3,2},{4,5},{5,4},{6,7},{7,6},{8,9},{9,8},{10,11... | collective-permute-start | bytes 73736 | tf_op jit(solution)/shard_map/ppermute | solution.py:20
  19.5 3.6 %collective-permute-start.9 = (bf16[16,768]{1,0:T(8,128)(2,1)S(1)}, bf16[16,768]{1,0:T(8,128)(2,1)S(1)}, u32[]{:S(2)}, u32[]{:S(2)}) collective-permute-start(bf16[16,768]{1,0:T(8,128)(2,1)S(1)} %get-tuple-element.26), channel_id=1, source_target_pairs={{0,5},{1,4},{2,7},{3,6},{4,1},{5,0},{6,3},{7,2},{8,13},{9,12},{10,... | collective-permute-start | bytes 73736 | tf_op jit(solution)/shard_map/ppermute | solution.py:490

commit v4 on v3

--- a/solution.py
+++ b/solution.py
@@ -166,7 +166,6 @@
 
 
 SPLIT = 2
-FAR = 4
 HOLD_COPIES = 4
 TABLE_PIECES = 3
 SPLITTER = 65537.0
@@ -177,26 +176,9 @@
     return lax.ppermute(array, "seq", pairs)
 
 
-def swap_by_core(array, offsets):
-    pairs = [
-        (2 * i + core, 2 * (i ^ offsets[core]) + core)
-        for i in range(lax.axis_size("seq"))
-        for core in range(2)
-    ]
-    return lax.ppermute(array, ("seq", "branch"), pairs)
-
-
-FIRST = (SPLIT, SPLIT + FAR)
-SECOND = (SPLIT + FAR, SPLIT)
-THIRD = (1, FAR)
-FOURTH = (FAR, 1)
-
-
-def place_offsets():
-    received = [(0, 0), FIRST, SECOND, THIRD, FOURTH]
-    passed_on = [(a + 1, b + 1) for a, b in (FIRST, SECOND, (FAR, FAR))]
-    core = lax.axis_index("branch")
-    return [jnp.where(core == 0, a, b) for a, b in received + passed_on]
+def place_offsets(shard_count):
+    line = list(range(0, shard_count, SPLIT))
+    return line + [offset + 1 for offset in line]
 
 
 def pack_kernel(
@@ -239,7 +221,7 @@
 
     lane = lax.broadcasted_iota(jnp.int32, (1, limits_ref.shape[1]), 1)
     lane_limit = jnp.zeros(lane.shape, jnp.int32)
-    for place, offset in enumerate(place_offsets()):
+    for place, offset in enumerate(place_offsets(shard_count)):
         lane_limit = jnp.where(lane // tok_dev == place, counts_ref[shard ^ offset], lane_limit)
     limits_ref[0:1, :] = (lane % tok_dev < lane_limit).astype(jnp.int32)
     limits_ref[1:2, :] = jnp.full(lane.shape, counts_ref[shard], jnp.int32)
@@ -299,16 +281,9 @@
     keep_ref, send_ref, message_ref, table_ref, lines_ref = refs[set_count:]
     tok_dev, half_width = keep_ref.shape
     half_heads = half_width // HDIM
-    on_first_core = lax.axis_index("branch") == 0
     shard = lax.axis_index("seq")
     head_columns = [pl.ds(head * HDIM, HDIM) for head in range(half_heads)]
     key_valid = limits_ref[0:1, :] > 0
-
-    def served_rows(array):
-        near = jnp.where(
-            on_first_core, array[tok_dev : 2 * tok_dev], array[2 * tok_dev : 3 * tok_dev]
-        )
-        return jnp.concatenate([array[:tok_dev], near], axis=0)
 
     all_scores = [
         head_scores(gathered(set_refs, 2, columns), gathered(set_refs, 0, columns))
@@ -323,7 +298,7 @@
         weights = jnp.exp(scores - top_score)
         weight_sum = jnp.sum(weights, axis=1, keepdims=True)
         lines = jnp.where(lane == head, top_score + jnp.log(weight_sum), lines)
-        served.append((served_rows(weights).astype(jnp.bfloat16), served_rows(weight_sum)))
+        served.append((weights[: 2 * tok_dev].astype(jnp.bfloat16), weight_sum[: 2 * tok_dev]))
     row = lax.broadcasted_iota(jnp.int32, (tok_dev, HDIM), 0)
     for columns, (rounded, weight_sum) in zip(head_columns, served):
         mixed = jnp.dot(
@@ -336,7 +311,7 @@
         send_ref[:, columns] = sent.astype(jnp.bfloat16)
         message_ref[pl.ds(0, tok_dev), columns] = sent.astype(jnp.bfloat16)
 
-    for place, offset in enumerate(place_offsets()):
+    for place, offset in enumerate(place_offsets(set_count)):
         rows = pl.ds(pl.multiple_of((shard ^ offset) * tok_dev, tok_dev), tok_dev)
         lines_ref[rows, :] = lines[place * tok_dev : (place + 1) * tok_dev]
     table = jnp.transpose(lines_ref[...])[: table_ref.shape[0]]
@@ -465,13 +440,11 @@
         ),
         name="hold",
     )(*distant(out_weight), *held(limits))
-    first = swap_by_core(other, FIRST)
-    second = swap_by_core(other, SECOND)
-    third = swap_by_core(own, THIRD)
-    fourth = swap_by_core(own, FOURTH)
-    far = jnp.where(lax.axis_index("branch") == 0, fourth, third)
-    passed_on = [swap_shards(array, 1) for array in (first, second, far)]
-    sets = [own, first, second, third, fourth] + passed_on
+    line = [own] + [
+        swap_shards(other if offset & SPLIT else own, offset)
+        for offset in range(SPLIT, seq_count, SPLIT)
+    ]
+    sets = line + [swap_shards(array, 1) for array in line]
     limits, weight_held = lax.optimization_barrier((limits, weight_held))
     keep, send, message, table = pl.pallas_call(
         functools.partial(attend_kernel, len(sets)),
@@ -518,7 +491,8 @@
 
 def solution(mesh):
     seq_count = mesh.shape["seq"]
-    small = seq_count == 2 * FAR
+    hypercube = seq_count > SPLIT and seq_count & (seq_count - 1) == 0
+    small = hypercube and seq_count <= HEADS
     return jax.shard_map(
         per_device_halves if small else per_device_exchange,
         mesh=mesh,

time: 24.7 us -> 24 us (0.972)
  waiting for transfers between devices: 5.72 us -> 5.29 us
  starting transfers between devices: 13.7 us -> 13.4 us
    ppermute x4 -> x8, starting transfers between devices: 4.3 us -> 12.5 us  [swap_shards(): return lax.ppermute(array, 'seq', pairs)]
    ppermute x4 -> x0, starting transfers between devices: 7.39 us -> none  [swap_by_core(): return lax.ppermute(array, ('seq', 'branch'), pairs)]
    ppermute x4 -> x0, waiting for transfers between devices: 2.46 us -> none  [swap_by_core(): return lax.ppermute(array, ('seq', 'branch'), pairs)]
    ppermute x4 -> x8, waiting for transfers between devices: 1.95 us -> 3.27 us  [swap_shards(): return lax.ppermute(array, 'seq', pairs)]
    ppermute x1, starting transfers between devices: 2.01 us -> 0.95 us  [per_device_halves(): partner_back = lax.ppermute(send, ('seq', 'branch'), across)]
    ppermute x1, waiting for transfers between devices: 1.3 us -> 1.78 us  [per_device_halves(): partner_back = lax.ppermute(send, ('seq', 'branch'), across)]
  transfers between devices with their start and end apart: 10 -> 10, of which waited for: 5 -> 6; matrix products, arithmetic and copies ran while one was open for 0% -> 0% of each run, Pallas kernels for 8% -> 8%
where the time goes in v4:
time: 24 us; the launch traced here: 23.7 us
  starting transfers between devices  13.4 us (56%)
  waiting for transfers between devices  5.29 us (22%)
  Pallas kernels  4.3 us (18%)
  between operations  0.68 us (3%)
    ppermute x8, starting transfers between devices, swap_shards(): return lax.ppermute(array, 'seq', pairs)  12.5 us
    ppermute x8, waiting for transfers between devices, swap_shards(): return lax.ppermute(array, 'seq', pairs)  3.27 us
    ppermute x1, waiting for transfers between devices, per_device_halves(): partner_back = lax.ppermute(send, ('seq', 'branch'), across)  1.78 us
    pallas_call x1, Pallas kernels, per_device_halves(): pl.pallas_call(hold_kernel, out_shape=pltpu.VMEM(out_weight.shape, jnp.bf...  1.63 us
    ppermute x1, starting transfers between devices, per_device_halves(): partner_back = lax.ppermute(send, ('seq', 'branch'), across)  0.95 us
    pallas_call x1, Pallas kernels, per_device_halves(): pl.pallas_call(pack_kernel, out_shape=[pltpu.VMEM((3 * tok_dev, half_widt...  0.92 us
    pallas_call x1, Pallas kernels, per_device_halves(): pl.pallas_call(project_kernel, out_shape=[jax.ShapeDtypeStruct((tok_dev,...  0.92 us
    pallas_call x1, Pallas kernels, per_device_halves(): pl.pallas_call(functools.partial(attend_kernel, len(sets)), out_shape=[pl...  0.55 us
  transfers between devices with their start and end apart: 10, of which 6 were waited for; matrix products, arithmetic and copies ran while one was open for 0% of the time, Pallas kernels for 8%

profile of v4, /device:TPU:0, one launch (start us, length us, event | category | flops | bytes accessed | tf_op | source)
XLA Modules:
  0.0 23.7 jit_solution(2231671911957648627)
XLA Ops:
  0.6 0.9 %pack.1 = (bf16[48,768]{1,0:T(8,128)(2,1)S(1)}, bf16[48,768]{1,0:T(8,128)(2,1)S(1)}, s32[8,128]{1,0:T(8,128)S(1)}, s32[2,8,128]{2,1,0:T(8,128)S(1)}, s32[2,8,128]{2,1,0:T(8,128)S(1)}) custom-call(bf16[1,16,1536]{2,1,0:T(8,128)(2,1)} %query_hbm.1, bf16[1,16,1536]{2,1,0:T(8,128)(2,1)} %key_hbm.1, bf16[1,16,1536]{2,1,0:T(8,128)(2,1)} %value_hbm.1, ...), custom_call_target="tpu_custom_call" | custom-call | tf_op jit(solution)/shard_map/pack/pallas_call | solution.py:411
  1.6 5.1 %collective-permute-start.2 = (bf16[48,768]{1,0:T(8,128)(2,1)S(1)}, bf16[48,768]{1,0:T(8,128)(2,1)S(1)}, u32[]{:S(2)}, u32[]{:S(2)}) collective-permute-start(bf16[48,768]{1,0:T(8,128)(2,1)S(1)} %get-tuple-element.20), channel_id=1, source_target_pairs={{0,12},{2,14},{4,8},{6,10},{8,4},{10,6},{12,0},{14,2},{1,13},{3,15... | collective-permute-start | bytes 221192 | tf_op jit(solution)/shard_map/ppermute | solution.py:176
  6.7 0.0 collective-permute-start
  6.7 0.6 %collective-permute-start.1 = (bf16[48,768]{1,0:T(8,128)(2,1)S(1)}, bf16[48,768]{1,0:T(8,128)(2,1)S(1)}, u32[]{:S(2)}, u32[]{:S(2)}) collective-permute-start(bf16[48,768]{1,0:T(8,128)(2,1)S(1)} %get-tuple-element.19.refs_0_), channel_id=1, source_target_pairs={{0,8},{2,10},{4,12},{6,14},{8,0},{10,2},{12,4},{14,6},{1,9},{3,11}... | collective-permute-start | bytes 221192 | tf_op jit(solution)/shard_map/ppermute | solution.py:176
  7.3 1.6 %collective-permute-start.3 = (bf16[48,768]{1,0:T(8,128)(2,1)S(1)}, bf16[48,768]{1,0:T(8,128)(2,1)S(1)}, u32[]{:S(2)}, u32[]{:S(2)}) collective-permute-start(bf16[48,768]{1,0:T(8,128)(2,1)S(1)} %get-tuple-element.19.refs_0_), channel_id=1, source_target_pairs={{0,2},{2,0},{4,6},{6,4},{8,10},{10,8},{12,14},{14,12},{1,3},{3,1},... | collective-permute-start | bytes 221192 | tf_op jit(solution)/shard_map/ppermute | solution.py:176
  9.0 0.9 %collective-permute-done.2.refs_3_ = bf16[48,768]{1,0:T(8,128)(2,1)S(1)} collective-permute-done((bf16[48,768]{1,0:T(8,128)(2,1)S(1)}, bf16[48,768]{1,0:T(8,128)(2,1)S(1)}, u32[]{:S(2)}, u32[]{:S(2)}) %collective-permute-start.2) | collective-permute-done | bytes 73760 | tf_op jit(solution)/shard_map/ppermute | solution.py:176
  9.8 1.5 %collective-permute-start.6 = (bf16[48,768]{1,0:T(8,128)(2,1)S(1)}, bf16[48,768]{1,0:T(8,128)(2,1)S(1)}, u32[]{:S(2)}, u32[]{:S(2)}) collective-permute-start(bf16[48,768]{1,0:T(8,128)(2,1)S(1)} %collective-permute-done.2.refs_3_), channel_id=1, source_target_pairs={{0,2},{2,0},{4,6},{6,4},{8,10},{10,8},{12,14},{14,12},{1,3},{3,1},... | collective-permute-start | bytes 221192 | tf_op jit(solution)/shard_map/ppermute | solution.py:176
  11.3 0.4 %collective-permute-done.refs_1_ = bf16[48,768]{1,0:T(8,128)(2,1)S(1)} collective-permute-done((bf16[48,768]{1,0:T(8,128)(2,1)S(1)}, bf16[48,768]{1,0:T(8,128)(2,1)S(1)}, u32[]{:S(2)}, u32[]{:S(2)}) %collective-permute-start) | collective-permute-done | bytes 73760 | tf_op jit(solution)/shard_map/ppermute | solution.py:176
  11.7 1.6 %collective-permute-start.4 = (bf16[48,768]{1,0:T(8,128)(2,1)S(1)}, bf16[48,768]{1,0:T(8,128)(2,1)S(1)}, u32[]{:S(2)}, u32[]{:S(2)}) collective-permute-start(bf16[48,768]{1,0:T(8,128)(2,1)S(1)} %collective-permute-done.refs_1_), channel_id=1, source_target_pairs={{0,2},{2,0},{4,6},{6,4},{8,10},{10,8},{12,14},{14,12},{1,3},{3,1},... | collective-permute-start | bytes 221192 | tf_op jit(solution)/shard_map/ppermute | solution.py:176
  13.4 0.0 collective-permute-done.1.refs_2_
  13.4 0.7 %collective-permute-start.5 = (bf16[48,768]{1,0:T(8,128)(2,1)S(1)}, bf16[48,768]{1,0:T(8,128)(2,1)S(1)}, u32[]{:S(2)}, u32[]{:S(2)}) collective-permute-start(bf16[48,768]{1,0:T(8,128)(2,1)S(1)} %collective-permute-done.1.refs_2_), channel_id=1, source_target_pairs={{0,2},{2,0},{4,6},{6,4},{8,10},{10,8},{12,14},{14,12},{1,3},{3,1},... | collective-permute-start | bytes 221192 | tf_op jit(solution)/shard_map/ppermute | solution.py:176
  14.1 1.6 %hold.1.weight_ref = bf16[1536,768]{1,0:T(8,128)(2,1)S(1)} custom-call(bf16[1536,768]{1,0:T(8,128)(2,1)} %weight_hbm.1, s32[8,128]{1,0:T(8,128)S(1)} %get-tuple-element.18.after_ref.limits_ref), custom_call_target="tpu_custom_call" | custom-call | bytes 4718592 | tf_op jit(solution)/shard_map/hold/pallas_call | solution.py:431
  15.7 0.0 collective-permute-done.3.refs_4_
  15.7 0.0 collective-permute-done.6.refs_7_
  15.7 1.1 %collective-permute-done.4.refs_5_ = bf16[48,768]{1,0:T(8,128)(2,1)S(1)} collective-permute-done((bf16[48,768]{1,0:T(8,128)(2,1)S(1)}, bf16[48,768]{1,0:T(8,128)(2,1)S(1)}, u32[]{:S(2)}, u32[]{:S(2)}) %collective-permute-start.4) | collective-permute-done | bytes 73760 | tf_op jit(solution)/shard_map/ppermute | solution.py:176
  16.8 0.9 %collective-permute-done.5.refs_6_ = bf16[48,768]{1,0:T(8,128)(2,1)S(1)} collective-permute-done((bf16[48,768]{1,0:T(8,128)(2,1)S(1)}, bf16[48,768]{1,0:T(8,128)(2,1)S(1)}, u32[]{:S(2)}, u32[]{:S(2)}) %collective-permute-start.5) | collective-permute-done | bytes 73760 | tf_op jit(solution)/shard_map/ppermute | solution.py:176
  17.7 0.5 %attend.1 = (bf16[16,768]{1,0:T(8,128)(2,1)S(1)}, bf16[16,768]{1,0:T(8,128)(2,1)S(1)}, bf16[32,768]{1,0:T(8,128)(2,1)S(1)}, f32[8,128]{1,0:T(8,128)S(1)}) custom-call(s32[8,128]{1,0:T(8,128)S(1)} %get-tuple-element.18.after_ref.limits_ref, bf16[48,768]{1,0:T(8,128)(2,1)S(1)} %get-tuple-element.19.refs_0_, bf16[48,768]{1,0:T(8,128)(2,1)S(1)} %collective-permute-done.refs_1_, ...), custom_call_target="tpu_custom_call" | custom-call | tf_op jit(solution)/shard_map/attend/pallas_call | solution.py:449
  18.3 1.3 %collective-permute-start.8 = (bf16[32,768]{1,0:T(8,128)(2,1)S(1)}, bf16[32,768]{1,0:T(8,128)(2,1)S(1)}, u32[]{:S(2)}, u32[]{:S(2)}) collective-permute-start(bf16[32,768]{1,0:T(8,128)(2,1)S(1)} %get-tuple-element.25), channel_id=1, source_target_pairs={{0,4},{2,6},{4,0},{6,2},{8,12},{10,14},{12,8},{14,10},{1,5},{3,7},... | collective-permute-start | bytes 147464 | tf_op jit(solution)/shard_map/ppermute | solution.py:176
  19.5 0.0 collective-permute-start.7
  19.5 0.9 %collective-permute-start.9 = (bf16[16,768]{1,0:T(8,128)(2,1)S(1)}, bf16[16,768]{1,0:T(8,128)(2,1)S(1)}, u32[]{:S(2)}, u32[]{:S(2)}) collective-permute-start(bf16[16,768]{1,0:T(8,128)(2,1)S(1)} %get-tuple-element.26), channel_id=1, source_target_pairs={{0,5},{1,4},{2,7},{3,6},{4,1},{5,0},{6,3},{7,2},{8,13},{9,12},{10,... | collective-permute-start | bytes 73736 | tf_op jit(solution)/shard_map/ppermute | solution.py:463
  20.5 0.2 %collective-permute-done.7.partner_keep_ref = bf16[16,768]{1,0:T(8,128)(2,1)S(1)} collective-permute-done((bf16[16,768]{1,0:T(8,128)(2,1)S(1)}, bf16[16,768]{1,0:T(8,128)(2,1)S(1)}, u32[]{:S(2)}, u32[]{:S(2)}) %collective-permute-start.7) | collective-permute-done | bytes 24608 | tf_op jit(solution)/shard_map/ppermute | solution.py:20
  20.7 0.3 %keep.1 = (f32[16,768]{1,0:T(8,128)S(1)}, f32[16,128]{1,0:T(8,128)S(1)}) custom-call(bf16[16,768]{1,0:T(8,128)(2,1)S(1)} %get-tuple-element.21.keep_ref, bf16[16,768]{1,0:T(8,128)(2,1)S(1)} %collective-permute-done.7.partner_keep_ref, bf16[1536,768]{1,0:T(8,128)(2,1)S(1)} %hold.1.weight_ref), custom_call_target="tpu_custom_call" | custom-call | tf_op jit(solution)/shard_map/keep/pallas_call | solution.py:466
  21.0 1.8 %collective-permute-done.9.partner_back_ref = bf16[16,768]{1,0:T(8,128)(2,1)S(1)} collective-permute-done((bf16[16,768]{1,0:T(8,128)(2,1)S(1)}, bf16[16,768]{1,0:T(8,128)(2,1)S(1)}, u32[]{:S(2)}, u32[]{:S(2)}) %collective-permute-start.9) | collective-permute-done | bytes 24608 | tf_op jit(solution)/shard_map/ppermute | solution.py:463
  22.8 0.0 collective-permute-done.8.message_ref
  22.8 0.9 %project.1 = (bf16[16,768]{1,0:T(8,128)(2,1)}, f32[2,8,16]{2,1,0:T(8,128)}) custom-call(f32[16,768]{1,0:T(8,128)S(1)} %get-tuple-element.23.total_ref, f32[16,128]{1,0:T(8,128)S(1)} %get-tuple-element.24.size_ref, bf16[32,768]{1,0:T(8,128)(2,1)S(1)} %collective-permute-done.8.message_ref, bf16[16,768]{1,0:T(8,128)(2,1)S(1)} %collective-permute-done.9.partner_back_ref, ...), custom_call_target="tpu_custom_call" | custom-call | tf_op jit(solution)/shard_map/project/pallas_call | solution.py:477
Async XLA Ops:
  1.6 8.3 %collective-permute-start.2 = (bf16[48,768]{1,0:T(8,128)(2,1)S(1)}, bf16[48,768]{1,0:T(8,128)(2,1)S(1)}, u32[]{:S(2)}, u32[]{:S(2)}) collective-permute-start(bf16[48,768]{1,0:T(8,128)(2,1)S(1)} %get-tuple-element.20), channel_id=1, source_target_pairs={{0,12},{2,14},{4,8},{6,10},{8,4},{10,6},{12,0},{14,2},{1,13},{3,15... | collective-permute-start | bytes 221192 | tf_op jit(solution)/shard_map/ppermute | solution.py:176
  6.7 5.0 %collective-permute-start = (bf16[48,768]{1,0:T(8,128)(2,1)S(1)}, bf16[48,768]{1,0:T(8,128)(2,1)S(1)}, u32[]{:S(2)}, u32[]{:S(2)}) collective-permute-start(bf16[48,768]{1,0:T(8,128)(2,1)S(1)} %get-tuple-element.20), channel_id=1, source_target_pairs={{0,4},{2,6},{4,0},{6,2},{8,12},{10,14},{12,8},{14,10},{1,5},{3,7},... | collective-permute-start | bytes 221192 | tf_op jit(solution)/shard_map/ppermute | solution.py:176
  6.7 6.7 %collective-permute-start.1 = (bf16[48,768]{1,0:T(8,128)(2,1)S(1)}, bf16[48,768]{1,0:T(8,128)(2,1)S(1)}, u32[]{:S(2)}, u32[]{:S(2)}) collective-permute-start(bf16[48,768]{1,0:T(8,128)(2,1)S(1)} %get-tuple-element.19.refs_0_), channel_id=1, source_target_pairs={{0,8},{2,10},{4,12},{6,14},{8,0},{10,2},{12,4},{14,6},{1,9},{3,11}... | collective-permute-start | bytes 221192 | tf_op jit(solution)/shard_map/ppermute | solution.py:176
  7.3 8.4 %collective-permute-start.3 = (bf16[48,768]{1,0:T(8,128)(2,1)S(1)}, bf16[48,768]{1,0:T(8,128)(2,1)S(1)}, u32[]{:S(2)}, u32[]{:S(2)}) collective-permute-start(bf16[48,768]{1,0:T(8,128)(2,1)S(1)} %get-tuple-element.19.refs_0_), channel_id=1, source_target_pairs={{0,2},{2,0},{4,6},{6,4},{8,10},{10,8},{12,14},{14,12},{1,3},{3,1},... | collective-permute-start | bytes 221192 | tf_op jit(solution)/shard_map/ppermute | solution.py:176
  9.8 5.9 %collective-permute-start.6 = (bf16[48,768]{1,0:T(8,128)(2,1)S(1)}, bf16[48,768]{1,0:T(8,128)(2,1)S(1)}, u32[]{:S(2)}, u32[]{:S(2)}) collective-permute-start(bf16[48,768]{1,0:T(8,128)(2,1)S(1)} %collective-permute-done.2.refs_3_), channel_id=1, source_target_pairs={{0,2},{2,0},{4,6},{6,4},{8,10},{10,8},{12,14},{14,12},{1,3},{3,1},... | collective-permute-start | bytes 221192 | tf_op jit(solution)/shard_map/ppermute | solution.py:176
  11.7 5.1 %collective-permute-start.4 = (bf16[48,768]{1,0:T(8,128)(2,1)S(1)}, bf16[48,768]{1,0:T(8,128)(2,1)S(1)}, u32[]{:S(2)}, u32[]{:S(2)}) collective-permute-start(bf16[48,768]{1,0:T(8,128)(2,1)S(1)} %collective-permute-done.refs_1_), channel_id=1, source_target_pairs={{0,2},{2,0},{4,6},{6,4},{8,10},{10,8},{12,14},{14,12},{1,3},{3,1},... | collective-permute-start | bytes 221192 | tf_op jit(solution)/shard_map/ppermute | solution.py:176
  13.4 4.4 %collective-permute-start.5 = (bf16[48,768]{1,0:T(8,128)(2,1)S(1)}, bf16[48,768]{1,0:T(8,128)(2,1)S(1)}, u32[]{:S(2)}, u32[]{:S(2)}) collective-permute-start(bf16[48,768]{1,0:T(8,128)(2,1)S(1)} %collective-permute-done.1.refs_2_), channel_id=1, source_target_pairs={{0,2},{2,0},{4,6},{6,4},{8,10},{10,8},{12,14},{14,12},{1,3},{3,1},... | collective-permute-start | bytes 221192 | tf_op jit(solution)/shard_map/ppermute | solution.py:176
  18.3 4.5 %collective-permute-start.8 = (bf16[32,768]{1,0:T(8,128)(2,1)S(1)}, bf16[32,768]{1,0:T(8,128)(2,1)S(1)}, u32[]{:S(2)}, u32[]{:S(2)}) collective-permute-start(bf16[32,768]{1,0:T(8,128)(2,1)S(1)} %get-tuple-element.25), channel_id=1, source_target_pairs={{0,4},{2,6},{4,0},{6,2},{8,12},{10,14},{12,8},{14,10},{1,5},{3,7},... | collective-permute-start | bytes 147464 | tf_op jit(solution)/shard_map/ppermute | solution.py:176
  19.5 1.2 %collective-permute-start.7 = (bf16[16,768]{1,0:T(8,128)(2,1)S(1)}, bf16[16,768]{1,0:T(8,128)(2,1)S(1)}, u32[]{:S(2)}, u32[]{:S(2)}) collective-permute-start(bf16[16,768]{1,0:T(8,128)(2,1)S(1)} %get-tuple-element.21.keep_ref), channel_id=1, source_target_pairs={{0,1},{1,0},{2,3},{3,2},{4,5},{5,4},{6,7},{7,6},{8,9},{9,8},{10,11... | collective-permute-start | bytes 73736 | tf_op jit(solution)/shard_map/ppermute | solution.py:20
  19.5 3.3 %collective-permute-start.9 = (bf16[16,768]{1,0:T(8,128)(2,1)S(1)}, bf16[16,768]{1,0:T(8,128)(2,1)S(1)}, u32[]{:S(2)}, u32[]{:S(2)}) collective-permute-start(bf16[16,768]{1,0:T(8,128)(2,1)S(1)} %get-tuple-element.26), channel_id=1, source_target_pairs={{0,5},{1,4},{2,7},{3,6},{4,1},{5,0},{6,3},{7,2},{8,13},{9,12},{10,... | collective-permute-start | bytes 73736 | tf_op jit(solution)/shard_map/ppermute | solution.py:463

commit v5 on v4

--- a/solution.py
+++ b/solution.py
@@ -264,6 +264,10 @@
         copy.wait()
 
 
+def part_blocks(half_heads, tok_dev):
+    return -(-half_heads * TABLE_PIECES // tok_dev)
+
+
 def gathered(set_refs, part, columns):
     tok_dev = set_refs[0].shape[0] // 3
     rows = pl.ds(part * tok_dev, tok_dev)
@@ -278,7 +282,7 @@
 
 def attend_kernel(set_count, limits_ref, *refs):
     set_refs = refs[:set_count]
-    keep_ref, send_ref, message_ref, table_ref, lines_ref = refs[set_count:]
+    keep_ref, message_ref, table_ref, lines_ref = refs[set_count:]
     tok_dev, half_width = keep_ref.shape
     half_heads = half_width // HDIM
     shard = lax.axis_index("seq")
@@ -308,8 +312,7 @@
         kept = jnp.where(row < limits_ref[1:2, :HDIM], attended[:tok_dev], 0.0)
         sent = jnp.where(row < limits_ref[2:3, :HDIM], attended[tok_dev:], 0.0)
         keep_ref[:, columns] = kept.astype(jnp.bfloat16)
-        send_ref[:, columns] = sent.astype(jnp.bfloat16)
-        message_ref[pl.ds(0, tok_dev), columns] = sent.astype(jnp.bfloat16)
+        message_ref[:, columns] = sent.astype(jnp.bfloat16)
 
     for place, offset in enumerate(place_offsets(set_count)):
         rows = pl.ds(pl.multiple_of((shard ^ offset) * tok_dev, tok_dev), tok_dev)
@@ -317,16 +320,18 @@
     table = jnp.transpose(lines_ref[...])[: table_ref.shape[0]]
     table_ref[...] = table
     row = lax.broadcasted_iota(jnp.int32, (tok_dev, lines.shape[0]), 0)
+    blocks = [jnp.zeros(row.shape, jnp.float32) for _ in range(part_blocks(half_heads, tok_dev))]
     for head in range(half_heads):
         rest = jnp.broadcast_to(table[head : head + 1], row.shape)
-        block = jnp.zeros(row.shape, jnp.float32)
         for piece in range(TABLE_PIECES):
             scaled = rest * SPLITTER
             part = scaled - (scaled - rest)
-            block = jnp.where(row == piece, part, block)
+            block, at_row = divmod(head * TABLE_PIECES + piece, tok_dev)
+            blocks[block] = jnp.where(row == at_row, part, blocks[block])
             rest = rest - part
-        columns = pl.ds(head * lines.shape[0], lines.shape[0])
-        message_ref[pl.ds(tok_dev, tok_dev), columns] = block.astype(jnp.bfloat16)
+    message_ref[:, pl.ds(half_width, len(blocks) * lines.shape[0])] = jnp.concatenate(
+        blocks, axis=1
+    ).astype(jnp.bfloat16)
 
 
 def guidance(own, partner):
@@ -355,8 +360,8 @@
 def project_kernel(
     total_ref,
     size_ref,
+    partner_back_ref,
     message_ref,
-    partner_back_ref,
     weight_ref,
     table_ref,
     pick_ref,
@@ -364,27 +369,32 @@
     projected_ref,
     saved_ref,
 ):
-    tok_dev, half_width = partner_back_ref.shape
+    tok_dev = message_ref.shape[0]
+    half_width = weight_ref.shape[0] // 2
     half_heads = half_width // HDIM
     tokens = table_ref.shape[1]
     half = (lax.axis_index("seq") // SPLIT) % 2
-    guided = guidance(message_ref[pl.ds(0, tok_dev), :], partner_back_ref[...])
+    rows = pl.ds(0, half_width)
+    guided = guidance(message_ref[:, rows], partner_back_ref[:, rows])
     size = size_ref[:, 0:1] + jnp.sum(jnp.abs(guided), axis=1, keepdims=True)
     magnitude = size / (2 * half_width)
     total = total_ref[...] + half_product(guided, weight_ref, 1 - half)
     projected_ref[...] = (total / (magnitude + EPSILON)).astype(jnp.bfloat16)
 
+    parts = message_ref[:, pl.ds(half_width, message_ref.shape[1] - half_width)].astype(jnp.float32)
+    others = []
+    for head in range(half_heads):
+        other = jnp.zeros((1, tokens), jnp.float32)
+        for piece in range(TABLE_PIECES):
+            block, at_row = divmod(head * TABLE_PIECES + piece, tok_dev)
+            other = other + parts[at_row : at_row + 1, block * tokens : (block + 1) * tokens]
+        others.append(other)
     for slot in range(saved_ref.shape[0]):
         slot_head = slot_head_ref[slot, 0:1, :]
         line = jnp.zeros((1, tokens), jnp.float32)
         for head in range(half_heads):
-            pieces = message_ref[pl.ds(tok_dev, tok_dev), pl.ds(head * tokens, tokens)]
-            pieces = pieces.astype(jnp.float32)
-            other = pieces[0:1]
-            for piece in range(1, TABLE_PIECES):
-                other = other + pieces[piece : piece + 1]
             line = jnp.where(slot_head == half * half_heads + head, table_ref[head : head + 1], line)
-            line = jnp.where(slot_head == (1 - half) * half_heads + head, other, line)
+            line = jnp.where(slot_head == (1 - half) * half_heads + head, others[head], line)
         pick = pick_ref[slot]
         spread = jnp.broadcast_to(line, pick.shape)
         taken = jnp.take_along_axis(spread, jnp.maximum(pick, 0), axis=1)
@@ -399,6 +409,7 @@
     slot_count = head_of.shape[1]
     fewest = max(1, seq_count * slot_count // (2 * HEADS))
     row_cap = (tok_dev + fewest - 1) // fewest
+    message_width = half_width + part_blocks(half_width // HDIM, tok_dev) * tokens
     any_spec = pl.BlockSpec(memory_space=pl.ANY)
     vmem = pl.BlockSpec(memory_space=pltpu.VMEM)
 
@@ -446,21 +457,21 @@
     ]
     sets = line + [swap_shards(array, 1) for array in line]
     limits, weight_held = lax.optimization_barrier((limits, weight_held))
-    keep, send, message, table = pl.pallas_call(
+    keep, message, table = pl.pallas_call(
         functools.partial(attend_kernel, len(sets)),
-        out_shape=[pltpu.VMEM((tok_dev, half_width), jnp.bfloat16)] * 2
-        + [
-            pltpu.VMEM((2 * tok_dev, half_width), jnp.bfloat16),
+        out_shape=[
+            pltpu.VMEM((tok_dev, half_width), jnp.bfloat16),
+            pltpu.VMEM((tok_dev, message_width), jnp.bfloat16),
             pltpu.VMEM((half_width // HDIM + 7 & -8, tokens), jnp.float32),
         ],
         in_specs=[vmem] * (1 + len(sets)),
-        out_specs=[vmem] * 4,
+        out_specs=[vmem] * 3,
         scratch_shapes=[pltpu.VMEM((tokens, HDIM), jnp.float32)],
         compiler_params=KERNEL_PARAMS,
         name="attend",
     )(*held(limits, *sets))
     across = [(2 * i + b, 2 * (i ^ SPLIT) + 1 - b) for i in range(seq_count) for b in range(2)]
-    partner_back = lax.ppermute(send, ("seq", "branch"), across)
+    partner_back = lax.ppermute(message, ("seq", "branch"), across)
     partner_keep = partner_2(keep, "branch", 0)
     back = swap_shards(message, SPLIT)
     total, size = pl.pallas_call(
@@ -484,7 +495,7 @@
         out_specs=[vmem] * 2,
         compiler_params=KERNEL_PARAMS,
         name="project",
-    )(*held(total, size, back, partner_back, weight_held, table, pick, slot_head))
+    )(*held(total, size, partner_back, back, weight_held, table, pick, slot_head))
     saved = jnp.transpose(saved, (0, 2, 1))
     return (projected, saved.reshape(1, 1, slot_count, row_cap, seq_count))
 

time: 24 us -> 24.1 us (level)
    ppermute x1, waiting for transfers between devices: 1.78 us -> 0.7 us  [per_device_halves(): partner_back = lax.ppermute(message, ('seq', 'branch'), across)]
    ppermute x1, starting transfers between devices: 0.01 us -> 0.95 us  [partner_2(): lax.ppermute(array, axis, [(i, i ^ 1 << stride) for i in range(lax.axis_s...]
    ppermute x1, starting transfers between devices: 0.95 us -> 0.01 us  [per_device_halves(): partner_back = lax.ppermute(message, ('seq', 'branch'), across)]
    ppermute x8, waiting for transfers between devices: 3.27 us -> 3.9 us  [swap_shards(): return lax.ppermute(array, 'seq', pairs)]
    ppermute x1, waiting for transfers between devices: 0.25 us -> 0.85 us  [partner_2(): lax.ppermute(array, axis, [(i, i ^ 1 << stride) for i in range(lax.axis_s...]
  transfers between devices with their start and end apart: 10 -> 10, of which waited for: 6 -> 7; matrix products, arithmetic and copies ran while one was open for 0% -> 0% of each run, Pallas kernels for 8% -> 8%
where the time goes in v5:
time: 24.1 us; the launch traced here: 23.9 us
  starting transfers between devices  13.4 us (56%)
  waiting for transfers between devices  5.45 us (23%)
  Pallas kernels  4.3 us (18%)
  between operations  0.68 us (3%)
    ppermute x8, starting transfers between devices, swap_shards(): return lax.ppermute(array, 'seq', pairs)  12.5 us
    ppermute x8, waiting for transfers between devices, swap_shards(): return lax.ppermute(array, 'seq', pairs)  3.9 us
    pallas_call x1, Pallas kernels, per_device_halves(): pl.pallas_call(hold_kernel, out_shape=pltpu.VMEM(out_weight.shape, jnp.bf...  1.63 us
    ppermute x1, starting transfers between devices, partner_2(): lax.ppermute(array, axis, [(i, i ^ 1 << stride) for i in range(lax.axis_s...  0.95 us
    pallas_call x1, Pallas kernels, per_device_halves(): pl.pallas_call(pack_kernel, out_shape=[pltpu.VMEM((3 * tok_dev, half_widt...  0.92 us
    pallas_call x1, Pallas kernels, per_device_halves(): pl.pallas_call(project_kernel, out_shape=[jax.ShapeDtypeStruct((tok_dev,...  0.91 us
    ppermute x1, waiting for transfers between devices, partner_2(): lax.ppermute(array, axis, [(i, i ^ 1 << stride) for i in range(lax.axis_s...  0.85 us
    ppermute x1, waiting for transfers between devices, per_device_halves(): partner_back = lax.ppermute(message, ('seq', 'branch'), across)  0.7 us
  transfers between devices with their start and end apart: 10, of which 7 were waited for; matrix products, arithmetic and copies ran while one was open for 0% of the time, Pallas kernels for 8%

profile of v5, /device:TPU:0, one launch (start us, length us, event | category | flops | bytes accessed | tf_op | source)
XLA Modules:
  0.0 23.9 jit_solution(6216399919966559959)
XLA Ops:
  0.6 0.9 %pack.1 = (bf16[48,768]{1,0:T(8,128)(2,1)S(1)}, bf16[48,768]{1,0:T(8,128)(2,1)S(1)}, s32[8,128]{1,0:T(8,128)S(1)}, s32[2,8,128]{2,1,0:T(8,128)S(1)}, s32[2,8,128]{2,1,0:T(8,128)S(1)}) custom-call(bf16[1,16,1536]{2,1,0:T(8,128)(2,1)} %query_hbm.1, bf16[1,16,1536]{2,1,0:T(8,128)(2,1)} %key_hbm.1, bf16[1,16,1536]{2,1,0:T(8,128)(2,1)} %value_hbm.1, ...), custom_call_target="tpu_custom_call" | custom-call | tf_op jit(solution)/shard_map/pack/pallas_call | solution.py:422
  1.6 5.1 %collective-permute-start.2 = (bf16[48,768]{1,0:T(8,128)(2,1)S(1)}, bf16[48,768]{1,0:T(8,128)(2,1)S(1)}, u32[]{:S(2)}, u32[]{:S(2)}) collective-permute-start(bf16[48,768]{1,0:T(8,128)(2,1)S(1)} %get-tuple-element.19), channel_id=1, source_target_pairs={{0,12},{2,14},{4,8},{6,10},{8,4},{10,6},{12,0},{14,2},{1,13},{3,15... | collective-permute-start | bytes 221192 | tf_op jit(solution)/shard_map/ppermute | solution.py:176
  6.7 0.0 collective-permute-start
  6.7 0.6 %collective-permute-start.1 = (bf16[48,768]{1,0:T(8,128)(2,1)S(1)}, bf16[48,768]{1,0:T(8,128)(2,1)S(1)}, u32[]{:S(2)}, u32[]{:S(2)}) collective-permute-start(bf16[48,768]{1,0:T(8,128)(2,1)S(1)} %get-tuple-element.18.refs_0_), channel_id=1, source_target_pairs={{0,8},{2,10},{4,12},{6,14},{8,0},{10,2},{12,4},{14,6},{1,9},{3,11}... | collective-permute-start | bytes 221192 | tf_op jit(solution)/shard_map/ppermute | solution.py:176
  7.3 1.6 %collective-permute-start.3 = (bf16[48,768]{1,0:T(8,128)(2,1)S(1)}, bf16[48,768]{1,0:T(8,128)(2,1)S(1)}, u32[]{:S(2)}, u32[]{:S(2)}) collective-permute-start(bf16[48,768]{1,0:T(8,128)(2,1)S(1)} %get-tuple-element.18.refs_0_), channel_id=1, source_target_pairs={{0,2},{2,0},{4,6},{6,4},{8,10},{10,8},{12,14},{14,12},{1,3},{3,1},... | collective-permute-start | bytes 221192 | tf_op jit(solution)/shard_map/ppermute | solution.py:176
  9.0 0.9 %collective-permute-done.2.refs_3_ = bf16[48,768]{1,0:T(8,128)(2,1)S(1)} collective-permute-done((bf16[48,768]{1,0:T(8,128)(2,1)S(1)}, bf16[48,768]{1,0:T(8,128)(2,1)S(1)}, u32[]{:S(2)}, u32[]{:S(2)}) %collective-permute-start.2) | collective-permute-done | bytes 73760 | tf_op jit(solution)/shard_map/ppermute | solution.py:176
  9.8 1.5 %collective-permute-start.6 = (bf16[48,768]{1,0:T(8,128)(2,1)S(1)}, bf16[48,768]{1,0:T(8,128)(2,1)S(1)}, u32[]{:S(2)}, u32[]{:S(2)}) collective-permute-start(bf16[48,768]{1,0:T(8,128)(2,1)S(1)} %collective-permute-done.2.refs_3_), channel_id=1, source_target_pairs={{0,2},{2,0},{4,6},{6,4},{8,10},{10,8},{12,14},{14,12},{1,3},{3,1},... | collective-permute-start | bytes 221192 | tf_op jit(solution)/shard_map/ppermute | solution.py:176
  11.3 0.4 %collective-permute-done.refs_1_ = bf16[48,768]{1,0:T(8,128)(2,1)S(1)} collective-permute-done((bf16[48,768]{1,0:T(8,128)(2,1)S(1)}, bf16[48,768]{1,0:T(8,128)(2,1)S(1)}, u32[]{:S(2)}, u32[]{:S(2)}) %collective-permute-start) | collective-permute-done | bytes 73760 | tf_op jit(solution)/shard_map/ppermute | solution.py:176
  11.7 1.6 %collective-permute-start.4 = (bf16[48,768]{1,0:T(8,128)(2,1)S(1)}, bf16[48,768]{1,0:T(8,128)(2,1)S(1)}, u32[]{:S(2)}, u32[]{:S(2)}) collective-permute-start(bf16[48,768]{1,0:T(8,128)(2,1)S(1)} %collective-permute-done.refs_1_), channel_id=1, source_target_pairs={{0,2},{2,0},{4,6},{6,4},{8,10},{10,8},{12,14},{14,12},{1,3},{3,1},... | collective-permute-start | bytes 221192 | tf_op jit(solution)/shard_map/ppermute | solution.py:176
  13.4 0.0 collective-permute-done.1.refs_2_
  13.4 0.7 %collective-permute-start.5 = (bf16[48,768]{1,0:T(8,128)(2,1)S(1)}, bf16[48,768]{1,0:T(8,128)(2,1)S(1)}, u32[]{:S(2)}, u32[]{:S(2)}) collective-permute-start(bf16[48,768]{1,0:T(8,128)(2,1)S(1)} %collective-permute-done.1.refs_2_), channel_id=1, source_target_pairs={{0,2},{2,0},{4,6},{6,4},{8,10},{10,8},{12,14},{14,12},{1,3},{3,1},... | collective-permute-start | bytes 221192 | tf_op jit(solution)/shard_map/ppermute | solution.py:176
  14.1 1.6 %hold.1.weight_ref = bf16[1536,768]{1,0:T(8,128)(2,1)S(1)} custom-call(bf16[1536,768]{1,0:T(8,128)(2,1)} %weight_hbm.1, s32[8,128]{1,0:T(8,128)S(1)} %get-tuple-element.17.after_ref.limits_ref), custom_call_target="tpu_custom_call" | custom-call | bytes 4718592 | tf_op jit(solution)/shard_map/hold/pallas_call | solution.py:442
  15.7 0.0 collective-permute-done.3.refs_4_
  15.7 0.0 collective-permute-done.6.refs_7_
  15.7 1.1 %collective-permute-done.4.refs_5_ = bf16[48,768]{1,0:T(8,128)(2,1)S(1)} collective-permute-done((bf16[48,768]{1,0:T(8,128)(2,1)S(1)}, bf16[48,768]{1,0:T(8,128)(2,1)S(1)}, u32[]{:S(2)}, u32[]{:S(2)}) %collective-permute-start.4) | collective-permute-done | bytes 73760 | tf_op jit(solution)/shard_map/ppermute | solution.py:176
  16.8 0.9 %collective-permute-done.5.refs_6_ = bf16[48,768]{1,0:T(8,128)(2,1)S(1)} collective-permute-done((bf16[48,768]{1,0:T(8,128)(2,1)S(1)}, bf16[48,768]{1,0:T(8,128)(2,1)S(1)}, u32[]{:S(2)}, u32[]{:S(2)}) %collective-permute-start.5) | collective-permute-done | bytes 73760 | tf_op jit(solution)/shard_map/ppermute | solution.py:176
  17.7 0.6 %attend.1 = (bf16[16,768]{1,0:T(8,128)(2,1)S(1)}, bf16[16,1024]{1,0:T(8,128)(2,1)S(1)}, f32[8,128]{1,0:T(8,128)S(1)}) custom-call(s32[8,128]{1,0:T(8,128)S(1)} %get-tuple-element.17.after_ref.limits_ref, bf16[48,768]{1,0:T(8,128)(2,1)S(1)} %get-tuple-element.18.refs_0_, bf16[48,768]{1,0:T(8,128)(2,1)S(1)} %collective-permute-done.refs_1_, ...), custom_call_target="tpu_custom_call" | custom-call | tf_op jit(solution)/shard_map/attend/pallas_call | solution.py:460
  18.3 1.3 %collective-permute-start.9 = (bf16[16,1024]{1,0:T(8,128)(2,1)S(1)}, bf16[16,1024]{1,0:T(8,128)(2,1)S(1)}, u32[]{:S(2)}, u32[]{:S(2)}) collective-permute-start(bf16[16,1024]{1,0:T(8,128)(2,1)S(1)} %get-tuple-element.24), channel_id=1, source_target_pairs={{0,4},{2,6},{4,0},{6,2},{8,12},{10,14},{12,8},{14,10},{1,5},{3,7},... | collective-permute-start | bytes 98312 | tf_op jit(solution)/shard_map/ppermute | solution.py:176
  19.5 0.0 collective-permute-start.8
  19.5 0.9 %collective-permute-start.7 = (bf16[16,768]{1,0:T(8,128)(2,1)S(1)}, bf16[16,768]{1,0:T(8,128)(2,1)S(1)}, u32[]{:S(2)}, u32[]{:S(2)}) collective-permute-start(bf16[16,768]{1,0:T(8,128)(2,1)S(1)} %get-tuple-element.20.keep_ref), channel_id=1, source_target_pairs={{0,1},{1,0},{2,3},{3,2},{4,5},{5,4},{6,7},{7,6},{8,9},{9,8},{10,11... | collective-permute-start | bytes 73736 | tf_op jit(solution)/shard_map/ppermute | solution.py:20
  20.5 0.8 %collective-permute-done.7.partner_keep_ref = bf16[16,768]{1,0:T(8,128)(2,1)S(1)} collective-permute-done((bf16[16,768]{1,0:T(8,128)(2,1)S(1)}, bf16[16,768]{1,0:T(8,128)(2,1)S(1)}, u32[]{:S(2)}, u32[]{:S(2)}) %collective-permute-start.7) | collective-permute-done | bytes 24608 | tf_op jit(solution)/shard_map/ppermute | solution.py:20
  21.3 0.3 %keep.1 = (f32[16,768]{1,0:T(8,128)S(1)}, f32[16,128]{1,0:T(8,128)S(1)}) custom-call(bf16[16,768]{1,0:T(8,128)(2,1)S(1)} %get-tuple-element.20.keep_ref, bf16[16,768]{1,0:T(8,128)(2,1)S(1)} %collective-permute-done.7.partner_keep_ref, bf16[1536,768]{1,0:T(8,128)(2,1)S(1)} %hold.1.weight_ref), custom_call_target="tpu_custom_call" | custom-call | tf_op jit(solution)/shard_map/keep/pallas_call | solution.py:477
  21.6 0.6 %collective-permute-done.9.message_ref = bf16[16,1024]{1,0:T(8,128)(2,1)S(1)} collective-permute-done((bf16[16,1024]{1,0:T(8,128)(2,1)S(1)}, bf16[16,1024]{1,0:T(8,128)(2,1)S(1)}, u32[]{:S(2)}, u32[]{:S(2)}) %collective-permute-start.9) | collective-permute-done | bytes 32800 | tf_op jit(solution)/shard_map/ppermute | solution.py:176
  22.2 0.7 %collective-permute-done.8.partner_back_ref = bf16[16,1024]{1,0:T(8,128)(2,1)S(1)} collective-permute-done((bf16[16,1024]{1,0:T(8,128)(2,1)S(1)}, bf16[16,1024]{1,0:T(8,128)(2,1)S(1)}, u32[]{:S(2)}, u32[]{:S(2)}) %collective-permute-start.8) | collective-permute-done | bytes 32800 | tf_op jit(solution)/shard_map/ppermute | solution.py:474
  22.9 0.9 %project.1 = (bf16[16,768]{1,0:T(8,128)(2,1)}, f32[2,8,16]{2,1,0:T(8,128)}) custom-call(f32[16,768]{1,0:T(8,128)S(1)} %get-tuple-element.22.total_ref, f32[16,128]{1,0:T(8,128)S(1)} %get-tuple-element.23.size_ref, bf16[16,1024]{1,0:T(8,128)(2,1)S(1)} %collective-permute-done.8.partner_back_ref, bf16[16,1024]{1,0:T(8,128)(2,1)S(1)} %collective-permute-done.9.message_ref, ...), custom_call_target="tpu_custom_call" | custom-call | tf_op jit(solution)/shard_map/project/pallas_call | solution.py:488
Async XLA Ops:
  1.6 8.3 %collective-permute-start.2 = (bf16[48,768]{1,0:T(8,128)(2,1)S(1)}, bf16[48,768]{1,0:T(8,128)(2,1)S(1)}, u32[]{:S(2)}, u32[]{:S(2)}) collective-permute-start(bf16[48,768]{1,0:T(8,128)(2,1)S(1)} %get-tuple-element.19), channel_id=1, source_target_pairs={{0,12},{2,14},{4,8},{6,10},{8,4},{10,6},{12,0},{14,2},{1,13},{3,15... | collective-permute-start | bytes 221192 | tf_op jit(solution)/shard_map/ppermute | solution.py:176
  6.7 5.0 %collective-permute-start = (bf16[48,768]{1,0:T(8,128)(2,1)S(1)}, bf16[48,768]{1,0:T(8,128)(2,1)S(1)}, u32[]{:S(2)}, u32[]{:S(2)}) collective-permute-start(bf16[48,768]{1,0:T(8,128)(2,1)S(1)} %get-tuple-element.19), channel_id=1, source_target_pairs={{0,4},{2,6},{4,0},{6,2},{8,12},{10,14},{12,8},{14,10},{1,5},{3,7},... | collective-permute-start | bytes 221192 | tf_op jit(solution)/shard_map/ppermute | solution.py:176
  6.7 6.7 %collective-permute-start.1 = (bf16[48,768]{1,0:T(8,128)(2,1)S(1)}, bf16[48,768]{1,0:T(8,128)(2,1)S(1)}, u32[]{:S(2)}, u32[]{:S(2)}) collective-permute-start(bf16[48,768]{1,0:T(8,128)(2,1)S(1)} %get-tuple-element.18.refs_0_), channel_id=1, source_target_pairs={{0,8},{2,10},{4,12},{6,14},{8,0},{10,2},{12,4},{14,6},{1,9},{3,11}... | collective-permute-start | bytes 221192 | tf_op jit(solution)/shard_map/ppermute | solution.py:176
  7.3 8.4 %collective-permute-start.3 = (bf16[48,768]{1,0:T(8,128)(2,1)S(1)}, bf16[48,768]{1,0:T(8,128)(2,1)S(1)}, u32[]{:S(2)}, u32[]{:S(2)}) collective-permute-start(bf16[48,768]{1,0:T(8,128)(2,1)S(1)} %get-tuple-element.18.refs_0_), channel_id=1, source_target_pairs={{0,2},{2,0},{4,6},{6,4},{8,10},{10,8},{12,14},{14,12},{1,3},{3,1},... | collective-permute-start | bytes 221192 | tf_op jit(solution)/shard_map/ppermute | solution.py:176
  9.8 5.9 %collective-permute-start.6 = (bf16[48,768]{1,0:T(8,128)(2,1)S(1)}, bf16[48,768]{1,0:T(8,128)(2,1)S(1)}, u32[]{:S(2)}, u32[]{:S(2)}) collective-permute-start(bf16[48,768]{1,0:T(8,128)(2,1)S(1)} %collective-permute-done.2.refs_3_), channel_id=1, source_target_pairs={{0,2},{2,0},{4,6},{6,4},{8,10},{10,8},{12,14},{14,12},{1,3},{3,1},... | collective-permute-start | bytes 221192 | tf_op jit(solution)/shard_map/ppermute | solution.py:176
  11.7 5.1 %collective-permute-start.4 = (bf16[48,768]{1,0:T(8,128)(2,1)S(1)}, bf16[48,768]{1,0:T(8,128)(2,1)S(1)}, u32[]{:S(2)}, u32[]{:S(2)}) collective-permute-start(bf16[48,768]{1,0:T(8,128)(2,1)S(1)} %collective-permute-done.refs_1_), channel_id=1, source_target_pairs={{0,2},{2,0},{4,6},{6,4},{8,10},{10,8},{12,14},{14,12},{1,3},{3,1},... | collective-permute-start | bytes 221192 | tf_op jit(solution)/shard_map/ppermute | solution.py:176
  13.4 4.4 %collective-permute-start.5 = (bf16[48,768]{1,0:T(8,128)(2,1)S(1)}, bf16[48,768]{1,0:T(8,128)(2,1)S(1)}, u32[]{:S(2)}, u32[]{:S(2)}) collective-permute-start(bf16[48,768]{1,0:T(8,128)(2,1)S(1)} %collective-permute-done.1.refs_2_), channel_id=1, source_target_pairs={{0,2},{2,0},{4,6},{6,4},{8,10},{10,8},{12,14},{14,12},{1,3},{3,1},... | collective-permute-start | bytes 221192 | tf_op jit(solution)/shard_map/ppermute | solution.py:176
  18.3 4.0 %collective-permute-start.9 = (bf16[16,1024]{1,0:T(8,128)(2,1)S(1)}, bf16[16,1024]{1,0:T(8,128)(2,1)S(1)}, u32[]{:S(2)}, u32[]{:S(2)}) collective-permute-start(bf16[16,1024]{1,0:T(8,128)(2,1)S(1)} %get-tuple-element.24), channel_id=1, source_target_pairs={{0,4},{2,6},{4,0},{6,2},{8,12},{10,14},{12,8},{14,10},{1,5},{3,7},... | collective-permute-start | bytes 98312 | tf_op jit(solution)/shard_map/ppermute | solution.py:176
  19.5 3.4 %collective-permute-start.8 = (bf16[16,1024]{1,0:T(8,128)(2,1)S(1)}, bf16[16,1024]{1,0:T(8,128)(2,1)S(1)}, u32[]{:S(2)}, u32[]{:S(2)}) collective-permute-start(bf16[16,1024]{1,0:T(8,128)(2,1)S(1)} %get-tuple-element.24), channel_id=1, source_target_pairs={{0,5},{1,4},{2,7},{3,6},{4,1},{5,0},{6,3},{7,2},{8,13},{9,12},{10,... | collective-permute-start | bytes 98312 | tf_op jit(solution)/shard_map/ppermute | solution.py:474
  19.5 1.8 %collective-permute-start.7 = (bf16[16,768]{1,0:T(8,128)(2,1)S(1)}, bf16[16,768]{1,0:T(8,128)(2,1)S(1)}, u32[]{:S(2)}, u32[]{:S(2)}) collective-permute-start(bf16[16,768]{1,0:T(8,128)(2,1)S(1)} %get-tuple-element.20.keep_ref), channel_id=1, source_target_pairs={{0,1},{1,0},{2,3},{3,2},{4,5},{5,4},{6,7},{7,6},{8,9},{9,8},{10,11... | collective-permute-start | bytes 73736 | tf_op jit(solution)/shard_map/ppermute | solution.py:20

commit v6 on v5

--- a/solution.py
+++ b/solution.py
@@ -360,8 +360,8 @@
 def project_kernel(
     total_ref,
     size_ref,
+    message_ref,
     partner_back_ref,
-    message_ref,
     weight_ref,
     table_ref,
     pick_ref,
@@ -470,10 +470,9 @@
         compiler_params=KERNEL_PARAMS,
         name="attend",
     )(*held(limits, *sets))
-    across = [(2 * i + b, 2 * (i ^ SPLIT) + 1 - b) for i in range(seq_count) for b in range(2)]
-    partner_back = lax.ppermute(message, ("seq", "branch"), across)
     partner_keep = partner_2(keep, "branch", 0)
     back = swap_shards(message, SPLIT)
+    partner_back = partner_2(back, "branch", 0)
     total, size = pl.pallas_call(
         keep_kernel,
         out_shape=[
@@ -495,7 +494,7 @@
         out_specs=[vmem] * 2,
         compiler_params=KERNEL_PARAMS,
         name="project",
-    )(*held(total, size, partner_back, back, weight_held, table, pick, slot_head))
+    )(*held(total, size, back, partner_back, weight_held, table, pick, slot_head))
     saved = jnp.transpose(saved, (0, 2, 1))
     return (projected, saved.reshape(1, 1, slot_count, row_cap, seq_count))
 

time: 24.1 us -> 25 us (1.037)
  waiting for transfers between devices: 5.45 us -> 6.84 us
  starting transfers between devices: 13.4 us -> 13 us
    ppermute x8, waiting for transfers between devices: 3.9 us -> 5.99 us  [swap_shards(): return lax.ppermute(array, 'seq', pairs)]
    ppermute x1 -> x0, waiting for transfers between devices: 0.7 us -> none  [per_device_halves(): partner_back = lax.ppermute(message, ('seq', 'branch'), across)]
    ppermute x1 -> x2, starting transfers between devices: 0.95 us -> 0.51 us  [partner_2(): lax.ppermute(array, axis, [(i, i ^ 1 << stride) for i in range(lax.axis_s...]
    ppermute x1 -> x2, waiting for transfers between devices: 0.85 us -> 0.85 us  [partner_2(): lax.ppermute(array, axis, [(i, i ^ 1 << stride) for i in range(lax.axis_s...]
  transfers between devices with their start and end apart: 10 -> 10, of which waited for: 7 -> 6; matrix products, arithmetic and copies ran while one was open for 0% -> 0% of each run, Pallas kernels for 8% -> 8%
where the time goes in v6:
time: 25 us; the launch traced here: 24.8 us
  starting transfers between devices  13 us (52%)
  waiting for transfers between devices  6.84 us (27%)
  Pallas kernels  4.32 us (17%)
  between operations  0.68 us (3%)
    ppermute x8, starting transfers between devices, swap_shards(): return lax.ppermute(array, 'seq', pairs)  12.5 us
    ppermute x8, waiting for transfers between devices, swap_shards(): return lax.ppermute(array, 'seq', pairs)  5.99 us
    pallas_call x1, Pallas kernels, per_device_halves(): pl.pallas_call(hold_kernel, out_shape=pltpu.VMEM(out_weight.shape, jnp.bf...  1.63 us
    pallas_call x1, Pallas kernels, per_device_halves(): pl.pallas_call(project_kernel, out_shape=[jax.ShapeDtypeStruct((tok_dev,...  0.93 us
    pallas_call x1, Pallas kernels, per_device_halves(): pl.pallas_call(pack_kernel, out_shape=[pltpu.VMEM((3 * tok_dev, half_widt...  0.92 us
    ppermute x2, waiting for transfers between devices, partner_2(): lax.ppermute(array, axis, [(i, i ^ 1 << stride) for i in range(lax.axis_s...  0.85 us
    pallas_call x1, Pallas kernels, per_device_halves(): pl.pallas_call(functools.partial(attend_kernel, len(sets)), out_shape=[pl...  0.55 us
    ppermute x2, starting transfers between devices, partner_2(): lax.ppermute(array, axis, [(i, i ^ 1 << stride) for i in range(lax.axis_s...  0.51 us
  transfers between devices with their start and end apart: 10, of which 6 were waited for; matrix products, arithmetic and copies ran while one was open for 0% of the time, Pallas kernels for 8%

profile of v6, /device:TPU:0, one launch (start us, length us, event | category | flops | bytes accessed | tf_op | source)
XLA Modules:
  0.0 24.8 jit_solution(11380559827208810195)
XLA Ops:
  0.6 0.9 %pack.1 = (bf16[48,768]{1,0:T(8,128)(2,1)S(1)}, bf16[48,768]{1,0:T(8,128)(2,1)S(1)}, s32[8,128]{1,0:T(8,128)S(1)}, s32[2,8,128]{2,1,0:T(8,128)S(1)}, s32[2,8,128]{2,1,0:T(8,128)S(1)}) custom-call(bf16[1,16,1536]{2,1,0:T(8,128)(2,1)} %query_hbm.1, bf16[1,16,1536]{2,1,0:T(8,128)(2,1)} %key_hbm.1, bf16[1,16,1536]{2,1,0:T(8,128)(2,1)} %value_hbm.1, ...), custom_call_target="tpu_custom_call" | custom-call | tf_op jit(solution)/shard_map/pack/pallas_call | solution.py:422
  1.6 5.1 %collective-permute-start.2 = (bf16[48,768]{1,0:T(8,128)(2,1)S(1)}, bf16[48,768]{1,0:T(8,128)(2,1)S(1)}, u32[]{:S(2)}, u32[]{:S(2)}) collective-permute-start(bf16[48,768]{1,0:T(8,128)(2,1)S(1)} %get-tuple-element.19), channel_id=1, source_target_pairs={{0,12},{2,14},{4,8},{6,10},{8,4},{10,6},{12,0},{14,2},{1,13},{3,15... | collective-permute-start | bytes 221192 | tf_op jit(solution)/shard_map/ppermute | solution.py:176
  6.7 0.0 collective-permute-start
  6.7 0.6 %collective-permute-start.1 = (bf16[48,768]{1,0:T(8,128)(2,1)S(1)}, bf16[48,768]{1,0:T(8,128)(2,1)S(1)}, u32[]{:S(2)}, u32[]{:S(2)}) collective-permute-start(bf16[48,768]{1,0:T(8,128)(2,1)S(1)} %get-tuple-element.18.refs_0_), channel_id=1, source_target_pairs={{0,8},{2,10},{4,12},{6,14},{8,0},{10,2},{12,4},{14,6},{1,9},{3,11}... | collective-permute-start | bytes 221192 | tf_op jit(solution)/shard_map/ppermute | solution.py:176
  7.3 1.6 %collective-permute-start.3 = (bf16[48,768]{1,0:T(8,128)(2,1)S(1)}, bf16[48,768]{1,0:T(8,128)(2,1)S(1)}, u32[]{:S(2)}, u32[]{:S(2)}) collective-permute-start(bf16[48,768]{1,0:T(8,128)(2,1)S(1)} %get-tuple-element.18.refs_0_), channel_id=1, source_target_pairs={{0,2},{2,0},{4,6},{6,4},{8,10},{10,8},{12,14},{14,12},{1,3},{3,1},... | collective-permute-start | bytes 221192 | tf_op jit(solution)/shard_map/ppermute | solution.py:176
  9.0 0.9 %collective-permute-done.2.refs_3_ = bf16[48,768]{1,0:T(8,128)(2,1)S(1)} collective-permute-done((bf16[48,768]{1,0:T(8,128)(2,1)S(1)}, bf16[48,768]{1,0:T(8,128)(2,1)S(1)}, u32[]{:S(2)}, u32[]{:S(2)}) %collective-permute-start.2) | collective-permute-done | bytes 73760 | tf_op jit(solution)/shard_map/ppermute | solution.py:176
  9.8 1.5 %collective-permute-start.6 = (bf16[48,768]{1,0:T(8,128)(2,1)S(1)}, bf16[48,768]{1,0:T(8,128)(2,1)S(1)}, u32[]{:S(2)}, u32[]{:S(2)}) collective-permute-start(bf16[48,768]{1,0:T(8,128)(2,1)S(1)} %collective-permute-done.2.refs_3_), channel_id=1, source_target_pairs={{0,2},{2,0},{4,6},{6,4},{8,10},{10,8},{12,14},{14,12},{1,3},{3,1},... | collective-permute-start | bytes 221192 | tf_op jit(solution)/shard_map/ppermute | solution.py:176
  11.3 0.4 %collective-permute-done.refs_1_ = bf16[48,768]{1,0:T(8,128)(2,1)S(1)} collective-permute-done((bf16[48,768]{1,0:T(8,128)(2,1)S(1)}, bf16[48,768]{1,0:T(8,128)(2,1)S(1)}, u32[]{:S(2)}, u32[]{:S(2)}) %collective-permute-start) | collective-permute-done | bytes 73760 | tf_op jit(solution)/shard_map/ppermute | solution.py:176
  11.7 1.6 %collective-permute-start.4 = (bf16[48,768]{1,0:T(8,128)(2,1)S(1)}, bf16[48,768]{1,0:T(8,128)(2,1)S(1)}, u32[]{:S(2)}, u32[]{:S(2)}) collective-permute-start(bf16[48,768]{1,0:T(8,128)(2,1)S(1)} %collective-permute-done.refs_1_), channel_id=1, source_target_pairs={{0,2},{2,0},{4,6},{6,4},{8,10},{10,8},{12,14},{14,12},{1,3},{3,1},... | collective-permute-start | bytes 221192 | tf_op jit(solution)/shard_map/ppermute | solution.py:176
  13.4 0.0 collective-permute-done.1.refs_2_
  13.4 0.7 %collective-permute-start.5 = (bf16[48,768]{1,0:T(8,128)(2,1)S(1)}, bf16[48,768]{1,0:T(8,128)(2,1)S(1)}, u32[]{:S(2)}, u32[]{:S(2)}) collective-permute-start(bf16[48,768]{1,0:T(8,128)(2,1)S(1)} %collective-permute-done.1.refs_2_), channel_id=1, source_target_pairs={{0,2},{2,0},{4,6},{6,4},{8,10},{10,8},{12,14},{14,12},{1,3},{3,1},... | collective-permute-start | bytes 221192 | tf_op jit(solution)/shard_map/ppermute | solution.py:176
  14.1 1.6 %hold.1.weight_ref = bf16[1536,768]{1,0:T(8,128)(2,1)S(1)} custom-call(bf16[1536,768]{1,0:T(8,128)(2,1)} %weight_hbm.1, s32[8,128]{1,0:T(8,128)S(1)} %get-tuple-element.17.after_ref.limits_ref), custom_call_target="tpu_custom_call" | custom-call | bytes 4718592 | tf_op jit(solution)/shard_map/hold/pallas_call | solution.py:442
  15.7 0.0 collective-permute-done.3.refs_4_
  15.7 0.0 collective-permute-done.6.refs_7_
  15.7 1.1 %collective-permute-done.4.refs_5_ = bf16[48,768]{1,0:T(8,128)(2,1)S(1)} collective-permute-done((bf16[48,768]{1,0:T(8,128)(2,1)S(1)}, bf16[48,768]{1,0:T(8,128)(2,1)S(1)}, u32[]{:S(2)}, u32[]{:S(2)}) %collective-permute-start.4) | collective-permute-done | bytes 73760 | tf_op jit(solution)/shard_map/ppermute | solution.py:176
  16.8 0.9 %collective-permute-done.5.refs_6_ = bf16[48,768]{1,0:T(8,128)(2,1)S(1)} collective-permute-done((bf16[48,768]{1,0:T(8,128)(2,1)S(1)}, bf16[48,768]{1,0:T(8,128)(2,1)S(1)}, u32[]{:S(2)}, u32[]{:S(2)}) %collective-permute-start.5) | collective-permute-done | bytes 73760 | tf_op jit(solution)/shard_map/ppermute | solution.py:176
  17.7 0.6 %attend.1 = (bf16[16,768]{1,0:T(8,128)(2,1)S(1)}, bf16[16,1024]{1,0:T(8,128)(2,1)S(1)}, f32[8,128]{1,0:T(8,128)S(1)}) custom-call(s32[8,128]{1,0:T(8,128)S(1)} %get-tuple-element.17.after_ref.limits_ref, bf16[48,768]{1,0:T(8,128)(2,1)S(1)} %get-tuple-element.18.refs_0_, bf16[48,768]{1,0:T(8,128)(2,1)S(1)} %collective-permute-done.refs_1_, ...), custom_call_target="tpu_custom_call" | custom-call | tf_op jit(solution)/shard_map/attend/pallas_call | solution.py:460
  18.3 1.3 %collective-permute-start.8 = (bf16[16,1024]{1,0:T(8,128)(2,1)S(1)}, bf16[16,1024]{1,0:T(8,128)(2,1)S(1)}, u32[]{:S(2)}, u32[]{:S(2)}) collective-permute-start(bf16[16,1024]{1,0:T(8,128)(2,1)S(1)} %get-tuple-element.24), channel_id=1, source_target_pairs={{0,4},{2,6},{4,0},{6,2},{8,12},{10,14},{12,8},{14,10},{1,5},{3,7},... | collective-permute-start | bytes 98312 | tf_op jit(solution)/shard_map/ppermute | solution.py:176
  19.5 2.7 %collective-permute-done.8.message_ref = bf16[16,1024]{1,0:T(8,128)(2,1)S(1)} collective-permute-done((bf16[16,1024]{1,0:T(8,128)(2,1)S(1)}, bf16[16,1024]{1,0:T(8,128)(2,1)S(1)}, u32[]{:S(2)}, u32[]{:S(2)}) %collective-permute-start.8) | collective-permute-done | bytes 32800 | tf_op jit(solution)/shard_map/ppermute | solution.py:176
  22.2 0.0 collective-permute-start.9
  22.3 0.5 %collective-permute-start.7 = (bf16[16,768]{1,0:T(8,128)(2,1)S(1)}, bf16[16,768]{1,0:T(8,128)(2,1)S(1)}, u32[]{:S(2)}, u32[]{:S(2)}) collective-permute-start(bf16[16,768]{1,0:T(8,128)(2,1)S(1)} %get-tuple-element.20.keep_ref), channel_id=1, source_target_pairs={{0,1},{1,0},{2,3},{3,2},{4,5},{5,4},{6,7},{7,6},{8,9},{9,8},{10,11... | collective-permute-start | bytes 73736 | tf_op jit(solution)/shard_map/ppermute | solution.py:20
  22.8 0.8 %collective-permute-done.7.partner_keep_ref = bf16[16,768]{1,0:T(8,128)(2,1)S(1)} collective-permute-done((bf16[16,768]{1,0:T(8,128)(2,1)S(1)}, bf16[16,768]{1,0:T(8,128)(2,1)S(1)}, u32[]{:S(2)}, u32[]{:S(2)}) %collective-permute-start.7) | collective-permute-done | bytes 24608 | tf_op jit(solution)/shard_map/ppermute | solution.py:20
  23.6 0.3 %keep.1 = (f32[16,768]{1,0:T(8,128)S(1)}, f32[16,128]{1,0:T(8,128)S(1)}) custom-call(bf16[16,768]{1,0:T(8,128)(2,1)S(1)} %get-tuple-element.20.keep_ref, bf16[16,768]{1,0:T(8,128)(2,1)S(1)} %collective-permute-done.7.partner_keep_ref, bf16[1536,768]{1,0:T(8,128)(2,1)S(1)} %hold.1.weight_ref), custom_call_target="tpu_custom_call" | custom-call | tf_op jit(solution)/shard_map/keep/pallas_call | solution.py:476
  23.9 0.0 collective-permute-done.9.partner_back_ref
  23.9 0.9 %project.1 = (bf16[16,768]{1,0:T(8,128)(2,1)}, f32[2,8,16]{2,1,0:T(8,128)}) custom-call(f32[16,768]{1,0:T(8,128)S(1)} %get-tuple-element.22.total_ref, f32[16,128]{1,0:T(8,128)S(1)} %get-tuple-element.23.size_ref, bf16[16,1024]{1,0:T(8,128)(2,1)S(1)} %collective-permute-done.8.message_ref, bf16[16,1024]{1,0:T(8,128)(2,1)S(1)} %collective-permute-done.9.partner_back_ref, ...), custom_call_target="tpu_custom_call" | custom-call | tf_op jit(solution)/shard_map/project/pallas_call | solution.py:487
Async XLA Ops:
  1.6 8.3 %collective-permute-start.2 = (bf16[48,768]{1,0:T(8,128)(2,1)S(1)}, bf16[48,768]{1,0:T(8,128)(2,1)S(1)}, u32[]{:S(2)}, u32[]{:S(2)}) collective-permute-start(bf16[48,768]{1,0:T(8,128)(2,1)S(1)} %get-tuple-element.19), channel_id=1, source_target_pairs={{0,12},{2,14},{4,8},{6,10},{8,4},{10,6},{12,0},{14,2},{1,13},{3,15... | collective-permute-start | bytes 221192 | tf_op jit(solution)/shard_map/ppermute | solution.py:176
  6.7 5.0 %collective-permute-start = (bf16[48,768]{1,0:T(8,128)(2,1)S(1)}, bf16[48,768]{1,0:T(8,128)(2,1)S(1)}, u32[]{:S(2)}, u32[]{:S(2)}) collective-permute-start(bf16[48,768]{1,0:T(8,128)(2,1)S(1)} %get-tuple-element.19), channel_id=1, source_target_pairs={{0,4},{2,6},{4,0},{6,2},{8,12},{10,14},{12,8},{14,10},{1,5},{3,7},... | collective-permute-start | bytes 221192 | tf_op jit(solution)/shard_map/ppermute | solution.py:176
  6.7 6.7 %collective-permute-start.1 = (bf16[48,768]{1,0:T(8,128)(2,1)S(1)}, bf16[48,768]{1,0:T(8,128)(2,1)S(1)}, u32[]{:S(2)}, u32[]{:S(2)}) collective-permute-start(bf16[48,768]{1,0:T(8,128)(2,1)S(1)} %get-tuple-element.18.refs_0_), channel_id=1, source_target_pairs={{0,8},{2,10},{4,12},{6,14},{8,0},{10,2},{12,4},{14,6},{1,9},{3,11}... | collective-permute-start | bytes 221192 | tf_op jit(solution)/shard_map/ppermute | solution.py:176
  7.3 8.4 %collective-permute-start.3 = (bf16[48,768]{1,0:T(8,128)(2,1)S(1)}, bf16[48,768]{1,0:T(8,128)(2,1)S(1)}, u32[]{:S(2)}, u32[]{:S(2)}) collective-permute-start(bf16[48,768]{1,0:T(8,128)(2,1)S(1)} %get-tuple-element.18.refs_0_), channel_id=1, source_target_pairs={{0,2},{2,0},{4,6},{6,4},{8,10},{10,8},{12,14},{14,12},{1,3},{3,1},... | collective-permute-start | bytes 221192 | tf_op jit(solution)/shard_map/ppermute | solution.py:176
  9.8 5.9 %collective-permute-start.6 = (bf16[48,768]{1,0:T(8,128)(2,1)S(1)}, bf16[48,768]{1,0:T(8,128)(2,1)S(1)}, u32[]{:S(2)}, u32[]{:S(2)}) collective-permute-start(bf16[48,768]{1,0:T(8,128)(2,1)S(1)} %collective-permute-done.2.refs_3_), channel_id=1, source_target_pairs={{0,2},{2,0},{4,6},{6,4},{8,10},{10,8},{12,14},{14,12},{1,3},{3,1},... | collective-permute-start | bytes 221192 | tf_op jit(solution)/shard_map/ppermute | solution.py:176
  11.7 5.1 %collective-permute-start.4 = (bf16[48,768]{1,0:T(8,128)(2,1)S(1)}, bf16[48,768]{1,0:T(8,128)(2,1)S(1)}, u32[]{:S(2)}, u32[]{:S(2)}) collective-permute-start(bf16[48,768]{1,0:T(8,128)(2,1)S(1)} %collective-permute-done.refs_1_), channel_id=1, source_target_pairs={{0,2},{2,0},{4,6},{6,4},{8,10},{10,8},{12,14},{14,12},{1,3},{3,1},... | collective-permute-start | bytes 221192 | tf_op jit(solution)/shard_map/ppermute | solution.py:176
  13.4 4.4 %collective-permute-start.5 = (bf16[48,768]{1,0:T(8,128)(2,1)S(1)}, bf16[48,768]{1,0:T(8,128)(2,1)S(1)}, u32[]{:S(2)}, u32[]{:S(2)}) collective-permute-start(bf16[48,768]{1,0:T(8,128)(2,1)S(1)} %collective-permute-done.1.refs_2_), channel_id=1, source_target_pairs={{0,2},{2,0},{4,6},{6,4},{8,10},{10,8},{12,14},{14,12},{1,3},{3,1},... | collective-permute-start | bytes 221192 | tf_op jit(solution)/shard_map/ppermute | solution.py:176
  18.3 4.0 %collective-permute-start.8 = (bf16[16,1024]{1,0:T(8,128)(2,1)S(1)}, bf16[16,1024]{1,0:T(8,128)(2,1)S(1)}, u32[]{:S(2)}, u32[]{:S(2)}) collective-permute-start(bf16[16,1024]{1,0:T(8,128)(2,1)S(1)} %get-tuple-element.24), channel_id=1, source_target_pairs={{0,4},{2,6},{4,0},{6,2},{8,12},{10,14},{12,8},{14,10},{1,5},{3,7},... | collective-permute-start | bytes 98312 | tf_op jit(solution)/shard_map/ppermute | solution.py:176
  22.2 1.6 %collective-permute-start.9 = (bf16[16,1024]{1,0:T(8,128)(2,1)S(1)}, bf16[16,1024]{1,0:T(8,128)(2,1)S(1)}, u32[]{:S(2)}, u32[]{:S(2)}) collective-permute-start(bf16[16,1024]{1,0:T(8,128)(2,1)S(1)} %collective-permute-done.8.message_ref), channel_id=1, source_target_pairs={{0,1},{1,0},{2,3},{3,2},{4,5},{5,4},{6,7},{7,6},{8,9},{9,8},{10,11... | collective-permute-start | bytes 98312 | tf_op jit(solution)/shard_map/ppermute | solution.py:20
  22.3 1.4 %collective-permute-start.7 = (bf16[16,768]{1,0:T(8,128)(2,1)S(1)}, bf16[16,768]{1,0:T(8,128)(2,1)S(1)}, u32[]{:S(2)}, u32[]{:S(2)}) collective-permute-start(bf16[16,768]{1,0:T(8,128)(2,1)S(1)} %get-tuple-element.20.keep_ref), channel_id=1, source_target_pairs={{0,1},{1,0},{2,3},{3,2},{4,5},{5,4},{6,7},{7,6},{8,9},{9,8},{10,11... | collective-permute-start | bytes 73736 | tf_op jit(solution)/shard_map/ppermute | solution.py:20

commit v7 on v6

--- a/solution.py
+++ b/solution.py
@@ -472,7 +472,6 @@
     )(*held(limits, *sets))
     partner_keep = partner_2(keep, "branch", 0)
     back = swap_shards(message, SPLIT)
-    partner_back = partner_2(back, "branch", 0)
     total, size = pl.pallas_call(
         keep_kernel,
         out_shape=[
@@ -484,6 +483,8 @@
         compiler_params=KERNEL_PARAMS,
         name="keep",
     )(*held(keep, partner_keep, weight_held))
+    back, total, size = lax.optimization_barrier((back, total, size))
+    partner_back = partner_2(back, "branch", 0)
     projected, saved = pl.pallas_call(
         project_kernel,
         out_shape=[

time: 25 us -> 24.6 us (0.984)
  starting transfers between devices: 13 us -> 12.5 us
    ppermute x2, waiting for transfers between devices: 0.85 us -> 2.4 us  [partner_2(): lax.ppermute(array, axis, [(i, i ^ 1 << stride) for i in range(lax.axis_s...]
    ppermute x8, waiting for transfers between devices: 5.99 us -> 4.51 us  [swap_shards(): return lax.ppermute(array, 'seq', pairs)]
    ppermute x2, starting transfers between devices: 0.51 us -> 0.01 us  [partner_2(): lax.ppermute(array, axis, [(i, i ^ 1 << stride) for i in range(lax.axis_s...]
  transfers between devices with their start and end apart: 10 -> 10, of which waited for: 6 -> 7; matrix products, arithmetic and copies ran while one was open for 0% -> 0% of each run, Pallas kernels for 8% -> 8%
where the time goes in v7:
time: 24.6 us; the launch traced here: 24.4 us
  starting transfers between devices  12.5 us (51%)
  waiting for transfers between devices  6.9 us (28%)
  Pallas kernels  4.3 us (17%)
  between operations  0.68 us (3%)
    ppermute x8, starting transfers between devices, swap_shards(): return lax.ppermute(array, 'seq', pairs)  12.5 us
    ppermute x8, waiting for transfers between devices, swap_shards(): return lax.ppermute(array, 'seq', pairs)  4.51 us
    ppermute x2, waiting for transfers between devices, partner_2(): lax.ppermute(array, axis, [(i, i ^ 1 << stride) for i in range(lax.axis_s...  2.4 us
    pallas_call x1, Pallas kernels, per_device_halves(): pl.pallas_call(hold_kernel, out_shape=pltpu.VMEM(out_weight.shape, jnp.bf...  1.63 us
    pallas_call x1, Pallas kernels, per_device_halves(): pl.pallas_call(pack_kernel, out_shape=[pltpu.VMEM((3 * tok_dev, half_widt...  0.92 us
    pallas_call x1, Pallas kernels, per_device_halves(): pl.pallas_call(project_kernel, out_shape=[jax.ShapeDtypeStruct((tok_dev,...  0.91 us
    pallas_call x1, Pallas kernels, per_device_halves(): pl.pallas_call(functools.partial(attend_kernel, len(sets)), out_shape=[pl...  0.55 us
  transfers between devices with their start and end apart: 10, of which 7 were waited for; matrix products, arithmetic and copies ran while one was open for 0% of the time, Pallas kernels for 8%

profile of v7, /device:TPU:0, one launch (start us, length us, event | category | flops | bytes accessed | tf_op | source)
XLA Modules:
  0.0 24.4 jit_solution(3259364783929396787)
XLA Ops:
  0.6 0.9 %pack.1 = (bf16[48,768]{1,0:T(8,128)(2,1)S(1)}, bf16[48,768]{1,0:T(8,128)(2,1)S(1)}, s32[8,128]{1,0:T(8,128)S(1)}, s32[2,8,128]{2,1,0:T(8,128)S(1)}, s32[2,8,128]{2,1,0:T(8,128)S(1)}) custom-call(bf16[1,16,1536]{2,1,0:T(8,128)(2,1)} %query_hbm.1, bf16[1,16,1536]{2,1,0:T(8,128)(2,1)} %key_hbm.1, bf16[1,16,1536]{2,1,0:T(8,128)(2,1)} %value_hbm.1, ...), custom_call_target="tpu_custom_call" | custom-call | tf_op jit(solution)/shard_map/pack/pallas_call | solution.py:422
  1.6 5.1 %collective-permute-start.2 = (bf16[48,768]{1,0:T(8,128)(2,1)S(1)}, bf16[48,768]{1,0:T(8,128)(2,1)S(1)}, u32[]{:S(2)}, u32[]{:S(2)}) collective-permute-start(bf16[48,768]{1,0:T(8,128)(2,1)S(1)} %get-tuple-element.22), channel_id=1, source_target_pairs={{0,12},{2,14},{4,8},{6,10},{8,4},{10,6},{12,0},{14,2},{1,13},{3,15... | collective-permute-start | bytes 221192 | tf_op jit(solution)/shard_map/ppermute | solution.py:176
  6.7 0.0 collective-permute-start
  6.7 0.6 %collective-permute-start.1 = (bf16[48,768]{1,0:T(8,128)(2,1)S(1)}, bf16[48,768]{1,0:T(8,128)(2,1)S(1)}, u32[]{:S(2)}, u32[]{:S(2)}) collective-permute-start(bf16[48,768]{1,0:T(8,128)(2,1)S(1)} %get-tuple-element.21.refs_0_), channel_id=1, source_target_pairs={{0,8},{2,10},{4,12},{6,14},{8,0},{10,2},{12,4},{14,6},{1,9},{3,11}... | collective-permute-start | bytes 221192 | tf_op jit(solution)/shard_map/ppermute | solution.py:176
  7.3 1.6 %collective-permute-start.3 = (bf16[48,768]{1,0:T(8,128)(2,1)S(1)}, bf16[48,768]{1,0:T(8,128)(2,1)S(1)}, u32[]{:S(2)}, u32[]{:S(2)}) collective-permute-start(bf16[48,768]{1,0:T(8,128)(2,1)S(1)} %get-tuple-element.21.refs_0_), channel_id=1, source_target_pairs={{0,2},{2,0},{4,6},{6,4},{8,10},{10,8},{12,14},{14,12},{1,3},{3,1},... | collective-permute-start | bytes 221192 | tf_op jit(solution)/shard_map/ppermute | solution.py:176
  9.0 0.9 %collective-permute-done.2.refs_3_ = bf16[48,768]{1,0:T(8,128)(2,1)S(1)} collective-permute-done((bf16[48,768]{1,0:T(8,128)(2,1)S(1)}, bf16[48,768]{1,0:T(8,128)(2,1)S(1)}, u32[]{:S(2)}, u32[]{:S(2)}) %collective-permute-start.2) | collective-permute-done | bytes 73760 | tf_op jit(solution)/shard_map/ppermute | solution.py:176
  9.8 1.5 %collective-permute-start.6 = (bf16[48,768]{1,0:T(8,128)(2,1)S(1)}, bf16[48,768]{1,0:T(8,128)(2,1)S(1)}, u32[]{:S(2)}, u32[]{:S(2)}) collective-permute-start(bf16[48,768]{1,0:T(8,128)(2,1)S(1)} %collective-permute-done.2.refs_3_), channel_id=1, source_target_pairs={{0,2},{2,0},{4,6},{6,4},{8,10},{10,8},{12,14},{14,12},{1,3},{3,1},... | collective-permute-start | bytes 221192 | tf_op jit(solution)/shard_map/ppermute | solution.py:176
  11.3 0.4 %collective-permute-done.refs_1_ = bf16[48,768]{1,0:T(8,128)(2,1)S(1)} collective-permute-done((bf16[48,768]{1,0:T(8,128)(2,1)S(1)}, bf16[48,768]{1,0:T(8,128)(2,1)S(1)}, u32[]{:S(2)}, u32[]{:S(2)}) %collective-permute-start) | collective-permute-done | bytes 73760 | tf_op jit(solution)/shard_map/ppermute | solution.py:176
  11.7 1.6 %collective-permute-start.4 = (bf16[48,768]{1,0:T(8,128)(2,1)S(1)}, bf16[48,768]{1,0:T(8,128)(2,1)S(1)}, u32[]{:S(2)}, u32[]{:S(2)}) collective-permute-start(bf16[48,768]{1,0:T(8,128)(2,1)S(1)} %collective-permute-done.refs_1_), channel_id=1, source_target_pairs={{0,2},{2,0},{4,6},{6,4},{8,10},{10,8},{12,14},{14,12},{1,3},{3,1},... | collective-permute-start | bytes 221192 | tf_op jit(solution)/shard_map/ppermute | solution.py:176
  13.4 0.0 collective-permute-done.1.refs_2_
  13.4 0.7 %collective-permute-start.5 = (bf16[48,768]{1,0:T(8,128)(2,1)S(1)}, bf16[48,768]{1,0:T(8,128)(2,1)S(1)}, u32[]{:S(2)}, u32[]{:S(2)}) collective-permute-start(bf16[48,768]{1,0:T(8,128)(2,1)S(1)} %collective-permute-done.1.refs_2_), channel_id=1, source_target_pairs={{0,2},{2,0},{4,6},{6,4},{8,10},{10,8},{12,14},{14,12},{1,3},{3,1},... | collective-permute-start | bytes 221192 | tf_op jit(solution)/shard_map/ppermute | solution.py:176
  14.1 1.6 %hold.1.weight_ref = bf16[1536,768]{1,0:T(8,128)(2,1)S(1)} custom-call(bf16[1536,768]{1,0:T(8,128)(2,1)} %weight_hbm.1, s32[8,128]{1,0:T(8,128)S(1)} %get-tuple-element.20.after_ref.limits_ref), custom_call_target="tpu_custom_call" | custom-call | bytes 4718592 | tf_op jit(solution)/shard_map/hold/pallas_call | solution.py:442
  15.7 0.0 collective-permute-done.3.refs_4_
  15.7 0.0 collective-permute-done.6.refs_7_
  15.7 1.1 %collective-permute-done.4.refs_5_ = bf16[48,768]{1,0:T(8,128)(2,1)S(1)} collective-permute-done((bf16[48,768]{1,0:T(8,128)(2,1)S(1)}, bf16[48,768]{1,0:T(8,128)(2,1)S(1)}, u32[]{:S(2)}, u32[]{:S(2)}) %collective-permute-start.4) | collective-permute-done | bytes 73760 | tf_op jit(solution)/shard_map/ppermute | solution.py:176
  16.8 0.9 %collective-permute-done.5.refs_6_ = bf16[48,768]{1,0:T(8,128)(2,1)S(1)} collective-permute-done((bf16[48,768]{1,0:T(8,128)(2,1)S(1)}, bf16[48,768]{1,0:T(8,128)(2,1)S(1)}, u32[]{:S(2)}, u32[]{:S(2)}) %collective-permute-start.5) | collective-permute-done | bytes 73760 | tf_op jit(solution)/shard_map/ppermute | solution.py:176
  17.7 0.6 %attend.1 = (bf16[16,768]{1,0:T(8,128)(2,1)S(1)}, bf16[16,1024]{1,0:T(8,128)(2,1)S(1)}, f32[8,128]{1,0:T(8,128)S(1)}) custom-call(s32[8,128]{1,0:T(8,128)S(1)} %get-tuple-element.20.after_ref.limits_ref, bf16[48,768]{1,0:T(8,128)(2,1)S(1)} %get-tuple-element.21.refs_0_, bf16[48,768]{1,0:T(8,128)(2,1)S(1)} %collective-permute-done.refs_1_, ...), custom_call_target="tpu_custom_call" | custom-call | tf_op jit(solution)/shard_map/attend/pallas_call | solution.py:460
  18.3 1.3 %collective-permute-start.7 = (bf16[16,1024]{1,0:T(8,128)(2,1)S(1)}, bf16[16,1024]{1,0:T(8,128)(2,1)S(1)}, u32[]{:S(2)}, u32[]{:S(2)}) collective-permute-start(bf16[16,1024]{1,0:T(8,128)(2,1)S(1)} %get-tuple-element.23), channel_id=1, source_target_pairs={{0,4},{2,6},{4,0},{6,2},{8,12},{10,14},{12,8},{14,10},{1,5},{3,7},... | collective-permute-start | bytes 98312 | tf_op jit(solution)/shard_map/ppermute | solution.py:176
  19.5 0.0 collective-permute-start.8
  19.5 1.2 %collective-permute-done.8.partner_keep_ref = bf16[16,768]{1,0:T(8,128)(2,1)S(1)} collective-permute-done((bf16[16,768]{1,0:T(8,128)(2,1)S(1)}, bf16[16,768]{1,0:T(8,128)(2,1)S(1)}, u32[]{:S(2)}, u32[]{:S(2)}) %collective-permute-start.8) | collective-permute-done | bytes 24608 | tf_op jit(solution)/shard_map/ppermute | solution.py:20
  20.7 0.3 %keep.1 = (f32[16,768]{1,0:T(8,128)S(1)}, f32[16,128]{1,0:T(8,128)S(1)}) custom-call(bf16[16,768]{1,0:T(8,128)(2,1)S(1)} %get-tuple-element.24.keep_ref, bf16[16,768]{1,0:T(8,128)(2,1)S(1)} %collective-permute-done.8.partner_keep_ref, bf16[1536,768]{1,0:T(8,128)(2,1)S(1)} %hold.1.weight_ref), custom_call_target="tpu_custom_call" | custom-call | tf_op jit(solution)/shard_map/keep/pallas_call | solution.py:475
  21.0 1.2 %collective-permute-done.7.message_ref = bf16[16,1024]{1,0:T(8,128)(2,1)S(1)} collective-permute-done((bf16[16,1024]{1,0:T(8,128)(2,1)S(1)}, bf16[16,1024]{1,0:T(8,128)(2,1)S(1)}, u32[]{:S(2)}, u32[]{:S(2)}) %collective-permute-start.7) | collective-permute-done | bytes 32800 | tf_op jit(solution)/shard_map/ppermute | solution.py:176
  22.2 0.0 collective-permute-start.9
  22.3 1.2 %collective-permute-done.9.partner_back_ref = bf16[16,1024]{1,0:T(8,128)(2,1)S(1)} collective-permute-done((bf16[16,1024]{1,0:T(8,128)(2,1)S(1)}, bf16[16,1024]{1,0:T(8,128)(2,1)S(1)}, u32[]{:S(2)}, u32[]{:S(2)}) %collective-permute-start.9) | collective-permute-done | bytes 32800 | tf_op jit(solution)/shard_map/ppermute | solution.py:20
  23.5 0.9 %project.1 = (bf16[16,768]{1,0:T(8,128)(2,1)}, f32[2,8,16]{2,1,0:T(8,128)}) custom-call(f32[16,768]{1,0:T(8,128)S(1)} %get-tuple-element.28.total_ref, f32[16,128]{1,0:T(8,128)S(1)} %get-tuple-element.29.size_ref, bf16[16,1024]{1,0:T(8,128)(2,1)S(1)} %collective-permute-done.7.message_ref, bf16[16,1024]{1,0:T(8,128)(2,1)S(1)} %collective-permute-done.9.partner_back_ref, ...), custom_call_target="tpu_custom_call" | custom-call | tf_op jit(solution)/shard_map/project/pallas_call | solution.py:488
Async XLA Ops:
  1.6 8.3 %collective-permute-start.2 = (bf16[48,768]{1,0:T(8,128)(2,1)S(1)}, bf16[48,768]{1,0:T(8,128)(2,1)S(1)}, u32[]{:S(2)}, u32[]{:S(2)}) collective-permute-start(bf16[48,768]{1,0:T(8,128)(2,1)S(1)} %get-tuple-element.22), channel_id=1, source_target_pairs={{0,12},{2,14},{4,8},{6,10},{8,4},{10,6},{12,0},{14,2},{1,13},{3,15... | collective-permute-start | bytes 221192 | tf_op jit(solution)/shard_map/ppermute | solution.py:176
  6.7 5.0 %collective-permute-start = (bf16[48,768]{1,0:T(8,128)(2,1)S(1)}, bf16[48,768]{1,0:T(8,128)(2,1)S(1)}, u32[]{:S(2)}, u32[]{:S(2)}) collective-permute-start(bf16[48,768]{1,0:T(8,128)(2,1)S(1)} %get-tuple-element.22), channel_id=1, source_target_pairs={{0,4},{2,6},{4,0},{6,2},{8,12},{10,14},{12,8},{14,10},{1,5},{3,7},... | collective-permute-start | bytes 221192 | tf_op jit(solution)/shard_map/ppermute | solution.py:176
  6.7 6.7 %collective-permute-start.1 = (bf16[48,768]{1,0:T(8,128)(2,1)S(1)}, bf16[48,768]{1,0:T(8,128)(2,1)S(1)}, u32[]{:S(2)}, u32[]{:S(2)}) collective-permute-start(bf16[48,768]{1,0:T(8,128)(2,1)S(1)} %get-tuple-element.21.refs_0_), channel_id=1, source_target_pairs={{0,8},{2,10},{4,12},{6,14},{8,0},{10,2},{12,4},{14,6},{1,9},{3,11}... | collective-permute-start | bytes 221192 | tf_op jit(solution)/shard_map/ppermute | solution.py:176
  7.3 8.4 %collective-permute-start.3 = (bf16[48,768]{1,0:T(8,128)(2,1)S(1)}, bf16[48,768]{1,0:T(8,128)(2,1)S(1)}, u32[]{:S(2)}, u32[]{:S(2)}) collective-permute-start(bf16[48,768]{1,0:T(8,128)(2,1)S(1)} %get-tuple-element.21.refs_0_), channel_id=1, source_target_pairs={{0,2},{2,0},{4,6},{6,4},{8,10},{10,8},{12,14},{14,12},{1,3},{3,1},... | collective-permute-start | bytes 221192 | tf_op jit(solution)/shard_map/ppermute | solution.py:176
  9.8 5.9 %collective-permute-start.6 = (bf16[48,768]{1,0:T(8,128)(2,1)S(1)}, bf16[48,768]{1,0:T(8,128)(2,1)S(1)}, u32[]{:S(2)}, u32[]{:S(2)}) collective-permute-start(bf16[48,768]{1,0:T(8,128)(2,1)S(1)} %collective-permute-done.2.refs_3_), channel_id=1, source_target_pairs={{0,2},{2,0},{4,6},{6,4},{8,10},{10,8},{12,14},{14,12},{1,3},{3,1},... | collective-permute-start | bytes 221192 | tf_op jit(solution)/shard_map/ppermute | solution.py:176
  11.7 5.1 %collective-permute-start.4 = (bf16[48,768]{1,0:T(8,128)(2,1)S(1)}, bf16[48,768]{1,0:T(8,128)(2,1)S(1)}, u32[]{:S(2)}, u32[]{:S(2)}) collective-permute-start(bf16[48,768]{1,0:T(8,128)(2,1)S(1)} %collective-permute-done.refs_1_), channel_id=1, source_target_pairs={{0,2},{2,0},{4,6},{6,4},{8,10},{10,8},{12,14},{14,12},{1,3},{3,1},... | collective-permute-start | bytes 221192 | tf_op jit(solution)/shard_map/ppermute | solution.py:176
  13.4 4.4 %collective-permute-start.5 = (bf16[48,768]{1,0:T(8,128)(2,1)S(1)}, bf16[48,768]{1,0:T(8,128)(2,1)S(1)}, u32[]{:S(2)}, u32[]{:S(2)}) collective-permute-start(bf16[48,768]{1,0:T(8,128)(2,1)S(1)} %collective-permute-done.1.refs_2_), channel_id=1, source_target_pairs={{0,2},{2,0},{4,6},{6,4},{8,10},{10,8},{12,14},{14,12},{1,3},{3,1},... | collective-permute-start | bytes 221192 | tf_op jit(solution)/shard_map/ppermute | solution.py:176
  18.3 4.0 %collective-permute-start.7 = (bf16[16,1024]{1,0:T(8,128)(2,1)S(1)}, bf16[16,1024]{1,0:T(8,128)(2,1)S(1)}, u32[]{:S(2)}, u32[]{:S(2)}) collective-permute-start(bf16[16,1024]{1,0:T(8,128)(2,1)S(1)} %get-tuple-element.23), channel_id=1, source_target_pairs={{0,4},{2,6},{4,0},{6,2},{8,12},{10,14},{12,8},{14,10},{1,5},{3,7},... | collective-permute-start | bytes 98312 | tf_op jit(solution)/shard_map/ppermute | solution.py:176
  19.5 1.2 %collective-permute-start.8 = (bf16[16,768]{1,0:T(8,128)(2,1)S(1)}, bf16[16,768]{1,0:T(8,128)(2,1)S(1)}, u32[]{:S(2)}, u32[]{:S(2)}) collective-permute-start(bf16[16,768]{1,0:T(8,128)(2,1)S(1)} %get-tuple-element.24.keep_ref), channel_id=1, source_target_pairs={{0,1},{1,0},{2,3},{3,2},{4,5},{5,4},{6,7},{7,6},{8,9},{9,8},{10,11... | collective-permute-start | bytes 73736 | tf_op jit(solution)/shard_map/ppermute | solution.py:20
  22.2 1.2 %collective-permute-start.9 = (bf16[16,1024]{1,0:T(8,128)(2,1)S(1)}, bf16[16,1024]{1,0:T(8,128)(2,1)S(1)}, u32[]{:S(2)}, u32[]{:S(2)}) collective-permute-start(bf16[16,1024]{1,0:T(8,128)(2,1)S(1)} %collective-permute-done.7.message_ref), channel_id=1, source_target_pairs={{0,1},{1,0},{2,3},{3,2},{4,5},{5,4},{6,7},{7,6},{8,9},{9,8},{10,11... | collective-permute-start | bytes 98312 | tf_op jit(solution)/shard_map/ppermute | solution.py:20

commit v8 on v6

--- a/solution.py
+++ b/solution.py
@@ -470,9 +470,10 @@
         compiler_params=KERNEL_PARAMS,
         name="attend",
     )(*held(limits, *sets))
+    across = [(2 * i + b, 2 * (i ^ SPLIT) + 1 - b) for i in range(seq_count) for b in range(2)]
+    partner_back = lax.ppermute(message, ("seq", "branch"), across)
     partner_keep = partner_2(keep, "branch", 0)
     back = swap_shards(message, SPLIT)
-    partner_back = partner_2(back, "branch", 0)
     total, size = pl.pallas_call(
         keep_kernel,
         out_shape=[

time: 25 us -> 23.5 us (0.940)
  waiting for transfers between devices: 6.84 us -> 5.2 us
    ppermute x8, waiting for transfers between devices: 5.99 us -> 3.91 us  [swap_shards(): return lax.ppermute(array, 'seq', pairs)]
    ppermute x0 -> x1, waiting for transfers between devices: none -> 0.44 us  [per_device_halves(): partner_back = lax.ppermute(message, ('seq', 'branch'), across)]
    ppermute x2 -> x1, starting transfers between devices: 0.51 us -> 0.59 us  [partner_2(): lax.ppermute(array, axis, [(i, i ^ 1 << stride) for i in range(lax.axis_s...]
    ppermute x2 -> x1, waiting for transfers between devices: 0.85 us -> 0.85 us  [partner_2(): lax.ppermute(array, axis, [(i, i ^ 1 << stride) for i in range(lax.axis_s...]
  transfers between devices with their start and end apart: 10 -> 10, of which waited for: 6 -> 7; matrix products, arithmetic and copies ran while one was open for 0% -> 0% of each run, Pallas kernels for 8% -> 8%
where the time goes in v8:
time: 23.5 us; the launch traced here: 23.3 us
  starting transfers between devices  13.1 us (56%)
  waiting for transfers between devices  5.2 us (22%)
  Pallas kernels  4.3 us (18%)
  between operations  0.69 us (3%)
    ppermute x8, starting transfers between devices, swap_shards(): return lax.ppermute(array, 'seq', pairs)  12.5 us
    ppermute x8, waiting for transfers between devices, swap_shards(): return lax.ppermute(array, 'seq', pairs)  3.91 us
    pallas_call x1, Pallas kernels, per_device_halves(): pl.pallas_call(hold_kernel, out_shape=pltpu.VMEM(out_weight.shape, jnp.bf...  1.63 us
    pallas_call x1, Pallas kernels, per_device_halves(): pl.pallas_call(pack_kernel, out_shape=[pltpu.VMEM((3 * tok_dev, half_widt...  0.92 us
    pallas_call x1, Pallas kernels, per_device_halves(): pl.pallas_call(project_kernel, out_shape=[jax.ShapeDtypeStruct((tok_dev,...  0.91 us
    ppermute x1, waiting for transfers between devices, partner_2(): lax.ppermute(array, axis, [(i, i ^ 1 << stride) for i in range(lax.axis_s...  0.85 us
    ppermute x1, starting transfers between devices, partner_2(): lax.ppermute(array, axis, [(i, i ^ 1 << stride) for i in range(lax.axis_s...  0.59 us
    pallas_call x1, Pallas kernels, per_device_halves(): pl.pallas_call(functools.partial(attend_kernel, len(sets)), out_shape=[pl...  0.55 us
  transfers between devices with their start and end apart: 10, of which 7 were waited for; matrix products, arithmetic and copies ran while one was open for 0% of the time, Pallas kernels for 8%

profile of v8, /device:TPU:0, one launch (start us, length us, event | category | flops | bytes accessed | tf_op | source)
XLA Modules:
  0.0 23.3 jit_solution(7358180181296123117)
XLA Ops:
  0.6 0.9 %pack.1 = (bf16[48,768]{1,0:T(8,128)(2,1)S(1)}, bf16[48,768]{1,0:T(8,128)(2,1)S(1)}, s32[8,128]{1,0:T(8,128)S(1)}, s32[2,8,128]{2,1,0:T(8,128)S(1)}, s32[2,8,128]{2,1,0:T(8,128)S(1)}) custom-call(bf16[1,16,1536]{2,1,0:T(8,128)(2,1)} %query_hbm.1, bf16[1,16,1536]{2,1,0:T(8,128)(2,1)} %key_hbm.1, bf16[1,16,1536]{2,1,0:T(8,128)(2,1)} %value_hbm.1, ...), custom_call_target="tpu_custom_call" | custom-call | tf_op jit(solution)/shard_map/pack/pallas_call | solution.py:422
  1.6 5.1 %collective-permute-start.2 = (bf16[48,768]{1,0:T(8,128)(2,1)S(1)}, bf16[48,768]{1,0:T(8,128)(2,1)S(1)}, u32[]{:S(2)}, u32[]{:S(2)}) collective-permute-start(bf16[48,768]{1,0:T(8,128)(2,1)S(1)} %get-tuple-element.19), channel_id=1, source_target_pairs={{0,12},{2,14},{4,8},{6,10},{8,4},{10,6},{12,0},{14,2},{1,13},{3,15... | collective-permute-start | bytes 221192 | tf_op jit(solution)/shard_map/ppermute | solution.py:176
  6.7 0.0 collective-permute-start
  6.7 0.6 %collective-permute-start.1 = (bf16[48,768]{1,0:T(8,128)(2,1)S(1)}, bf16[48,768]{1,0:T(8,128)(2,1)S(1)}, u32[]{:S(2)}, u32[]{:S(2)}) collective-permute-start(bf16[48,768]{1,0:T(8,128)(2,1)S(1)} %get-tuple-element.18.refs_0_), channel_id=1, source_target_pairs={{0,8},{2,10},{4,12},{6,14},{8,0},{10,2},{12,4},{14,6},{1,9},{3,11}... | collective-permute-start | bytes 221192 | tf_op jit(solution)/shard_map/ppermute | solution.py:176
  7.3 1.6 %collective-permute-start.3 = (bf16[48,768]{1,0:T(8,128)(2,1)S(1)}, bf16[48,768]{1,0:T(8,128)(2,1)S(1)}, u32[]{:S(2)}, u32[]{:S(2)}) collective-permute-start(bf16[48,768]{1,0:T(8,128)(2,1)S(1)} %get-tuple-element.18.refs_0_), channel_id=1, source_target_pairs={{0,2},{2,0},{4,6},{6,4},{8,10},{10,8},{12,14},{14,12},{1,3},{3,1},... | collective-permute-start | bytes 221192 | tf_op jit(solution)/shard_map/ppermute | solution.py:176
  9.0 0.9 %collective-permute-done.2.refs_3_ = bf16[48,768]{1,0:T(8,128)(2,1)S(1)} collective-permute-done((bf16[48,768]{1,0:T(8,128)(2,1)S(1)}, bf16[48,768]{1,0:T(8,128)(2,1)S(1)}, u32[]{:S(2)}, u32[]{:S(2)}) %collective-permute-start.2) | collective-permute-done | bytes 73760 | tf_op jit(solution)/shard_map/ppermute | solution.py:176
  9.8 1.5 %collective-permute-start.6 = (bf16[48,768]{1,0:T(8,128)(2,1)S(1)}, bf16[48,768]{1,0:T(8,128)(2,1)S(1)}, u32[]{:S(2)}, u32[]{:S(2)}) collective-permute-start(bf16[48,768]{1,0:T(8,128)(2,1)S(1)} %collective-permute-done.2.refs_3_), channel_id=1, source_target_pairs={{0,2},{2,0},{4,6},{6,4},{8,10},{10,8},{12,14},{14,12},{1,3},{3,1},... | collective-permute-start | bytes 221192 | tf_op jit(solution)/shard_map/ppermute | solution.py:176
  11.3 0.4 %collective-permute-done.refs_1_ = bf16[48,768]{1,0:T(8,128)(2,1)S(1)} collective-permute-done((bf16[48,768]{1,0:T(8,128)(2,1)S(1)}, bf16[48,768]{1,0:T(8,128)(2,1)S(1)}, u32[]{:S(2)}, u32[]{:S(2)}) %collective-permute-start) | collective-permute-done | bytes 73760 | tf_op jit(solution)/shard_map/ppermute | solution.py:176
  11.7 1.6 %collective-permute-start.4 = (bf16[48,768]{1,0:T(8,128)(2,1)S(1)}, bf16[48,768]{1,0:T(8,128)(2,1)S(1)}, u32[]{:S(2)}, u32[]{:S(2)}) collective-permute-start(bf16[48,768]{1,0:T(8,128)(2,1)S(1)} %collective-permute-done.refs_1_), channel_id=1, source_target_pairs={{0,2},{2,0},{4,6},{6,4},{8,10},{10,8},{12,14},{14,12},{1,3},{3,1},... | collective-permute-start | bytes 221192 | tf_op jit(solution)/shard_map/ppermute | solution.py:176
  13.4 0.0 collective-permute-done.1.refs_2_
  13.4 0.7 %collective-permute-start.5 = (bf16[48,768]{1,0:T(8,128)(2,1)S(1)}, bf16[48,768]{1,0:T(8,128)(2,1)S(1)}, u32[]{:S(2)}, u32[]{:S(2)}) collective-permute-start(bf16[48,768]{1,0:T(8,128)(2,1)S(1)} %collective-permute-done.1.refs_2_), channel_id=1, source_target_pairs={{0,2},{2,0},{4,6},{6,4},{8,10},{10,8},{12,14},{14,12},{1,3},{3,1},... | collective-permute-start | bytes 221192 | tf_op jit(solution)/shard_map/ppermute | solution.py:176
  14.1 1.6 %hold.1.weight_ref = bf16[1536,768]{1,0:T(8,128)(2,1)S(1)} custom-call(bf16[1536,768]{1,0:T(8,128)(2,1)} %weight_hbm.1, s32[8,128]{1,0:T(8,128)S(1)} %get-tuple-element.17.after_ref.limits_ref), custom_call_target="tpu_custom_call" | custom-call | bytes 4718592 | tf_op jit(solution)/shard_map/hold/pallas_call | solution.py:442
  15.7 0.0 collective-permute-done.3.refs_4_
  15.7 0.0 collective-permute-done.6.refs_7_
  15.7 1.1 %collective-permute-done.4.refs_5_ = bf16[48,768]{1,0:T(8,128)(2,1)S(1)} collective-permute-done((bf16[48,768]{1,0:T(8,128)(2,1)S(1)}, bf16[48,768]{1,0:T(8,128)(2,1)S(1)}, u32[]{:S(2)}, u32[]{:S(2)}) %collective-permute-start.4) | collective-permute-done | bytes 73760 | tf_op jit(solution)/shard_map/ppermute | solution.py:176
  16.8 0.9 %collective-permute-done.5.refs_6_ = bf16[48,768]{1,0:T(8,128)(2,1)S(1)} collective-permute-done((bf16[48,768]{1,0:T(8,128)(2,1)S(1)}, bf16[48,768]{1,0:T(8,128)(2,1)S(1)}, u32[]{:S(2)}, u32[]{:S(2)}) %collective-permute-start.5) | collective-permute-done | bytes 73760 | tf_op jit(solution)/shard_map/ppermute | solution.py:176
  17.7 0.6 %attend.1 = (bf16[16,768]{1,0:T(8,128)(2,1)S(1)}, bf16[16,1024]{1,0:T(8,128)(2,1)S(1)}, f32[8,128]{1,0:T(8,128)S(1)}) custom-call(s32[8,128]{1,0:T(8,128)S(1)} %get-tuple-element.17.after_ref.limits_ref, bf16[48,768]{1,0:T(8,128)(2,1)S(1)} %get-tuple-element.18.refs_0_, bf16[48,768]{1,0:T(8,128)(2,1)S(1)} %collective-permute-done.refs_1_, ...), custom_call_target="tpu_custom_call" | custom-call | tf_op jit(solution)/shard_map/attend/pallas_call | solution.py:460
  18.3 0.1 collective-permute-start.9
  18.3 1.3 %collective-permute-start.8 = (bf16[16,1024]{1,0:T(8,128)(2,1)S(1)}, bf16[16,1024]{1,0:T(8,128)(2,1)S(1)}, u32[]{:S(2)}, u32[]{:S(2)}) collective-permute-start(bf16[16,1024]{1,0:T(8,128)(2,1)S(1)} %get-tuple-element.24), channel_id=1, source_target_pairs={{0,4},{2,6},{4,0},{6,2},{8,12},{10,14},{12,8},{14,10},{1,5},{3,7},... | collective-permute-start | bytes 98312 | tf_op jit(solution)/shard_map/ppermute | solution.py:176
  19.6 0.6 %collective-permute-start.7 = (bf16[16,768]{1,0:T(8,128)(2,1)S(1)}, bf16[16,768]{1,0:T(8,128)(2,1)S(1)}, u32[]{:S(2)}, u32[]{:S(2)}) collective-permute-start(bf16[16,768]{1,0:T(8,128)(2,1)S(1)} %get-tuple-element.20.keep_ref), channel_id=1, source_target_pairs={{0,1},{1,0},{2,3},{3,2},{4,5},{5,4},{6,7},{7,6},{8,9},{9,8},{10,11... | collective-permute-start | bytes 73736 | tf_op jit(solution)/shard_map/ppermute | solution.py:20
  20.2 0.8 %collective-permute-done.7.partner_keep_ref = bf16[16,768]{1,0:T(8,128)(2,1)S(1)} collective-permute-done((bf16[16,768]{1,0:T(8,128)(2,1)S(1)}, bf16[16,768]{1,0:T(8,128)(2,1)S(1)}, u32[]{:S(2)}, u32[]{:S(2)}) %collective-permute-start.7) | collective-permute-done | bytes 24608 | tf_op jit(solution)/shard_map/ppermute | solution.py:20
  21.0 0.3 %keep.1 = (f32[16,768]{1,0:T(8,128)S(1)}, f32[16,128]{1,0:T(8,128)S(1)}) custom-call(bf16[16,768]{1,0:T(8,128)(2,1)S(1)} %get-tuple-element.20.keep_ref, bf16[16,768]{1,0:T(8,128)(2,1)S(1)} %collective-permute-done.7.partner_keep_ref, bf16[1536,768]{1,0:T(8,128)(2,1)S(1)} %hold.1.weight_ref), custom_call_target="tpu_custom_call" | custom-call | tf_op jit(solution)/shard_map/keep/pallas_call | solution.py:477
  21.3 0.4 %collective-permute-done.9.partner_back_ref = bf16[16,1024]{1,0:T(8,128)(2,1)S(1)} collective-permute-done((bf16[16,1024]{1,0:T(8,128)(2,1)S(1)}, bf16[16,1024]{1,0:T(8,128)(2,1)S(1)}, u32[]{:S(2)}, u32[]{:S(2)}) %collective-permute-start.9) | collective-permute-done | bytes 32800 | tf_op jit(solution)/shard_map/ppermute | solution.py:474
  21.8 0.6 %collective-permute-done.8.message_ref = bf16[16,1024]{1,0:T(8,128)(2,1)S(1)} collective-permute-done((bf16[16,1024]{1,0:T(8,128)(2,1)S(1)}, bf16[16,1024]{1,0:T(8,128)(2,1)S(1)}, u32[]{:S(2)}, u32[]{:S(2)}) %collective-permute-start.8) | collective-permute-done | bytes 32800 | tf_op jit(solution)/shard_map/ppermute | solution.py:176
  22.4 0.9 %project.1 = (bf16[16,768]{1,0:T(8,128)(2,1)}, f32[2,8,16]{2,1,0:T(8,128)}) custom-call(f32[16,768]{1,0:T(8,128)S(1)} %get-tuple-element.22.total_ref, f32[16,128]{1,0:T(8,128)S(1)} %get-tuple-element.23.size_ref, bf16[16,1024]{1,0:T(8,128)(2,1)S(1)} %collective-permute-done.8.message_ref, bf16[16,1024]{1,0:T(8,128)(2,1)S(1)} %collective-permute-done.9.partner_back_ref, ...), custom_call_target="tpu_custom_call" | custom-call | tf_op jit(solution)/shard_map/project/pallas_call | solution.py:488
Async XLA Ops:
  1.6 8.3 %collective-permute-start.2 = (bf16[48,768]{1,0:T(8,128)(2,1)S(1)}, bf16[48,768]{1,0:T(8,128)(2,1)S(1)}, u32[]{:S(2)}, u32[]{:S(2)}) collective-permute-start(bf16[48,768]{1,0:T(8,128)(2,1)S(1)} %get-tuple-element.19), channel_id=1, source_target_pairs={{0,12},{2,14},{4,8},{6,10},{8,4},{10,6},{12,0},{14,2},{1,13},{3,15... | collective-permute-start | bytes 221192 | tf_op jit(solution)/shard_map/ppermute | solution.py:176
  6.7 5.0 %collective-permute-start = (bf16[48,768]{1,0:T(8,128)(2,1)S(1)}, bf16[48,768]{1,0:T(8,128)(2,1)S(1)}, u32[]{:S(2)}, u32[]{:S(2)}) collective-permute-start(bf16[48,768]{1,0:T(8,128)(2,1)S(1)} %get-tuple-element.19), channel_id=1, source_target_pairs={{0,4},{2,6},{4,0},{6,2},{8,12},{10,14},{12,8},{14,10},{1,5},{3,7},... | collective-permute-start | bytes 221192 | tf_op jit(solution)/shard_map/ppermute | solution.py:176
  6.7 6.7 %collective-permute-start.1 = (bf16[48,768]{1,0:T(8,128)(2,1)S(1)}, bf16[48,768]{1,0:T(8,128)(2,1)S(1)}, u32[]{:S(2)}, u32[]{:S(2)}) collective-permute-start(bf16[48,768]{1,0:T(8,128)(2,1)S(1)} %get-tuple-element.18.refs_0_), channel_id=1, source_target_pairs={{0,8},{2,10},{4,12},{6,14},{8,0},{10,2},{12,4},{14,6},{1,9},{3,11}... | collective-permute-start | bytes 221192 | tf_op jit(solution)/shard_map/ppermute | solution.py:176
  7.3 8.4 %collective-permute-start.3 = (bf16[48,768]{1,0:T(8,128)(2,1)S(1)}, bf16[48,768]{1,0:T(8,128)(2,1)S(1)}, u32[]{:S(2)}, u32[]{:S(2)}) collective-permute-start(bf16[48,768]{1,0:T(8,128)(2,1)S(1)} %get-tuple-element.18.refs_0_), channel_id=1, source_target_pairs={{0,2},{2,0},{4,6},{6,4},{8,10},{10,8},{12,14},{14,12},{1,3},{3,1},... | collective-permute-start | bytes 221192 | tf_op jit(solution)/shard_map/ppermute | solution.py:176
  9.8 5.9 %collective-permute-start.6 = (bf16[48,768]{1,0:T(8,128)(2,1)S(1)}, bf16[48,768]{1,0:T(8,128)(2,1)S(1)}, u32[]{:S(2)}, u32[]{:S(2)}) collective-permute-start(bf16[48,768]{1,0:T(8,128)(2,1)S(1)} %collective-permute-done.2.refs_3_), channel_id=1, source_target_pairs={{0,2},{2,0},{4,6},{6,4},{8,10},{10,8},{12,14},{14,12},{1,3},{3,1},... | collective-permute-start | bytes 221192 | tf_op jit(solution)/shard_map/ppermute | solution.py:176
  11.7 5.1 %collective-permute-start.4 = (bf16[48,768]{1,0:T(8,128)(2,1)S(1)}, bf16[48,768]{1,0:T(8,128)(2,1)S(1)}, u32[]{:S(2)}, u32[]{:S(2)}) collective-permute-start(bf16[48,768]{1,0:T(8,128)(2,1)S(1)} %collective-permute-done.refs_1_), channel_id=1, source_target_pairs={{0,2},{2,0},{4,6},{6,4},{8,10},{10,8},{12,14},{14,12},{1,3},{3,1},... | collective-permute-start | bytes 221192 | tf_op jit(solution)/shard_map/ppermute | solution.py:176
  13.4 4.4 %collective-permute-start.5 = (bf16[48,768]{1,0:T(8,128)(2,1)S(1)}, bf16[48,768]{1,0:T(8,128)(2,1)S(1)}, u32[]{:S(2)}, u32[]{:S(2)}) collective-permute-start(bf16[48,768]{1,0:T(8,128)(2,1)S(1)} %collective-permute-done.1.refs_2_), channel_id=1, source_target_pairs={{0,2},{2,0},{4,6},{6,4},{8,10},{10,8},{12,14},{14,12},{1,3},{3,1},... | collective-permute-start | bytes 221192 | tf_op jit(solution)/shard_map/ppermute | solution.py:176
  18.3 3.5 %collective-permute-start.9 = (bf16[16,1024]{1,0:T(8,128)(2,1)S(1)}, bf16[16,1024]{1,0:T(8,128)(2,1)S(1)}, u32[]{:S(2)}, u32[]{:S(2)}) collective-permute-start(bf16[16,1024]{1,0:T(8,128)(2,1)S(1)} %get-tuple-element.24), channel_id=1, source_target_pairs={{0,5},{1,4},{2,7},{3,6},{4,1},{5,0},{6,3},{7,2},{8,13},{9,12},{10,... | collective-permute-start | bytes 98312 | tf_op jit(solution)/shard_map/ppermute | solution.py:474
  18.3 4.1 %collective-permute-start.8 = (bf16[16,1024]{1,0:T(8,128)(2,1)S(1)}, bf16[16,1024]{1,0:T(8,128)(2,1)S(1)}, u32[]{:S(2)}, u32[]{:S(2)}) collective-permute-start(bf16[16,1024]{1,0:T(8,128)(2,1)S(1)} %get-tuple-element.24), channel_id=1, source_target_pairs={{0,4},{2,6},{4,0},{6,2},{8,12},{10,14},{12,8},{14,10},{1,5},{3,7},... | collective-permute-start | bytes 98312 | tf_op jit(solution)/shard_map/ppermute | solution.py:176
  19.6 1.4 %collective-permute-start.7 = (bf16[16,768]{1,0:T(8,128)(2,1)S(1)}, bf16[16,768]{1,0:T(8,128)(2,1)S(1)}, u32[]{:S(2)}, u32[]{:S(2)}) collective-permute-start(bf16[16,768]{1,0:T(8,128)(2,1)S(1)} %get-tuple-element.20.keep_ref), channel_id=1, source_target_pairs={{0,1},{1,0},{2,3},{3,2},{4,5},{5,4},{6,7},{7,6},{8,9},{9,8},{10,11... | collective-permute-start | bytes 73736 | tf_op jit(solution)/shard_map/ppermute | solution.py:20

commit v9 on v8

--- a/solution.py
+++ b/solution.py
@@ -166,7 +166,7 @@
 
 
 SPLIT = 2
-HOLD_COPIES = 4
+WEIGHT_COPIES = 4
 TABLE_PIECES = 3
 SPLITTER = 65537.0
 
@@ -181,30 +181,11 @@
     return line + [offset + 1 for offset in line]
 
 
-def pack_kernel(
-    query_hbm,
-    key_hbm,
-    value_hbm,
-    counts_hbm,
-    head_hbm,
-    own_ref,
-    other_ref,
-    limits_ref,
-    pick_ref,
-    slot_head_ref,
-    counts_ref,
-    head_ref,
-    copy_sems,
-):
+def pack_kernel(query_hbm, key_hbm, value_hbm, own_ref, other_ref, copy_sems):
     tok_dev = own_ref.shape[0] // 3
     half_width = own_ref.shape[1]
-    slot_count, shard_count = head_ref.shape
-    shard = lax.axis_index("seq")
-    half = (shard // SPLIT) % 2
-    copies = [
-        pltpu.make_async_copy(counts_hbm, counts_ref, copy_sems.at[0]),
-        pltpu.make_async_copy(head_hbm, head_ref, copy_sems.at[1]),
-    ]
+    half = (lax.axis_index("seq") // SPLIT) % 2
+    copies = []
     for target, place in ((other_ref, 1 - half), (own_ref, half)):
         columns = pl.ds(pl.multiple_of(place * half_width, half_width), half_width)
         for part, source in enumerate((key_hbm, value_hbm, query_hbm)):
@@ -214,6 +195,40 @@
                     source.at[0, :, columns], target.at[rows, :], copy_sems.at[len(copies)]
                 )
             )
+    for copy in copies:
+        copy.start()
+    for copy in copies:
+        copy.wait()
+
+
+def plan_kernel(
+    weight_hbm,
+    counts_hbm,
+    head_hbm,
+    after_ref,
+    weight_ref,
+    limits_ref,
+    pick_ref,
+    slot_head_ref,
+    counts_ref,
+    head_ref,
+    copy_sems,
+):
+    tok_dev = after_ref.shape[0] // 3
+    slot_count, shard_count = head_ref.shape
+    shard = lax.axis_index("seq")
+    copies = [
+        pltpu.make_async_copy(counts_hbm, counts_ref, copy_sems.at[0]),
+        pltpu.make_async_copy(head_hbm, head_ref, copy_sems.at[1]),
+    ]
+    share = weight_ref.shape[0] // WEIGHT_COPIES
+    for number in range(WEIGHT_COPIES):
+        rows = pl.ds(number * share, share)
+        copies.append(
+            pltpu.make_async_copy(
+                weight_hbm.at[rows, :], weight_ref.at[rows, :], copy_sems.at[len(copies)]
+            )
+        )
     for copy in copies:
         copy.start()
     copies[0].wait()
@@ -245,22 +260,6 @@
             )
         slot_head_ref[slot] = jnp.full(slot_head_ref.shape[1:], head, jnp.int32)
     for copy in copies[2:]:
-        copy.wait()
-
-
-def hold_kernel(weight_hbm, after_ref, weight_ref, copy_sems):
-    share = weight_ref.shape[0] // HOLD_COPIES
-    copies = []
-    for number in range(HOLD_COPIES):
-        rows = pl.ds(number * share, share)
-        copies.append(
-            pltpu.make_async_copy(
-                weight_hbm.at[rows, :], weight_ref.at[rows, :], copy_sems.at[number]
-            )
-        )
-    for copy in copies:
-        copy.start()
-    for copy in copies:
         copy.wait()
 
 
@@ -419,44 +418,41 @@
     def distant(*arrays):
         return [pltpu.with_memory_space_constraint(array, pltpu.HBM) for array in arrays]
 
-    own, other, limits, pick, slot_head = pl.pallas_call(
+    own, other = pl.pallas_call(
         pack_kernel,
+        out_shape=[pltpu.VMEM((3 * tok_dev, half_width), jnp.bfloat16)] * 2,
+        in_specs=[any_spec] * 3,
+        out_specs=[vmem] * 2,
+        scratch_shapes=[pltpu.SemaphoreType.DMA((6,))],
+        compiler_params=KERNEL_PARAMS,
+        name="pack",
+    )(*distant(queries, key_rows, value_rows))
+    weight_held, limits, pick, slot_head = pl.pallas_call(
+        plan_kernel,
         out_shape=[
-            pltpu.VMEM((3 * tok_dev, half_width), jnp.bfloat16),
-            pltpu.VMEM((3 * tok_dev, half_width), jnp.bfloat16),
+            pltpu.VMEM(out_weight.shape, jnp.bfloat16),
             pltpu.VMEM((8, tokens), jnp.int32),
             pltpu.VMEM((slot_count, seq_count, tokens), jnp.int32),
             pltpu.VMEM((slot_count, 8, tokens), jnp.int32),
         ],
-        in_specs=[any_spec] * 5,
-        out_specs=[vmem] * 5,
+        in_specs=[any_spec] * 3 + [vmem],
+        out_specs=[vmem] * 4,
         scratch_shapes=[
             pltpu.SMEM((seq_count,), jnp.int32),
             pltpu.SMEM((slot_count, seq_count), jnp.int32),
-            pltpu.SemaphoreType.DMA((8,)),
+            pltpu.SemaphoreType.DMA((2 + WEIGHT_COPIES,)),
         ],
-        compiler_params=KERNEL_PARAMS,
-        name="pack",
-    )(*distant(queries, key_rows, value_rows, counts, jnp.transpose(head_of)))
-
-    weight_held = pl.pallas_call(
-        hold_kernel,
-        out_shape=pltpu.VMEM(out_weight.shape, jnp.bfloat16),
-        in_specs=[any_spec, vmem],
-        out_specs=vmem,
-        scratch_shapes=[pltpu.SemaphoreType.DMA((HOLD_COPIES,))],
         compiler_params=KERNEL_PARAMS,
         cost_estimate=pl.CostEstimate(
             flops=0, bytes_accessed=4 * out_weight.size, transcendentals=0
         ),
-        name="hold",
-    )(*distant(out_weight), *held(limits))
+        name="plan",
+    )(*distant(out_weight, counts, jnp.transpose(head_of)), *held(own))
     line = [own] + [
         swap_shards(other if offset & SPLIT else own, offset)
         for offset in range(SPLIT, seq_count, SPLIT)
     ]
     sets = line + [swap_shards(array, 1) for array in line]
-    limits, weight_held = lax.optimization_barrier((limits, weight_held))
     keep, message, table = pl.pallas_call(
         functools.partial(attend_kernel, len(sets)),
         out_shape=[

time: 23.5 us -> 23.5 us (level)
  no operation moved by 1% of the time
where the time goes in v9:
time: 23.5 us; the launch traced here: 23.3 us
  starting transfers between devices  13.1 us (56%)
  waiting for transfers between devices  5.18 us (22%)
  Pallas kernels  4.3 us (18%)
  between operations  0.69 us (3%)
    ppermute x8, starting transfers between devices, swap_shards(): return lax.ppermute(array, 'seq', pairs)  12.5 us
    ppermute x8, waiting for transfers between devices, swap_shards(): return lax.ppermute(array, 'seq', pairs)  3.89 us
    pallas_call x1, Pallas kernels, per_device_halves(): pl.pallas_call(plan_kernel, out_shape=[pltpu.VMEM(out_weight.shape, jnp.b...  1.65 us
    pallas_call x1, Pallas kernels, per_device_halves(): pl.pallas_call(project_kernel, out_shape=[jax.ShapeDtypeStruct((tok_dev,...  0.91 us
    pallas_call x1, Pallas kernels, per_device_halves(): pl.pallas_call(pack_kernel, out_shape=[pltpu.VMEM((3 * tok_dev, half_widt...  0.9 us
    ppermute x1, waiting for transfers between devices, partner_2(): lax.ppermute(array, axis, [(i, i ^ 1 << stride) for i in range(lax.axis_s...  0.85 us
    ppermute x1, starting transfers between devices, partner_2(): lax.ppermute(array, axis, [(i, i ^ 1 << stride) for i in range(lax.axis_s...  0.59 us
    pallas_call x1, Pallas kernels, per_device_halves(): pl.pallas_call(functools.partial(attend_kernel, len(sets)), out_shape=[pl...  0.56 us
  transfers between devices with their start and end apart: 10, of which 7 were waited for; matrix products, arithmetic and copies ran while one was open for 0% of the time, Pallas kernels for 8%

profile of v9, /device:TPU:0, one launch (start us, length us, event | category | flops | bytes accessed | tf_op | source)
XLA Modules:
  0.0 23.3 jit_solution(5789896030580647550)
XLA Ops:
  0.6 0.9 %pack.1 = (bf16[48,768]{1,0:T(8,128)(2,1)S(1)}, bf16[48,768]{1,0:T(8,128)(2,1)S(1)}) custom-call(bf16[1,16,1536]{2,1,0:T(8,128)(2,1)} %query_hbm.1, bf16[1,16,1536]{2,1,0:T(8,128)(2,1)} %key_hbm.1, bf16[1,16,1536]{2,1,0:T(8,128)(2,1)} %value_hbm.1), custom_call_target="tpu_custom_call" | custom-call | tf_op jit(solution)/shard_map/pack/pallas_call | solution.py:421
  1.5 5.1 %collective-permute-start.2 = (bf16[48,768]{1,0:T(8,128)(2,1)S(1)}, bf16[48,768]{1,0:T(8,128)(2,1)S(1)}, u32[]{:S(2)}, u32[]{:S(2)}) collective-permute-start(bf16[48,768]{1,0:T(8,128)(2,1)S(1)} %get-tuple-element.17), channel_id=1, source_target_pairs={{0,12},{2,14},{4,8},{6,10},{8,4},{10,6},{12,0},{14,2},{1,13},{3,15... | collective-permute-start | bytes 221192 | tf_op jit(solution)/shard_map/ppermute | solution.py:176
  6.7 0.0 collective-permute-start
  6.7 0.6 %collective-permute-start.1 = (bf16[48,768]{1,0:T(8,128)(2,1)S(1)}, bf16[48,768]{1,0:T(8,128)(2,1)S(1)}, u32[]{:S(2)}, u32[]{:S(2)}) collective-permute-start(bf16[48,768]{1,0:T(8,128)(2,1)S(1)} %get-tuple-element.15.after_ref.refs_0_), channel_id=1, source_target_pairs={{0,8},{2,10},{4,12},{6,14},{8,0},{10,2},{12,4},{14,6},{1,9},{3,11}... | collective-permute-start | bytes 221192 | tf_op jit(solution)/shard_map/ppermute | solution.py:176
  7.3 1.6 %collective-permute-start.3 = (bf16[48,768]{1,0:T(8,128)(2,1)S(1)}, bf16[48,768]{1,0:T(8,128)(2,1)S(1)}, u32[]{:S(2)}, u32[]{:S(2)}) collective-permute-start(bf16[48,768]{1,0:T(8,128)(2,1)S(1)} %get-tuple-element.15.after_ref.refs_0_), channel_id=1, source_target_pairs={{0,2},{2,0},{4,6},{6,4},{8,10},{10,8},{12,14},{14,12},{1,3},{3,1},... | collective-permute-start | bytes 221192 | tf_op jit(solution)/shard_map/ppermute | solution.py:176
  8.9 0.9 %collective-permute-done.2.refs_3_ = bf16[48,768]{1,0:T(8,128)(2,1)S(1)} collective-permute-done((bf16[48,768]{1,0:T(8,128)(2,1)S(1)}, bf16[48,768]{1,0:T(8,128)(2,1)S(1)}, u32[]{:S(2)}, u32[]{:S(2)}) %collective-permute-start.2) | collective-permute-done | bytes 73760 | tf_op jit(solution)/shard_map/ppermute | solution.py:176
  9.8 1.5 %collective-permute-start.6 = (bf16[48,768]{1,0:T(8,128)(2,1)S(1)}, bf16[48,768]{1,0:T(8,128)(2,1)S(1)}, u32[]{:S(2)}, u32[]{:S(2)}) collective-permute-start(bf16[48,768]{1,0:T(8,128)(2,1)S(1)} %collective-permute-done.2.refs_3_), channel_id=1, source_target_pairs={{0,2},{2,0},{4,6},{6,4},{8,10},{10,8},{12,14},{14,12},{1,3},{3,1},... | collective-permute-start | bytes 221192 | tf_op jit(solution)/shard_map/ppermute | solution.py:176
  11.3 0.4 %collective-permute-done.refs_1_ = bf16[48,768]{1,0:T(8,128)(2,1)S(1)} collective-permute-done((bf16[48,768]{1,0:T(8,128)(2,1)S(1)}, bf16[48,768]{1,0:T(8,128)(2,1)S(1)}, u32[]{:S(2)}, u32[]{:S(2)}) %collective-permute-start) | collective-permute-done | bytes 73760 | tf_op jit(solution)/shard_map/ppermute | solution.py:176
  11.7 1.6 %collective-permute-start.4 = (bf16[48,768]{1,0:T(8,128)(2,1)S(1)}, bf16[48,768]{1,0:T(8,128)(2,1)S(1)}, u32[]{:S(2)}, u32[]{:S(2)}) collective-permute-start(bf16[48,768]{1,0:T(8,128)(2,1)S(1)} %collective-permute-done.refs_1_), channel_id=1, source_target_pairs={{0,2},{2,0},{4,6},{6,4},{8,10},{10,8},{12,14},{14,12},{1,3},{3,1},... | collective-permute-start | bytes 221192 | tf_op jit(solution)/shard_map/ppermute | solution.py:176
  13.3 0.0 collective-permute-done.1.refs_2_
  13.3 0.7 %collective-permute-start.5 = (bf16[48,768]{1,0:T(8,128)(2,1)S(1)}, bf16[48,768]{1,0:T(8,128)(2,1)S(1)}, u32[]{:S(2)}, u32[]{:S(2)}) collective-permute-start(bf16[48,768]{1,0:T(8,128)(2,1)S(1)} %collective-permute-done.1.refs_2_), channel_id=1, source_target_pairs={{0,2},{2,0},{4,6},{6,4},{8,10},{10,8},{12,14},{14,12},{1,3},{3,1},... | collective-permute-start | bytes 221192 | tf_op jit(solution)/shard_map/ppermute | solution.py:176
  14.1 1.6 %plan.1 = (bf16[1536,768]{1,0:T(8,128)(2,1)S(1)}, s32[8,128]{1,0:T(8,128)S(1)}, s32[2,8,128]{2,1,0:T(8,128)S(1)}, s32[2,8,128]{2,1,0:T(8,128)S(1)}) custom-call(bf16[1536,768]{1,0:T(8,128)(2,1)} %weight_hbm.1, s32[8]{0:T(128)} %counts_hbm.1, s32[2,8]{1,0:T(2,128)} %bitcast.4, bf16[48,768]{1,0:T(8,128)(2,1)S(1)} %get-tuple-element.15.after_ref.refs_0_), custom_call_target="tpu_custom_call" | custom-call | bytes 4718592 | tf_op jit(solution)/shard_map/plan/pallas_call | solution.py:430
  15.7 0.0 collective-permute-done.3.refs_4_
  15.7 0.0 collective-permute-done.6.refs_7_
  15.7 1.1 %collective-permute-done.4.refs_5_ = bf16[48,768]{1,0:T(8,128)(2,1)S(1)} collective-permute-done((bf16[48,768]{1,0:T(8,128)(2,1)S(1)}, bf16[48,768]{1,0:T(8,128)(2,1)S(1)}, u32[]{:S(2)}, u32[]{:S(2)}) %collective-permute-start.4) | collective-permute-done | bytes 73760 | tf_op jit(solution)/shard_map/ppermute | solution.py:176
  16.8 0.9 %collective-permute-done.5.refs_6_ = bf16[48,768]{1,0:T(8,128)(2,1)S(1)} collective-permute-done((bf16[48,768]{1,0:T(8,128)(2,1)S(1)}, bf16[48,768]{1,0:T(8,128)(2,1)S(1)}, u32[]{:S(2)}, u32[]{:S(2)}) %collective-permute-start.5) | collective-permute-done | bytes 73760 | tf_op jit(solution)/shard_map/ppermute | solution.py:176
  17.7 0.6 %attend.1 = (bf16[16,768]{1,0:T(8,128)(2,1)S(1)}, bf16[16,1024]{1,0:T(8,128)(2,1)S(1)}, f32[8,128]{1,0:T(8,128)S(1)}) custom-call(s32[8,128]{1,0:T(8,128)S(1)} %get-tuple-element.16.limits_ref, bf16[48,768]{1,0:T(8,128)(2,1)S(1)} %get-tuple-element.15.after_ref.refs_0_, bf16[48,768]{1,0:T(8,128)(2,1)S(1)} %collective-permute-done.refs_1_, ...), custom_call_target="tpu_custom_call" | custom-call | tf_op jit(solution)/shard_map/attend/pallas_call | solution.py:456
  18.3 0.1 collective-permute-start.9
  18.3 1.3 %collective-permute-start.8 = (bf16[16,1024]{1,0:T(8,128)(2,1)S(1)}, bf16[16,1024]{1,0:T(8,128)(2,1)S(1)}, u32[]{:S(2)}, u32[]{:S(2)}) collective-permute-start(bf16[16,1024]{1,0:T(8,128)(2,1)S(1)} %get-tuple-element.22), channel_id=1, source_target_pairs={{0,4},{2,6},{4,0},{6,2},{8,12},{10,14},{12,8},{14,10},{1,5},{3,7},... | collective-permute-start | bytes 98312 | tf_op jit(solution)/shard_map/ppermute | solution.py:176
  19.6 0.6 %collective-permute-start.7 = (bf16[16,768]{1,0:T(8,128)(2,1)S(1)}, bf16[16,768]{1,0:T(8,128)(2,1)S(1)}, u32[]{:S(2)}, u32[]{:S(2)}) collective-permute-start(bf16[16,768]{1,0:T(8,128)(2,1)S(1)} %get-tuple-element.18.keep_ref), channel_id=1, source_target_pairs={{0,1},{1,0},{2,3},{3,2},{4,5},{5,4},{6,7},{7,6},{8,9},{9,8},{10,11... | collective-permute-start | bytes 73736 | tf_op jit(solution)/shard_map/ppermute | solution.py:20
  20.2 0.8 %collective-permute-done.7.partner_keep_ref = bf16[16,768]{1,0:T(8,128)(2,1)S(1)} collective-permute-done((bf16[16,768]{1,0:T(8,128)(2,1)S(1)}, bf16[16,768]{1,0:T(8,128)(2,1)S(1)}, u32[]{:S(2)}, u32[]{:S(2)}) %collective-permute-start.7) | collective-permute-done | bytes 24608 | tf_op jit(solution)/shard_map/ppermute | solution.py:20
  21.0 0.3 %keep.1 = (f32[16,768]{1,0:T(8,128)S(1)}, f32[16,128]{1,0:T(8,128)S(1)}) custom-call(bf16[16,768]{1,0:T(8,128)(2,1)S(1)} %get-tuple-element.18.keep_ref, bf16[16,768]{1,0:T(8,128)(2,1)S(1)} %collective-permute-done.7.partner_keep_ref, bf16[1536,768]{1,0:T(8,128)(2,1)S(1)} %get-tuple-element.19.weight_ref), custom_call_target="tpu_custom_call" | custom-call | tf_op jit(solution)/shard_map/keep/pallas_call | solution.py:473
  21.3 0.4 %collective-permute-done.9.partner_back_ref = bf16[16,1024]{1,0:T(8,128)(2,1)S(1)} collective-permute-done((bf16[16,1024]{1,0:T(8,128)(2,1)S(1)}, bf16[16,1024]{1,0:T(8,128)(2,1)S(1)}, u32[]{:S(2)}, u32[]{:S(2)}) %collective-permute-start.9) | collective-permute-done | bytes 32800 | tf_op jit(solution)/shard_map/ppermute | solution.py:470
  21.8 0.6 %collective-permute-done.8.message_ref = bf16[16,1024]{1,0:T(8,128)(2,1)S(1)} collective-permute-done((bf16[16,1024]{1,0:T(8,128)(2,1)S(1)}, bf16[16,1024]{1,0:T(8,128)(2,1)S(1)}, u32[]{:S(2)}, u32[]{:S(2)}) %collective-permute-start.8) | collective-permute-done | bytes 32800 | tf_op jit(solution)/shard_map/ppermute | solution.py:176
  22.4 0.9 %project.1 = (bf16[16,768]{1,0:T(8,128)(2,1)}, f32[2,8,16]{2,1,0:T(8,128)}) custom-call(f32[16,768]{1,0:T(8,128)S(1)} %get-tuple-element.20.total_ref, f32[16,128]{1,0:T(8,128)S(1)} %get-tuple-element.21.size_ref, bf16[16,1024]{1,0:T(8,128)(2,1)S(1)} %collective-permute-done.8.message_ref, bf16[16,1024]{1,0:T(8,128)(2,1)S(1)} %collective-permute-done.9.partner_back_ref, ...), custom_call_target="tpu_custom_call" | custom-call | tf_op jit(solution)/shard_map/project/pallas_call | solution.py:484
Async XLA Ops:
  1.5 8.3 %collective-permute-start.2 = (bf16[48,768]{1,0:T(8,128)(2,1)S(1)}, bf16[48,768]{1,0:T(8,128)(2,1)S(1)}, u32[]{:S(2)}, u32[]{:S(2)}) collective-permute-start(bf16[48,768]{1,0:T(8,128)(2,1)S(1)} %get-tuple-element.17), channel_id=1, source_target_pairs={{0,12},{2,14},{4,8},{6,10},{8,4},{10,6},{12,0},{14,2},{1,13},{3,15... | collective-permute-start | bytes 221192 | tf_op jit(solution)/shard_map/ppermute | solution.py:176
  6.7 5.0 %collective-permute-start = (bf16[48,768]{1,0:T(8,128)(2,1)S(1)}, bf16[48,768]{1,0:T(8,128)(2,1)S(1)}, u32[]{:S(2)}, u32[]{:S(2)}) collective-permute-start(bf16[48,768]{1,0:T(8,128)(2,1)S(1)} %get-tuple-element.17), channel_id=1, source_target_pairs={{0,4},{2,6},{4,0},{6,2},{8,12},{10,14},{12,8},{14,10},{1,5},{3,7},... | collective-permute-start | bytes 221192 | tf_op jit(solution)/shard_map/ppermute | solution.py:176
  6.7 6.7 %collective-permute-start.1 = (bf16[48,768]{1,0:T(8,128)(2,1)S(1)}, bf16[48,768]{1,0:T(8,128)(2,1)S(1)}, u32[]{:S(2)}, u32[]{:S(2)}) collective-permute-start(bf16[48,768]{1,0:T(8,128)(2,1)S(1)} %get-tuple-element.15.after_ref.refs_0_), channel_id=1, source_target_pairs={{0,8},{2,10},{4,12},{6,14},{8,0},{10,2},{12,4},{14,6},{1,9},{3,11}... | collective-permute-start | bytes 221192 | tf_op jit(solution)/shard_map/ppermute | solution.py:176
  7.3 8.4 %collective-permute-start.3 = (bf16[48,768]{1,0:T(8,128)(2,1)S(1)}, bf16[48,768]{1,0:T(8,128)(2,1)S(1)}, u32[]{:S(2)}, u32[]{:S(2)}) collective-permute-start(bf16[48,768]{1,0:T(8,128)(2,1)S(1)} %get-tuple-element.15.after_ref.refs_0_), channel_id=1, source_target_pairs={{0,2},{2,0},{4,6},{6,4},{8,10},{10,8},{12,14},{14,12},{1,3},{3,1},... | collective-permute-start | bytes 221192 | tf_op jit(solution)/shard_map/ppermute | solution.py:176
  9.8 5.9 %collective-permute-start.6 = (bf16[48,768]{1,0:T(8,128)(2,1)S(1)}, bf16[48,768]{1,0:T(8,128)(2,1)S(1)}, u32[]{:S(2)}, u32[]{:S(2)}) collective-permute-start(bf16[48,768]{1,0:T(8,128)(2,1)S(1)} %collective-permute-done.2.refs_3_), channel_id=1, source_target_pairs={{0,2},{2,0},{4,6},{6,4},{8,10},{10,8},{12,14},{14,12},{1,3},{3,1},... | collective-permute-start | bytes 221192 | tf_op jit(solution)/shard_map/ppermute | solution.py:176
  11.7 5.1 %collective-permute-start.4 = (bf16[48,768]{1,0:T(8,128)(2,1)S(1)}, bf16[48,768]{1,0:T(8,128)(2,1)S(1)}, u32[]{:S(2)}, u32[]{:S(2)}) collective-permute-start(bf16[48,768]{1,0:T(8,128)(2,1)S(1)} %collective-permute-done.refs_1_), channel_id=1, source_target_pairs={{0,2},{2,0},{4,6},{6,4},{8,10},{10,8},{12,14},{14,12},{1,3},{3,1},... | collective-permute-start | bytes 221192 | tf_op jit(solution)/shard_map/ppermute | solution.py:176
  13.3 4.4 %collective-permute-start.5 = (bf16[48,768]{1,0:T(8,128)(2,1)S(1)}, bf16[48,768]{1,0:T(8,128)(2,1)S(1)}, u32[]{:S(2)}, u32[]{:S(2)}) collective-permute-start(bf16[48,768]{1,0:T(8,128)(2,1)S(1)} %collective-permute-done.1.refs_2_), channel_id=1, source_target_pairs={{0,2},{2,0},{4,6},{6,4},{8,10},{10,8},{12,14},{14,12},{1,3},{3,1},... | collective-permute-start | bytes 221192 | tf_op jit(solution)/shard_map/ppermute | solution.py:176
  18.3 3.5 %collective-permute-start.9 = (bf16[16,1024]{1,0:T(8,128)(2,1)S(1)}, bf16[16,1024]{1,0:T(8,128)(2,1)S(1)}, u32[]{:S(2)}, u32[]{:S(2)}) collective-permute-start(bf16[16,1024]{1,0:T(8,128)(2,1)S(1)} %get-tuple-element.22), channel_id=1, source_target_pairs={{0,5},{1,4},{2,7},{3,6},{4,1},{5,0},{6,3},{7,2},{8,13},{9,12},{10,... | collective-permute-start | bytes 98312 | tf_op jit(solution)/shard_map/ppermute | solution.py:470
  18.3 4.1 %collective-permute-start.8 = (bf16[16,1024]{1,0:T(8,128)(2,1)S(1)}, bf16[16,1024]{1,0:T(8,128)(2,1)S(1)}, u32[]{:S(2)}, u32[]{:S(2)}) collective-permute-start(bf16[16,1024]{1,0:T(8,128)(2,1)S(1)} %get-tuple-element.22), channel_id=1, source_target_pairs={{0,4},{2,6},{4,0},{6,2},{8,12},{10,14},{12,8},{14,10},{1,5},{3,7},... | collective-permute-start | bytes 98312 | tf_op jit(solution)/shard_map/ppermute | solution.py:176
  19.6 1.4 %collective-permute-start.7 = (bf16[16,768]{1,0:T(8,128)(2,1)S(1)}, bf16[16,768]{1,0:T(8,128)(2,1)S(1)}, u32[]{:S(2)}, u32[]{:S(2)}) collective-permute-start(bf16[16,768]{1,0:T(8,128)(2,1)S(1)} %get-tuple-element.18.keep_ref), channel_id=1, source_target_pairs={{0,1},{1,0},{2,3},{3,2},{4,5},{5,4},{6,7},{7,6},{8,9},{9,8},{10,11... | collective-permute-start | bytes 73736 | tf_op jit(solution)/shard_map/ppermute | solution.py:20

commit v10 on v8

--- a/solution.py
+++ b/solution.py
@@ -176,9 +176,28 @@
     return lax.ppermute(array, "seq", pairs)
 
 
-def place_offsets(shard_count):
-    line = list(range(0, shard_count, SPLIT))
-    return line + [offset + 1 for offset in line]
+FAR = 2 * SPLIT
+NEXT = 1
+THIRD = (NEXT, FAR)
+FOURTH = (FAR, NEXT)
+
+
+def swap_by_core(array, offsets):
+    pairs = [
+        (2 * i + core, 2 * (i ^ offsets[core]) + core)
+        for i in range(lax.axis_size("seq"))
+        for core in range(2)
+    ]
+    return lax.ppermute(array, ("seq", "branch"), pairs)
+
+
+def by_core(first, second):
+    return jnp.where(lax.axis_index("branch") == 0, first, second)
+
+
+def place_offsets():
+    received = [0, SPLIT, SPLIT + FAR, by_core(*THIRD), by_core(*FOURTH)]
+    return received + [offset + NEXT for offset in (SPLIT, SPLIT + FAR, FAR)]
 
 
 def pack_kernel(
@@ -221,7 +240,7 @@
 
     lane = lax.broadcasted_iota(jnp.int32, (1, limits_ref.shape[1]), 1)
     lane_limit = jnp.zeros(lane.shape, jnp.int32)
-    for place, offset in enumerate(place_offsets(shard_count)):
+    for place, offset in enumerate(place_offsets()):
         lane_limit = jnp.where(lane // tok_dev == place, counts_ref[shard ^ offset], lane_limit)
     limits_ref[0:1, :] = (lane % tok_dev < lane_limit).astype(jnp.int32)
     limits_ref[1:2, :] = jnp.full(lane.shape, counts_ref[shard], jnp.int32)
@@ -314,7 +333,7 @@
         keep_ref[:, columns] = kept.astype(jnp.bfloat16)
         message_ref[:, columns] = sent.astype(jnp.bfloat16)
 
-    for place, offset in enumerate(place_offsets(set_count)):
+    for place, offset in enumerate(place_offsets()):
         rows = pl.ds(pl.multiple_of((shard ^ offset) * tok_dev, tok_dev), tok_dev)
         lines_ref[rows, :] = lines[place * tok_dev : (place + 1) * tok_dev]
     table = jnp.transpose(lines_ref[...])[: table_ref.shape[0]]
@@ -451,11 +470,13 @@
         ),
         name="hold",
     )(*distant(out_weight), *held(limits))
-    line = [own] + [
-        swap_shards(other if offset & SPLIT else own, offset)
-        for offset in range(SPLIT, seq_count, SPLIT)
-    ]
-    sets = line + [swap_shards(array, 1) for array in line]
+    near = swap_shards(other, SPLIT)
+    across_line = swap_shards(other, SPLIT + FAR)
+    third = swap_by_core(own, THIRD)
+    fourth = swap_by_core(own, FOURTH)
+    far = by_core(fourth, third)
+    passed_on = [swap_shards(array, NEXT) for array in (near, across_line, far)]
+    sets = [own, near, across_line, third, fourth] + passed_on
     limits, weight_held = lax.optimization_barrier((limits, weight_held))
     keep, message, table = pl.pallas_call(
         functools.partial(attend_kernel, len(sets)),
@@ -502,8 +523,7 @@
 
 def solution(mesh):
     seq_count = mesh.shape["seq"]
-    hypercube = seq_count > SPLIT and seq_count & (seq_count - 1) == 0
-    small = hypercube and seq_count <= HEADS
+    small = seq_count == 2 * FAR
     return jax.shard_map(
         per_device_halves if small else per_device_exchange,
         mesh=mesh,

time: 23.5 us -> 24.4 us (1.038)
  starting transfers between devices: 13.1 us -> 13.8 us
    ppermute x8 -> x6, starting transfers between devices: 12.5 us -> 10.1 us  [swap_shards(): return lax.ppermute(array, 'seq', pairs)]
    ppermute x0 -> x2, starting transfers between devices: none -> 2.27 us  [swap_by_core(): return lax.ppermute(array, ('seq', 'branch'), pairs)]
    ppermute x1, starting transfers between devices: 0.59 us -> 1.37 us  [partner_2(): lax.ppermute(array, axis, [(i, i ^ 1 << stride) for i in range(lax.axis_s...]
    ppermute x0 -> x2, waiting for transfers between devices: none -> 0.73 us  [swap_by_core(): return lax.ppermute(array, ('seq', 'branch'), pairs)]
    ppermute x8 -> x6, waiting for transfers between devices: 3.91 us -> 3.41 us  [swap_shards(): return lax.ppermute(array, 'seq', pairs)]
  transfers between devices with their start and end apart: 10 -> 10, of which waited for: 7 -> 6; matrix products, arithmetic and copies ran while one was open for 0% -> 0% of each run, Pallas kernels for 8% -> 8%
where the time goes in v10:
time: 24.4 us; the launch traced here: 24.1 us
  starting transfers between devices  13.8 us (57%)
  waiting for transfers between devices  5.34 us (22%)
  Pallas kernels  4.3 us (18%)
  between operations  0.69 us (3%)
    ppermute x6, starting transfers between devices, swap_shards(): return lax.ppermute(array, 'seq', pairs)  10.1 us
    ppermute x6, waiting for transfers between devices, swap_shards(): return lax.ppermute(array, 'seq', pairs)  3.41 us
    ppermute x2, starting transfers between devices, swap_by_core(): return lax.ppermute(array, ('seq', 'branch'), pairs)  2.27 us
    pallas_call x1, Pallas kernels, per_device_halves(): pl.pallas_call(hold_kernel, out_shape=pltpu.VMEM(out_weight.shape, jnp.bf...  1.63 us
    ppermute x1, starting transfers between devices, partner_2(): lax.ppermute(array, axis, [(i, i ^ 1 << stride) for i in range(lax.axis_s...  1.37 us
    pallas_call x1, Pallas kernels, per_device_halves(): pl.pallas_call(pack_kernel, out_shape=[pltpu.VMEM((3 * tok_dev, half_widt...  0.92 us
    pallas_call x1, Pallas kernels, per_device_halves(): pl.pallas_call(project_kernel, out_shape=[jax.ShapeDtypeStruct((tok_dev,...  0.91 us
    ppermute x1, waiting for transfers between devices, partner_2(): lax.ppermute(array, axis, [(i, i ^ 1 << stride) for i in range(lax.axis_s...  0.85 us
  transfers between devices with their start and end apart: 10, of which 6 were waited for; matrix products, arithmetic and copies ran while one was open for 0% of the time, Pallas kernels for 8%

profile of v10, /device:TPU:0, one launch (start us, length us, event | category | flops | bytes accessed | tf_op | source)
XLA Modules:
  0.0 24.1 jit_solution(5198592063085141397)
XLA Ops:
  0.6 0.9 %pack.1 = (bf16[48,768]{1,0:T(8,128)(2,1)S(1)}, bf16[48,768]{1,0:T(8,128)(2,1)S(1)}, s32[8,128]{1,0:T(8,128)S(1)}, s32[2,8,128]{2,1,0:T(8,128)S(1)}, s32[2,8,128]{2,1,0:T(8,128)S(1)}) custom-call(bf16[1,16,1536]{2,1,0:T(8,128)(2,1)} %query_hbm.1, bf16[1,16,1536]{2,1,0:T(8,128)(2,1)} %key_hbm.1, bf16[1,16,1536]{2,1,0:T(8,128)(2,1)} %value_hbm.1, ...), custom_call_target="tpu_custom_call" | custom-call | tf_op jit(solution)/shard_map/pack/pallas_call | solution.py:441
  1.6 5.1 %collective-permute-start.1 = (bf16[48,768]{1,0:T(8,128)(2,1)S(1)}, bf16[48,768]{1,0:T(8,128)(2,1)S(1)}, u32[]{:S(2)}, u32[]{:S(2)}) collective-permute-start(bf16[48,768]{1,0:T(8,128)(2,1)S(1)} %get-tuple-element.19), channel_id=1, source_target_pairs={{0,12},{2,14},{4,8},{6,10},{8,4},{10,6},{12,0},{14,2},{1,13},{3,15... | collective-permute-start | bytes 221192 | tf_op jit(solution)/shard_map/ppermute | solution.py:176
  6.7 0.0 collective-permute-start
  6.7 0.6 %collective-permute-start.3 = (bf16[48,768]{1,0:T(8,128)(2,1)S(1)}, bf16[48,768]{1,0:T(8,128)(2,1)S(1)}, u32[]{:S(2)}, u32[]{:S(2)}) collective-permute-start(bf16[48,768]{1,0:T(8,128)(2,1)S(1)} %get-tuple-element.18.refs_0_), channel_id=1, source_target_pairs={{0,8},{1,3},{2,10},{3,1},{4,12},{5,7},{6,14},{7,5},{8,0},{9,11},{1... | collective-permute-start | bytes 221192 | tf_op jit(solution)/shard_map/ppermute | solution.py:191
  7.3 1.6 %collective-permute-start.2 = (bf16[48,768]{1,0:T(8,128)(2,1)S(1)}, bf16[48,768]{1,0:T(8,128)(2,1)S(1)}, u32[]{:S(2)}, u32[]{:S(2)}) collective-permute-start(bf16[48,768]{1,0:T(8,128)(2,1)S(1)} %get-tuple-element.18.refs_0_), channel_id=1, source_target_pairs={{0,2},{1,9},{2,0},{3,11},{4,6},{5,13},{6,4},{7,15},{8,10},{9,1},{1... | collective-permute-start | bytes 221192 | tf_op jit(solution)/shard_map/ppermute | solution.py:191
  9.0 0.9 %collective-permute-done.1.refs_2_ = bf16[48,768]{1,0:T(8,128)(2,1)S(1)} collective-permute-done((bf16[48,768]{1,0:T(8,128)(2,1)S(1)}, bf16[48,768]{1,0:T(8,128)(2,1)S(1)}, u32[]{:S(2)}, u32[]{:S(2)}) %collective-permute-start.1) | collective-permute-done | bytes 73760 | tf_op jit(solution)/shard_map/ppermute | solution.py:176
  9.8 1.5 %collective-permute-start.5 = (bf16[48,768]{1,0:T(8,128)(2,1)S(1)}, bf16[48,768]{1,0:T(8,128)(2,1)S(1)}, u32[]{:S(2)}, u32[]{:S(2)}) collective-permute-start(bf16[48,768]{1,0:T(8,128)(2,1)S(1)} %collective-permute-done.1.refs_2_), channel_id=1, source_target_pairs={{0,2},{2,0},{4,6},{6,4},{8,10},{10,8},{12,14},{14,12},{1,3},{3,1},... | collective-permute-start | bytes 221192 | tf_op jit(solution)/shard_map/ppermute | solution.py:176
  11.3 0.0 collective-permute-done.refs_1_
  11.3 2.1 %collective-permute-start.4 = (bf16[48,768]{1,0:T(8,128)(2,1)S(1)}, bf16[48,768]{1,0:T(8,128)(2,1)S(1)}, u32[]{:S(2)}, u32[]{:S(2)}) collective-permute-start(bf16[48,768]{1,0:T(8,128)(2,1)S(1)} %collective-permute-done.refs_1_), channel_id=1, source_target_pairs={{0,2},{2,0},{4,6},{6,4},{8,10},{10,8},{12,14},{14,12},{1,3},{3,1},... | collective-permute-start | bytes 221192 | tf_op jit(solution)/shard_map/ppermute | solution.py:176
  13.4 0.7 %collective-permute-done.3.refs_4_ = bf16[48,768]{1,0:T(8,128)(2,1)S(1)} collective-permute-done((bf16[48,768]{1,0:T(8,128)(2,1)S(1)}, bf16[48,768]{1,0:T(8,128)(2,1)S(1)}, u32[]{:S(2)}, u32[]{:S(2)}) %collective-permute-start.3) | collective-permute-done | bytes 73760 | tf_op jit(solution)/shard_map/ppermute | solution.py:191
  14.1 0.0 collective-permute-done.2.refs_3_
  14.1 0.9 %collective-permute-start.6 = (bf16[48,768]{1,0:T(8,128)(2,1)S(1)}, bf16[48,768]{1,0:T(8,128)(2,1)S(1)}, u32[]{:S(2)}, u32[]{:S(2)}) collective-permute-start(bf16[48,768]{1,0:T(8,128)(2,1)S(1)} %broadcast_select_fusion), channel_id=1, source_target_pairs={{0,2},{2,0},{4,6},{6,4},{8,10},{10,8},{12,14},{14,12},{1,3},{3,1},... | collective-permute-start | bytes 221192 | tf_op jit(solution)/shard_map/ppermute | solution.py:176
  15.1 1.6 %hold.1.weight_ref = bf16[1536,768]{1,0:T(8,128)(2,1)S(1)} custom-call(bf16[1536,768]{1,0:T(8,128)(2,1)} %weight_hbm.1, s32[8,128]{1,0:T(8,128)S(1)} %get-tuple-element.17.after_ref.limits_ref), custom_call_target="tpu_custom_call" | custom-call | bytes 4718592 | tf_op jit(solution)/shard_map/hold/pallas_call | solution.py:461
  16.7 0.0 collective-permute-done.5.refs_6_
  16.7 0.0 collective-permute-done.4.refs_5_
  16.7 1.8 %collective-permute-done.6.refs_7_ = bf16[48,768]{1,0:T(8,128)(2,1)S(1)} collective-permute-done((bf16[48,768]{1,0:T(8,128)(2,1)S(1)}, bf16[48,768]{1,0:T(8,128)(2,1)S(1)}, u32[]{:S(2)}, u32[]{:S(2)}) %collective-permute-start.6) | collective-permute-done | bytes 73760 | tf_op jit(solution)/shard_map/ppermute | solution.py:176
  18.6 0.6 %attend.1 = (bf16[16,768]{1,0:T(8,128)(2,1)S(1)}, bf16[16,1024]{1,0:T(8,128)(2,1)S(1)}, f32[8,128]{1,0:T(8,128)S(1)}) custom-call(s32[8,128]{1,0:T(8,128)S(1)} %get-tuple-element.17.after_ref.limits_ref, bf16[48,768]{1,0:T(8,128)(2,1)S(1)} %get-tuple-element.18.refs_0_, bf16[48,768]{1,0:T(8,128)(2,1)S(1)} %collective-permute-done.refs_1_, ...), custom_call_target="tpu_custom_call" | custom-call | tf_op jit(solution)/shard_map/attend/pallas_call | solution.py:481
  19.1 0.1 collective-permute-start.9
  19.2 0.5 %collective-permute-start.8 = (bf16[16,1024]{1,0:T(8,128)(2,1)S(1)}, bf16[16,1024]{1,0:T(8,128)(2,1)S(1)}, u32[]{:S(2)}, u32[]{:S(2)}) collective-permute-start(bf16[16,1024]{1,0:T(8,128)(2,1)S(1)} %get-tuple-element.24), channel_id=1, source_target_pairs={{0,4},{2,6},{4,0},{6,2},{8,12},{10,14},{12,8},{14,10},{1,5},{3,7},... | collective-permute-start | bytes 98312 | tf_op jit(solution)/shard_map/ppermute | solution.py:176
  19.7 1.4 %collective-permute-start.7 = (bf16[16,768]{1,0:T(8,128)(2,1)S(1)}, bf16[16,768]{1,0:T(8,128)(2,1)S(1)}, u32[]{:S(2)}, u32[]{:S(2)}) collective-permute-start(bf16[16,768]{1,0:T(8,128)(2,1)S(1)} %get-tuple-element.20.keep_ref), channel_id=1, source_target_pairs={{0,1},{1,0},{2,3},{3,2},{4,5},{5,4},{6,7},{7,6},{8,9},{9,8},{10,11... | collective-permute-start | bytes 73736 | tf_op jit(solution)/shard_map/ppermute | solution.py:20
  21.1 0.8 %collective-permute-done.7.partner_keep_ref = bf16[16,768]{1,0:T(8,128)(2,1)S(1)} collective-permute-done((bf16[16,768]{1,0:T(8,128)(2,1)S(1)}, bf16[16,768]{1,0:T(8,128)(2,1)S(1)}, u32[]{:S(2)}, u32[]{:S(2)}) %collective-permute-start.7) | collective-permute-done | bytes 24608 | tf_op jit(solution)/shard_map/ppermute | solution.py:20
  21.9 0.3 %keep.1 = (f32[16,768]{1,0:T(8,128)S(1)}, f32[16,128]{1,0:T(8,128)S(1)}) custom-call(bf16[16,768]{1,0:T(8,128)(2,1)S(1)} %get-tuple-element.20.keep_ref, bf16[16,768]{1,0:T(8,128)(2,1)S(1)} %collective-permute-done.7.partner_keep_ref, bf16[1536,768]{1,0:T(8,128)(2,1)S(1)} %hold.1.weight_ref), custom_call_target="tpu_custom_call" | custom-call | tf_op jit(solution)/shard_map/keep/pallas_call | solution.py:498
  22.2 0.3 %collective-permute-done.9.partner_back_ref = bf16[16,1024]{1,0:T(8,128)(2,1)S(1)} collective-permute-done((bf16[16,1024]{1,0:T(8,128)(2,1)S(1)}, bf16[16,1024]{1,0:T(8,128)(2,1)S(1)}, u32[]{:S(2)}, u32[]{:S(2)}) %collective-permute-start.9) | collective-permute-done | bytes 32800 | tf_op jit(solution)/shard_map/ppermute | solution.py:495
  22.5 0.7 %collective-permute-done.8.message_ref = bf16[16,1024]{1,0:T(8,128)(2,1)S(1)} collective-permute-done((bf16[16,1024]{1,0:T(8,128)(2,1)S(1)}, bf16[16,1024]{1,0:T(8,128)(2,1)S(1)}, u32[]{:S(2)}, u32[]{:S(2)}) %collective-permute-start.8) | collective-permute-done | bytes 32800 | tf_op jit(solution)/shard_map/ppermute | solution.py:176
  23.2 0.9 %project.1 = (bf16[16,768]{1,0:T(8,128)(2,1)}, f32[2,8,16]{2,1,0:T(8,128)}) custom-call(f32[16,768]{1,0:T(8,128)S(1)} %get-tuple-element.22.total_ref, f32[16,128]{1,0:T(8,128)S(1)} %get-tuple-element.23.size_ref, bf16[16,1024]{1,0:T(8,128)(2,1)S(1)} %collective-permute-done.8.message_ref, bf16[16,1024]{1,0:T(8,128)(2,1)S(1)} %collective-permute-done.9.partner_back_ref, ...), custom_call_target="tpu_custom_call" | custom-call | tf_op jit(solution)/shard_map/project/pallas_call | solution.py:509
  (1 shorter events, 0.0 us)
Async XLA Ops:
  1.6 8.3 %collective-permute-start.1 = (bf16[48,768]{1,0:T(8,128)(2,1)S(1)}, bf16[48,768]{1,0:T(8,128)(2,1)S(1)}, u32[]{:S(2)}, u32[]{:S(2)}) collective-permute-start(bf16[48,768]{1,0:T(8,128)(2,1)S(1)} %get-tuple-element.19), channel_id=1, source_target_pairs={{0,12},{2,14},{4,8},{6,10},{8,4},{10,6},{12,0},{14,2},{1,13},{3,15... | collective-permute-start | bytes 221192 | tf_op jit(solution)/shard_map/ppermute | solution.py:176
  6.7 4.7 %collective-permute-start = (bf16[48,768]{1,0:T(8,128)(2,1)S(1)}, bf16[48,768]{1,0:T(8,128)(2,1)S(1)}, u32[]{:S(2)}, u32[]{:S(2)}) collective-permute-start(bf16[48,768]{1,0:T(8,128)(2,1)S(1)} %get-tuple-element.19), channel_id=1, source_target_pairs={{0,4},{2,6},{4,0},{6,2},{8,12},{10,14},{12,8},{14,10},{1,5},{3,7},... | collective-permute-start | bytes 221192 | tf_op jit(solution)/shard_map/ppermute | solution.py:176
  6.7 7.5 %collective-permute-start.3 = (bf16[48,768]{1,0:T(8,128)(2,1)S(1)}, bf16[48,768]{1,0:T(8,128)(2,1)S(1)}, u32[]{:S(2)}, u32[]{:S(2)}) collective-permute-start(bf16[48,768]{1,0:T(8,128)(2,1)S(1)} %get-tuple-element.18.refs_0_), channel_id=1, source_target_pairs={{0,8},{1,3},{2,10},{3,1},{4,12},{5,7},{6,14},{7,5},{8,0},{9,11},{1... | collective-permute-start | bytes 221192 | tf_op jit(solution)/shard_map/ppermute | solution.py:191
  7.3 6.8 %collective-permute-start.2 = (bf16[48,768]{1,0:T(8,128)(2,1)S(1)}, bf16[48,768]{1,0:T(8,128)(2,1)S(1)}, u32[]{:S(2)}, u32[]{:S(2)}) collective-permute-start(bf16[48,768]{1,0:T(8,128)(2,1)S(1)} %get-tuple-element.18.refs_0_), channel_id=1, source_target_pairs={{0,2},{1,9},{2,0},{3,11},{4,6},{5,13},{6,4},{7,15},{8,10},{9,1},{1... | collective-permute-start | bytes 221192 | tf_op jit(solution)/shard_map/ppermute | solution.py:191
  9.8 6.9 %collective-permute-start.5 = (bf16[48,768]{1,0:T(8,128)(2,1)S(1)}, bf16[48,768]{1,0:T(8,128)(2,1)S(1)}, u32[]{:S(2)}, u32[]{:S(2)}) collective-permute-start(bf16[48,768]{1,0:T(8,128)(2,1)S(1)} %collective-permute-done.1.refs_2_), channel_id=1, source_target_pairs={{0,2},{2,0},{4,6},{6,4},{8,10},{10,8},{12,14},{14,12},{1,3},{3,1},... | collective-permute-start | bytes 221192 | tf_op jit(solution)/shard_map/ppermute | solution.py:176
  11.3 5.4 %collective-permute-start.4 = (bf16[48,768]{1,0:T(8,128)(2,1)S(1)}, bf16[48,768]{1,0:T(8,128)(2,1)S(1)}, u32[]{:S(2)}, u32[]{:S(2)}) collective-permute-start(bf16[48,768]{1,0:T(8,128)(2,1)S(1)} %collective-permute-done.refs_1_), channel_id=1, source_target_pairs={{0,2},{2,0},{4,6},{6,4},{8,10},{10,8},{12,14},{14,12},{1,3},{3,1},... | collective-permute-start | bytes 221192 | tf_op jit(solution)/shard_map/ppermute | solution.py:176
  14.1 4.4 %collective-permute-start.6 = (bf16[48,768]{1,0:T(8,128)(2,1)S(1)}, bf16[48,768]{1,0:T(8,128)(2,1)S(1)}, u32[]{:S(2)}, u32[]{:S(2)}) collective-permute-start(bf16[48,768]{1,0:T(8,128)(2,1)S(1)} %broadcast_select_fusion), channel_id=1, source_target_pairs={{0,2},{2,0},{4,6},{6,4},{8,10},{10,8},{12,14},{14,12},{1,3},{3,1},... | collective-permute-start | bytes 221192 | tf_op jit(solution)/shard_map/ppermute | solution.py:176
  19.1 3.4 %collective-permute-start.9 = (bf16[16,1024]{1,0:T(8,128)(2,1)S(1)}, bf16[16,1024]{1,0:T(8,128)(2,1)S(1)}, u32[]{:S(2)}, u32[]{:S(2)}) collective-permute-start(bf16[16,1024]{1,0:T(8,128)(2,1)S(1)} %get-tuple-element.24), channel_id=1, source_target_pairs={{0,5},{1,4},{2,7},{3,6},{4,1},{5,0},{6,3},{7,2},{8,13},{9,12},{10,... | collective-permute-start | bytes 98312 | tf_op jit(solution)/shard_map/ppermute | solution.py:495
  19.2 4.0 %collective-permute-start.8 = (bf16[16,1024]{1,0:T(8,128)(2,1)S(1)}, bf16[16,1024]{1,0:T(8,128)(2,1)S(1)}, u32[]{:S(2)}, u32[]{:S(2)}) collective-permute-start(bf16[16,1024]{1,0:T(8,128)(2,1)S(1)} %get-tuple-element.24), channel_id=1, source_target_pairs={{0,4},{2,6},{4,0},{6,2},{8,12},{10,14},{12,8},{14,10},{1,5},{3,7},... | collective-permute-start | bytes 98312 | tf_op jit(solution)/shard_map/ppermute | solution.py:176
  19.7 2.2 %collective-permute-start.7 = (bf16[16,768]{1,0:T(8,128)(2,1)S(1)}, bf16[16,768]{1,0:T(8,128)(2,1)S(1)}, u32[]{:S(2)}, u32[]{:S(2)}) collective-permute-start(bf16[16,768]{1,0:T(8,128)(2,1)S(1)} %get-tuple-element.20.keep_ref), channel_id=1, source_target_pairs={{0,1},{1,0},{2,3},{3,2},{4,5},{5,4},{6,7},{7,6},{8,9},{9,8},{10,11... | collective-permute-start | bytes 73736 | tf_op jit(solution)/shard_map/ppermute | solution.py:20

commit v11 on v8

--- a/solution.py
+++ b/solution.py
@@ -166,6 +166,7 @@
 
 
 SPLIT = 2
+SET_ORDER = (0, 3, 2, 1, 4, 7, 6, 5)
 HOLD_COPIES = 4
 TABLE_PIECES = 3
 SPLITTER = 65537.0
@@ -189,6 +190,8 @@
     head_hbm,
     own_ref,
     other_ref,
+    own_copy_ref,
+    other_copy_ref,
     limits_ref,
     pick_ref,
     slot_head_ref,
@@ -205,7 +208,7 @@
         pltpu.make_async_copy(counts_hbm, counts_ref, copy_sems.at[0]),
         pltpu.make_async_copy(head_hbm, head_ref, copy_sems.at[1]),
     ]
-    for target, place in ((other_ref, 1 - half), (own_ref, half)):
+    for target, place in ((other_ref, 1 - half), (own_ref, half), (own_copy_ref, half), (other_copy_ref, 1 - half)):
         columns = pl.ds(pl.multiple_of(place * half_width, half_width), half_width)
         for part, source in enumerate((key_hbm, value_hbm, query_hbm)):
             rows = pl.ds(part * tok_dev, tok_dev)
@@ -281,7 +284,7 @@
 
 
 def attend_kernel(set_count, limits_ref, *refs):
-    set_refs = refs[:set_count]
+    set_refs = [refs[SET_ORDER.index(i)] for i in range(set_count)]
     keep_ref, message_ref, table_ref, lines_ref = refs[set_count:]
     tok_dev, half_width = keep_ref.shape
     half_heads = half_width // HDIM
@@ -419,9 +422,11 @@
     def distant(*arrays):
         return [pltpu.with_memory_space_constraint(array, pltpu.HBM) for array in arrays]
 
-    own, other, limits, pick, slot_head = pl.pallas_call(
+    own, other, own_copy, other_copy, limits, pick, slot_head = pl.pallas_call(
         pack_kernel,
         out_shape=[
+            pltpu.VMEM((3 * tok_dev, half_width), jnp.bfloat16),
+            pltpu.VMEM((3 * tok_dev, half_width), jnp.bfloat16),
             pltpu.VMEM((3 * tok_dev, half_width), jnp.bfloat16),
             pltpu.VMEM((3 * tok_dev, half_width), jnp.bfloat16),
             pltpu.VMEM((8, tokens), jnp.int32),
@@ -429,11 +434,11 @@
             pltpu.VMEM((slot_count, 8, tokens), jnp.int32),
         ],
         in_specs=[any_spec] * 5,
-        out_specs=[vmem] * 5,
+        out_specs=[vmem] * 7,
         scratch_shapes=[
             pltpu.SMEM((seq_count,), jnp.int32),
             pltpu.SMEM((slot_count, seq_count), jnp.int32),
-            pltpu.SemaphoreType.DMA((8,)),
+            pltpu.SemaphoreType.DMA((14,)),
         ],
         compiler_params=KERNEL_PARAMS,
         name="pack",
@@ -452,10 +457,11 @@
         name="hold",
     )(*distant(out_weight), *held(limits))
     line = [own] + [
-        swap_shards(other if offset & SPLIT else own, offset)
+        swap_shards({4: own_copy, 6: other_copy}.get(offset, other if offset & SPLIT else own), offset)
         for offset in range(SPLIT, seq_count, SPLIT)
     ]
     sets = line + [swap_shards(array, 1) for array in line]
+    sets = [sets[i] for i in SET_ORDER]
     limits, weight_held = lax.optimization_barrier((limits, weight_held))
     keep, message, table = pl.pallas_call(
         functools.partial(attend_kernel, len(sets)),

time: 23.5 us -> 24.7 us (1.051)
  waiting for transfers between devices: 5.2 us -> 6.15 us
    ppermute x8, waiting for transfers between devices: 3.91 us -> 4.95 us  [swap_shards(): return lax.ppermute(array, 'seq', pairs)]
    ppermute x1, starting transfers between devices: 0.59 us -> 1.03 us  [partner_2(): lax.ppermute(array, axis, [(i, i ^ 1 << stride) for i in range(lax.axis_s...]
    ppermute x8, starting transfers between devices: 12.5 us -> 12.1 us  [swap_shards(): return lax.ppermute(array, 'seq', pairs)]
where the time goes in v11:
time: 24.7 us; the launch traced here: 24.5 us
  starting transfers between devices  13.2 us (53%)
  waiting for transfers between devices  6.15 us (25%)
  Pallas kernels  4.47 us (18%)
  between operations  0.69 us (3%)
    ppermute x8, starting transfers between devices, swap_shards(): return lax.ppermute(array, 'seq', pairs)  12.1 us
    ppermute x8, waiting for transfers between devices, swap_shards(): return lax.ppermute(array, 'seq', pairs)  4.95 us
    pallas_call x1, Pallas kernels, per_device_halves(): pl.pallas_call(hold_kernel, out_shape=pltpu.VMEM(out_weight.shape, jnp.bf...  1.63 us
    pallas_call x1, Pallas kernels, per_device_halves(): pl.pallas_call(pack_kernel, out_shape=[pltpu.VMEM((3 * tok_dev, half_widt...  1.09 us
    ppermute x1, starting transfers between devices, partner_2(): lax.ppermute(array, axis, [(i, i ^ 1 << stride) for i in range(lax.axis_s...  1.03 us
    pallas_call x1, Pallas kernels, per_device_halves(): pl.pallas_call(project_kernel, out_shape=[jax.ShapeDtypeStruct((tok_dev,...  0.91 us
    ppermute x1, waiting for transfers between devices, partner_2(): lax.ppermute(array, axis, [(i, i ^ 1 << stride) for i in range(lax.axis_s...  0.85 us
    pallas_call x1, Pallas kernels, per_device_halves(): pl.pallas_call(functools.partial(attend_kernel, len(sets)), out_shape=[pl...  0.56 us
  transfers between devices with their start and end apart: 10, of which 7 were waited for; matrix products, arithmetic and copies ran while one was open for 0% of the time, Pallas kernels for 8%

profile of v11, /device:TPU:0, one launch (start us, length us, event | category | flops | bytes accessed | tf_op | source)
XLA Modules:
  0.0 24.5 jit_solution(1336185152405175423)
XLA Ops:
  0.6 1.1 %pack.1 = (bf16[48,768]{1,0:T(8,128)(2,1)S(1)}, bf16[48,768]{1,0:T(8,128)(2,1)S(1)}, bf16[48,768]{1,0:T(8,128)(2,1)S(1)}, bf16[48,768]{1,0:T(8,128)(2,1)S(1)}, s...) custom-call(bf16[1,16,1536]{2,1,0:T(8,128)(2,1)} %query_hbm.1, ...), custom_call_target="tpu_custom_call" | custom-call | tf_op jit(solution)/shard_map/pack/pallas_call | solution.py:425
  1.7 5.1 %collective-permute-start = (bf16[48,768]{1,0:T(8,128)(2,1)S(1)}, bf16[48,768]{1,0:T(8,128)(2,1)S(1)}, u32[]{:S(2)}, u32[]{:S(2)}) collective-permute-start(bf16[48,768]{1,0:T(8,128)(2,1)S(1)} %get-tuple-element.21), channel_id=1, source_target_pairs={{0,12},{2,14},{4,8},{6,10},{8,4},{10,6},{12,0},{14,2},{1,13},{3,15... | collective-permute-start | bytes 221192 | tf_op jit(solution)/shard_map/ppermute | solution.py:177
  6.8 0.0 collective-permute-start.1
  6.8 0.6 %collective-permute-start.2 = (bf16[48,768]{1,0:T(8,128)(2,1)S(1)}, bf16[48,768]{1,0:T(8,128)(2,1)S(1)}, u32[]{:S(2)}, u32[]{:S(2)}) collective-permute-start(bf16[48,768]{1,0:T(8,128)(2,1)S(1)} %get-tuple-element.23), channel_id=1, source_target_pairs={{0,4},{2,6},{4,0},{6,2},{8,12},{10,14},{12,8},{14,10},{1,5},{3,7},... | collective-permute-start | bytes 221192 | tf_op jit(solution)/shard_map/ppermute | solution.py:177
  7.5 1.6 %collective-permute-start.3 = (bf16[48,768]{1,0:T(8,128)(2,1)S(1)}, bf16[48,768]{1,0:T(8,128)(2,1)S(1)}, u32[]{:S(2)}, u32[]{:S(2)}) collective-permute-start(bf16[48,768]{1,0:T(8,128)(2,1)S(1)} %get-tuple-element.20.refs_0_), channel_id=1, source_target_pairs={{0,2},{2,0},{4,6},{6,4},{8,10},{10,8},{12,14},{14,12},{1,3},{3,1},... | collective-permute-start | bytes 221192 | tf_op jit(solution)/shard_map/ppermute | solution.py:177
  9.1 0.5 %collective-permute-done.refs_1_ = bf16[48,768]{1,0:T(8,128)(2,1)S(1)} collective-permute-done((bf16[48,768]{1,0:T(8,128)(2,1)S(1)}, bf16[48,768]{1,0:T(8,128)(2,1)S(1)}, u32[]{:S(2)}, u32[]{:S(2)}) %collective-permute-start) | collective-permute-done | bytes 73760 | tf_op jit(solution)/shard_map/ppermute | solution.py:177
  9.6 1.9 %collective-permute-start.4 = (bf16[48,768]{1,0:T(8,128)(2,1)S(1)}, bf16[48,768]{1,0:T(8,128)(2,1)S(1)}, u32[]{:S(2)}, u32[]{:S(2)}) collective-permute-start(bf16[48,768]{1,0:T(8,128)(2,1)S(1)} %collective-permute-done.refs_1_), channel_id=1, source_target_pairs={{0,2},{2,0},{4,6},{6,4},{8,10},{10,8},{12,14},{14,12},{1,3},{3,1},... | collective-permute-start | bytes 221192 | tf_op jit(solution)/shard_map/ppermute | solution.py:177
  11.5 1.6 %collective-permute-done.1.refs_2_ = bf16[48,768]{1,0:T(8,128)(2,1)S(1)} collective-permute-done((bf16[48,768]{1,0:T(8,128)(2,1)S(1)}, bf16[48,768]{1,0:T(8,128)(2,1)S(1)}, u32[]{:S(2)}, u32[]{:S(2)}) %collective-permute-start.1) | collective-permute-done | bytes 73760 | tf_op jit(solution)/shard_map/ppermute | solution.py:177
  13.1 1.5 %collective-permute-start.5 = (bf16[48,768]{1,0:T(8,128)(2,1)S(1)}, bf16[48,768]{1,0:T(8,128)(2,1)S(1)}, u32[]{:S(2)}, u32[]{:S(2)}) collective-permute-start(bf16[48,768]{1,0:T(8,128)(2,1)S(1)} %collective-permute-done.1.refs_2_), channel_id=1, source_target_pairs={{0,2},{2,0},{4,6},{6,4},{8,10},{10,8},{12,14},{14,12},{1,3},{3,1},... | collective-permute-start | bytes 221192 | tf_op jit(solution)/shard_map/ppermute | solution.py:177
  14.6 0.0 collective-permute-done.2.refs_3_
  14.6 0.5 %collective-permute-start.6 = (bf16[48,768]{1,0:T(8,128)(2,1)S(1)}, bf16[48,768]{1,0:T(8,128)(2,1)S(1)}, u32[]{:S(2)}, u32[]{:S(2)}) collective-permute-start(bf16[48,768]{1,0:T(8,128)(2,1)S(1)} %collective-permute-done.2.refs_3_), channel_id=1, source_target_pairs={{0,2},{2,0},{4,6},{6,4},{8,10},{10,8},{12,14},{14,12},{1,3},{3,1},... | collective-permute-start | bytes 221192 | tf_op jit(solution)/shard_map/ppermute | solution.py:177
  15.1 1.6 %hold.1.weight_ref = bf16[1536,768]{1,0:T(8,128)(2,1)S(1)} custom-call(bf16[1536,768]{1,0:T(8,128)(2,1)} %weight_hbm.1, s32[8,128]{1,0:T(8,128)S(1)} %get-tuple-element.19.after_ref.limits_ref), custom_call_target="tpu_custom_call" | custom-call | bytes 4718592 | tf_op jit(solution)/shard_map/hold/pallas_call | solution.py:447
  16.7 0.0 collective-permute-done.3.refs_4_
  16.7 0.0 collective-permute-done.4.refs_5_
  16.8 1.4 %collective-permute-done.5.refs_6_ = bf16[48,768]{1,0:T(8,128)(2,1)S(1)} collective-permute-done((bf16[48,768]{1,0:T(8,128)(2,1)S(1)}, bf16[48,768]{1,0:T(8,128)(2,1)S(1)}, u32[]{:S(2)}, u32[]{:S(2)}) %collective-permute-start.5) | collective-permute-done | bytes 73760 | tf_op jit(solution)/shard_map/ppermute | solution.py:177
  18.1 0.8 %collective-permute-done.6.refs_7_ = bf16[48,768]{1,0:T(8,128)(2,1)S(1)} collective-permute-done((bf16[48,768]{1,0:T(8,128)(2,1)S(1)}, bf16[48,768]{1,0:T(8,128)(2,1)S(1)}, u32[]{:S(2)}, u32[]{:S(2)}) %collective-permute-start.6) | collective-permute-done | bytes 73760 | tf_op jit(solution)/shard_map/ppermute | solution.py:177
  18.9 0.6 %attend.1 = (bf16[16,768]{1,0:T(8,128)(2,1)S(1)}, bf16[16,1024]{1,0:T(8,128)(2,1)S(1)}, f32[8,128]{1,0:T(8,128)S(1)}) custom-call(s32[8,128]{1,0:T(8,128)S(1)} %get-tuple-element.19.after_ref.limits_ref, bf16[48,768]{1,0:T(8,128)(2,1)S(1)} %get-tuple-element.20.refs_0_, bf16[48,768]{1,0:T(8,128)(2,1)S(1)} %collective-permute-done.refs_1_, ...), custom_call_target="tpu_custom_call" | custom-call | tf_op jit(solution)/shard_map/attend/pallas_call | solution.py:466
  19.5 0.1 collective-permute-start.9
  19.6 0.8 %collective-permute-start.8 = (bf16[16,1024]{1,0:T(8,128)(2,1)S(1)}, bf16[16,1024]{1,0:T(8,128)(2,1)S(1)}, u32[]{:S(2)}, u32[]{:S(2)}) collective-permute-start(bf16[16,1024]{1,0:T(8,128)(2,1)S(1)} %get-tuple-element.28), channel_id=1, source_target_pairs={{0,4},{2,6},{4,0},{6,2},{8,12},{10,14},{12,8},{14,10},{1,5},{3,7},... | collective-permute-start | bytes 98312 | tf_op jit(solution)/shard_map/ppermute | solution.py:177
  20.4 1.0 %collective-permute-start.7 = (bf16[16,768]{1,0:T(8,128)(2,1)S(1)}, bf16[16,768]{1,0:T(8,128)(2,1)S(1)}, u32[]{:S(2)}, u32[]{:S(2)}) collective-permute-start(bf16[16,768]{1,0:T(8,128)(2,1)S(1)} %get-tuple-element.24.keep_ref), channel_id=1, source_target_pairs={{0,1},{1,0},{2,3},{3,2},{4,5},{5,4},{6,7},{7,6},{8,9},{9,8},{10,11... | collective-permute-start | bytes 73736 | tf_op jit(solution)/shard_map/ppermute | solution.py:20
  21.4 0.8 %collective-permute-done.7.partner_keep_ref = bf16[16,768]{1,0:T(8,128)(2,1)S(1)} collective-permute-done((bf16[16,768]{1,0:T(8,128)(2,1)S(1)}, bf16[16,768]{1,0:T(8,128)(2,1)S(1)}, u32[]{:S(2)}, u32[]{:S(2)}) %collective-permute-start.7) | collective-permute-done | bytes 24608 | tf_op jit(solution)/shard_map/ppermute | solution.py:20
  22.3 0.3 %keep.1 = (f32[16,768]{1,0:T(8,128)S(1)}, f32[16,128]{1,0:T(8,128)S(1)}) custom-call(bf16[16,768]{1,0:T(8,128)(2,1)S(1)} %get-tuple-element.24.keep_ref, bf16[16,768]{1,0:T(8,128)(2,1)S(1)} %collective-permute-done.7.partner_keep_ref, bf16[1536,768]{1,0:T(8,128)(2,1)S(1)} %hold.1.weight_ref), custom_call_target="tpu_custom_call" | custom-call | tf_op jit(solution)/shard_map/keep/pallas_call | solution.py:483
  22.5 0.3 %collective-permute-done.9.partner_back_ref = bf16[16,1024]{1,0:T(8,128)(2,1)S(1)} collective-permute-done((bf16[16,1024]{1,0:T(8,128)(2,1)S(1)}, bf16[16,1024]{1,0:T(8,128)(2,1)S(1)}, u32[]{:S(2)}, u32[]{:S(2)}) %collective-permute-start.9) | collective-permute-done | bytes 32800 | tf_op jit(solution)/shard_map/ppermute | solution.py:480
  22.9 0.7 %collective-permute-done.8.message_ref = bf16[16,1024]{1,0:T(8,128)(2,1)S(1)} collective-permute-done((bf16[16,1024]{1,0:T(8,128)(2,1)S(1)}, bf16[16,1024]{1,0:T(8,128)(2,1)S(1)}, u32[]{:S(2)}, u32[]{:S(2)}) %collective-permute-start.8) | collective-permute-done | bytes 32800 | tf_op jit(solution)/shard_map/ppermute | solution.py:177
  23.6 0.9 %project.1 = (bf16[16,768]{1,0:T(8,128)(2,1)}, f32[2,8,16]{2,1,0:T(8,128)}) custom-call(f32[16,768]{1,0:T(8,128)S(1)} %get-tuple-element.26.total_ref, f32[16,128]{1,0:T(8,128)S(1)} %get-tuple-element.27.size_ref, bf16[16,1024]{1,0:T(8,128)(2,1)S(1)} %collective-permute-done.8.message_ref, bf16[16,1024]{1,0:T(8,128)(2,1)S(1)} %collective-permute-done.9.partner_back_ref, ...), custom_call_target="tpu_custom_call" | custom-call | tf_op jit(solution)/shard_map/project/pallas_call | solution.py:494
Async XLA Ops:
  1.7 7.9 %collective-permute-start = (bf16[48,768]{1,0:T(8,128)(2,1)S(1)}, bf16[48,768]{1,0:T(8,128)(2,1)S(1)}, u32[]{:S(2)}, u32[]{:S(2)}) collective-permute-start(bf16[48,768]{1,0:T(8,128)(2,1)S(1)} %get-tuple-element.21), channel_id=1, source_target_pairs={{0,12},{2,14},{4,8},{6,10},{8,4},{10,6},{12,0},{14,2},{1,13},{3,15... | collective-permute-start | bytes 221192 | tf_op jit(solution)/shard_map/ppermute | solution.py:177
  6.8 6.2 %collective-permute-start.1 = (bf16[48,768]{1,0:T(8,128)(2,1)S(1)}, bf16[48,768]{1,0:T(8,128)(2,1)S(1)}, u32[]{:S(2)}, u32[]{:S(2)}) collective-permute-start(bf16[48,768]{1,0:T(8,128)(2,1)S(1)} %get-tuple-element.22), channel_id=1, source_target_pairs={{0,8},{2,10},{4,12},{6,14},{8,0},{10,2},{12,4},{14,6},{1,9},{3,11}... | collective-permute-start | bytes 221192 | tf_op jit(solution)/shard_map/ppermute | solution.py:177
  6.8 7.7 %collective-permute-start.2 = (bf16[48,768]{1,0:T(8,128)(2,1)S(1)}, bf16[48,768]{1,0:T(8,128)(2,1)S(1)}, u32[]{:S(2)}, u32[]{:S(2)}) collective-permute-start(bf16[48,768]{1,0:T(8,128)(2,1)S(1)} %get-tuple-element.23), channel_id=1, source_target_pairs={{0,4},{2,6},{4,0},{6,2},{8,12},{10,14},{12,8},{14,10},{1,5},{3,7},... | collective-permute-start | bytes 221192 | tf_op jit(solution)/shard_map/ppermute | solution.py:177
  7.5 9.2 %collective-permute-start.3 = (bf16[48,768]{1,0:T(8,128)(2,1)S(1)}, bf16[48,768]{1,0:T(8,128)(2,1)S(1)}, u32[]{:S(2)}, u32[]{:S(2)}) collective-permute-start(bf16[48,768]{1,0:T(8,128)(2,1)S(1)} %get-tuple-element.20.refs_0_), channel_id=1, source_target_pairs={{0,2},{2,0},{4,6},{6,4},{8,10},{10,8},{12,14},{14,12},{1,3},{3,1},... | collective-permute-start | bytes 221192 | tf_op jit(solution)/shard_map/ppermute | solution.py:177
  9.6 7.1 %collective-permute-start.4 = (bf16[48,768]{1,0:T(8,128)(2,1)S(1)}, bf16[48,768]{1,0:T(8,128)(2,1)S(1)}, u32[]{:S(2)}, u32[]{:S(2)}) collective-permute-start(bf16[48,768]{1,0:T(8,128)(2,1)S(1)} %collective-permute-done.refs_1_), channel_id=1, source_target_pairs={{0,2},{2,0},{4,6},{6,4},{8,10},{10,8},{12,14},{14,12},{1,3},{3,1},... | collective-permute-start | bytes 221192 | tf_op jit(solution)/shard_map/ppermute | solution.py:177
  13.1 5.0 %collective-permute-start.5 = (bf16[48,768]{1,0:T(8,128)(2,1)S(1)}, bf16[48,768]{1,0:T(8,128)(2,1)S(1)}, u32[]{:S(2)}, u32[]{:S(2)}) collective-permute-start(bf16[48,768]{1,0:T(8,128)(2,1)S(1)} %collective-permute-done.1.refs_2_), channel_id=1, source_target_pairs={{0,2},{2,0},{4,6},{6,4},{8,10},{10,8},{12,14},{14,12},{1,3},{3,1},... | collective-permute-start | bytes 221192 | tf_op jit(solution)/shard_map/ppermute | solution.py:177
  14.6 4.4 %collective-permute-start.6 = (bf16[48,768]{1,0:T(8,128)(2,1)S(1)}, bf16[48,768]{1,0:T(8,128)(2,1)S(1)}, u32[]{:S(2)}, u32[]{:S(2)}) collective-permute-start(bf16[48,768]{1,0:T(8,128)(2,1)S(1)} %collective-permute-done.2.refs_3_), channel_id=1, source_target_pairs={{0,2},{2,0},{4,6},{6,4},{8,10},{10,8},{12,14},{14,12},{1,3},{3,1},... | collective-permute-start | bytes 221192 | tf_op jit(solution)/shard_map/ppermute | solution.py:177
  19.5 3.4 %collective-permute-start.9 = (bf16[16,1024]{1,0:T(8,128)(2,1)S(1)}, bf16[16,1024]{1,0:T(8,128)(2,1)S(1)}, u32[]{:S(2)}, u32[]{:S(2)}) collective-permute-start(bf16[16,1024]{1,0:T(8,128)(2,1)S(1)} %get-tuple-element.28), channel_id=1, source_target_pairs={{0,5},{1,4},{2,7},{3,6},{4,1},{5,0},{6,3},{7,2},{8,13},{9,12},{10,... | collective-permute-start | bytes 98312 | tf_op jit(solution)/shard_map/ppermute | solution.py:480
  19.6 4.0 %collective-permute-start.8 = (bf16[16,1024]{1,0:T(8,128)(2,1)S(1)}, bf16[16,1024]{1,0:T(8,128)(2,1)S(1)}, u32[]{:S(2)}, u32[]{:S(2)}) collective-permute-start(bf16[16,1024]{1,0:T(8,128)(2,1)S(1)} %get-tuple-element.28), channel_id=1, source_target_pairs={{0,4},{2,6},{4,0},{6,2},{8,12},{10,14},{12,8},{14,10},{1,5},{3,7},... | collective-permute-start | bytes 98312 | tf_op jit(solution)/shard_map/ppermute | solution.py:177
  20.4 1.9 %collective-permute-start.7 = (bf16[16,768]{1,0:T(8,128)(2,1)S(1)}, bf16[16,768]{1,0:T(8,128)(2,1)S(1)}, u32[]{:S(2)}, u32[]{:S(2)}) collective-permute-start(bf16[16,768]{1,0:T(8,128)(2,1)S(1)} %get-tuple-element.24.keep_ref), channel_id=1, source_target_pairs={{0,1},{1,0},{2,3},{3,2},{4,5},{5,4},{6,7},{7,6},{8,9},{9,8},{10,11... | collective-permute-start | bytes 73736 | tf_op jit(solution)/shard_map/ppermute | solution.py:20

commit v12 on v8

--- a/solution.py
+++ b/solution.py
@@ -166,6 +166,7 @@
 
 
 SPLIT = 2
+SET_ORDER = (0, 3, 2, 1, 4, 7, 6, 5)
 HOLD_COPIES = 4
 TABLE_PIECES = 3
 SPLITTER = 65537.0
@@ -281,7 +282,7 @@
 
 
 def attend_kernel(set_count, limits_ref, *refs):
-    set_refs = refs[:set_count]
+    set_refs = [refs[SET_ORDER.index(i)] for i in range(set_count)]
     keep_ref, message_ref, table_ref, lines_ref = refs[set_count:]
     tok_dev, half_width = keep_ref.shape
     half_heads = half_width // HDIM
@@ -456,6 +457,7 @@
         for offset in range(SPLIT, seq_count, SPLIT)
     ]
     sets = line + [swap_shards(array, 1) for array in line]
+    sets = [sets[i] for i in SET_ORDER]
     limits, weight_held = lax.optimization_barrier((limits, weight_held))
     keep, message, table = pl.pallas_call(
         functools.partial(attend_kernel, len(sets)),

time: 23.5 us -> 24.4 us (1.038)
  waiting for transfers between devices: 5.2 us -> 6.59 us
  starting transfers between devices: 13.1 us -> 12.6 us
    ppermute x8, waiting for transfers between devices: 3.91 us -> 5.39 us  [swap_shards(): return lax.ppermute(array, 'seq', pairs)]
    ppermute x8, starting transfers between devices: 12.5 us -> 11.5 us  [swap_shards(): return lax.ppermute(array, 'seq', pairs)]
    ppermute x1, starting transfers between devices: 0.59 us -> 1.08 us  [partner_2(): lax.ppermute(array, axis, [(i, i ^ 1 << stride) for i in range(lax.axis_s...]
  transfers between devices with their start and end apart: 10 -> 10, of which waited for: 7 -> 6; matrix products, arithmetic and copies ran while one was open for 0% -> 0% of each run, Pallas kernels for 8% -> 8%
where the time goes in v12:
time: 24.4 us; the launch traced here: 24.2 us
  starting transfers between devices  12.6 us (52%)
  waiting for transfers between devices  6.59 us (27%)
  Pallas kernels  4.3 us (18%)
  between operations  0.69 us (3%)
    ppermute x8, starting transfers between devices, swap_shards(): return lax.ppermute(array, 'seq', pairs)  11.5 us
    ppermute x8, waiting for transfers between devices, swap_shards(): return lax.ppermute(array, 'seq', pairs)  5.39 us
    pallas_call x1, Pallas kernels, per_device_halves(): pl.pallas_call(hold_kernel, out_shape=pltpu.VMEM(out_weight.shape, jnp.bf...  1.63 us
    ppermute x1, starting transfers between devices, partner_2(): lax.ppermute(array, axis, [(i, i ^ 1 << stride) for i in range(lax.axis_s...  1.08 us
    pallas_call x1, Pallas kernels, per_device_halves(): pl.pallas_call(pack_kernel, out_shape=[pltpu.VMEM((3 * tok_dev, half_widt...  0.92 us
    pallas_call x1, Pallas kernels, per_device_halves(): pl.pallas_call(project_kernel, out_shape=[jax.ShapeDtypeStruct((tok_dev,...  0.91 us
    ppermute x1, waiting for transfers between devices, partner_2(): lax.ppermute(array, axis, [(i, i ^ 1 << stride) for i in range(lax.axis_s...  0.85 us
    pallas_call x1, Pallas kernels, per_device_halves(): pl.pallas_call(functools.partial(attend_kernel, len(sets)), out_shape=[pl...  0.55 us
  transfers between devices with their start and end apart: 10, of which 6 were waited for; matrix products, arithmetic and copies ran while one was open for 0% of the time, Pallas kernels for 8%

profile of v12, /device:TPU:0, one launch (start us, length us, event | category | flops | bytes accessed | tf_op | source)
XLA Modules:
  0.0 24.2 jit_solution(5070349285385335233)
XLA Ops:
  0.6 0.9 %pack.1 = (bf16[48,768]{1,0:T(8,128)(2,1)S(1)}, bf16[48,768]{1,0:T(8,128)(2,1)S(1)}, s32[8,128]{1,0:T(8,128)S(1)}, s32[2,8,128]{2,1,0:T(8,128)S(1)}, s32[2,8,128]{2,1,0:T(8,128)S(1)}) custom-call(bf16[1,16,1536]{2,1,0:T(8,128)(2,1)} %query_hbm.1, bf16[1,16,1536]{2,1,0:T(8,128)(2,1)} %key_hbm.1, bf16[1,16,1536]{2,1,0:T(8,128)(2,1)} %value_hbm.1, ...), custom_call_target="tpu_custom_call" | custom-call | tf_op jit(solution)/shard_map/pack/pallas_call | solution.py:423
  1.6 3.1 %collective-permute-start.2 = (bf16[48,768]{1,0:T(8,128)(2,1)S(1)}, bf16[48,768]{1,0:T(8,128)(2,1)S(1)}, u32[]{:S(2)}, u32[]{:S(2)}) collective-permute-start(bf16[48,768]{1,0:T(8,128)(2,1)S(1)} %get-tuple-element.19), channel_id=1, source_target_pairs={{0,4},{2,6},{4,0},{6,2},{8,12},{10,14},{12,8},{14,10},{1,5},{3,7},... | collective-permute-start | bytes 221192 | tf_op jit(solution)/shard_map/ppermute | solution.py:177
  4.6 2.5 %collective-permute-start = (bf16[48,768]{1,0:T(8,128)(2,1)S(1)}, bf16[48,768]{1,0:T(8,128)(2,1)S(1)}, u32[]{:S(2)}, u32[]{:S(2)}) collective-permute-start(bf16[48,768]{1,0:T(8,128)(2,1)S(1)} %get-tuple-element.19), channel_id=1, source_target_pairs={{0,12},{2,14},{4,8},{6,10},{8,4},{10,6},{12,0},{14,2},{1,13},{3,15... | collective-permute-start | bytes 221192 | tf_op jit(solution)/shard_map/ppermute | solution.py:177
  7.1 0.1 collective-permute-start.1
  7.2 1.5 %collective-permute-start.3 = (bf16[48,768]{1,0:T(8,128)(2,1)S(1)}, bf16[48,768]{1,0:T(8,128)(2,1)S(1)}, u32[]{:S(2)}, u32[]{:S(2)}) collective-permute-start(bf16[48,768]{1,0:T(8,128)(2,1)S(1)} %get-tuple-element.18.refs_0_), channel_id=1, source_target_pairs={{0,2},{2,0},{4,6},{6,4},{8,10},{10,8},{12,14},{14,12},{1,3},{3,1},... | collective-permute-start | bytes 221192 | tf_op jit(solution)/shard_map/ppermute | solution.py:177
  8.7 0.0 collective-permute-done.2.refs_3_
  8.7 0.5 %collective-permute-start.6 = (bf16[48,768]{1,0:T(8,128)(2,1)S(1)}, bf16[48,768]{1,0:T(8,128)(2,1)S(1)}, u32[]{:S(2)}, u32[]{:S(2)}) collective-permute-start(bf16[48,768]{1,0:T(8,128)(2,1)S(1)} %collective-permute-done.2.refs_3_), channel_id=1, source_target_pairs={{0,2},{2,0},{4,6},{6,4},{8,10},{10,8},{12,14},{14,12},{1,3},{3,1},... | collective-permute-start | bytes 221192 | tf_op jit(solution)/shard_map/ppermute | solution.py:177
  9.3 2.6 %collective-permute-done.refs_1_ = bf16[48,768]{1,0:T(8,128)(2,1)S(1)} collective-permute-done((bf16[48,768]{1,0:T(8,128)(2,1)S(1)}, bf16[48,768]{1,0:T(8,128)(2,1)S(1)}, u32[]{:S(2)}, u32[]{:S(2)}) %collective-permute-start) | collective-permute-done | bytes 73760 | tf_op jit(solution)/shard_map/ppermute | solution.py:177
  11.9 1.5 %collective-permute-start.4 = (bf16[48,768]{1,0:T(8,128)(2,1)S(1)}, bf16[48,768]{1,0:T(8,128)(2,1)S(1)}, u32[]{:S(2)}, u32[]{:S(2)}) collective-permute-start(bf16[48,768]{1,0:T(8,128)(2,1)S(1)} %collective-permute-done.refs_1_), channel_id=1, source_target_pairs={{0,2},{2,0},{4,6},{6,4},{8,10},{10,8},{12,14},{14,12},{1,3},{3,1},... | collective-permute-start | bytes 221192 | tf_op jit(solution)/shard_map/ppermute | solution.py:177
  13.3 0.8 %collective-permute-done.1.refs_2_ = bf16[48,768]{1,0:T(8,128)(2,1)S(1)} collective-permute-done((bf16[48,768]{1,0:T(8,128)(2,1)S(1)}, bf16[48,768]{1,0:T(8,128)(2,1)S(1)}, u32[]{:S(2)}, u32[]{:S(2)}) %collective-permute-start.1) | collective-permute-done | bytes 73760 | tf_op jit(solution)/shard_map/ppermute | solution.py:177
  14.2 1.5 %collective-permute-start.5 = (bf16[48,768]{1,0:T(8,128)(2,1)S(1)}, bf16[48,768]{1,0:T(8,128)(2,1)S(1)}, u32[]{:S(2)}, u32[]{:S(2)}) collective-permute-start(bf16[48,768]{1,0:T(8,128)(2,1)S(1)} %collective-permute-done.1.refs_2_), channel_id=1, source_target_pairs={{0,2},{2,0},{4,6},{6,4},{8,10},{10,8},{12,14},{14,12},{1,3},{3,1},... | collective-permute-start | bytes 221192 | tf_op jit(solution)/shard_map/ppermute | solution.py:177
  15.7 1.6 %hold.1.weight_ref = bf16[1536,768]{1,0:T(8,128)(2,1)S(1)} custom-call(bf16[1536,768]{1,0:T(8,128)(2,1)} %weight_hbm.1, s32[8,128]{1,0:T(8,128)S(1)} %get-tuple-element.17.after_ref.limits_ref), custom_call_target="tpu_custom_call" | custom-call | bytes 4718592 | tf_op jit(solution)/shard_map/hold/pallas_call | solution.py:443
  17.3 0.0 collective-permute-done.3.refs_4_
  17.3 0.0 collective-permute-done.6.refs_7_
  17.3 0.0 collective-permute-done.4.refs_5_
  17.3 1.2 %collective-permute-done.5.refs_6_ = bf16[48,768]{1,0:T(8,128)(2,1)S(1)} collective-permute-done((bf16[48,768]{1,0:T(8,128)(2,1)S(1)}, bf16[48,768]{1,0:T(8,128)(2,1)S(1)}, u32[]{:S(2)}, u32[]{:S(2)}) %collective-permute-start.5) | collective-permute-done | bytes 73760 | tf_op jit(solution)/shard_map/ppermute | solution.py:177
  18.5 0.5 %attend.1 = (bf16[16,768]{1,0:T(8,128)(2,1)S(1)}, bf16[16,1024]{1,0:T(8,128)(2,1)S(1)}, f32[8,128]{1,0:T(8,128)S(1)}) custom-call(s32[8,128]{1,0:T(8,128)S(1)} %get-tuple-element.17.after_ref.limits_ref, bf16[48,768]{1,0:T(8,128)(2,1)S(1)} %get-tuple-element.18.refs_0_, bf16[48,768]{1,0:T(8,128)(2,1)S(1)} %collective-permute-done.refs_1_, ...), custom_call_target="tpu_custom_call" | custom-call | tf_op jit(solution)/shard_map/attend/pallas_call | solution.py:462
  19.1 0.1 collective-permute-start.9
  19.2 0.8 %collective-permute-start.8 = (bf16[16,1024]{1,0:T(8,128)(2,1)S(1)}, bf16[16,1024]{1,0:T(8,128)(2,1)S(1)}, u32[]{:S(2)}, u32[]{:S(2)}) collective-permute-start(bf16[16,1024]{1,0:T(8,128)(2,1)S(1)} %get-tuple-element.24), channel_id=1, source_target_pairs={{0,4},{2,6},{4,0},{6,2},{8,12},{10,14},{12,8},{14,10},{1,5},{3,7},... | collective-permute-start | bytes 98312 | tf_op jit(solution)/shard_map/ppermute | solution.py:177
  19.9 1.1 %collective-permute-start.7 = (bf16[16,768]{1,0:T(8,128)(2,1)S(1)}, bf16[16,768]{1,0:T(8,128)(2,1)S(1)}, u32[]{:S(2)}, u32[]{:S(2)}) collective-permute-start(bf16[16,768]{1,0:T(8,128)(2,1)S(1)} %get-tuple-element.20.keep_ref), channel_id=1, source_target_pairs={{0,1},{1,0},{2,3},{3,2},{4,5},{5,4},{6,7},{7,6},{8,9},{9,8},{10,11... | collective-permute-start | bytes 73736 | tf_op jit(solution)/shard_map/ppermute | solution.py:20
  21.0 0.8 %collective-permute-done.7.partner_keep_ref = bf16[16,768]{1,0:T(8,128)(2,1)S(1)} collective-permute-done((bf16[16,768]{1,0:T(8,128)(2,1)S(1)}, bf16[16,768]{1,0:T(8,128)(2,1)S(1)}, u32[]{:S(2)}, u32[]{:S(2)}) %collective-permute-start.7) | collective-permute-done | bytes 24608 | tf_op jit(solution)/shard_map/ppermute | solution.py:20
  21.9 0.3 %keep.1 = (f32[16,768]{1,0:T(8,128)S(1)}, f32[16,128]{1,0:T(8,128)S(1)}) custom-call(bf16[16,768]{1,0:T(8,128)(2,1)S(1)} %get-tuple-element.20.keep_ref, bf16[16,768]{1,0:T(8,128)(2,1)S(1)} %collective-permute-done.7.partner_keep_ref, bf16[1536,768]{1,0:T(8,128)(2,1)S(1)} %hold.1.weight_ref), custom_call_target="tpu_custom_call" | custom-call | tf_op jit(solution)/shard_map/keep/pallas_call | solution.py:479
  22.2 0.3 %collective-permute-done.9.partner_back_ref = bf16[16,1024]{1,0:T(8,128)(2,1)S(1)} collective-permute-done((bf16[16,1024]{1,0:T(8,128)(2,1)S(1)}, bf16[16,1024]{1,0:T(8,128)(2,1)S(1)}, u32[]{:S(2)}, u32[]{:S(2)}) %collective-permute-start.9) | collective-permute-done | bytes 32800 | tf_op jit(solution)/shard_map/ppermute | solution.py:476
  22.5 0.8 %collective-permute-done.8.message_ref = bf16[16,1024]{1,0:T(8,128)(2,1)S(1)} collective-permute-done((bf16[16,1024]{1,0:T(8,128)(2,1)S(1)}, bf16[16,1024]{1,0:T(8,128)(2,1)S(1)}, u32[]{:S(2)}, u32[]{:S(2)}) %collective-permute-start.8) | collective-permute-done | bytes 32800 | tf_op jit(solution)/shard_map/ppermute | solution.py:177
  23.3 0.9 %project.1 = (bf16[16,768]{1,0:T(8,128)(2,1)}, f32[2,8,16]{2,1,0:T(8,128)}) custom-call(f32[16,768]{1,0:T(8,128)S(1)} %get-tuple-element.22.total_ref, f32[16,128]{1,0:T(8,128)S(1)} %get-tuple-element.23.size_ref, bf16[16,1024]{1,0:T(8,128)(2,1)S(1)} %collective-permute-done.8.message_ref, bf16[16,1024]{1,0:T(8,128)(2,1)S(1)} %collective-permute-done.9.partner_back_ref, ...), custom_call_target="tpu_custom_call" | custom-call | tf_op jit(solution)/shard_map/project/pallas_call | solution.py:490
Async XLA Ops:
  1.6 7.2 %collective-permute-start.2 = (bf16[48,768]{1,0:T(8,128)(2,1)S(1)}, bf16[48,768]{1,0:T(8,128)(2,1)S(1)}, u32[]{:S(2)}, u32[]{:S(2)}) collective-permute-start(bf16[48,768]{1,0:T(8,128)(2,1)S(1)} %get-tuple-element.19), channel_id=1, source_target_pairs={{0,4},{2,6},{4,0},{6,2},{8,12},{10,14},{12,8},{14,10},{1,5},{3,7},... | collective-permute-start | bytes 221192 | tf_op jit(solution)/shard_map/ppermute | solution.py:177
  4.6 7.2 %collective-permute-start = (bf16[48,768]{1,0:T(8,128)(2,1)S(1)}, bf16[48,768]{1,0:T(8,128)(2,1)S(1)}, u32[]{:S(2)}, u32[]{:S(2)}) collective-permute-start(bf16[48,768]{1,0:T(8,128)(2,1)S(1)} %get-tuple-element.19), channel_id=1, source_target_pairs={{0,12},{2,14},{4,8},{6,10},{8,4},{10,6},{12,0},{14,2},{1,13},{3,15... | collective-permute-start | bytes 221192 | tf_op jit(solution)/shard_map/ppermute | solution.py:177
  7.1 7.1 %collective-permute-start.1 = (bf16[48,768]{1,0:T(8,128)(2,1)S(1)}, bf16[48,768]{1,0:T(8,128)(2,1)S(1)}, u32[]{:S(2)}, u32[]{:S(2)}) collective-permute-start(bf16[48,768]{1,0:T(8,128)(2,1)S(1)} %get-tuple-element.18.refs_0_), channel_id=1, source_target_pairs={{0,8},{2,10},{4,12},{6,14},{8,0},{10,2},{12,4},{14,6},{1,9},{3,11}... | collective-permute-start | bytes 221192 | tf_op jit(solution)/shard_map/ppermute | solution.py:177
  7.2 10.1 %collective-permute-start.3 = (bf16[48,768]{1,0:T(8,128)(2,1)S(1)}, bf16[48,768]{1,0:T(8,128)(2,1)S(1)}, u32[]{:S(2)}, u32[]{:S(2)}) collective-permute-start(bf16[48,768]{1,0:T(8,128)(2,1)S(1)} %get-tuple-element.18.refs_0_), channel_id=1, source_target_pairs={{0,2},{2,0},{4,6},{6,4},{8,10},{10,8},{12,14},{14,12},{1,3},{3,1},... | collective-permute-start | bytes 221192 | tf_op jit(solution)/shard_map/ppermute | solution.py:177
  8.7 8.6 %collective-permute-start.6 = (bf16[48,768]{1,0:T(8,128)(2,1)S(1)}, bf16[48,768]{1,0:T(8,128)(2,1)S(1)}, u32[]{:S(2)}, u32[]{:S(2)}) collective-permute-start(bf16[48,768]{1,0:T(8,128)(2,1)S(1)} %collective-permute-done.2.refs_3_), channel_id=1, source_target_pairs={{0,2},{2,0},{4,6},{6,4},{8,10},{10,8},{12,14},{14,12},{1,3},{3,1},... | collective-permute-start | bytes 221192 | tf_op jit(solution)/shard_map/ppermute | solution.py:177
  11.9 5.5 %collective-permute-start.4 = (bf16[48,768]{1,0:T(8,128)(2,1)S(1)}, bf16[48,768]{1,0:T(8,128)(2,1)S(1)}, u32[]{:S(2)}, u32[]{:S(2)}) collective-permute-start(bf16[48,768]{1,0:T(8,128)(2,1)S(1)} %collective-permute-done.refs_1_), channel_id=1, source_target_pairs={{0,2},{2,0},{4,6},{6,4},{8,10},{10,8},{12,14},{14,12},{1,3},{3,1},... | collective-permute-start | bytes 221192 | tf_op jit(solution)/shard_map/ppermute | solution.py:177
  14.2 4.4 %collective-permute-start.5 = (bf16[48,768]{1,0:T(8,128)(2,1)S(1)}, bf16[48,768]{1,0:T(8,128)(2,1)S(1)}, u32[]{:S(2)}, u32[]{:S(2)}) collective-permute-start(bf16[48,768]{1,0:T(8,128)(2,1)S(1)} %collective-permute-done.1.refs_2_), channel_id=1, source_target_pairs={{0,2},{2,0},{4,6},{6,4},{8,10},{10,8},{12,14},{14,12},{1,3},{3,1},... | collective-permute-start | bytes 221192 | tf_op jit(solution)/shard_map/ppermute | solution.py:177
  19.1 3.4 %collective-permute-start.9 = (bf16[16,1024]{1,0:T(8,128)(2,1)S(1)}, bf16[16,1024]{1,0:T(8,128)(2,1)S(1)}, u32[]{:S(2)}, u32[]{:S(2)}) collective-permute-start(bf16[16,1024]{1,0:T(8,128)(2,1)S(1)} %get-tuple-element.24), channel_id=1, source_target_pairs={{0,5},{1,4},{2,7},{3,6},{4,1},{5,0},{6,3},{7,2},{8,13},{9,12},{10,... | collective-permute-start | bytes 98312 | tf_op jit(solution)/shard_map/ppermute | solution.py:476
  19.2 4.1 %collective-permute-start.8 = (bf16[16,1024]{1,0:T(8,128)(2,1)S(1)}, bf16[16,1024]{1,0:T(8,128)(2,1)S(1)}, u32[]{:S(2)}, u32[]{:S(2)}) collective-permute-start(bf16[16,1024]{1,0:T(8,128)(2,1)S(1)} %get-tuple-element.24), channel_id=1, source_target_pairs={{0,4},{2,6},{4,0},{6,2},{8,12},{10,14},{12,8},{14,10},{1,5},{3,7},... | collective-permute-start | bytes 98312 | tf_op jit(solution)/shard_map/ppermute | solution.py:177
  19.9 1.9 %collective-permute-start.7 = (bf16[16,768]{1,0:T(8,128)(2,1)S(1)}, bf16[16,768]{1,0:T(8,128)(2,1)S(1)}, u32[]{:S(2)}, u32[]{:S(2)}) collective-permute-start(bf16[16,768]{1,0:T(8,128)(2,1)S(1)} %get-tuple-element.20.keep_ref), channel_id=1, source_target_pairs={{0,1},{1,0},{2,3},{3,2},{4,5},{5,4},{6,7},{7,6},{8,9},{9,8},{10,11... | collective-permute-start | bytes 73736 | tf_op jit(solution)/shard_map/ppermute | solution.py:20

commit v13 on v8

--- a/solution.py
+++ b/solution.py
@@ -167,7 +167,7 @@
 
 SPLIT = 2
 HOLD_COPIES = 4
-TABLE_PIECES = 3
+TABLE_PIECES = 2
 SPLITTER = 65537.0
 
 

time: 23.5 us -> 23.5 us (level)
  no operation moved by 1% of the time
where the time goes in v13:
time: 23.5 us; the launch traced here: 23.2 us
  starting transfers between devices  13.1 us (56%)
  waiting for transfers between devices  5.11 us (22%)
  Pallas kernels  4.29 us (18%)
  between operations  0.69 us (3%)
    ppermute x8, starting transfers between devices, swap_shards(): return lax.ppermute(array, 'seq', pairs)  12.5 us
    ppermute x8, waiting for transfers between devices, swap_shards(): return lax.ppermute(array, 'seq', pairs)  3.91 us
    pallas_call x1, Pallas kernels, per_device_halves(): pl.pallas_call(hold_kernel, out_shape=pltpu.VMEM(out_weight.shape, jnp.bf...  1.63 us
    pallas_call x1, Pallas kernels, per_device_halves(): pl.pallas_call(pack_kernel, out_shape=[pltpu.VMEM((3 * tok_dev, half_widt...  0.92 us
    pallas_call x1, Pallas kernels, per_device_halves(): pl.pallas_call(project_kernel, out_shape=[jax.ShapeDtypeStruct((tok_dev,...  0.91 us
    ppermute x1, waiting for transfers between devices, partner_2(): lax.ppermute(array, axis, [(i, i ^ 1 << stride) for i in range(lax.axis_s...  0.85 us
    ppermute x1, starting transfers between devices, partner_2(): lax.ppermute(array, axis, [(i, i ^ 1 << stride) for i in range(lax.axis_s...  0.59 us
    pallas_call x1, Pallas kernels, per_device_halves(): pl.pallas_call(functools.partial(attend_kernel, len(sets)), out_shape=[pl...  0.54 us
  transfers between devices with their start and end apart: 10, of which 7 were waited for; matrix products, arithmetic and copies ran while one was open for 0% of the time, Pallas kernels for 8%

profile of v13, /device:TPU:0, one launch (start us, length us, event | category | flops | bytes accessed | tf_op | source)
XLA Modules:
  0.0 23.2 jit_solution(5268152347710968937)
XLA Ops:
  0.6 0.9 %pack.1 = (bf16[48,768]{1,0:T(8,128)(2,1)S(1)}, bf16[48,768]{1,0:T(8,128)(2,1)S(1)}, s32[8,128]{1,0:T(8,128)S(1)}, s32[2,8,128]{2,1,0:T(8,128)S(1)}, s32[2,8,128]{2,1,0:T(8,128)S(1)}) custom-call(bf16[1,16,1536]{2,1,0:T(8,128)(2,1)} %query_hbm.1, bf16[1,16,1536]{2,1,0:T(8,128)(2,1)} %key_hbm.1, bf16[1,16,1536]{2,1,0:T(8,128)(2,1)} %value_hbm.1, ...), custom_call_target="tpu_custom_call" | custom-call | tf_op jit(solution)/shard_map/pack/pallas_call | solution.py:422
  1.6 5.1 %collective-permute-start.2 = (bf16[48,768]{1,0:T(8,128)(2,1)S(1)}, bf16[48,768]{1,0:T(8,128)(2,1)S(1)}, u32[]{:S(2)}, u32[]{:S(2)}) collective-permute-start(bf16[48,768]{1,0:T(8,128)(2,1)S(1)} %get-tuple-element.19), channel_id=1, source_target_pairs={{0,12},{2,14},{4,8},{6,10},{8,4},{10,6},{12,0},{14,2},{1,13},{3,15... | collective-permute-start | bytes 221192 | tf_op jit(solution)/shard_map/ppermute | solution.py:176
  6.7 0.0 collective-permute-start
  6.7 0.6 %collective-permute-start.1 = (bf16[48,768]{1,0:T(8,128)(2,1)S(1)}, bf16[48,768]{1,0:T(8,128)(2,1)S(1)}, u32[]{:S(2)}, u32[]{:S(2)}) collective-permute-start(bf16[48,768]{1,0:T(8,128)(2,1)S(1)} %get-tuple-element.18.refs_0_), channel_id=1, source_target_pairs={{0,8},{2,10},{4,12},{6,14},{8,0},{10,2},{12,4},{14,6},{1,9},{3,11}... | collective-permute-start | bytes 221192 | tf_op jit(solution)/shard_map/ppermute | solution.py:176
  7.3 1.6 %collective-permute-start.3 = (bf16[48,768]{1,0:T(8,128)(2,1)S(1)}, bf16[48,768]{1,0:T(8,128)(2,1)S(1)}, u32[]{:S(2)}, u32[]{:S(2)}) collective-permute-start(bf16[48,768]{1,0:T(8,128)(2,1)S(1)} %get-tuple-element.18.refs_0_), channel_id=1, source_target_pairs={{0,2},{2,0},{4,6},{6,4},{8,10},{10,8},{12,14},{14,12},{1,3},{3,1},... | collective-permute-start | bytes 221192 | tf_op jit(solution)/shard_map/ppermute | solution.py:176
  9.0 0.9 %collective-permute-done.2.refs_3_ = bf16[48,768]{1,0:T(8,128)(2,1)S(1)} collective-permute-done((bf16[48,768]{1,0:T(8,128)(2,1)S(1)}, bf16[48,768]{1,0:T(8,128)(2,1)S(1)}, u32[]{:S(2)}, u32[]{:S(2)}) %collective-permute-start.2) | collective-permute-done | bytes 73760 | tf_op jit(solution)/shard_map/ppermute | solution.py:176
  9.8 1.5 %collective-permute-start.6 = (bf16[48,768]{1,0:T(8,128)(2,1)S(1)}, bf16[48,768]{1,0:T(8,128)(2,1)S(1)}, u32[]{:S(2)}, u32[]{:S(2)}) collective-permute-start(bf16[48,768]{1,0:T(8,128)(2,1)S(1)} %collective-permute-done.2.refs_3_), channel_id=1, source_target_pairs={{0,2},{2,0},{4,6},{6,4},{8,10},{10,8},{12,14},{14,12},{1,3},{3,1},... | collective-permute-start | bytes 221192 | tf_op jit(solution)/shard_map/ppermute | solution.py:176
  11.3 0.4 %collective-permute-done.refs_1_ = bf16[48,768]{1,0:T(8,128)(2,1)S(1)} collective-permute-done((bf16[48,768]{1,0:T(8,128)(2,1)S(1)}, bf16[48,768]{1,0:T(8,128)(2,1)S(1)}, u32[]{:S(2)}, u32[]{:S(2)}) %collective-permute-start) | collective-permute-done | bytes 73760 | tf_op jit(solution)/shard_map/ppermute | solution.py:176
  11.7 1.6 %collective-permute-start.4 = (bf16[48,768]{1,0:T(8,128)(2,1)S(1)}, bf16[48,768]{1,0:T(8,128)(2,1)S(1)}, u32[]{:S(2)}, u32[]{:S(2)}) collective-permute-start(bf16[48,768]{1,0:T(8,128)(2,1)S(1)} %collective-permute-done.refs_1_), channel_id=1, source_target_pairs={{0,2},{2,0},{4,6},{6,4},{8,10},{10,8},{12,14},{14,12},{1,3},{3,1},... | collective-permute-start | bytes 221192 | tf_op jit(solution)/shard_map/ppermute | solution.py:176
  13.4 0.0 collective-permute-done.1.refs_2_
  13.4 0.7 %collective-permute-start.5 = (bf16[48,768]{1,0:T(8,128)(2,1)S(1)}, bf16[48,768]{1,0:T(8,128)(2,1)S(1)}, u32[]{:S(2)}, u32[]{:S(2)}) collective-permute-start(bf16[48,768]{1,0:T(8,128)(2,1)S(1)} %collective-permute-done.1.refs_2_), channel_id=1, source_target_pairs={{0,2},{2,0},{4,6},{6,4},{8,10},{10,8},{12,14},{14,12},{1,3},{3,1},... | collective-permute-start | bytes 221192 | tf_op jit(solution)/shard_map/ppermute | solution.py:176
  14.1 1.6 %hold.1.weight_ref = bf16[1536,768]{1,0:T(8,128)(2,1)S(1)} custom-call(bf16[1536,768]{1,0:T(8,128)(2,1)} %weight_hbm.1, s32[8,128]{1,0:T(8,128)S(1)} %get-tuple-element.17.after_ref.limits_ref), custom_call_target="tpu_custom_call" | custom-call | bytes 4718592 | tf_op jit(solution)/shard_map/hold/pallas_call | solution.py:442
  15.7 0.0 collective-permute-done.3.refs_4_
  15.7 0.0 collective-permute-done.6.refs_7_
  15.7 1.1 %collective-permute-done.4.refs_5_ = bf16[48,768]{1,0:T(8,128)(2,1)S(1)} collective-permute-done((bf16[48,768]{1,0:T(8,128)(2,1)S(1)}, bf16[48,768]{1,0:T(8,128)(2,1)S(1)}, u32[]{:S(2)}, u32[]{:S(2)}) %collective-permute-start.4) | collective-permute-done | bytes 73760 | tf_op jit(solution)/shard_map/ppermute | solution.py:176
  16.8 0.9 %collective-permute-done.5.refs_6_ = bf16[48,768]{1,0:T(8,128)(2,1)S(1)} collective-permute-done((bf16[48,768]{1,0:T(8,128)(2,1)S(1)}, bf16[48,768]{1,0:T(8,128)(2,1)S(1)}, u32[]{:S(2)}, u32[]{:S(2)}) %collective-permute-start.5) | collective-permute-done | bytes 73760 | tf_op jit(solution)/shard_map/ppermute | solution.py:176
  17.7 0.5 %attend.1 = (bf16[16,768]{1,0:T(8,128)(2,1)S(1)}, bf16[16,896]{1,0:T(8,128)(2,1)S(1)}, f32[8,128]{1,0:T(8,128)S(1)}) custom-call(s32[8,128]{1,0:T(8,128)S(1)} %get-tuple-element.17.after_ref.limits_ref, bf16[48,768]{1,0:T(8,128)(2,1)S(1)} %get-tuple-element.18.refs_0_, bf16[48,768]{1,0:T(8,128)(2,1)S(1)} %collective-permute-done.refs_1_, ...), custom_call_target="tpu_custom_call" | custom-call | tf_op jit(solution)/shard_map/attend/pallas_call | solution.py:460
  18.3 0.1 collective-permute-start.9
  18.3 1.3 %collective-permute-start.8 = (bf16[16,896]{1,0:T(8,128)(2,1)S(1)}, bf16[16,896]{1,0:T(8,128)(2,1)S(1)}, u32[]{:S(2)}, u32[]{:S(2)}) collective-permute-start(bf16[16,896]{1,0:T(8,128)(2,1)S(1)} %get-tuple-element.24), channel_id=1, source_target_pairs={{0,4},{2,6},{4,0},{6,2},{8,12},{10,14},{12,8},{14,10},{1,5},{3,7},... | collective-permute-start | bytes 86024 | tf_op jit(solution)/shard_map/ppermute | solution.py:176
  19.6 0.6 %collective-permute-start.7 = (bf16[16,768]{1,0:T(8,128)(2,1)S(1)}, bf16[16,768]{1,0:T(8,128)(2,1)S(1)}, u32[]{:S(2)}, u32[]{:S(2)}) collective-permute-start(bf16[16,768]{1,0:T(8,128)(2,1)S(1)} %get-tuple-element.20.keep_ref), channel_id=1, source_target_pairs={{0,1},{1,0},{2,3},{3,2},{4,5},{5,4},{6,7},{7,6},{8,9},{9,8},{10,11... | collective-permute-start | bytes 73736 | tf_op jit(solution)/shard_map/ppermute | solution.py:20
  20.2 0.8 %collective-permute-done.7.partner_keep_ref = bf16[16,768]{1,0:T(8,128)(2,1)S(1)} collective-permute-done((bf16[16,768]{1,0:T(8,128)(2,1)S(1)}, bf16[16,768]{1,0:T(8,128)(2,1)S(1)}, u32[]{:S(2)}, u32[]{:S(2)}) %collective-permute-start.7) | collective-permute-done | bytes 24608 | tf_op jit(solution)/shard_map/ppermute | solution.py:20
  21.0 0.3 %keep.1 = (f32[16,768]{1,0:T(8,128)S(1)}, f32[16,128]{1,0:T(8,128)S(1)}) custom-call(bf16[16,768]{1,0:T(8,128)(2,1)S(1)} %get-tuple-element.20.keep_ref, bf16[16,768]{1,0:T(8,128)(2,1)S(1)} %collective-permute-done.7.partner_keep_ref, bf16[1536,768]{1,0:T(8,128)(2,1)S(1)} %hold.1.weight_ref), custom_call_target="tpu_custom_call" | custom-call | tf_op jit(solution)/shard_map/keep/pallas_call | solution.py:477
  21.3 0.4 %collective-permute-done.9.partner_back_ref = bf16[16,896]{1,0:T(8,128)(2,1)S(1)} collective-permute-done((bf16[16,896]{1,0:T(8,128)(2,1)S(1)}, bf16[16,896]{1,0:T(8,128)(2,1)S(1)}, u32[]{:S(2)}, u32[]{:S(2)}) %collective-permute-start.9) | collective-permute-done | bytes 28704 | tf_op jit(solution)/shard_map/ppermute | solution.py:474
  21.7 0.6 %collective-permute-done.8.message_ref = bf16[16,896]{1,0:T(8,128)(2,1)S(1)} collective-permute-done((bf16[16,896]{1,0:T(8,128)(2,1)S(1)}, bf16[16,896]{1,0:T(8,128)(2,1)S(1)}, u32[]{:S(2)}, u32[]{:S(2)}) %collective-permute-start.8) | collective-permute-done | bytes 28704 | tf_op jit(solution)/shard_map/ppermute | solution.py:176
  22.3 0.9 %project.1 = (bf16[16,768]{1,0:T(8,128)(2,1)}, f32[2,8,16]{2,1,0:T(8,128)}) custom-call(f32[16,768]{1,0:T(8,128)S(1)} %get-tuple-element.22.total_ref, f32[16,128]{1,0:T(8,128)S(1)} %get-tuple-element.23.size_ref, bf16[16,896]{1,0:T(8,128)(2,1)S(1)} %collective-permute-done.8.message_ref, bf16[16,896]{1,0:T(8,128)(2,1)S(1)} %collective-permute-done.9.partner_back_ref, ...), custom_call_target="tpu_custom_call" | custom-call | tf_op jit(solution)/shard_map/project/pallas_call | solution.py:488
Async XLA Ops:
  1.6 8.3 %collective-permute-start.2 = (bf16[48,768]{1,0:T(8,128)(2,1)S(1)}, bf16[48,768]{1,0:T(8,128)(2,1)S(1)}, u32[]{:S(2)}, u32[]{:S(2)}) collective-permute-start(bf16[48,768]{1,0:T(8,128)(2,1)S(1)} %get-tuple-element.19), channel_id=1, source_target_pairs={{0,12},{2,14},{4,8},{6,10},{8,4},{10,6},{12,0},{14,2},{1,13},{3,15... | collective-permute-start | bytes 221192 | tf_op jit(solution)/shard_map/ppermute | solution.py:176
  6.7 5.0 %collective-permute-start = (bf16[48,768]{1,0:T(8,128)(2,1)S(1)}, bf16[48,768]{1,0:T(8,128)(2,1)S(1)}, u32[]{:S(2)}, u32[]{:S(2)}) collective-permute-start(bf16[48,768]{1,0:T(8,128)(2,1)S(1)} %get-tuple-element.19), channel_id=1, source_target_pairs={{0,4},{2,6},{4,0},{6,2},{8,12},{10,14},{12,8},{14,10},{1,5},{3,7},... | collective-permute-start | bytes 221192 | tf_op jit(solution)/shard_map/ppermute | solution.py:176
  6.7 6.7 %collective-permute-start.1 = (bf16[48,768]{1,0:T(8,128)(2,1)S(1)}, bf16[48,768]{1,0:T(8,128)(2,1)S(1)}, u32[]{:S(2)}, u32[]{:S(2)}) collective-permute-start(bf16[48,768]{1,0:T(8,128)(2,1)S(1)} %get-tuple-element.18.refs_0_), channel_id=1, source_target_pairs={{0,8},{2,10},{4,12},{6,14},{8,0},{10,2},{12,4},{14,6},{1,9},{3,11}... | collective-permute-start | bytes 221192 | tf_op jit(solution)/shard_map/ppermute | solution.py:176
  7.3 8.4 %collective-permute-start.3 = (bf16[48,768]{1,0:T(8,128)(2,1)S(1)}, bf16[48,768]{1,0:T(8,128)(2,1)S(1)}, u32[]{:S(2)}, u32[]{:S(2)}) collective-permute-start(bf16[48,768]{1,0:T(8,128)(2,1)S(1)} %get-tuple-element.18.refs_0_), channel_id=1, source_target_pairs={{0,2},{2,0},{4,6},{6,4},{8,10},{10,8},{12,14},{14,12},{1,3},{3,1},... | collective-permute-start | bytes 221192 | tf_op jit(solution)/shard_map/ppermute | solution.py:176
  9.8 5.9 %collective-permute-start.6 = (bf16[48,768]{1,0:T(8,128)(2,1)S(1)}, bf16[48,768]{1,0:T(8,128)(2,1)S(1)}, u32[]{:S(2)}, u32[]{:S(2)}) collective-permute-start(bf16[48,768]{1,0:T(8,128)(2,1)S(1)} %collective-permute-done.2.refs_3_), channel_id=1, source_target_pairs={{0,2},{2,0},{4,6},{6,4},{8,10},{10,8},{12,14},{14,12},{1,3},{3,1},... | collective-permute-start | bytes 221192 | tf_op jit(solution)/shard_map/ppermute | solution.py:176
  11.7 5.1 %collective-permute-start.4 = (bf16[48,768]{1,0:T(8,128)(2,1)S(1)}, bf16[48,768]{1,0:T(8,128)(2,1)S(1)}, u32[]{:S(2)}, u32[]{:S(2)}) collective-permute-start(bf16[48,768]{1,0:T(8,128)(2,1)S(1)} %collective-permute-done.refs_1_), channel_id=1, source_target_pairs={{0,2},{2,0},{4,6},{6,4},{8,10},{10,8},{12,14},{14,12},{1,3},{3,1},... | collective-permute-start | bytes 221192 | tf_op jit(solution)/shard_map/ppermute | solution.py:176
  13.4 4.4 %collective-permute-start.5 = (bf16[48,768]{1,0:T(8,128)(2,1)S(1)}, bf16[48,768]{1,0:T(8,128)(2,1)S(1)}, u32[]{:S(2)}, u32[]{:S(2)}) collective-permute-start(bf16[48,768]{1,0:T(8,128)(2,1)S(1)} %collective-permute-done.1.refs_2_), channel_id=1, source_target_pairs={{0,2},{2,0},{4,6},{6,4},{8,10},{10,8},{12,14},{14,12},{1,3},{3,1},... | collective-permute-start | bytes 221192 | tf_op jit(solution)/shard_map/ppermute | solution.py:176
  18.3 3.4 %collective-permute-start.9 = (bf16[16,896]{1,0:T(8,128)(2,1)S(1)}, bf16[16,896]{1,0:T(8,128)(2,1)S(1)}, u32[]{:S(2)}, u32[]{:S(2)}) collective-permute-start(bf16[16,896]{1,0:T(8,128)(2,1)S(1)} %get-tuple-element.24), channel_id=1, source_target_pairs={{0,5},{1,4},{2,7},{3,6},{4,1},{5,0},{6,3},{7,2},{8,13},{9,12},{10,... | collective-permute-start | bytes 86024 | tf_op jit(solution)/shard_map/ppermute | solution.py:474
  18.3 4.0 %collective-permute-start.8 = (bf16[16,896]{1,0:T(8,128)(2,1)S(1)}, bf16[16,896]{1,0:T(8,128)(2,1)S(1)}, u32[]{:S(2)}, u32[]{:S(2)}) collective-permute-start(bf16[16,896]{1,0:T(8,128)(2,1)S(1)} %get-tuple-element.24), channel_id=1, source_target_pairs={{0,4},{2,6},{4,0},{6,2},{8,12},{10,14},{12,8},{14,10},{1,5},{3,7},... | collective-permute-start | bytes 86024 | tf_op jit(solution)/shard_map/ppermute | solution.py:176
  19.6 1.4 %collective-permute-start.7 = (bf16[16,768]{1,0:T(8,128)(2,1)S(1)}, bf16[16,768]{1,0:T(8,128)(2,1)S(1)}, u32[]{:S(2)}, u32[]{:S(2)}) collective-permute-start(bf16[16,768]{1,0:T(8,128)(2,1)S(1)} %get-tuple-element.20.keep_ref), channel_id=1, source_target_pairs={{0,1},{1,0},{2,3},{3,2},{4,5},{5,4},{6,7},{7,6},{8,9},{9,8},{10,11... | collective-permute-start | bytes 73736 | tf_op jit(solution)/shard_map/ppermute | solution.py:20

commit v14 on v13

--- a/solution.py
+++ b/solution.py
@@ -366,8 +366,11 @@
     table_ref,
     pick_ref,
     slot_head_ref,
+    projected_hbm,
+    saved_hbm,
     projected_ref,
     saved_ref,
+    copy_sems,
 ):
     tok_dev = message_ref.shape[0]
     half_width = weight_ref.shape[0] // 2
@@ -378,9 +381,6 @@
     guided = guidance(message_ref[:, rows], partner_back_ref[:, rows])
     size = size_ref[:, 0:1] + jnp.sum(jnp.abs(guided), axis=1, keepdims=True)
     magnitude = size / (2 * half_width)
-    total = total_ref[...] + half_product(guided, weight_ref, 1 - half)
-    projected_ref[...] = (total / (magnitude + EPSILON)).astype(jnp.bfloat16)
-
     parts = message_ref[:, pl.ds(half_width, message_ref.shape[1] - half_width)].astype(jnp.float32)
     others = []
     for head in range(half_heads):
@@ -399,6 +399,28 @@
         spread = jnp.broadcast_to(line, pick.shape)
         taken = jnp.take_along_axis(spread, jnp.maximum(pick, 0), axis=1)
         saved_ref[slot] = jnp.where(pick >= 0, taken, 0.0)[:, : saved_ref.shape[2]]
+    copies = [pltpu.make_async_copy(saved_ref, saved_hbm, copy_sems.at[0])]
+    copies[0].start()
+
+    rounded = guided.astype(jnp.bfloat16)
+    rows = pl.ds(pl.multiple_of((1 - half) * half_width, half_width), half_width)
+    share = projected_ref.shape[1] // 2
+    for number in range(2):
+        columns = pl.ds(number * share, share)
+        total = total_ref[:, columns] + jnp.dot(
+            rounded, weight_ref[rows, columns], preferred_element_type=jnp.float32
+        )
+        projected_ref[:, columns] = (total / (magnitude + EPSILON)).astype(jnp.bfloat16)
+        copies.append(
+            pltpu.make_async_copy(
+                projected_ref.at[:, columns],
+                projected_hbm.at[:, columns],
+                copy_sems.at[number + 1],
+            )
+        )
+        copies[-1].start()
+    for copy in copies:
+        copy.wait()
 
 
 def per_device_halves(queries, key_rows, value_rows, counts, head_of, out_weight):
@@ -492,7 +514,12 @@
             jax.ShapeDtypeStruct((slot_count, seq_count, row_cap), jnp.float32),
         ],
         in_specs=[vmem] * 8,
-        out_specs=[vmem] * 2,
+        out_specs=[any_spec] * 2,
+        scratch_shapes=[
+            pltpu.VMEM((tok_dev, out_weight.shape[1]), jnp.bfloat16),
+            pltpu.VMEM((slot_count, seq_count, row_cap), jnp.float32),
+            pltpu.SemaphoreType.DMA((3,)),
+        ],
         compiler_params=KERNEL_PARAMS,
         name="project",
     )(*held(total, size, back, partner_back, weight_held, table, pick, slot_head))

time: 23.5 us -> 23.5 us (level)
  no operation moved by 1% of the time
where the time goes in v14:
time: 23.5 us; the launch traced here: 23.2 us
  starting transfers between devices  13.1 us (56%)
  waiting for transfers between devices  5.11 us (22%)
  Pallas kernels  4.29 us (18%)
  between operations  0.69 us (3%)
    ppermute x8, starting transfers between devices, swap_shards(): return lax.ppermute(array, 'seq', pairs)  12.5 us
    ppermute x8, waiting for transfers between devices, swap_shards(): return lax.ppermute(array, 'seq', pairs)  3.91 us
    pallas_call x1, Pallas kernels, per_device_halves(): pl.pallas_call(hold_kernel, out_shape=pltpu.VMEM(out_weight.shape, jnp.bf...  1.63 us
    pallas_call x1, Pallas kernels, per_device_halves(): pl.pallas_call(pack_kernel, out_shape=[pltpu.VMEM((3 * tok_dev, half_widt...  0.92 us
    pallas_call x1, Pallas kernels, per_device_halves(): pl.pallas_call(project_kernel, out_shape=[jax.ShapeDtypeStruct((tok_dev,...  0.91 us
    ppermute x1, waiting for transfers between devices, partner_2(): lax.ppermute(array, axis, [(i, i ^ 1 << stride) for i in range(lax.axis_s...  0.85 us
    ppermute x1, starting transfers between devices, partner_2(): lax.ppermute(array, axis, [(i, i ^ 1 << stride) for i in range(lax.axis_s...  0.59 us
    pallas_call x1, Pallas kernels, per_device_halves(): pl.pallas_call(functools.partial(attend_kernel, len(sets)), out_shape=[pl...  0.54 us
  transfers between devices with their start and end apart: 10, of which 7 were waited for; matrix products, arithmetic and copies ran while one was open for 0% of the time, Pallas kernels for 8%

profile of v14, /device:TPU:0, one launch (start us, length us, event | category | flops | bytes accessed | tf_op | source)
XLA Modules:
  0.0 23.2 jit_solution(4386929663451339634)
XLA Ops:
  0.6 0.9 %pack.1 = (bf16[48,768]{1,0:T(8,128)(2,1)S(1)}, bf16[48,768]{1,0:T(8,128)(2,1)S(1)}, s32[8,128]{1,0:T(8,128)S(1)}, s32[2,8,128]{2,1,0:T(8,128)S(1)}, s32[2,8,128]{2,1,0:T(8,128)S(1)}) custom-call(bf16[1,16,1536]{2,1,0:T(8,128)(2,1)} %query_hbm.1, bf16[1,16,1536]{2,1,0:T(8,128)(2,1)} %key_hbm.1, bf16[1,16,1536]{2,1,0:T(8,128)(2,1)} %value_hbm.1, ...), custom_call_target="tpu_custom_call" | custom-call | tf_op jit(solution)/shard_map/pack/pallas_call | solution.py:444
  1.6 5.1 %collective-permute-start.2 = (bf16[48,768]{1,0:T(8,128)(2,1)S(1)}, bf16[48,768]{1,0:T(8,128)(2,1)S(1)}, u32[]{:S(2)}, u32[]{:S(2)}) collective-permute-start(bf16[48,768]{1,0:T(8,128)(2,1)S(1)} %get-tuple-element.19), channel_id=1, source_target_pairs={{0,12},{2,14},{4,8},{6,10},{8,4},{10,6},{12,0},{14,2},{1,13},{3,15... | collective-permute-start | bytes 221192 | tf_op jit(solution)/shard_map/ppermute | solution.py:176
  6.7 0.0 collective-permute-start
  6.7 0.6 %collective-permute-start.1 = (bf16[48,768]{1,0:T(8,128)(2,1)S(1)}, bf16[48,768]{1,0:T(8,128)(2,1)S(1)}, u32[]{:S(2)}, u32[]{:S(2)}) collective-permute-start(bf16[48,768]{1,0:T(8,128)(2,1)S(1)} %get-tuple-element.18.refs_0_), channel_id=1, source_target_pairs={{0,8},{2,10},{4,12},{6,14},{8,0},{10,2},{12,4},{14,6},{1,9},{3,11}... | collective-permute-start | bytes 221192 | tf_op jit(solution)/shard_map/ppermute | solution.py:176
  7.3 1.6 %collective-permute-start.3 = (bf16[48,768]{1,0:T(8,128)(2,1)S(1)}, bf16[48,768]{1,0:T(8,128)(2,1)S(1)}, u32[]{:S(2)}, u32[]{:S(2)}) collective-permute-start(bf16[48,768]{1,0:T(8,128)(2,1)S(1)} %get-tuple-element.18.refs_0_), channel_id=1, source_target_pairs={{0,2},{2,0},{4,6},{6,4},{8,10},{10,8},{12,14},{14,12},{1,3},{3,1},... | collective-permute-start | bytes 221192 | tf_op jit(solution)/shard_map/ppermute | solution.py:176
  9.0 0.9 %collective-permute-done.2.refs_3_ = bf16[48,768]{1,0:T(8,128)(2,1)S(1)} collective-permute-done((bf16[48,768]{1,0:T(8,128)(2,1)S(1)}, bf16[48,768]{1,0:T(8,128)(2,1)S(1)}, u32[]{:S(2)}, u32[]{:S(2)}) %collective-permute-start.2) | collective-permute-done | bytes 73760 | tf_op jit(solution)/shard_map/ppermute | solution.py:176
  9.8 1.5 %collective-permute-start.6 = (bf16[48,768]{1,0:T(8,128)(2,1)S(1)}, bf16[48,768]{1,0:T(8,128)(2,1)S(1)}, u32[]{:S(2)}, u32[]{:S(2)}) collective-permute-start(bf16[48,768]{1,0:T(8,128)(2,1)S(1)} %collective-permute-done.2.refs_3_), channel_id=1, source_target_pairs={{0,2},{2,0},{4,6},{6,4},{8,10},{10,8},{12,14},{14,12},{1,3},{3,1},... | collective-permute-start | bytes 221192 | tf_op jit(solution)/shard_map/ppermute | solution.py:176
  11.3 0.4 %collective-permute-done.refs_1_ = bf16[48,768]{1,0:T(8,128)(2,1)S(1)} collective-permute-done((bf16[48,768]{1,0:T(8,128)(2,1)S(1)}, bf16[48,768]{1,0:T(8,128)(2,1)S(1)}, u32[]{:S(2)}, u32[]{:S(2)}) %collective-permute-start) | collective-permute-done | bytes 73760 | tf_op jit(solution)/shard_map/ppermute | solution.py:176
  11.7 1.6 %collective-permute-start.4 = (bf16[48,768]{1,0:T(8,128)(2,1)S(1)}, bf16[48,768]{1,0:T(8,128)(2,1)S(1)}, u32[]{:S(2)}, u32[]{:S(2)}) collective-permute-start(bf16[48,768]{1,0:T(8,128)(2,1)S(1)} %collective-permute-done.refs_1_), channel_id=1, source_target_pairs={{0,2},{2,0},{4,6},{6,4},{8,10},{10,8},{12,14},{14,12},{1,3},{3,1},... | collective-permute-start | bytes 221192 | tf_op jit(solution)/shard_map/ppermute | solution.py:176
  13.4 0.0 collective-permute-done.1.refs_2_
  13.4 0.7 %collective-permute-start.5 = (bf16[48,768]{1,0:T(8,128)(2,1)S(1)}, bf16[48,768]{1,0:T(8,128)(2,1)S(1)}, u32[]{:S(2)}, u32[]{:S(2)}) collective-permute-start(bf16[48,768]{1,0:T(8,128)(2,1)S(1)} %collective-permute-done.1.refs_2_), channel_id=1, source_target_pairs={{0,2},{2,0},{4,6},{6,4},{8,10},{10,8},{12,14},{14,12},{1,3},{3,1},... | collective-permute-start | bytes 221192 | tf_op jit(solution)/shard_map/ppermute | solution.py:176
  14.1 1.6 %hold.1.weight_ref = bf16[1536,768]{1,0:T(8,128)(2,1)S(1)} custom-call(bf16[1536,768]{1,0:T(8,128)(2,1)} %weight_hbm.1, s32[8,128]{1,0:T(8,128)S(1)} %get-tuple-element.17.after_ref.limits_ref), custom_call_target="tpu_custom_call" | custom-call | bytes 4718592 | tf_op jit(solution)/shard_map/hold/pallas_call | solution.py:464
  15.7 0.0 collective-permute-done.3.refs_4_
  15.7 0.0 collective-permute-done.6.refs_7_
  15.7 1.1 %collective-permute-done.4.refs_5_ = bf16[48,768]{1,0:T(8,128)(2,1)S(1)} collective-permute-done((bf16[48,768]{1,0:T(8,128)(2,1)S(1)}, bf16[48,768]{1,0:T(8,128)(2,1)S(1)}, u32[]{:S(2)}, u32[]{:S(2)}) %collective-permute-start.4) | collective-permute-done | bytes 73760 | tf_op jit(solution)/shard_map/ppermute | solution.py:176
  16.8 0.9 %collective-permute-done.5.refs_6_ = bf16[48,768]{1,0:T(8,128)(2,1)S(1)} collective-permute-done((bf16[48,768]{1,0:T(8,128)(2,1)S(1)}, bf16[48,768]{1,0:T(8,128)(2,1)S(1)}, u32[]{:S(2)}, u32[]{:S(2)}) %collective-permute-start.5) | collective-permute-done | bytes 73760 | tf_op jit(solution)/shard_map/ppermute | solution.py:176
  17.7 0.5 %attend.1 = (bf16[16,768]{1,0:T(8,128)(2,1)S(1)}, bf16[16,896]{1,0:T(8,128)(2,1)S(1)}, f32[8,128]{1,0:T(8,128)S(1)}) custom-call(s32[8,128]{1,0:T(8,128)S(1)} %get-tuple-element.17.after_ref.limits_ref, bf16[48,768]{1,0:T(8,128)(2,1)S(1)} %get-tuple-element.18.refs_0_, bf16[48,768]{1,0:T(8,128)(2,1)S(1)} %collective-permute-done.refs_1_, ...), custom_call_target="tpu_custom_call" | custom-call | tf_op jit(solution)/shard_map/attend/pallas_call | solution.py:482
  18.3 0.1 collective-permute-start.9
  18.3 1.3 %collective-permute-start.8 = (bf16[16,896]{1,0:T(8,128)(2,1)S(1)}, bf16[16,896]{1,0:T(8,128)(2,1)S(1)}, u32[]{:S(2)}, u32[]{:S(2)}) collective-permute-start(bf16[16,896]{1,0:T(8,128)(2,1)S(1)} %get-tuple-element.24), channel_id=1, source_target_pairs={{0,4},{2,6},{4,0},{6,2},{8,12},{10,14},{12,8},{14,10},{1,5},{3,7},... | collective-permute-start | bytes 86024 | tf_op jit(solution)/shard_map/ppermute | solution.py:176
  19.6 0.6 %collective-permute-start.7 = (bf16[16,768]{1,0:T(8,128)(2,1)S(1)}, bf16[16,768]{1,0:T(8,128)(2,1)S(1)}, u32[]{:S(2)}, u32[]{:S(2)}) collective-permute-start(bf16[16,768]{1,0:T(8,128)(2,1)S(1)} %get-tuple-element.20.keep_ref), channel_id=1, source_target_pairs={{0,1},{1,0},{2,3},{3,2},{4,5},{5,4},{6,7},{7,6},{8,9},{9,8},{10,11... | collective-permute-start | bytes 73736 | tf_op jit(solution)/shard_map/ppermute | solution.py:20
  20.2 0.8 %collective-permute-done.7.partner_keep_ref = bf16[16,768]{1,0:T(8,128)(2,1)S(1)} collective-permute-done((bf16[16,768]{1,0:T(8,128)(2,1)S(1)}, bf16[16,768]{1,0:T(8,128)(2,1)S(1)}, u32[]{:S(2)}, u32[]{:S(2)}) %collective-permute-start.7) | collective-permute-done | bytes 24608 | tf_op jit(solution)/shard_map/ppermute | solution.py:20
  21.0 0.3 %keep.1 = (f32[16,768]{1,0:T(8,128)S(1)}, f32[16,128]{1,0:T(8,128)S(1)}) custom-call(bf16[16,768]{1,0:T(8,128)(2,1)S(1)} %get-tuple-element.20.keep_ref, bf16[16,768]{1,0:T(8,128)(2,1)S(1)} %collective-permute-done.7.partner_keep_ref, bf16[1536,768]{1,0:T(8,128)(2,1)S(1)} %hold.1.weight_ref), custom_call_target="tpu_custom_call" | custom-call | tf_op jit(solution)/shard_map/keep/pallas_call | solution.py:499
  21.3 0.4 %collective-permute-done.9.partner_back_ref = bf16[16,896]{1,0:T(8,128)(2,1)S(1)} collective-permute-done((bf16[16,896]{1,0:T(8,128)(2,1)S(1)}, bf16[16,896]{1,0:T(8,128)(2,1)S(1)}, u32[]{:S(2)}, u32[]{:S(2)}) %collective-permute-start.9) | collective-permute-done | bytes 28704 | tf_op jit(solution)/shard_map/ppermute | solution.py:496
  21.7 0.6 %collective-permute-done.8.message_ref = bf16[16,896]{1,0:T(8,128)(2,1)S(1)} collective-permute-done((bf16[16,896]{1,0:T(8,128)(2,1)S(1)}, bf16[16,896]{1,0:T(8,128)(2,1)S(1)}, u32[]{:S(2)}, u32[]{:S(2)}) %collective-permute-start.8) | collective-permute-done | bytes 28704 | tf_op jit(solution)/shard_map/ppermute | solution.py:176
  22.3 0.9 %project.1 = (bf16[16,768]{1,0:T(8,128)(2,1)}, f32[2,8,16]{2,1,0:T(8,128)}) custom-call(f32[16,768]{1,0:T(8,128)S(1)} %get-tuple-element.22.total_ref, f32[16,128]{1,0:T(8,128)S(1)} %get-tuple-element.23.size_ref, bf16[16,896]{1,0:T(8,128)(2,1)S(1)} %collective-permute-done.8.message_ref, bf16[16,896]{1,0:T(8,128)(2,1)S(1)} %collective-permute-done.9.partner_back_ref, ...), custom_call_target="tpu_custom_call" | custom-call | tf_op jit(solution)/shard_map/project/pallas_call | solution.py:510
Async XLA Ops:
  1.6 8.3 %collective-permute-start.2 = (bf16[48,768]{1,0:T(8,128)(2,1)S(1)}, bf16[48,768]{1,0:T(8,128)(2,1)S(1)}, u32[]{:S(2)}, u32[]{:S(2)}) collective-permute-start(bf16[48,768]{1,0:T(8,128)(2,1)S(1)} %get-tuple-element.19), channel_id=1, source_target_pairs={{0,12},{2,14},{4,8},{6,10},{8,4},{10,6},{12,0},{14,2},{1,13},{3,15... | collective-permute-start | bytes 221192 | tf_op jit(solution)/shard_map/ppermute | solution.py:176
  6.7 5.0 %collective-permute-start = (bf16[48,768]{1,0:T(8,128)(2,1)S(1)}, bf16[48,768]{1,0:T(8,128)(2,1)S(1)}, u32[]{:S(2)}, u32[]{:S(2)}) collective-permute-start(bf16[48,768]{1,0:T(8,128)(2,1)S(1)} %get-tuple-element.19), channel_id=1, source_target_pairs={{0,4},{2,6},{4,0},{6,2},{8,12},{10,14},{12,8},{14,10},{1,5},{3,7},... | collective-permute-start | bytes 221192 | tf_op jit(solution)/shard_map/ppermute | solution.py:176
  6.7 6.7 %collective-permute-start.1 = (bf16[48,768]{1,0:T(8,128)(2,1)S(1)}, bf16[48,768]{1,0:T(8,128)(2,1)S(1)}, u32[]{:S(2)}, u32[]{:S(2)}) collective-permute-start(bf16[48,768]{1,0:T(8,128)(2,1)S(1)} %get-tuple-element.18.refs_0_), channel_id=1, source_target_pairs={{0,8},{2,10},{4,12},{6,14},{8,0},{10,2},{12,4},{14,6},{1,9},{3,11}... | collective-permute-start | bytes 221192 | tf_op jit(solution)/shard_map/ppermute | solution.py:176
  7.3 8.4 %collective-permute-start.3 = (bf16[48,768]{1,0:T(8,128)(2,1)S(1)}, bf16[48,768]{1,0:T(8,128)(2,1)S(1)}, u32[]{:S(2)}, u32[]{:S(2)}) collective-permute-start(bf16[48,768]{1,0:T(8,128)(2,1)S(1)} %get-tuple-element.18.refs_0_), channel_id=1, source_target_pairs={{0,2},{2,0},{4,6},{6,4},{8,10},{10,8},{12,14},{14,12},{1,3},{3,1},... | collective-permute-start | bytes 221192 | tf_op jit(solution)/shard_map/ppermute | solution.py:176
  9.8 5.9 %collective-permute-start.6 = (bf16[48,768]{1,0:T(8,128)(2,1)S(1)}, bf16[48,768]{1,0:T(8,128)(2,1)S(1)}, u32[]{:S(2)}, u32[]{:S(2)}) collective-permute-start(bf16[48,768]{1,0:T(8,128)(2,1)S(1)} %collective-permute-done.2.refs_3_), channel_id=1, source_target_pairs={{0,2},{2,0},{4,6},{6,4},{8,10},{10,8},{12,14},{14,12},{1,3},{3,1},... | collective-permute-start | bytes 221192 | tf_op jit(solution)/shard_map/ppermute | solution.py:176
  11.7 5.1 %collective-permute-start.4 = (bf16[48,768]{1,0:T(8,128)(2,1)S(1)}, bf16[48,768]{1,0:T(8,128)(2,1)S(1)}, u32[]{:S(2)}, u32[]{:S(2)}) collective-permute-start(bf16[48,768]{1,0:T(8,128)(2,1)S(1)} %collective-permute-done.refs_1_), channel_id=1, source_target_pairs={{0,2},{2,0},{4,6},{6,4},{8,10},{10,8},{12,14},{14,12},{1,3},{3,1},... | collective-permute-start | bytes 221192 | tf_op jit(solution)/shard_map/ppermute | solution.py:176
  13.4 4.4 %collective-permute-start.5 = (bf16[48,768]{1,0:T(8,128)(2,1)S(1)}, bf16[48,768]{1,0:T(8,128)(2,1)S(1)}, u32[]{:S(2)}, u32[]{:S(2)}) collective-permute-start(bf16[48,768]{1,0:T(8,128)(2,1)S(1)} %collective-permute-done.1.refs_2_), channel_id=1, source_target_pairs={{0,2},{2,0},{4,6},{6,4},{8,10},{10,8},{12,14},{14,12},{1,3},{3,1},... | collective-permute-start | bytes 221192 | tf_op jit(solution)/shard_map/ppermute | solution.py:176
  18.3 3.4 %collective-permute-start.9 = (bf16[16,896]{1,0:T(8,128)(2,1)S(1)}, bf16[16,896]{1,0:T(8,128)(2,1)S(1)}, u32[]{:S(2)}, u32[]{:S(2)}) collective-permute-start(bf16[16,896]{1,0:T(8,128)(2,1)S(1)} %get-tuple-element.24), channel_id=1, source_target_pairs={{0,5},{1,4},{2,7},{3,6},{4,1},{5,0},{6,3},{7,2},{8,13},{9,12},{10,... | collective-permute-start | bytes 86024 | tf_op jit(solution)/shard_map/ppermute | solution.py:496
  18.3 4.0 %collective-permute-start.8 = (bf16[16,896]{1,0:T(8,128)(2,1)S(1)}, bf16[16,896]{1,0:T(8,128)(2,1)S(1)}, u32[]{:S(2)}, u32[]{:S(2)}) collective-permute-start(bf16[16,896]{1,0:T(8,128)(2,1)S(1)} %get-tuple-element.24), channel_id=1, source_target_pairs={{0,4},{2,6},{4,0},{6,2},{8,12},{10,14},{12,8},{14,10},{1,5},{3,7},... | collective-permute-start | bytes 86024 | tf_op jit(solution)/shard_map/ppermute | solution.py:176
  19.6 1.4 %collective-permute-start.7 = (bf16[16,768]{1,0:T(8,128)(2,1)S(1)}, bf16[16,768]{1,0:T(8,128)(2,1)S(1)}, u32[]{:S(2)}, u32[]{:S(2)}) collective-permute-start(bf16[16,768]{1,0:T(8,128)(2,1)S(1)} %get-tuple-element.20.keep_ref), channel_id=1, source_target_pairs={{0,1},{1,0},{2,3},{3,2},{4,5},{5,4},{6,7},{7,6},{8,9},{9,8},{10,11... | collective-permute-start | bytes 73736 | tf_op jit(solution)/shard_map/ppermute | solution.py:20

commit v15 on v9

--- a/solution.py
+++ b/solution.py
@@ -167,7 +167,7 @@
 
 SPLIT = 2
 WEIGHT_COPIES = 4
-TABLE_PIECES = 3
+TABLE_PIECES = 2
 SPLITTER = 65537.0
 
 

time: 23.5 us -> 23.4 us (level)
  no operation moved by 1% of the time
where the time goes in v15:
time: 23.4 us; the launch traced here: 23.2 us
  starting transfers between devices  13.1 us (56%)
  waiting for transfers between devices  5.09 us (22%)
  Pallas kernels  4.29 us (18%)
  between operations  0.69 us (3%)
    ppermute x8, starting transfers between devices, swap_shards(): return lax.ppermute(array, 'seq', pairs)  12.5 us
    ppermute x8, waiting for transfers between devices, swap_shards(): return lax.ppermute(array, 'seq', pairs)  3.89 us
    pallas_call x1, Pallas kernels, per_device_halves(): pl.pallas_call(plan_kernel, out_shape=[pltpu.VMEM(out_weight.shape, jnp.b...  1.65 us
    pallas_call x1, Pallas kernels, per_device_halves(): pl.pallas_call(project_kernel, out_shape=[jax.ShapeDtypeStruct((tok_dev,...  0.92 us
    pallas_call x1, Pallas kernels, per_device_halves(): pl.pallas_call(pack_kernel, out_shape=[pltpu.VMEM((3 * tok_dev, half_widt...  0.9 us
    ppermute x1, waiting for transfers between devices, partner_2(): lax.ppermute(array, axis, [(i, i ^ 1 << stride) for i in range(lax.axis_s...  0.85 us
    ppermute x1, starting transfers between devices, partner_2(): lax.ppermute(array, axis, [(i, i ^ 1 << stride) for i in range(lax.axis_s...  0.59 us
    pallas_call x1, Pallas kernels, per_device_halves(): pl.pallas_call(functools.partial(attend_kernel, len(sets)), out_shape=[pl...  0.54 us
  transfers between devices with their start and end apart: 10, of which 7 were waited for; matrix products, arithmetic and copies ran while one was open for 0% of the time, Pallas kernels for 8%

profile of v15, /device:TPU:0, one launch (start us, length us, event | category | flops | bytes accessed | tf_op | source)
XLA Modules:
  0.0 23.2 jit_solution(982837835927172172)
XLA Ops:
  0.6 0.9 %pack.1 = (bf16[48,768]{1,0:T(8,128)(2,1)S(1)}, bf16[48,768]{1,0:T(8,128)(2,1)S(1)}) custom-call(bf16[1,16,1536]{2,1,0:T(8,128)(2,1)} %query_hbm.1, bf16[1,16,1536]{2,1,0:T(8,128)(2,1)} %key_hbm.1, bf16[1,16,1536]{2,1,0:T(8,128)(2,1)} %value_hbm.1), custom_call_target="tpu_custom_call" | custom-call | tf_op jit(solution)/shard_map/pack/pallas_call | solution.py:421
  1.5 5.1 %collective-permute-start.2 = (bf16[48,768]{1,0:T(8,128)(2,1)S(1)}, bf16[48,768]{1,0:T(8,128)(2,1)S(1)}, u32[]{:S(2)}, u32[]{:S(2)}) collective-permute-start(bf16[48,768]{1,0:T(8,128)(2,1)S(1)} %get-tuple-element.17), channel_id=1, source_target_pairs={{0,12},{2,14},{4,8},{6,10},{8,4},{10,6},{12,0},{14,2},{1,13},{3,15... | collective-permute-start | bytes 221192 | tf_op jit(solution)/shard_map/ppermute | solution.py:176
  6.7 0.0 collective-permute-start
  6.7 0.6 %collective-permute-start.1 = (bf16[48,768]{1,0:T(8,128)(2,1)S(1)}, bf16[48,768]{1,0:T(8,128)(2,1)S(1)}, u32[]{:S(2)}, u32[]{:S(2)}) collective-permute-start(bf16[48,768]{1,0:T(8,128)(2,1)S(1)} %get-tuple-element.15.after_ref.refs_0_), channel_id=1, source_target_pairs={{0,8},{2,10},{4,12},{6,14},{8,0},{10,2},{12,4},{14,6},{1,9},{3,11}... | collective-permute-start | bytes 221192 | tf_op jit(solution)/shard_map/ppermute | solution.py:176
  7.3 1.6 %collective-permute-start.3 = (bf16[48,768]{1,0:T(8,128)(2,1)S(1)}, bf16[48,768]{1,0:T(8,128)(2,1)S(1)}, u32[]{:S(2)}, u32[]{:S(2)}) collective-permute-start(bf16[48,768]{1,0:T(8,128)(2,1)S(1)} %get-tuple-element.15.after_ref.refs_0_), channel_id=1, source_target_pairs={{0,2},{2,0},{4,6},{6,4},{8,10},{10,8},{12,14},{14,12},{1,3},{3,1},... | collective-permute-start | bytes 221192 | tf_op jit(solution)/shard_map/ppermute | solution.py:176
  8.9 0.9 %collective-permute-done.2.refs_3_ = bf16[48,768]{1,0:T(8,128)(2,1)S(1)} collective-permute-done((bf16[48,768]{1,0:T(8,128)(2,1)S(1)}, bf16[48,768]{1,0:T(8,128)(2,1)S(1)}, u32[]{:S(2)}, u32[]{:S(2)}) %collective-permute-start.2) | collective-permute-done | bytes 73760 | tf_op jit(solution)/shard_map/ppermute | solution.py:176
  9.8 1.5 %collective-permute-start.6 = (bf16[48,768]{1,0:T(8,128)(2,1)S(1)}, bf16[48,768]{1,0:T(8,128)(2,1)S(1)}, u32[]{:S(2)}, u32[]{:S(2)}) collective-permute-start(bf16[48,768]{1,0:T(8,128)(2,1)S(1)} %collective-permute-done.2.refs_3_), channel_id=1, source_target_pairs={{0,2},{2,0},{4,6},{6,4},{8,10},{10,8},{12,14},{14,12},{1,3},{3,1},... | collective-permute-start | bytes 221192 | tf_op jit(solution)/shard_map/ppermute | solution.py:176
  11.3 0.4 %collective-permute-done.refs_1_ = bf16[48,768]{1,0:T(8,128)(2,1)S(1)} collective-permute-done((bf16[48,768]{1,0:T(8,128)(2,1)S(1)}, bf16[48,768]{1,0:T(8,128)(2,1)S(1)}, u32[]{:S(2)}, u32[]{:S(2)}) %collective-permute-start) | collective-permute-done | bytes 73760 | tf_op jit(solution)/shard_map/ppermute | solution.py:176
  11.7 1.6 %collective-permute-start.4 = (bf16[48,768]{1,0:T(8,128)(2,1)S(1)}, bf16[48,768]{1,0:T(8,128)(2,1)S(1)}, u32[]{:S(2)}, u32[]{:S(2)}) collective-permute-start(bf16[48,768]{1,0:T(8,128)(2,1)S(1)} %collective-permute-done.refs_1_), channel_id=1, source_target_pairs={{0,2},{2,0},{4,6},{6,4},{8,10},{10,8},{12,14},{14,12},{1,3},{3,1},... | collective-permute-start | bytes 221192 | tf_op jit(solution)/shard_map/ppermute | solution.py:176
  13.3 0.0 collective-permute-done.1.refs_2_
  13.3 0.7 %collective-permute-start.5 = (bf16[48,768]{1,0:T(8,128)(2,1)S(1)}, bf16[48,768]{1,0:T(8,128)(2,1)S(1)}, u32[]{:S(2)}, u32[]{:S(2)}) collective-permute-start(bf16[48,768]{1,0:T(8,128)(2,1)S(1)} %collective-permute-done.1.refs_2_), channel_id=1, source_target_pairs={{0,2},{2,0},{4,6},{6,4},{8,10},{10,8},{12,14},{14,12},{1,3},{3,1},... | collective-permute-start | bytes 221192 | tf_op jit(solution)/shard_map/ppermute | solution.py:176
  14.1 1.6 %plan.1 = (bf16[1536,768]{1,0:T(8,128)(2,1)S(1)}, s32[8,128]{1,0:T(8,128)S(1)}, s32[2,8,128]{2,1,0:T(8,128)S(1)}, s32[2,8,128]{2,1,0:T(8,128)S(1)}) custom-call(bf16[1536,768]{1,0:T(8,128)(2,1)} %weight_hbm.1, s32[8]{0:T(128)} %counts_hbm.1, s32[2,8]{1,0:T(2,128)} %bitcast.4, bf16[48,768]{1,0:T(8,128)(2,1)S(1)} %get-tuple-element.15.after_ref.refs_0_), custom_call_target="tpu_custom_call" | custom-call | bytes 4718592 | tf_op jit(solution)/shard_map/plan/pallas_call | solution.py:430
  15.7 0.0 collective-permute-done.3.refs_4_
  15.7 0.0 collective-permute-done.6.refs_7_
  15.7 1.1 %collective-permute-done.4.refs_5_ = bf16[48,768]{1,0:T(8,128)(2,1)S(1)} collective-permute-done((bf16[48,768]{1,0:T(8,128)(2,1)S(1)}, bf16[48,768]{1,0:T(8,128)(2,1)S(1)}, u32[]{:S(2)}, u32[]{:S(2)}) %collective-permute-start.4) | collective-permute-done | bytes 73760 | tf_op jit(solution)/shard_map/ppermute | solution.py:176
  16.8 0.9 %collective-permute-done.5.refs_6_ = bf16[48,768]{1,0:T(8,128)(2,1)S(1)} collective-permute-done((bf16[48,768]{1,0:T(8,128)(2,1)S(1)}, bf16[48,768]{1,0:T(8,128)(2,1)S(1)}, u32[]{:S(2)}, u32[]{:S(2)}) %collective-permute-start.5) | collective-permute-done | bytes 73760 | tf_op jit(solution)/shard_map/ppermute | solution.py:176
  17.7 0.5 %attend.1 = (bf16[16,768]{1,0:T(8,128)(2,1)S(1)}, bf16[16,896]{1,0:T(8,128)(2,1)S(1)}, f32[8,128]{1,0:T(8,128)S(1)}) custom-call(s32[8,128]{1,0:T(8,128)S(1)} %get-tuple-element.16.limits_ref, bf16[48,768]{1,0:T(8,128)(2,1)S(1)} %get-tuple-element.15.after_ref.refs_0_, bf16[48,768]{1,0:T(8,128)(2,1)S(1)} %collective-permute-done.refs_1_, ...), custom_call_target="tpu_custom_call" | custom-call | tf_op jit(solution)/shard_map/attend/pallas_call | solution.py:456
  18.2 0.1 collective-permute-start.9
  18.3 1.3 %collective-permute-start.8 = (bf16[16,896]{1,0:T(8,128)(2,1)S(1)}, bf16[16,896]{1,0:T(8,128)(2,1)S(1)}, u32[]{:S(2)}, u32[]{:S(2)}) collective-permute-start(bf16[16,896]{1,0:T(8,128)(2,1)S(1)} %get-tuple-element.22), channel_id=1, source_target_pairs={{0,4},{2,6},{4,0},{6,2},{8,12},{10,14},{12,8},{14,10},{1,5},{3,7},... | collective-permute-start | bytes 86024 | tf_op jit(solution)/shard_map/ppermute | solution.py:176
  19.6 0.6 %collective-permute-start.7 = (bf16[16,768]{1,0:T(8,128)(2,1)S(1)}, bf16[16,768]{1,0:T(8,128)(2,1)S(1)}, u32[]{:S(2)}, u32[]{:S(2)}) collective-permute-start(bf16[16,768]{1,0:T(8,128)(2,1)S(1)} %get-tuple-element.18.keep_ref), channel_id=1, source_target_pairs={{0,1},{1,0},{2,3},{3,2},{4,5},{5,4},{6,7},{7,6},{8,9},{9,8},{10,11... | collective-permute-start | bytes 73736 | tf_op jit(solution)/shard_map/ppermute | solution.py:20
  20.2 0.8 %collective-permute-done.7.partner_keep_ref = bf16[16,768]{1,0:T(8,128)(2,1)S(1)} collective-permute-done((bf16[16,768]{1,0:T(8,128)(2,1)S(1)}, bf16[16,768]{1,0:T(8,128)(2,1)S(1)}, u32[]{:S(2)}, u32[]{:S(2)}) %collective-permute-start.7) | collective-permute-done | bytes 24608 | tf_op jit(solution)/shard_map/ppermute | solution.py:20
  21.0 0.3 %keep.1 = (f32[16,768]{1,0:T(8,128)S(1)}, f32[16,128]{1,0:T(8,128)S(1)}) custom-call(bf16[16,768]{1,0:T(8,128)(2,1)S(1)} %get-tuple-element.18.keep_ref, bf16[16,768]{1,0:T(8,128)(2,1)S(1)} %collective-permute-done.7.partner_keep_ref, bf16[1536,768]{1,0:T(8,128)(2,1)S(1)} %get-tuple-element.19.weight_ref), custom_call_target="tpu_custom_call" | custom-call | tf_op jit(solution)/shard_map/keep/pallas_call | solution.py:473
  21.3 0.4 %collective-permute-done.9.partner_back_ref = bf16[16,896]{1,0:T(8,128)(2,1)S(1)} collective-permute-done((bf16[16,896]{1,0:T(8,128)(2,1)S(1)}, bf16[16,896]{1,0:T(8,128)(2,1)S(1)}, u32[]{:S(2)}, u32[]{:S(2)}) %collective-permute-start.9) | collective-permute-done | bytes 28704 | tf_op jit(solution)/shard_map/ppermute | solution.py:470
  21.7 0.6 %collective-permute-done.8.message_ref = bf16[16,896]{1,0:T(8,128)(2,1)S(1)} collective-permute-done((bf16[16,896]{1,0:T(8,128)(2,1)S(1)}, bf16[16,896]{1,0:T(8,128)(2,1)S(1)}, u32[]{:S(2)}, u32[]{:S(2)}) %collective-permute-start.8) | collective-permute-done | bytes 28704 | tf_op jit(solution)/shard_map/ppermute | solution.py:176
  22.3 0.9 %project.1 = (bf16[16,768]{1,0:T(8,128)(2,1)}, f32[2,8,16]{2,1,0:T(8,128)}) custom-call(f32[16,768]{1,0:T(8,128)S(1)} %get-tuple-element.20.total_ref, f32[16,128]{1,0:T(8,128)S(1)} %get-tuple-element.21.size_ref, bf16[16,896]{1,0:T(8,128)(2,1)S(1)} %collective-permute-done.8.message_ref, bf16[16,896]{1,0:T(8,128)(2,1)S(1)} %collective-permute-done.9.partner_back_ref, ...), custom_call_target="tpu_custom_call" | custom-call | tf_op jit(solution)/shard_map/project/pallas_call | solution.py:484
Async XLA Ops:
  1.5 8.3 %collective-permute-start.2 = (bf16[48,768]{1,0:T(8,128)(2,1)S(1)}, bf16[48,768]{1,0:T(8,128)(2,1)S(1)}, u32[]{:S(2)}, u32[]{:S(2)}) collective-permute-start(bf16[48,768]{1,0:T(8,128)(2,1)S(1)} %get-tuple-element.17), channel_id=1, source_target_pairs={{0,12},{2,14},{4,8},{6,10},{8,4},{10,6},{12,0},{14,2},{1,13},{3,15... | collective-permute-start | bytes 221192 | tf_op jit(solution)/shard_map/ppermute | solution.py:176
  6.7 5.0 %collective-permute-start = (bf16[48,768]{1,0:T(8,128)(2,1)S(1)}, bf16[48,768]{1,0:T(8,128)(2,1)S(1)}, u32[]{:S(2)}, u32[]{:S(2)}) collective-permute-start(bf16[48,768]{1,0:T(8,128)(2,1)S(1)} %get-tuple-element.17), channel_id=1, source_target_pairs={{0,4},{2,6},{4,0},{6,2},{8,12},{10,14},{12,8},{14,10},{1,5},{3,7},... | collective-permute-start | bytes 221192 | tf_op jit(solution)/shard_map/ppermute | solution.py:176
  6.7 6.7 %collective-permute-start.1 = (bf16[48,768]{1,0:T(8,128)(2,1)S(1)}, bf16[48,768]{1,0:T(8,128)(2,1)S(1)}, u32[]{:S(2)}, u32[]{:S(2)}) collective-permute-start(bf16[48,768]{1,0:T(8,128)(2,1)S(1)} %get-tuple-element.15.after_ref.refs_0_), channel_id=1, source_target_pairs={{0,8},{2,10},{4,12},{6,14},{8,0},{10,2},{12,4},{14,6},{1,9},{3,11}... | collective-permute-start | bytes 221192 | tf_op jit(solution)/shard_map/ppermute | solution.py:176
  7.3 8.4 %collective-permute-start.3 = (bf16[48,768]{1,0:T(8,128)(2,1)S(1)}, bf16[48,768]{1,0:T(8,128)(2,1)S(1)}, u32[]{:S(2)}, u32[]{:S(2)}) collective-permute-start(bf16[48,768]{1,0:T(8,128)(2,1)S(1)} %get-tuple-element.15.after_ref.refs_0_), channel_id=1, source_target_pairs={{0,2},{2,0},{4,6},{6,4},{8,10},{10,8},{12,14},{14,12},{1,3},{3,1},... | collective-permute-start | bytes 221192 | tf_op jit(solution)/shard_map/ppermute | solution.py:176
  9.8 5.9 %collective-permute-start.6 = (bf16[48,768]{1,0:T(8,128)(2,1)S(1)}, bf16[48,768]{1,0:T(8,128)(2,1)S(1)}, u32[]{:S(2)}, u32[]{:S(2)}) collective-permute-start(bf16[48,768]{1,0:T(8,128)(2,1)S(1)} %collective-permute-done.2.refs_3_), channel_id=1, source_target_pairs={{0,2},{2,0},{4,6},{6,4},{8,10},{10,8},{12,14},{14,12},{1,3},{3,1},... | collective-permute-start | bytes 221192 | tf_op jit(solution)/shard_map/ppermute | solution.py:176
  11.7 5.1 %collective-permute-start.4 = (bf16[48,768]{1,0:T(8,128)(2,1)S(1)}, bf16[48,768]{1,0:T(8,128)(2,1)S(1)}, u32[]{:S(2)}, u32[]{:S(2)}) collective-permute-start(bf16[48,768]{1,0:T(8,128)(2,1)S(1)} %collective-permute-done.refs_1_), channel_id=1, source_target_pairs={{0,2},{2,0},{4,6},{6,4},{8,10},{10,8},{12,14},{14,12},{1,3},{3,1},... | collective-permute-start | bytes 221192 | tf_op jit(solution)/shard_map/ppermute | solution.py:176
  13.3 4.4 %collective-permute-start.5 = (bf16[48,768]{1,0:T(8,128)(2,1)S(1)}, bf16[48,768]{1,0:T(8,128)(2,1)S(1)}, u32[]{:S(2)}, u32[]{:S(2)}) collective-permute-start(bf16[48,768]{1,0:T(8,128)(2,1)S(1)} %collective-permute-done.1.refs_2_), channel_id=1, source_target_pairs={{0,2},{2,0},{4,6},{6,4},{8,10},{10,8},{12,14},{14,12},{1,3},{3,1},... | collective-permute-start | bytes 221192 | tf_op jit(solution)/shard_map/ppermute | solution.py:176
  18.2 3.4 %collective-permute-start.9 = (bf16[16,896]{1,0:T(8,128)(2,1)S(1)}, bf16[16,896]{1,0:T(8,128)(2,1)S(1)}, u32[]{:S(2)}, u32[]{:S(2)}) collective-permute-start(bf16[16,896]{1,0:T(8,128)(2,1)S(1)} %get-tuple-element.22), channel_id=1, source_target_pairs={{0,5},{1,4},{2,7},{3,6},{4,1},{5,0},{6,3},{7,2},{8,13},{9,12},{10,... | collective-permute-start | bytes 86024 | tf_op jit(solution)/shard_map/ppermute | solution.py:470
  18.3 4.0 %collective-permute-start.8 = (bf16[16,896]{1,0:T(8,128)(2,1)S(1)}, bf16[16,896]{1,0:T(8,128)(2,1)S(1)}, u32[]{:S(2)}, u32[]{:S(2)}) collective-permute-start(bf16[16,896]{1,0:T(8,128)(2,1)S(1)} %get-tuple-element.22), channel_id=1, source_target_pairs={{0,4},{2,6},{4,0},{6,2},{8,12},{10,14},{12,8},{14,10},{1,5},{3,7},... | collective-permute-start | bytes 86024 | tf_op jit(solution)/shard_map/ppermute | solution.py:176
  19.6 1.4 %collective-permute-start.7 = (bf16[16,768]{1,0:T(8,128)(2,1)S(1)}, bf16[16,768]{1,0:T(8,128)(2,1)S(1)}, u32[]{:S(2)}, u32[]{:S(2)}) collective-permute-start(bf16[16,768]{1,0:T(8,128)(2,1)S(1)} %get-tuple-element.18.keep_ref), channel_id=1, source_target_pairs={{0,1},{1,0},{2,3},{3,2},{4,5},{5,4},{6,7},{7,6},{8,9},{9,8},{10,11... | collective-permute-start | bytes 73736 | tf_op jit(solution)/shard_map/ppermute | solution.py:20
